TPU v7x, 128 devices: a whole 4x4x4 slice. The times are simulated.
128 devices in a mesh: brow: 16 (over x_hi, y, core), bcol: 8 (over x_lo, z).
Axes of the slice: x: 4 (x_hi: 2, x_lo: 2; x = x_hi * 2 + x_lo), y: 4, z: 4, core: 2. Of those that a mesh axis runs over, the one named last changes fastest.
Arguments:
- patterns: bfloat16 [2048, 16384], P(('brow', 'bcol')), may hold values from -70 to 70
- components: float32 [16384, 256], P('bcol'), may hold values from -0.046875 to 0.046875
Outputs:
- covariance: float32 [16384, 16384], P('brow', 'bcol')
- projected: float32 [16384, 256], P(('brow', 'bcol'))
- column_means: float32 [16384], P(('brow', 'bcol'))
All inputs are finite; a program needn't handle non-finite values.
Results may differ from a plain program's by a relative error of at most 0.0003.
Values may be sent and summed in bfloat16 or wider, within the bound.
No kernel may reach another device: no remote copies, remote signals or barrier semaphores. Data moves between devices by JAX's collectives and lax.ppermute only.
A program may use at most 128 MiB of HBM per device.

v0:
```python
import jax
import jax.numpy as jnp
from jax import lax
from jax.sharding import PartitionSpec as P


def on_device(patterns, components):
    brow_size = lax.axis_size("brow")
    bcol_size = lax.axis_size("bcol")
    local_rows, pixels = patterns.shape
    block_width = pixels // brow_size
    share_width = pixels // bcol_size
    means_width = pixels // (brow_size * bcol_size)
    total_rows = local_rows * brow_size * bcol_size
    row_index = lax.axis_index("brow")
    col_index = lax.axis_index("bcol")
    column_sums = lax.psum(jnp.sum(patterns, axis=0, dtype=jnp.float32), ("brow", "bcol"))
    column_means = column_sums / total_rows
    row_means = lax.dynamic_slice_in_dim(column_means, row_index * block_width, block_width, 0)
    share_means = lax.dynamic_slice_in_dim(column_means, col_index * share_width, share_width, 0)
    flat_index = row_index * bcol_size + col_index
    means_part = lax.dynamic_slice_in_dim(column_means, flat_index * means_width, means_width, 0)
    row_local = lax.all_to_all(patterns, "brow", split_axis=1, concat_axis=0, tiled=True)
    row_panel = lax.all_gather(row_local, "bcol", axis=0, tiled=True)
    row_grid = row_panel.reshape(bcol_size, brow_size, local_rows, block_width)
    col_local = lax.all_to_all(patterns, "bcol", split_axis=1, concat_axis=0, tiled=True)
    group_rows = bcol_size * local_rows
    segment = lax.all_gather(col_local, "brow", axis=0, tiled=True)
    groups = segment.shape[0] // group_rows
    shaped = segment.reshape(groups, bcol_size, local_rows, share_width)
    gram_block = lax.dot_general(
        row_grid, shaped, (((0, 1, 2), (1, 0, 2)), ((), ())), preferred_element_type=jnp.float32
    )
    covariance = (gram_block - total_rows * row_means[:, None] * share_means[None, :]) / (
        total_rows - 1
    )
    projected = lax.psum_scatter(
        jnp.dot(
            covariance,
            components,
            precision=lax.Precision.HIGHEST,
            preferred_element_type=jnp.float32,
        ),
        "bcol",
        scatter_dimension=0,
        tiled=True,
    )
    return (covariance, projected, means_part)


def solution(mesh):
    return jax.shard_map(
        on_device,
        mesh=mesh,
        in_specs=(P(("brow", "bcol"), None), P("bcol", None)),
        out_specs=(P("brow", "bcol"), P(("brow", "bcol"), None), P(("brow", "bcol"))),
        check_vma=False,
    )
```

profile of v0, /device:TPU:1, one launch (start us, length us, event | category | flops | bytes accessed | tf_op | source)
XLA Modules:
  0.0 267.8 jit_solution(12622617548363878391)
XLA Ops:
  8.0 0.0 copy-start
  8.0 2.0 copy.26
  10.0 8.4 %all-to-all-start = ((bf16[16,16,1024]{2,0,1:T(8,128)(2,1)}), bf16[16,16,1024]{2,0,1:T(8,128)(2,1)S(1)}, u32[]{:S(2)}, u32[]{:S(2)}) async-start(bf16[16,16,1024]{2,0,1:T(8,128)(2,1)} %bitcast.24), calls=%async_computation | async-start | bytes 1048576 | tf_op jit(solution)/shard_map/all_to_all | solution.py:23
  18.5 0.0 all-reduce.2.cloned.1.call-start
  18.5 1.9 convert_reduce_fusion
  20.4 0.0 all-reduce.2.cloned.1.call-update
  20.4 0.0 all-gather.3.cloned.1.call-start
  20.5 9.3 %all-to-all-done = bf16[16,16,1024]{2,0,1:T(8,128)(2,1)S(1)} async-done(((bf16[16,16,1024]{2,0,1:T(8,128)(2,1)}), bf16[16,16,1024]{2,0,1:T(8,128)(2,1)S(1)}, u32[]{:S(2)}, u32[]{:S(2)}) %all-to-all-start) | async-done | bytes 524320 | tf_op jit(solution)/shard_map/all_to_all | solution.py:23
  29.8 0.0 copy-start.2
  29.8 0.8 copy-done.2
  30.6 0.0 all-gather.3.cloned.1.call-update
  30.6 0.0 all-gather.5.cloned.1.call-start
  30.6 1.1 copy.25
  31.7 17.2 %all_to_all.38 = bf16[16,8,2048]{2,0,1:T(8,128)(2,1)} all-to-all(bf16[16,8,2048]{2,0,1:T(8,128)(2,1)S(1)} %bitcast.29), channel_id=1, replica_groups=mesh['brow'=16,'bcol'=8] {'bcol'}, dimensions={1} | all-to-all | bytes 1048576 | tf_op jit(solution)/shard_map/all_to_all | solution.py:26
  48.9 0.0 all-gather.5.cloned.1.call-update
  48.9 0.0 reduce-scatter.2.cloned.1.call-start
  49.0 155.0 %all-reduce.2.cloned.1.call-done = f32[16384]{0:T(1024)} async-done(((f32[16384]{0:T(1024)}), f32[16384]{0:T(1024)}) %all-reduce.2.cloned.1.call-update) | async-done | bytes 65552 | tf_op jit(solution)/shard_map/psum | solution.py:17
  204.0 0.8 broadcast_multiply_fusion
  204.9 0.0 all-gather.3.cloned.1.call-done
  204.9 0.0 all-gather.5.cloned.1.call-done
  204.9 13.1 %fusion = f32[1024,2048]{1,0:T(8,128)S(1)} fusion(bf16[8,16,16,1024]{3,2,1,0:T(8,128)(2,1)} %bitcast.31, bf16[16,8,16,2048]{3,2,1,0:T(8,128)(2,1)} %bitcast.30, f32[2048]{0:T(1024)S(1)} %dynamic_slice.10, f32[1024]{0:T(1024)S(1)} %dynamic-slice_multiply_fusion), kind=kOutput, calls=%fused_computation.1 | convolution fusion | flops 8596226048 | bytes 20983808 | tf_op jit(solution)/shard_map/dot_general | solution.py:31
  218.0 0.0 copy-start.1
  218.1 3.4 %copy-done.1 = f32[1024,2048]{1,0:T(8,128)} copy-done((f32[1024,2048]{1,0:T(8,128)}, f32[1024,2048]{1,0:T(8,128)S(1)}, u32[]{:S(2)}) %copy-start.1) | copy-done | bytes 8388632
  221.4 0.0 copy-done
  221.4 7.7 %fusion.5 = f32[1024,256]{1,0:T(8,128)} fusion(f32[1024,2048]{1,0:T(8,128)S(1)} %fusion, f32[2048,256]{1,0:T(8,128)S(1)} %copy-done), kind=kOutput, calls=%fused_computation.9 | convolution fusion | flops 6442450944 | bytes 11534336 | tf_op jit(solution)/shard_map/dot_general | solution.py:38
  229.1 0.0 reduce-scatter.2.cloned.1.call-update
  229.1 0.6 dynamic_slice.11
  229.7 30.5 %reduce-scatter.2.cloned.1.call-done = f32[128,256]{1,0:T(8,128)} async-done(((f32[1024,256]{1,0:T(8,128)}), f32[128,256]{1,0:T(8,128)}) %reduce-scatter.2.cloned.1.call-update) | async-done | bytes 131088 | tf_op jit(solution)/shard_map/reduce_scatter | solution.py:37
  (2 shorter events, 0.0 us)
Async XLA Ops:
  8.0 213.4 %copy-start = (f32[2048,256]{1,0:T(8,128)S(1)}, f32[2048,256]{1,0:T(8,128)}, u32[]{:S(2)}) copy-start(f32[2048,256]{1,0:T(8,128)} %param.3) | copy-start | bytes 6291460
  10.0 19.7 %all-to-all-start = ((bf16[16,16,1024]{2,0,1:T(8,128)(2,1)}), bf16[16,16,1024]{2,0,1:T(8,128)(2,1)S(1)}, u32[]{:S(2)}, u32[]{:S(2)}) async-start(bf16[16,16,1024]{2,0,1:T(8,128)(2,1)} %bitcast.24), calls=%async_computation | async-start | bytes 1048576 | tf_op jit(solution)/shard_map/all_to_all | solution.py:23
  18.5 185.5 %all-reduce.2.cloned.1.call-start = ((), (), s32[]{:S(2)}) async-start(), calls=%async_computation.5 | async-start | bytes 131072 | tf_op jit(solution)/shard_map/psum | solution.py:17
  20.4 184.5 %all-gather.3.cloned.1.call-start = ((), (), s32[]{:S(2)}) async-start(), calls=%async_computation.3 | async-start | bytes 4718592 | tf_op jit(solution)/shard_map/all_gather | solution.py:24
  29.8 0.8 copy-start.2
  30.6 174.3 %all-gather.5.cloned.1.call-start = ((), (), s32[]{:S(2)}) async-start(), calls=%async_computation.4 | async-start | bytes 8912896 | tf_op jit(solution)/shard_map/all_gather | solution.py:28
  48.9 211.2 %reduce-scatter.2.cloned.1.call-start = ((), (), s32[]{:S(2)}) async-start(), calls=%async_computation.6 | async-start | bytes 1179648 | tf_op jit(solution)/shard_map/reduce_scatter | solution.py:37
  218.0 3.4 %copy-start.1 = (f32[1024,2048]{1,0:T(8,128)}, f32[1024,2048]{1,0:T(8,128)S(1)}, u32[]{:S(2)}) copy-start(f32[1024,2048]{1,0:T(8,128)S(1)} %fusion) | copy-start | bytes 25165828
Sparse Core Ops, SparseCore 0:
  24.6 179.3 all-reduce.1
Sparse Core Ops, SparseCore 1:
  30.7 56.3 all-gather.2
  89.4 69.3 all-gather.4
  229.2 30.9 reduce-scatter.1
where the time goes:
time: 273 us; the launch traced here: 268 us
  waiting for transfers between devices  195 us (71%)
  matrix products  20.8 us (8%)
  blocking collectives  17.2 us (6%)
  between operations  15.7 us (6%)
  starting transfers between devices  8.61 us (3%)
  local copies, waits for them, and re-layouts  7.89 us (3%)
    psum x1, waiting for transfers between devices, on_device(): lax.psum(jnp.sum(patterns, axis=0, dtype=jnp.float32), ('brow', 'bcol'))  155 us
    reduce_scatter x1, waiting for transfers between devices, on_device(): lax.psum_scatter(jnp.dot(covariance, components, precision=lax.Precision....  30.5 us
    all_to_all x1, blocking collectives, on_device(): lax.all_to_all(patterns, 'bcol', split_axis=1, concat_axis=0, tiled=True)  17.2 us
    dot_general x1, matrix products, on_device(): lax.dot_general(row_grid, shaped, (((0, 1, 2), (1, 0, 2)), ((), ())), pre...  13.1 us
    all_to_all x1, waiting for transfers between devices, on_device(): lax.all_to_all(patterns, 'brow', split_axis=1, concat_axis=0, tiled=True)  9.32 us
    all_to_all x1, starting transfers between devices, on_device(): lax.all_to_all(patterns, 'brow', split_axis=1, concat_axis=0, tiled=True)  8.45 us
    dot_general x1, matrix products, on_device(): jnp.dot(covariance, components, precision=lax.Precision.HIGHEST, preferre...  7.65 us
  transfers between devices with their start and end apart: 5, of which 3 were waited for; matrix products, arithmetic and copies ran while one was open for 2% of the time, Pallas kernels for 0%

commit v1 on v0

v1 whole, which is shorter than its diff:
```python
import jax
import jax.numpy as jnp
from jax import lax
from jax.experimental import pallas as pl
from jax.experimental.pallas import tpu as pltpu
from jax.sharding import PartitionSpec as P

F32 = jnp.float32
BF16 = jnp.bfloat16
AXES = ("brow", "bcol")
SCANS = 2048
PIXELS = 16384
COMPS = 256
LOCAL = 16
PANEL = 2048
HALF = 1024
STEPS = (0, 1, -1, 2)
VMEM = pltpu.CompilerParams(vmem_limit_bytes=56 << 20)


def flat(x, y, z, k):
    return (((x // 2) * 4 + y) * 2 + k) * 8 + (x % 2) * 4 + z


def permute(value, move):
    pairs = []
    for x in range(4):
        for y in range(4):
            for z in range(4):
                for k in range(2):
                    x2, y2, z2, k2 = move(x, y, z, k)
                    pairs.append((flat(x, y, z, k), flat(x2, y2 % 4, z2 % 4, k2)))
    return lax.ppermute(value, AXES, pairs)


def spread_same(d):
    return lambda x, y, z, k: (x, y + d, z, k) if k == 0 else (x, y, z + d, k)


def spread_cross(d):
    return lambda x, y, z, k: (x, y, z + d, 1) if k == 0 else (x, y + d, z, 0)


def across(m):
    return lambda x, y, z, k: (x ^ m, y, z, k)


def around(d):
    return lambda x, y, z, k: (x, y, z + d, k) if k == 0 else (x, y + d, z, k)


def pick_kernel(at, patterns, *pieces):
    for n, piece in enumerate(pieces):
        for half in range(2):
            start = pl.multiple_of((half * 4 + at[n]) * PANEL, PANEL)
            piece[half] = patterns[:, pl.ds(start, PANEL)]


def pick(at, patterns):
    piece = jax.ShapeDtypeStruct((2, LOCAL, PANEL), BF16)
    return pl.pallas_call(
        pick_kernel,
        out_shape=[piece] * 8,
        in_specs=[pl.BlockSpec(memory_space=pltpu.SMEM), pl.BlockSpec(memory_space=pltpu.VMEM)],
        out_specs=[pl.BlockSpec(memory_space=pltpu.VMEM)] * 8,
        compiler_params=VMEM,
    )(at, patterns)


def group_kernel(at, *refs):
    pieces, groups = refs[:8], refs[8:]
    for n, group in enumerate(groups):
        half = at[n]
        for i, piece in enumerate(pieces):
            group[i] = piece[half]


def group(at, pieces):
    whole = jax.ShapeDtypeStruct((8, LOCAL, PANEL), BF16)
    return pl.pallas_call(
        group_kernel,
        out_shape=[whole] * 4,
        in_specs=[pl.BlockSpec(memory_space=pltpu.SMEM)] + [pl.BlockSpec(memory_space=pltpu.VMEM)] * 8,
        out_specs=[pl.BlockSpec(memory_space=pltpu.VMEM)] * 4,
        compiler_params=VMEM,
    )(at, *pieces)


def fetch(core, own, recv, rows, cols, sems):
    def start(row_from, col_from, first):
        for m in range(4):
            pltpu.make_async_copy(col_from[m], cols.at[m], sems.at[m]).start()
            for s in range(2):
                for dy in range(4):
                    pltpu.make_async_copy(
                        row_from[m].at[:, s, dy, :, pl.ds(first, HALF)], rows.at[m, dy, 1 - s], sems.at[m]
                    ).start()

    @pl.when(core == 0)
    def _():
        start(own, recv, 0)

    @pl.when(core == 1)
    def _():
        start(recv, own, HALF)


def fetched(own, rows, cols, sems, m):
    pltpu.make_async_copy(own[m], cols.at[m], sems.at[m]).wait()
    for s in range(2):
        for dy in range(4):
            pltpu.make_async_copy(
                own[m].at[:, s, dy, :, pl.ds(0, HALF)], rows.at[m, dy, 1 - s], sems.at[m]
            ).wait()


def project_kernel(at, *refs):
    own, recv, comps, parts = refs[:4], refs[4:8], refs[8], refs[9:13]
    rows, cols, high, low, scores, sems = refs[13:]
    fetch(at[4], own, recv, rows, cols, sems)
    value = comps[...]
    high[...] = value.astype(BF16)
    low[...] = (value - high[...].astype(F32)).astype(BF16)
    total = jnp.zeros((1, COMPS), F32)
    for m in range(4):
        fetched(own, rows, cols, sems, m)
        block = cols[m].reshape(512, PANEL)
        score = jnp.dot(block, high[...], preferred_element_type=F32) + jnp.dot(
            block, low[...], preferred_element_type=F32
        )
        scores[pl.ds(m * 512, 512), :] = score
        total += jnp.sum(score, axis=0, keepdims=True)
    centred = scores[...] - total / SCANS
    upper = centred.astype(BF16)
    lower = (centred - upper.astype(F32)).astype(BF16)
    panel = rows[...].reshape(SCANS, HALF)
    dims = (((0,), (0,)), ((), ()))
    result = lax.dot_general(upper, panel, dims, preferred_element_type=F32) + lax.dot_general(
        lower, panel, dims, preferred_element_type=F32
    )
    result = result / (SCANS - 1)
    for c in range(8):
        cell = result[:, c * 128 : (c + 1) * 128]
        xl, z = c // 4, c % 4
        for n in range(4):

            @pl.when(at[n] == z)
            def _():
                parts[n][xl] = cell


def project(at, own, recv, comps):
    part = jax.ShapeDtypeStruct((2, COMPS, 128), F32)
    return pl.pallas_call(
        project_kernel,
        out_shape=[part] * 4,
        in_specs=[pl.BlockSpec(memory_space=pltpu.SMEM)]
        + [pl.BlockSpec(memory_space=pl.ANY)] * 8
        + [pl.BlockSpec(memory_space=pltpu.VMEM)],
        out_specs=[pl.BlockSpec(memory_space=pltpu.VMEM)] * 4,
        scratch_shapes=[
            pltpu.VMEM((4, 4, 2, 4, LOCAL, HALF), BF16),
            pltpu.VMEM((4, 4, 2, 4, LOCAL, PANEL), BF16),
            pltpu.VMEM((PANEL, COMPS), BF16),
            pltpu.VMEM((PANEL, COMPS), BF16),
            pltpu.VMEM((SCANS, COMPS), F32),
            pltpu.SemaphoreType.DMA((4,)),
        ],
        compiler_params=VMEM,
        cost_estimate=pl.CostEstimate(flops=6 << 30, bytes_accessed=14 << 20, transcendentals=0),
    )(at, *own, *recv, comps)


def gram_kernel(at, *refs):
    own, recv, out, means = refs[:4], refs[4:8], refs[8], refs[9]
    rows, cols, row_sums, col_sums, stage, sems, out_sems = refs[10:]
    fetch(at[4], own, recv, rows, cols, sems)
    row_sums[...] = jnp.zeros_like(row_sums)
    col_sums[...] = jnp.zeros_like(col_sums)
    for m in range(4):
        fetched(own, rows, cols, sems, m)
        for a in range(4):
            row_sums[...] += jnp.sum(rows[m, a].reshape(128, HALF).astype(F32), axis=0, keepdims=True)
            col_sums[...] += jnp.sum(cols[m, a].reshape(128, PANEL).astype(F32), axis=0, keepdims=True)
    row_sums[...] = row_sums[...] / SCANS
    means[...] = row_sums[...]
    dims = (((0,), (0,)), ((), ()))
    copies = []
    for i in range(4):
        slot = i % 2
        if i >= 2:
            copies[i - 2].wait()
        left = rows[:, :, :, :, :, i * 256 : (i + 1) * 256].reshape(SCANS, 256)
        row_mean = jnp.transpose(jnp.broadcast_to(row_sums[:, i * 256 : (i + 1) * 256], (128, 256)))[:, :1]
        for j in range(8):
            span = slice(j * 256, (j + 1) * 256)
            right = cols[:, :, :, :, :, span].reshape(SCANS, 256)
            tile = lax.dot_general(left, right, dims, preferred_element_type=F32)
            stage[slot, :, span] = (tile - row_mean * col_sums[:, span]) * (1.0 / (SCANS - 1))
        copy = pltpu.make_async_copy(stage.at[slot], out.at[pl.ds(i * 256, 256), :], out_sems.at[slot])
        copy.start()
        copies.append(copy)
    copies[2].wait()
    copies[3].wait()


def gram(at, own, recv):
    return pl.pallas_call(
        gram_kernel,
        out_shape=[jax.ShapeDtypeStruct((HALF, PANEL), F32), jax.ShapeDtypeStruct((1, HALF), F32)],
        in_specs=[pl.BlockSpec(memory_space=pltpu.SMEM)] + [pl.BlockSpec(memory_space=pl.ANY)] * 8,
        out_specs=[pl.BlockSpec(memory_space=pl.ANY), pl.BlockSpec(memory_space=pltpu.VMEM)],
        scratch_shapes=[
            pltpu.VMEM((4, 4, 2, 4, LOCAL, HALF), BF16),
            pltpu.VMEM((4, 4, 2, 4, LOCAL, PANEL), BF16),
            pltpu.VMEM((1, HALF), F32),
            pltpu.VMEM((1, PANEL), F32),
            pltpu.VMEM((2, 256, PANEL), F32),
            pltpu.SemaphoreType.DMA((4,)),
            pltpu.SemaphoreType.DMA((2,)),
        ],
        compiler_params=VMEM,
        cost_estimate=pl.CostEstimate(flops=8 << 30, bytes_accessed=20 << 20, transcendentals=0),
    )(at, *own, *recv)


def on_device(patterns, components):
    row = lax.axis_index("brow")
    col = lax.axis_index("bcol")
    k, y, xh = row % 2, (row // 2) % 4, row // 8
    z, xl = col % 4, col // 4
    first = k == 0
    same = jnp.where(first, y, z)
    cross = jnp.where(first, z, y)
    at = jnp.stack([(same + d) % 4 for d in STEPS] + [(cross + d) % 4 for d in STEPS]).astype(jnp.int32)
    sends = pick(at, patterns)
    got = [sends[0]]
    got += [permute(sends[n], spread_same(STEPS[n])) for n in range(1, 4)]
    got += [permute(sends[4 + n], spread_cross(STEPS[n])) for n in range(4)]
    own_half = jnp.where(first, xh, xl)
    at = jnp.stack(
        [own_half, jnp.where(first, own_half, 1 - own_half), jnp.where(first, 1 - own_half, own_half), 1 - own_half]
    ).astype(jnp.int32)
    sends = group(at, got)
    groups = [sends[0]] + [permute(sends[m], across(m)) for m in (1, 2, 3)]
    own, recv = [], []
    for g in groups:
        whole = jnp.stack([g] + [permute(g, around(d)) for d in STEPS[1:]])
        whole = whole.reshape(4, 2, 4, LOCAL, PANEL)
        own.append(whole)
        recv.append(permute(whole, lambda x, y, z, k: (x, y, z, 1 - k)))
    at = jnp.stack([(z + d) % 4 for d in STEPS] + [k]).astype(jnp.int32)
    parts = project(at, own, recv, components)
    ring = [parts[0]] + [permute(parts[n], lambda x, y, z, k, d=STEPS[n]: (x, y, z + d, k)) for n in range(1, 4)]
    covariance, means = gram(at, own, recv)
    part = ring[0] + ring[1] + ring[2] + ring[3]
    mine = lax.dynamic_index_in_dim(part, xl, 0, keepdims=False)
    theirs = lax.dynamic_index_in_dim(part, 1 - xl, 0, keepdims=False)
    projected = (mine + permute(theirs, across(1))).T
    means_part = lax.dynamic_slice_in_dim(means[0], col * 128, 128, 0)
    return covariance, projected, means_part


def solution(mesh):
    return jax.shard_map(
        on_device,
        mesh=mesh,
        in_specs=(P(("brow", "bcol"), None), P("bcol", None)),
        out_specs=(P("brow", "bcol"), P(("brow", "bcol"), None), P(("brow", "bcol"))),
        check_vma=False,
    )
```

time: 273 us -> 154 us (0.56); the launches traced: 268 us -> 153 us
  waiting for transfers between devices: 195 us -> 61.6 us
  Pallas kernels: 0 us -> 38.5 us
  starting transfers between devices: 8.61 us -> 40.2 us
  matrix products: 20.8 us -> 0 us
  blocking collectives: 17.2 us -> 0 us
  between operations: 15.7 us -> 0.98 us
  other arithmetic: 2.7 us -> 7.9 us
  local copies, waits for them, and re-layouts: 7.89 us -> 3.86 us
    psum x1 -> x0, waiting for transfers between devices: 155 us -> none  [on_device(): lax.psum(jnp.sum(patterns, axis=0, dtype=jnp.float32), ('brow', 'bcol'))]
    ppermute x0 -> x30, waiting for transfers between devices: none -> 61.6 us  [permute(): return lax.ppermute(value, AXES, pairs)]
    ppermute x0 -> x30, starting transfers between devices: none -> 40.2 us  [permute(): return lax.ppermute(value, AXES, pairs)]
    pallas_call x0 -> x4, Pallas kernels: none -> 38.5 us  [the longest x1 17.2 us: gram(): pl.pallas_call(gram_kernel, out_shape=[jax.ShapeDtypeStruct((HALF, PANEL)...]
    reduce_scatter x1 -> x0, waiting for transfers between devices: 30.5 us -> none  [on_device(): lax.psum_scatter(jnp.dot(covariance, components, precision=lax.Precision....]
    dot_general x2 -> x0, matrix products: 20.8 us -> none  [the longest x1 13.1 us: on_device(): lax.dot_general(row_grid, shaped, (((0, 1, 2), (1, 0, 2)), ((), ())), pre...]
    all_to_all x1 -> x0, blocking collectives: 17.2 us -> none  [on_device(): lax.all_to_all(patterns, 'bcol', split_axis=1, concat_axis=0, tiled=True)]
    all_to_all x1 -> x0, waiting for transfers between devices: 9.32 us -> none  [on_device(): lax.all_to_all(patterns, 'brow', split_axis=1, concat_axis=0, tiled=True)]
  transfers between devices with their start and end apart: 5 -> 30, of which waited for: 3 -> 11; matrix products, arithmetic and copies ran while one was open for 2% -> 6% of each run, Pallas kernels for 0% -> 11%
where the time goes in v1:
time: 154 us; the launch traced here: 153 us
  waiting for transfers between devices  61.6 us (40%)
  starting transfers between devices  40.2 us (26%)
  Pallas kernels  38.5 us (25%)
  other arithmetic  7.9 us (5%)
  local copies, waits for them, and re-layouts  3.86 us (3%)
    ppermute x30, waiting for transfers between devices, permute(): return lax.ppermute(value, AXES, pairs)  61.6 us
    ppermute x30, starting transfers between devices, permute(): return lax.ppermute(value, AXES, pairs)  40.2 us
    pallas_call x1, Pallas kernels, gram(): pl.pallas_call(gram_kernel, out_shape=[jax.ShapeDtypeStruct((HALF, PANEL)...  17.2 us
    pallas_call x1, Pallas kernels, project(): pl.pallas_call(project_kernel, out_shape=[part] * 4, in_specs=[pl.BlockSp...  16.5 us
    another operation x4, other arithmetic, on_device(): whole = jnp.stack([g] + [permute(g, around(d)) for d in STEPS[1:]])  6.21 us
  transfers between devices with their start and end apart: 30, of which 11 were waited for; matrix products, arithmetic and copies ran while one was open for 6% of the time, Pallas kernels for 11%

profile of v1, /device:TPU:1, one launch (start us, length us, event | category | flops | bytes accessed | tf_op | source)
XLA Modules:
  0.0 153.1 jit_solution(9493686927616206817)
XLA Ops:
  1.4 2.1 %shard_map.49 = (bf16[2,16,2048]{2,1,0:T(8,128)(2,1)}, bf16[2,16,2048]{2,1,0:T(8,128)(2,1)}, bf16[2,16,2048]{2,1,0:T(8,128)(2,1)}, bf16[2,16,2048]{2,1,0:T(8,128...) custom-call(s32[8]{0:T(128)} %stack.139.at, ...), custom_call_target="tpu_custom_call" | custom-call | tf_op jit(solution)/shard_map/pallas_call | solution.py:61
  3.5 2.5 %collective-permute-start = (bf16[2,16,2048]{2,1,0:T(8,128)(2,1)}, bf16[2,16,2048]{2,1,0:T(8,128)(2,1)S(1)}, u32[]{:S(2)}, u32[]{:S(2)}) collective-permute-start(bf16[2,16,2048]{2,1,0:T(8,128)(2,1)} %get-tuple-element.22), channel_id=1, source_target_pairs={{0,16},{8,9},{1,17},{9,10},{2,18},{10,11},{3,19},{11,8},{16,32},{2... | collective-permute-start | bytes 393224 | tf_op jit(solution)/shard_map/ppermute | solution.py:33
  6.0 2.1 %collective-permute-start.1 = (bf16[2,16,2048]{2,1,0:T(8,128)(2,1)}, bf16[2,16,2048]{2,1,0:T(8,128)(2,1)S(1)}, u32[]{:S(2)}, u32[]{:S(2)}) collective-permute-start(bf16[2,16,2048]{2,1,0:T(8,128)(2,1)} %get-tuple-element.23), channel_id=1, source_target_pairs={{0,48},{8,11},{1,49},{9,8},{2,50},{10,9},{3,51},{11,10},{16,0},{24... | collective-permute-start | bytes 393224 | tf_op jit(solution)/shard_map/ppermute | solution.py:33
  8.1 1.3 collective-permute-start.2
  11.1 2.1 %collective-permute-start.5 = (bf16[2,16,2048]{2,1,0:T(8,128)(2,1)}, bf16[2,16,2048]{2,1,0:T(8,128)(2,1)S(1)}, u32[]{:S(2)}, u32[]{:S(2)}) collective-permute-start(bf16[2,16,2048]{2,1,0:T(8,128)(2,1)} %get-tuple-element.27), channel_id=1, source_target_pairs={{0,11},{8,48},{1,8},{9,49},{2,9},{10,50},{3,10},{11,51},{16,27},{2... | collective-permute-start | bytes 393224 | tf_op jit(solution)/shard_map/ppermute | solution.py:33
  13.2 3.0 %collective-permute-start.6 = (bf16[2,16,2048]{2,1,0:T(8,128)(2,1)}, bf16[2,16,2048]{2,1,0:T(8,128)(2,1)S(1)}, u32[]{:S(2)}, u32[]{:S(2)}) collective-permute-start(bf16[2,16,2048]{2,1,0:T(8,128)(2,1)} %get-tuple-element.28), channel_id=1, source_target_pairs={{0,10},{8,32},{1,11},{9,33},{2,8},{10,34},{3,9},{11,35},{16,26},{2... | collective-permute-start | bytes 393224 | tf_op jit(solution)/shard_map/ppermute | solution.py:33
  16.9 3.1 %collective-permute-done.6.refs_7_ = bf16[2,16,2048]{2,1,0:T(8,128)(2,1)S(1)} collective-permute-done((bf16[2,16,2048]{2,1,0:T(8,128)(2,1)}, bf16[2,16,2048]{2,1,0:T(8,128)(2,1)S(1)}, u32[]{:S(2)}, u32[]{:S(2)}) %collective-permute-start.6) | collective-permute-done | bytes 131104 | tf_op jit(solution)/shard_map/ppermute | solution.py:33
  20.7 2.7 %shard_map.50 = (bf16[8,16,2048]{2,1,0:T(8,128)(2,1)}, bf16[8,16,2048]{2,1,0:T(8,128)(2,1)}, bf16[8,16,2048]{2,1,0:T(8,128)(2,1)}, bf16[8,16,2048]{2,1,0:T(8,128)(2,1)}) custom-call(s32[4]{0:T(128)} %pad_add_fusion.at, bf16[2,16,2048]{2,1,0:T(8,128)(2,1)} %get-tuple-element.21.refs_0_, bf16[2,16,2048]{2,1,0:T(8,128)(2,1)} %copy-done.1, ...), custom_call_target="tpu_custom_call" | custom-call | tf_op jit(solution)/shard_map/pallas_call | solution.py:80
  23.4 2.5 %collective-permute-start.18 = (bf16[8,16,2048]{2,1,0:T(8,128)(2,1)}, bf16[8,16,2048]{2,1,0:T(8,128)(2,1)S(1)}, u32[]{:S(2)}, u32[]{:S(2)}) collective-permute-start(bf16[8,16,2048]{2,1,0:T(8,128)(2,1)} %get-tuple-element.32), channel_id=1, source_target_pairs={{0,68},{8,76},{1,69},{9,77},{2,70},{10,78},{3,71},{11,79},{16,84},... | collective-permute-start | bytes 1572872 | tf_op jit(solution)/shard_map/ppermute | solution.py:33
  26.7 2.6 %collective-permute-start.8 = (bf16[8,16,2048]{2,1,0:T(8,128)(2,1)}, bf16[8,16,2048]{2,1,0:T(8,128)(2,1)S(1)}, u32[]{:S(2)}, u32[]{:S(2)}) collective-permute-start(bf16[8,16,2048]{2,1,0:T(8,128)(2,1)} %get-tuple-element.29), channel_id=1, source_target_pairs={{0,3},{8,56},{1,0},{9,57},{2,1},{10,58},{3,2},{11,59},{16,19},{24,... | collective-permute-start | bytes 1572872 | tf_op jit(solution)/shard_map/ppermute | solution.py:33
  29.3 19.4 %collective-permute-done.18 = bf16[8,16,2048]{2,1,0:T(8,128)(2,1)S(1)} collective-permute-done((bf16[8,16,2048]{2,1,0:T(8,128)(2,1)}, bf16[8,16,2048]{2,1,0:T(8,128)(2,1)S(1)}, u32[]{:S(2)}, u32[]{:S(2)}) %collective-permute-start.18) | collective-permute-done | bytes 524320 | tf_op jit(solution)/shard_map/ppermute | solution.py:33
  49.8 2.4 %collective-permute-start.20 = (bf16[8,16,2048]{2,1,0:T(8,128)(2,1)S(1)}, bf16[8,16,2048]{2,1,0:T(8,128)(2,1)S(1)}, u32[]{:S(2)}, u32[]{:S(2)}) collective-permute-start(bf16[8,16,2048]{2,1,0:T(8,128)(2,1)S(1)} %collective-permute-done.18), channel_id=1, source_target_pairs={{0,3},{8,56},{1,0},{9,57},{2,1},{10,58},{3,2},{11,59},{16,19},{24,... | collective-permute-start | bytes 1572872 | tf_op jit(solution)/shard_map/ppermute | solution.py:33
  53.2 5.6 %collective-permute-done.9 = bf16[8,16,2048]{2,1,0:T(8,128)(2,1)S(1)} collective-permute-done((bf16[8,16,2048]{2,1,0:T(8,128)(2,1)}, bf16[8,16,2048]{2,1,0:T(8,128)(2,1)S(1)}, u32[]{:S(2)}, u32[]{:S(2)}) %collective-permute-start.9) | collective-permute-done | bytes 524320 | tf_op jit(solution)/shard_map/ppermute | solution.py:33
  59.3 5.1 %collective-permute-done.19 = bf16[8,16,2048]{2,1,0:T(8,128)(2,1)S(1)} collective-permute-done((bf16[8,16,2048]{2,1,0:T(8,128)(2,1)S(1)}, bf16[8,16,2048]{2,1,0:T(8,128)(2,1)S(1)}, u32[]{:S(2)}, u32[]{:S(2)}) %collective-permute-start.19) | collective-permute-done | bytes 524320 | tf_op jit(solution)/shard_map/ppermute | solution.py:33
  65.1 1.3 pad_maximum_fusion.refs_0_
  66.7 3.4 %collective-permute-done.21 = bf16[8,16,2048]{2,1,0:T(8,128)(2,1)S(1)} collective-permute-done((bf16[8,16,2048]{2,1,0:T(8,128)(2,1)S(1)}, bf16[8,16,2048]{2,1,0:T(8,128)(2,1)S(1)}, u32[]{:S(2)}, u32[]{:S(2)}) %collective-permute-start.21) | collective-permute-done | bytes 524320 | tf_op jit(solution)/shard_map/ppermute | solution.py:33
  70.6 5.0 %collective-permute-done.15 = bf16[8,16,2048]{2,1,0:T(8,128)(2,1)S(1)} collective-permute-done((bf16[8,16,2048]{2,1,0:T(8,128)(2,1)S(1)}, bf16[8,16,2048]{2,1,0:T(8,128)(2,1)S(1)}, u32[]{:S(2)}, u32[]{:S(2)}) %collective-permute-start.15) | collective-permute-done | bytes 524320 | tf_op jit(solution)/shard_map/ppermute | solution.py:33
  76.4 1.7 %pad_maximum_fusion.3.refs_3_ = bf16[4,2,4,16,2048]{4,3,2,1,0:T(8,128)(2,1)} fusion(bf16[1,2,4,16,2048]{4,3,2,1,0:T(8,128)(2,1)S(1)} %bitcast.54, bf16[1,2,4,16,2048]{4,3,2,1,0:T(8,128)(2,1)S(1)} %bitcast.50, bf16[1,2,4,16,2048]{4,3,2,1,0:T(8,128)(2,1)S(1)} %bitcast.47, bf16[1,2,4,16,2048]{4,3,2,1,0:T(8,128)(2,1)S(1)} %bitcast.45), kind=kLoop, calls=%fused_computation.3 | loop fusion | flops 3145728 | bytes 4194304 | tf_op jit(solution)/shard_map/stack | solution.py:248
  78.1 3.6 %collective-permute-start.22 = (bf16[4,2,4,16,2048]{4,3,2,1,0:T(8,128)(2,1)S(1)}, bf16[4,2,4,16,2048]{4,3,2,1,0:T(8,128)(2,1)}, u32[]{:S(2)}, u32[]{:S(2)}) collective-permute-start(bf16[4,2,4,16,2048]{4,3,2,1,0:T(8,128)(2,1)S(1)} %pad_maximum_fusion.refs_0_), channel_id=1, source_target_pairs={{0,8},{8,0},{1,9},{9,1},{2,10},{10,2},{3,11},{11,3},{16,24},{24,16... | collective-permute-start | bytes 6291464 | tf_op jit(solution)/shard_map/ppermute | solution.py:33
  81.6 2.3 %collective-permute-start.25 = (bf16[4,2,4,16,2048]{4,3,2,1,0:T(8,128)(2,1)}, bf16[4,2,4,16,2048]{4,3,2,1,0:T(8,128)(2,1)}, u32[]{:S(2)}, u32[]{:S(2)}) collective-permute-start(bf16[4,2,4,16,2048]{4,3,2,1,0:T(8,128)(2,1)} %pad_maximum_fusion.3.refs_3_), channel_id=1, source_target_pairs={{0,8},{8,0},{1,9},{9,1},{2,10},{10,2},{3,11},{11,3},{16,24},{24,16... | collective-permute-start | bytes 6291464 | tf_op jit(solution)/shard_map/ppermute | solution.py:33
  83.9 1.6 %pad_maximum_fusion.2.refs_2_ = bf16[4,2,4,16,2048]{4,3,2,1,0:T(8,128)(2,1)} fusion(bf16[1,2,4,16,2048]{4,3,2,1,0:T(8,128)(2,1)S(1)} %bitcast.55, bf16[1,2,4,16,2048]{4,3,2,1,0:T(8,128)(2,1)S(1)} %bitcast.52, bf16[1,2,4,16,2048]{4,3,2,1,0:T(8,128)(2,1)S(1)} %bitcast.48, bf16[1,2,4,16,2048]{4,3,2,1,0:T(8,128)(2,1)S(1)} %bitcast.44), kind=kLoop, calls=%fused_computation.2 | loop fusion | flops 3145728 | bytes 4194304 | tf_op jit(solution)/shard_map/stack | solution.py:248
  85.6 1.3 collective-permute-done.11
  86.8 2.5 %collective-permute-start.24 = (bf16[4,2,4,16,2048]{4,3,2,1,0:T(8,128)(2,1)}, bf16[4,2,4,16,2048]{4,3,2,1,0:T(8,128)(2,1)}, u32[]{:S(2)}, u32[]{:S(2)}) collective-permute-start(bf16[4,2,4,16,2048]{4,3,2,1,0:T(8,128)(2,1)} %pad_maximum_fusion.2.refs_2_), channel_id=1, source_target_pairs={{0,8},{8,0},{1,9},{9,1},{2,10},{10,2},{3,11},{11,3},{16,24},{24,16... | collective-permute-start | bytes 6291464 | tf_op jit(solution)/shard_map/ppermute | solution.py:33
  89.4 3.2 %collective-permute-done.13 = bf16[8,16,2048]{2,1,0:T(8,128)(2,1)S(1)} collective-permute-done((bf16[8,16,2048]{2,1,0:T(8,128)(2,1)S(1)}, bf16[8,16,2048]{2,1,0:T(8,128)(2,1)S(1)}, u32[]{:S(2)}, u32[]{:S(2)}) %collective-permute-start.13) | collective-permute-done | bytes 524320 | tf_op jit(solution)/shard_map/ppermute | solution.py:33
  92.6 1.6 %pad_maximum_fusion.1.refs_1_ = bf16[4,2,4,16,2048]{4,3,2,1,0:T(8,128)(2,1)} fusion(bf16[1,2,4,16,2048]{4,3,2,1,0:T(8,128)(2,1)S(1)} %bitcast.58, bf16[1,2,4,16,2048]{4,3,2,1,0:T(8,128)(2,1)S(1)} %bitcast.57, bf16[1,2,4,16,2048]{4,3,2,1,0:T(8,128)(2,1)S(1)} %bitcast.53, bf16[1,2,4,16,2048]{4,3,2,1,0:T(8,128)(2,1)S(1)} %bitcast.43), kind=kLoop, calls=%fused_computation.1 | loop fusion | flops 3145728 | bytes 4194304 | tf_op jit(solution)/shard_map/stack | solution.py:248
  94.2 2.5 %collective-permute-start.23 = (bf16[4,2,4,16,2048]{4,3,2,1,0:T(8,128)(2,1)}, bf16[4,2,4,16,2048]{4,3,2,1,0:T(8,128)(2,1)}, u32[]{:S(2)}, u32[]{:S(2)}) collective-permute-start(bf16[4,2,4,16,2048]{4,3,2,1,0:T(8,128)(2,1)} %pad_maximum_fusion.1.refs_1_), channel_id=1, source_target_pairs={{0,8},{8,0},{1,9},{9,1},{2,10},{10,2},{3,11},{11,3},{16,24},{24,16... | collective-permute-start | bytes 6291464 | tf_op jit(solution)/shard_map/ppermute | solution.py:33
  97.4 3.5 %collective-permute-done.23.refs_5_ = bf16[4,2,4,16,2048]{4,3,2,1,0:T(8,128)(2,1)} collective-permute-done((bf16[4,2,4,16,2048]{4,3,2,1,0:T(8,128)(2,1)}, bf16[4,2,4,16,2048]{4,3,2,1,0:T(8,128)(2,1)}, u32[]{:S(2)}, u32[]{:S(2)}) %collective-permute-start.23) | collective-permute-done | bytes 2097184 | tf_op jit(solution)/shard_map/ppermute | solution.py:33
  100.8 16.5 %shard_map.52 = (f32[2,256,128]{2,1,0:T(8,128)}, f32[2,256,128]{2,1,0:T(8,128)}, f32[2,256,128]{2,1,0:T(8,128)}, f32[2,256,128]{2,1,0:T(8,128)}) custom-call(s32[5]{0:T(128)} %stack.125.at, bf16[4,2,4,16,2048]{4,3,2,1,0:T(8,128)(2,1)} %copy-done, bf16[4,2,4,16,2048]{4,3,2,1,0:T(8,128)(2,1)} %pad_maximum_fusion.1.refs_1_, ...), custom_call_target="tpu_custom_call" | custom-call | flops 6442450944 | bytes 14680064 | tf_op jit(solution)/shard_map/pallas_call | solution.py:154
  118.1 2.0 %collective-permute-start.27 = (f32[2,256,128]{2,1,0:T(8,128)}, f32[2,256,128]{2,1,0:T(8,128)S(1)}, u32[]{:S(2)}, u32[]{:S(2)}) collective-permute-start(f32[2,256,128]{2,1,0:T(8,128)} %get-tuple-element.36), channel_id=1, source_target_pairs={{0,3},{8,11},{1,0},{9,8},{2,1},{10,9},{3,2},{11,10},{16,19},{24,27... | collective-permute-start | bytes 786440 | tf_op jit(solution)/shard_map/ppermute | solution.py:33
  120.9 5.5 %collective-permute-done.26 = f32[2,256,128]{2,1,0:T(8,128)S(1)} collective-permute-done((f32[2,256,128]{2,1,0:T(8,128)}, f32[2,256,128]{2,1,0:T(8,128)S(1)}, u32[]{:S(2)}, u32[]{:S(2)}) %collective-permute-start.26) | collective-permute-done | bytes 262176 | tf_op jit(solution)/shard_map/ppermute | solution.py:33
  126.4 6.4 %collective-permute-done.28 = f32[2,256,128]{2,1,0:T(8,128)S(1)} collective-permute-done((f32[2,256,128]{2,1,0:T(8,128)}, f32[2,256,128]{2,1,0:T(8,128)S(1)}, u32[]{:S(2)}, u32[]{:S(2)}) %collective-permute-start.28) | collective-permute-done | bytes 262176 | tf_op jit(solution)/shard_map/ppermute | solution.py:33
  133.9 17.2 %shard_map.51 = (f32[1024,2048]{1,0:T(8,128)}, f32[1,1024]{1,0:T(1,128)}) custom-call(s32[5]{0:T(128)} %stack.125.at, bf16[4,2,4,16,2048]{4,3,2,1,0:T(8,128)(2,1)} %copy-done, bf16[4,2,4,16,2048]{4,3,2,1,0:T(8,128)(2,1)} %pad_maximum_fusion.1.refs_1_, bf16[4,2,4,16,2048]{4,3,2,1,0:T(8,128)(2,1)} %pad_maximum_fusion.2.refs_2_, ...), custom_call_target="tpu_custom_call" | custom-call | flops 8589934592 | bytes 20971520 | tf_op jit(solution)/shard_map/pallas_call | solution.py:208
  (60 shorter events, 14.5 us)
Async XLA Ops:
  3.5 7.6 %collective-permute-start = (bf16[2,16,2048]{2,1,0:T(8,128)(2,1)}, bf16[2,16,2048]{2,1,0:T(8,128)(2,1)S(1)}, u32[]{:S(2)}, u32[]{:S(2)}) collective-permute-start(bf16[2,16,2048]{2,1,0:T(8,128)(2,1)} %get-tuple-element.22), channel_id=1, source_target_pairs={{0,16},{8,9},{1,17},{9,10},{2,18},{10,11},{3,19},{11,8},{16,32},{2... | collective-permute-start | bytes 393224 | tf_op jit(solution)/shard_map/ppermute | solution.py:33
  6.0 7.2 %collective-permute-start.1 = (bf16[2,16,2048]{2,1,0:T(8,128)(2,1)}, bf16[2,16,2048]{2,1,0:T(8,128)(2,1)S(1)}, u32[]{:S(2)}, u32[]{:S(2)}) collective-permute-start(bf16[2,16,2048]{2,1,0:T(8,128)(2,1)} %get-tuple-element.23), channel_id=1, source_target_pairs={{0,48},{8,11},{1,49},{9,8},{2,50},{10,9},{3,51},{11,10},{16,0},{24... | collective-permute-start | bytes 393224 | tf_op jit(solution)/shard_map/ppermute | solution.py:33
  8.1 8.7 %collective-permute-start.2 = (bf16[2,16,2048]{2,1,0:T(8,128)(2,1)}, bf16[2,16,2048]{2,1,0:T(8,128)(2,1)S(1)}, u32[]{:S(2)}, u32[]{:S(2)}) collective-permute-start(bf16[2,16,2048]{2,1,0:T(8,128)(2,1)} %get-tuple-element.24), channel_id=1, source_target_pairs={{0,32},{8,10},{1,33},{9,11},{2,34},{10,8},{3,35},{11,9},{16,48},{2... | collective-permute-start | bytes 393224 | tf_op jit(solution)/shard_map/ppermute | solution.py:33
  9.4 7.4 %collective-permute-start.3 = (bf16[2,16,2048]{2,1,0:T(8,128)(2,1)}, bf16[2,16,2048]{2,1,0:T(8,128)(2,1)S(1)}, u32[]{:S(2)}, u32[]{:S(2)}) collective-permute-start(bf16[2,16,2048]{2,1,0:T(8,128)(2,1)} %get-tuple-element.25), channel_id=1, source_target_pairs={{0,8},{8,0},{1,9},{9,1},{2,10},{10,2},{3,11},{11,3},{16,24},{24,16... | collective-permute-start | bytes 393224 | tf_op jit(solution)/shard_map/ppermute | solution.py:33
  10.2 6.6 %collective-permute-start.4 = (bf16[2,16,2048]{2,1,0:T(8,128)(2,1)}, bf16[2,16,2048]{2,1,0:T(8,128)(2,1)S(1)}, u32[]{:S(2)}, u32[]{:S(2)}) collective-permute-start(bf16[2,16,2048]{2,1,0:T(8,128)(2,1)} %get-tuple-element.26), channel_id=1, source_target_pairs={{0,9},{8,16},{1,10},{9,17},{2,11},{10,18},{3,8},{11,19},{16,25},{2... | collective-permute-start | bytes 393224 | tf_op jit(solution)/shard_map/ppermute | solution.py:33
  11.1 8.9 %copy-start.1 = (bf16[2,16,2048]{2,1,0:T(8,128)(2,1)}, bf16[2,16,2048]{2,1,0:T(8,128)(2,1)S(1)}, u32[]{:S(2)}) copy-start(bf16[2,16,2048]{2,1,0:T(8,128)(2,1)S(1)} %collective-permute-done.refs_1_) | copy-start | bytes 393220
  11.1 5.7 %collective-permute-start.5 = (bf16[2,16,2048]{2,1,0:T(8,128)(2,1)}, bf16[2,16,2048]{2,1,0:T(8,128)(2,1)S(1)}, u32[]{:S(2)}, u32[]{:S(2)}) collective-permute-start(bf16[2,16,2048]{2,1,0:T(8,128)(2,1)} %get-tuple-element.27), channel_id=1, source_target_pairs={{0,11},{8,48},{1,8},{9,49},{2,9},{10,50},{3,10},{11,51},{16,27},{2... | collective-permute-start | bytes 393224 | tf_op jit(solution)/shard_map/ppermute | solution.py:33
  13.2 6.8 %collective-permute-start.6 = (bf16[2,16,2048]{2,1,0:T(8,128)(2,1)}, bf16[2,16,2048]{2,1,0:T(8,128)(2,1)S(1)}, u32[]{:S(2)}, u32[]{:S(2)}) collective-permute-start(bf16[2,16,2048]{2,1,0:T(8,128)(2,1)} %get-tuple-element.28), channel_id=1, source_target_pairs={{0,10},{8,32},{1,11},{9,33},{2,8},{10,34},{3,9},{11,35},{16,26},{2... | collective-permute-start | bytes 393224 | tf_op jit(solution)/shard_map/ppermute | solution.py:33
  23.4 25.3 %collective-permute-start.18 = (bf16[8,16,2048]{2,1,0:T(8,128)(2,1)}, bf16[8,16,2048]{2,1,0:T(8,128)(2,1)S(1)}, u32[]{:S(2)}, u32[]{:S(2)}) collective-permute-start(bf16[8,16,2048]{2,1,0:T(8,128)(2,1)} %get-tuple-element.32), channel_id=1, source_target_pairs={{0,68},{8,76},{1,69},{9,77},{2,70},{10,78},{3,71},{11,79},{16,84},... | collective-permute-start | bytes 1572872 | tf_op jit(solution)/shard_map/ppermute | solution.py:33
  25.9 23.6 %collective-permute-start.14 = (bf16[8,16,2048]{2,1,0:T(8,128)(2,1)}, bf16[8,16,2048]{2,1,0:T(8,128)(2,1)S(1)}, u32[]{:S(2)}, u32[]{:S(2)}) collective-permute-start(bf16[8,16,2048]{2,1,0:T(8,128)(2,1)} %get-tuple-element.31), channel_id=1, source_target_pairs={{0,64},{8,72},{1,65},{9,73},{2,66},{10,74},{3,67},{11,75},{16,80},... | collective-permute-start | bytes 1572872 | tf_op jit(solution)/shard_map/ppermute | solution.py:33
  26.4 23.4 %collective-permute-start.10 = (bf16[8,16,2048]{2,1,0:T(8,128)(2,1)}, bf16[8,16,2048]{2,1,0:T(8,128)(2,1)S(1)}, u32[]{:S(2)}, u32[]{:S(2)}) collective-permute-start(bf16[8,16,2048]{2,1,0:T(8,128)(2,1)} %get-tuple-element.30), channel_id=1, source_target_pairs={{0,4},{8,12},{1,5},{9,13},{2,6},{10,14},{3,7},{11,15},{16,20},{24,... | collective-permute-start | bytes 1572872 | tf_op jit(solution)/shard_map/ppermute | solution.py:33
  26.6 25.5 %collective-permute-start.7 = (bf16[8,16,2048]{2,1,0:T(8,128)(2,1)}, bf16[8,16,2048]{2,1,0:T(8,128)(2,1)S(1)}, u32[]{:S(2)}, u32[]{:S(2)}) collective-permute-start(bf16[8,16,2048]{2,1,0:T(8,128)(2,1)} %get-tuple-element.29), channel_id=1, source_target_pairs={{0,1},{8,24},{1,2},{9,25},{2,3},{10,26},{3,0},{11,27},{16,17},{24,... | collective-permute-start | bytes 1572872 | tf_op jit(solution)/shard_map/ppermute | solution.py:33
  26.7 26.4 %collective-permute-start.8 = (bf16[8,16,2048]{2,1,0:T(8,128)(2,1)}, bf16[8,16,2048]{2,1,0:T(8,128)(2,1)S(1)}, u32[]{:S(2)}, u32[]{:S(2)}) collective-permute-start(bf16[8,16,2048]{2,1,0:T(8,128)(2,1)} %get-tuple-element.29), channel_id=1, source_target_pairs={{0,3},{8,56},{1,0},{9,57},{2,1},{10,58},{3,2},{11,59},{16,19},{24,... | collective-permute-start | bytes 1572872 | tf_op jit(solution)/shard_map/ppermute | solution.py:33
  48.7 10.1 %collective-permute-start.9 = (bf16[8,16,2048]{2,1,0:T(8,128)(2,1)}, bf16[8,16,2048]{2,1,0:T(8,128)(2,1)S(1)}, u32[]{:S(2)}, u32[]{:S(2)}) collective-permute-start(bf16[8,16,2048]{2,1,0:T(8,128)(2,1)} %get-tuple-element.29), channel_id=1, source_target_pairs={{0,2},{8,40},{1,3},{9,41},{2,0},{10,42},{3,1},{11,43},{16,18},{24,... | collective-permute-start | bytes 1572872 | tf_op jit(solution)/shard_map/ppermute | solution.py:33
  49.5 14.9 %collective-permute-start.19 = (bf16[8,16,2048]{2,1,0:T(8,128)(2,1)S(1)}, bf16[8,16,2048]{2,1,0:T(8,128)(2,1)S(1)}, u32[]{:S(2)}, u32[]{:S(2)}) collective-permute-start(bf16[8,16,2048]{2,1,0:T(8,128)(2,1)S(1)} %collective-permute-done.18), channel_id=1, source_target_pairs={{0,1},{8,24},{1,2},{9,25},{2,3},{10,26},{3,0},{11,27},{16,17},{24,... | collective-permute-start | bytes 1572872 | tf_op jit(solution)/shard_map/ppermute | solution.py:33
  49.8 16.7 %collective-permute-start.20 = (bf16[8,16,2048]{2,1,0:T(8,128)(2,1)S(1)}, bf16[8,16,2048]{2,1,0:T(8,128)(2,1)S(1)}, u32[]{:S(2)}, u32[]{:S(2)}) collective-permute-start(bf16[8,16,2048]{2,1,0:T(8,128)(2,1)S(1)} %collective-permute-done.18), channel_id=1, source_target_pairs={{0,3},{8,56},{1,0},{9,57},{2,1},{10,58},{3,2},{11,59},{16,19},{24,... | collective-permute-start | bytes 1572872 | tf_op jit(solution)/shard_map/ppermute | solution.py:33
  52.2 17.9 %collective-permute-start.21 = (bf16[8,16,2048]{2,1,0:T(8,128)(2,1)S(1)}, bf16[8,16,2048]{2,1,0:T(8,128)(2,1)S(1)}, u32[]{:S(2)}, u32[]{:S(2)}) collective-permute-start(bf16[8,16,2048]{2,1,0:T(8,128)(2,1)S(1)} %collective-permute-done.18), channel_id=1, source_target_pairs={{0,2},{8,40},{1,3},{9,41},{2,0},{10,42},{3,1},{11,43},{16,18},{24,... | collective-permute-start | bytes 1572872 | tf_op jit(solution)/shard_map/ppermute | solution.py:33
  53.2 22.4 %collective-permute-start.15 = (bf16[8,16,2048]{2,1,0:T(8,128)(2,1)S(1)}, bf16[8,16,2048]{2,1,0:T(8,128)(2,1)S(1)}, u32[]{:S(2)}, u32[]{:S(2)}) collective-permute-start(bf16[8,16,2048]{2,1,0:T(8,128)(2,1)S(1)} %collective-permute-done.14), channel_id=1, source_target_pairs={{0,1},{8,24},{1,2},{9,25},{2,3},{10,26},{3,0},{11,27},{16,17},{24,... | collective-permute-start | bytes 1572872 | tf_op jit(solution)/shard_map/ppermute | solution.py:33
  58.8 19.3 %collective-permute-start.16 = (bf16[8,16,2048]{2,1,0:T(8,128)(2,1)S(1)}, bf16[8,16,2048]{2,1,0:T(8,128)(2,1)S(1)}, u32[]{:S(2)}, u32[]{:S(2)}) collective-permute-start(bf16[8,16,2048]{2,1,0:T(8,128)(2,1)S(1)} %collective-permute-done.14), channel_id=1, source_target_pairs={{0,3},{8,56},{1,0},{9,57},{2,1},{10,58},{3,2},{11,59},{16,19},{24,... | collective-permute-start | bytes 1572872 | tf_op jit(solution)/shard_map/ppermute | solution.py:33
  64.4 17.3 %collective-permute-start.17 = (bf16[8,16,2048]{2,1,0:T(8,128)(2,1)S(1)}, bf16[8,16,2048]{2,1,0:T(8,128)(2,1)S(1)}, u32[]{:S(2)}, u32[]{:S(2)}) collective-permute-start(bf16[8,16,2048]{2,1,0:T(8,128)(2,1)S(1)} %collective-permute-done.14), channel_id=1, source_target_pairs={{0,2},{8,40},{1,3},{9,41},{2,0},{10,42},{3,1},{11,43},{16,18},{24,... | collective-permute-start | bytes 1572872 | tf_op jit(solution)/shard_map/ppermute | solution.py:33
  66.4 11.6 %copy-start = (bf16[4,2,4,16,2048]{4,3,2,1,0:T(8,128)(2,1)}, bf16[4,2,4,16,2048]{4,3,2,1,0:T(8,128)(2,1)S(1)}, u32[]{:S(2)}) copy-start(bf16[4,2,4,16,2048]{4,3,2,1,0:T(8,128)(2,1)S(1)} %pad_maximum_fusion.refs_0_) | copy-start | bytes 6291460
  66.5 20.4 %collective-permute-start.11 = (bf16[8,16,2048]{2,1,0:T(8,128)(2,1)S(1)}, bf16[8,16,2048]{2,1,0:T(8,128)(2,1)S(1)}, u32[]{:S(2)}, u32[]{:S(2)}) collective-permute-start(bf16[8,16,2048]{2,1,0:T(8,128)(2,1)S(1)} %collective-permute-done.10), channel_id=1, source_target_pairs={{0,1},{8,24},{1,2},{9,25},{2,3},{10,26},{3,0},{11,27},{16,17},{24,... | collective-permute-start | bytes 1572872 | tf_op jit(solution)/shard_map/ppermute | solution.py:33
  70.1 19.3 %collective-permute-start.12 = (bf16[8,16,2048]{2,1,0:T(8,128)(2,1)S(1)}, bf16[8,16,2048]{2,1,0:T(8,128)(2,1)S(1)}, u32[]{:S(2)}, u32[]{:S(2)}) collective-permute-start(bf16[8,16,2048]{2,1,0:T(8,128)(2,1)S(1)} %collective-permute-done.10), channel_id=1, source_target_pairs={{0,3},{8,56},{1,0},{9,57},{2,1},{10,58},{3,2},{11,59},{16,19},{24,... | collective-permute-start | bytes 1572872 | tf_op jit(solution)/shard_map/ppermute | solution.py:33
  75.6 17.0 %collective-permute-start.13 = (bf16[8,16,2048]{2,1,0:T(8,128)(2,1)S(1)}, bf16[8,16,2048]{2,1,0:T(8,128)(2,1)S(1)}, u32[]{:S(2)}, u32[]{:S(2)}) collective-permute-start(bf16[8,16,2048]{2,1,0:T(8,128)(2,1)S(1)} %collective-permute-done.10), channel_id=1, source_target_pairs={{0,2},{8,40},{1,3},{9,41},{2,0},{10,42},{3,1},{11,43},{16,18},{24,... | collective-permute-start | bytes 1572872 | tf_op jit(solution)/shard_map/ppermute | solution.py:33
  78.1 19.3 %collective-permute-start.22 = (bf16[4,2,4,16,2048]{4,3,2,1,0:T(8,128)(2,1)S(1)}, bf16[4,2,4,16,2048]{4,3,2,1,0:T(8,128)(2,1)}, u32[]{:S(2)}, u32[]{:S(2)}) collective-permute-start(bf16[4,2,4,16,2048]{4,3,2,1,0:T(8,128)(2,1)S(1)} %pad_maximum_fusion.refs_0_), channel_id=1, source_target_pairs={{0,8},{8,0},{1,9},{9,1},{2,10},{10,2},{3,11},{11,3},{16,24},{24,16... | collective-permute-start | bytes 6291464 | tf_op jit(solution)/shard_map/ppermute | solution.py:33
  81.6 15.7 %collective-permute-start.25 = (bf16[4,2,4,16,2048]{4,3,2,1,0:T(8,128)(2,1)}, bf16[4,2,4,16,2048]{4,3,2,1,0:T(8,128)(2,1)}, u32[]{:S(2)}, u32[]{:S(2)}) collective-permute-start(bf16[4,2,4,16,2048]{4,3,2,1,0:T(8,128)(2,1)} %pad_maximum_fusion.3.refs_3_), channel_id=1, source_target_pairs={{0,8},{8,0},{1,9},{9,1},{2,10},{10,2},{3,11},{11,3},{16,24},{24,16... | collective-permute-start | bytes 6291464 | tf_op jit(solution)/shard_map/ppermute | solution.py:33
  86.8 10.5 %collective-permute-start.24 = (bf16[4,2,4,16,2048]{4,3,2,1,0:T(8,128)(2,1)}, bf16[4,2,4,16,2048]{4,3,2,1,0:T(8,128)(2,1)}, u32[]{:S(2)}, u32[]{:S(2)}) collective-permute-start(bf16[4,2,4,16,2048]{4,3,2,1,0:T(8,128)(2,1)} %pad_maximum_fusion.2.refs_2_), channel_id=1, source_target_pairs={{0,8},{8,0},{1,9},{9,1},{2,10},{10,2},{3,11},{11,3},{16,24},{24,16... | collective-permute-start | bytes 6291464 | tf_op jit(solution)/shard_map/ppermute | solution.py:33
  94.2 6.7 %collective-permute-start.23 = (bf16[4,2,4,16,2048]{4,3,2,1,0:T(8,128)(2,1)}, bf16[4,2,4,16,2048]{4,3,2,1,0:T(8,128)(2,1)}, u32[]{:S(2)}, u32[]{:S(2)}) collective-permute-start(bf16[4,2,4,16,2048]{4,3,2,1,0:T(8,128)(2,1)} %pad_maximum_fusion.1.refs_1_), channel_id=1, source_target_pairs={{0,8},{8,0},{1,9},{9,1},{2,10},{10,2},{3,11},{11,3},{16,24},{24,16... | collective-permute-start | bytes 6291464 | tf_op jit(solution)/shard_map/ppermute | solution.py:33
  117.4 9.0 %collective-permute-start.26 = (f32[2,256,128]{2,1,0:T(8,128)}, f32[2,256,128]{2,1,0:T(8,128)S(1)}, u32[]{:S(2)}, u32[]{:S(2)}) collective-permute-start(f32[2,256,128]{2,1,0:T(8,128)} %get-tuple-element.35), channel_id=1, source_target_pairs={{0,1},{8,9},{1,2},{9,10},{2,3},{10,11},{3,0},{11,8},{16,17},{24,25... | collective-permute-start | bytes 786440 | tf_op jit(solution)/shard_map/ppermute | solution.py:33
  118.1 8.3 %collective-permute-start.27 = (f32[2,256,128]{2,1,0:T(8,128)}, f32[2,256,128]{2,1,0:T(8,128)S(1)}, u32[]{:S(2)}, u32[]{:S(2)}) collective-permute-start(f32[2,256,128]{2,1,0:T(8,128)} %get-tuple-element.36), channel_id=1, source_target_pairs={{0,3},{8,11},{1,0},{9,8},{2,1},{10,9},{3,2},{11,10},{16,19},{24,27... | collective-permute-start | bytes 786440 | tf_op jit(solution)/shard_map/ppermute | solution.py:33
  120.1 12.6 %collective-permute-start.28 = (f32[2,256,128]{2,1,0:T(8,128)}, f32[2,256,128]{2,1,0:T(8,128)S(1)}, u32[]{:S(2)}, u32[]{:S(2)}) collective-permute-start(f32[2,256,128]{2,1,0:T(8,128)} %get-tuple-element.37), channel_id=1, source_target_pairs={{0,2},{8,10},{1,3},{9,11},{2,0},{10,8},{3,1},{11,9},{16,18},{24,26... | collective-permute-start | bytes 786440 | tf_op jit(solution)/shard_map/ppermute | solution.py:33
  133.8 18.5 %collective-permute-start.29 = (f32[256,128]{1,0:T(8,128)S(1)}, f32[256,128]{1,0:T(8,128)S(1)}, u32[]{:S(2)}, u32[]{:S(2)}) collective-permute-start(f32[256,128]{1,0:T(8,128)S(1)} %dynamic-slice_bitcast_fusion), channel_id=1, source_target_pairs={{0,4},{8,12},{1,5},{9,13},{2,6},{10,14},{3,7},{11,15},{16,20},{24,... | collective-permute-start | bytes 393224 | tf_op jit(solution)/shard_map/ppermute | solution.py:33
  (6 other events, 20.3 us)

commit v2 on v1

v2 whole, which is shorter than its diff:
```python
import functools

import jax
import jax.numpy as jnp
from jax import lax
from jax.experimental import pallas as pl
from jax.experimental.pallas import tpu as pltpu
from jax.sharding import PartitionSpec as P

F32 = jnp.float32
BF16 = jnp.bfloat16
AXES = ("brow", "bcol")
SCANS = 2048
PIXELS = 16384
COMPS = 256
LOCAL = 16
PANEL = 2048
HALF = 1024
STEPS = (0, 1, -1, 2)
VMEM = pltpu.CompilerParams(vmem_limit_bytes=56 << 20)


def flat(x, y, z, k):
    return (((x // 2) * 4 + y) * 2 + k) * 8 + (x % 2) * 4 + z


def permute(value, move):
    pairs = []
    for x in range(4):
        for y in range(4):
            for z in range(4):
                for k in range(2):
                    x2, y2, z2, k2 = move(x, y, z, k)
                    pairs.append((flat(x, y, z, k), flat(x2, y2 % 4, z2 % 4, k2)))
    return lax.ppermute(value, AXES, pairs)


def spread_same(d):
    return lambda x, y, z, k: (x, y + d, z, k) if k == 0 else (x, y, z + d, k)


def spread_cross(d):
    return lambda x, y, z, k: (x, y, z + d, 1) if k == 0 else (x, y + d, z, 0)


def across(m):
    return lambda x, y, z, k: (x ^ m, y, z, k)


def around(d):
    return lambda x, y, z, k: (x, y, z + d, k) if k == 0 else (x, y + d, z, k)


def pick_kernel(at, patterns, *pieces):
    for n, piece in enumerate(pieces):
        for half in range(2):
            start = pl.multiple_of((half * 4 + at[n]) * PANEL, PANEL)
            piece[half] = patterns[:, pl.ds(start, PANEL)]


def pick(at, patterns):
    piece = jax.ShapeDtypeStruct((2, LOCAL, PANEL), BF16)
    return pl.pallas_call(
        pick_kernel,
        out_shape=[piece] * 8,
        in_specs=[pl.BlockSpec(memory_space=pltpu.SMEM), pl.BlockSpec(memory_space=pltpu.VMEM)],
        out_specs=[pl.BlockSpec(memory_space=pltpu.VMEM)] * 8,
        compiler_params=VMEM,
    )(at, patterns)


def group_kernel(at, *refs):
    pieces, groups = refs[:8], refs[8:]
    for n, group in enumerate(groups):
        half = at[n]
        for i, piece in enumerate(pieces):
            group[i] = piece[half]


def group(at, pieces):
    whole = jax.ShapeDtypeStruct((8, LOCAL, PANEL), BF16)
    return pl.pallas_call(
        group_kernel,
        out_shape=[whole] * 4,
        in_specs=[pl.BlockSpec(memory_space=pltpu.SMEM)] + [pl.BlockSpec(memory_space=pltpu.VMEM)] * 8,
        out_specs=[pl.BlockSpec(memory_space=pltpu.VMEM)] * 4,
        compiler_params=VMEM,
    )(at, *pieces)


def fetch(core, members, rows, cols, sems, row_first=0, row_width=HALF, only_rows=()):
    def start(by_core, offset):
        for own, recv, m, step in members:
            row_from, col_from = (own, recv) if by_core == 0 else (recv, own)
            if m not in only_rows:
                pltpu.make_async_copy(col_from, cols.at[m, step], sems.at[m]).start()
            for s in range(2):
                pltpu.make_async_copy(
                    row_from.at[s, :, :, pl.ds(offset, row_width)], rows.at[m, :, 1 - s, step], sems.at[m]
                ).start()

    @pl.when(core == 0)
    def _():
        start(0, row_first)

    @pl.when(core == 1)
    def _():
        start(1, HALF + row_first)


def fetched(members, rows, cols, sems, which, row_width=HALF, only_rows=()):
    for own, recv, m, step in members:
        if m == which:
            if m not in only_rows:
                pltpu.make_async_copy(own, cols.at[m, step], sems.at[m]).wait()
            for s in range(2):
                pltpu.make_async_copy(
                    own.at[s, :, :, pl.ds(0, row_width)], rows.at[m, :, 1 - s, step], sems.at[m]
                ).wait()


def views(own, recv, shapes):
    members = []
    for a, b, (groups, steps) in zip(own, recv, shapes):
        for i, m in enumerate(groups):
            for j, step in enumerate(steps):
                members.append((a.at[i, j], b.at[i, j], m, step))
    return members


SHAPE_OWN = [((0,), (0, 1, 2, 3))]
SHAPE_NEAR = [((1, 2), (n,)) for n in range(4)]
SHAPE_FAR = [((3,), (n,)) for n in range(4)]
ANY = pl.BlockSpec(memory_space=pl.ANY)
IN_VMEM = pl.BlockSpec(memory_space=pltpu.VMEM)
IN_SMEM = pl.BlockSpec(memory_space=pltpu.SMEM)
ROWS = pltpu.VMEM((4, 4, 2, 4, LOCAL, HALF), BF16)
COLS = pltpu.VMEM((4, 4, 2, 4, LOCAL, PANEL), BF16)


LEFT = (((0,), (0,)), ((), ()))


def ones_beside(block):
    return jnp.concatenate([block, jnp.ones((block.shape[0], 128), BF16)], axis=1)


def early_kernel(shapes, first, last, at, *refs):
    count = len(shapes)
    own, recv, comps = refs[:count], refs[count : 2 * count], refs[2 * count]
    refs = refs[2 * count + 1 :]
    if not first:
        t_in, rs_in, ys_in, origin_in = refs[:4]
        refs = refs[4:]
    if last:
        parts, means = refs[:2]
        refs = refs[2:]
    else:
        t_out, rs_out, ys_out, origin_out = refs[:4]
        refs = refs[4:]
    rows, cols, sems = refs
    members = views(own, recv, shapes)
    groups = sorted({member[2] for member in members})
    low = groups[0]
    members = [(a, b, m - low, step) for a, b, m, step in members]
    fetch(at[4], members, rows, cols, sems)
    total = jnp.zeros((COMPS, HALF), F32) if first else t_in[...]
    row_sum = jnp.zeros((1, HALF), F32) if first else rs_in[...]
    score_sum = jnp.zeros((1, COMPS), F32) if first else ys_in[...]
    origin = None if first else origin_in[...]
    for m in range(len(groups)):
        fetched(members, rows, cols, sems, m)
        score = jnp.dot(cols[m].reshape(512, PANEL), comps[...], preferred_element_type=F32)
        score = score[:, :COMPS] + score[:, COMPS:]
        added = jnp.sum(score, axis=0, keepdims=True)
        score_sum = score_sum + added
        if origin is None:
            origin = added / 512
        centred = score - origin
        high = centred.astype(BF16)
        lower = (centred - high.astype(F32)).astype(BF16)
        left = ones_beside(jnp.concatenate([high, lower], axis=1))
        product = lax.dot_general(left, rows[m].reshape(512, HALF), LEFT, preferred_element_type=F32)
        total = total + (product[:COMPS] + product[COMPS : 2 * COMPS])
        row_sum = row_sum + product[2 * COMPS : 2 * COMPS + 1]
    if last:
        shift = score_sum / SCANS - origin
        shift = jnp.transpose(jnp.broadcast_to(shift, (128, COMPS)))[:, :1]
        total = (total - shift * row_sum) * (1.0 / (SCANS - 1))
        for c in range(8):
            parts[c] = total[:, c * 128 : (c + 1) * 128]
        means[...] = row_sum * (1.0 / SCANS)
    else:
        t_out[...] = total
        rs_out[...] = row_sum
        ys_out[...] = score_sum
        origin_out[...] = origin


def early(at, own, recv, shapes, comps, before=(), last=False):
    count = len(own)
    groups = len({m for groups, _ in shapes for m in groups})
    state = [
        jax.ShapeDtypeStruct((COMPS, HALF), F32),
        jax.ShapeDtypeStruct((1, HALF), F32),
        jax.ShapeDtypeStruct((1, COMPS), F32),
        jax.ShapeDtypeStruct((1, COMPS), F32),
    ]
    result = [jax.ShapeDtypeStruct((8, COMPS, 128), F32), jax.ShapeDtypeStruct((1, HALF), F32)]
    return pl.pallas_call(
        functools.partial(early_kernel, shapes, not before, last),
        out_shape=result if last else state,
        in_specs=[IN_SMEM] + [ANY] * (2 * count) + [IN_VMEM] * (1 + len(before)),
        out_specs=[IN_VMEM] * (2 if last else 4),
        scratch_shapes=[
            pltpu.VMEM((groups, 4, 2, 4, LOCAL, HALF), BF16),
            pltpu.VMEM((groups, 4, 2, 4, LOCAL, PANEL), BF16),
            pltpu.SemaphoreType.DMA((4,)),
        ],
        compiler_params=pltpu.CompilerParams(vmem_limit_bytes=28 << 20),
        cost_estimate=pl.CostEstimate(flops=(2 * groups) << 30, bytes_accessed=(4 * groups) << 20, transcendentals=0),
    )(at, *own, *recv, comps, *before)


def gram_kernel(at, *refs):
    own, recv, row_means, out = refs[:9], refs[9:18], refs[18], refs[19]
    rows, cols, stage, col_sums, sems, out_sems = refs[20:]
    members = views(own, recv, SHAPE_OWN + SHAPE_NEAR + SHAPE_FAR)
    fetch(at[4], members, rows, cols, sems)
    copies = []
    for i in range(4):
        slot = i % 2
        if i >= 2:
            copies[i - 2].wait()
        span_i = slice(i * 256, (i + 1) * 256)
        row_mean = jnp.transpose(jnp.broadcast_to(row_means[:, span_i], (128, 256)))[:, :1]
        if i == 0:
            for m in range(4):
                fetched(members, rows, cols, sems, m)
                left = ones_beside(rows[m, :, :, :, :, span_i].reshape(512, 256))
                for j in range(8):
                    span = slice(j * 256, (j + 1) * 256)
                    right = cols[m, :, :, :, :, span].reshape(512, 256)
                    both = lax.dot_general(left, right, LEFT, preferred_element_type=F32)
                    tile, col_sum = both[:256], both[256:257]
                    if m > 0:
                        tile += stage[slot, :, span]
                        col_sum += col_sums[:, span]
                    if m == 3:
                        tile = (tile - row_mean * col_sum) * (1.0 / (SCANS - 1))
                    stage[slot, :, span] = tile
                    col_sums[:, span] = col_sum
        else:
            left = rows[:, :, :, :, :, span_i].reshape(SCANS, 256)
            for j in range(8):
                span = slice(j * 256, (j + 1) * 256)
                right = cols[:, :, :, :, :, span].reshape(SCANS, 256)
                tile = lax.dot_general(left, right, LEFT, preferred_element_type=F32)
                stage[slot, :, span] = (tile - row_mean * col_sums[:, span]) * (1.0 / (SCANS - 1))
        copy = pltpu.make_async_copy(stage.at[slot], out.at[pl.ds(i * 256, 256), :], out_sems.at[slot])
        copy.start()
        copies.append(copy)
    for copy in copies[2:]:
        copy.wait()


def gram(at, own, recv, row_means):
    return pl.pallas_call(
        gram_kernel,
        out_shape=jax.ShapeDtypeStruct((HALF, PANEL), F32),
        in_specs=[IN_SMEM] + [ANY] * 18 + [IN_VMEM],
        out_specs=ANY,
        scratch_shapes=[
            ROWS,
            COLS,
            pltpu.VMEM((2, 256, PANEL), F32),
            pltpu.VMEM((1, PANEL), F32),
            pltpu.SemaphoreType.DMA((4,)),
            pltpu.SemaphoreType.DMA((2,)),
        ],
        compiler_params=pltpu.CompilerParams(vmem_limit_bytes=30 << 20),
        cost_estimate=pl.CostEstimate(flops=8 << 30, bytes_accessed=20 << 20, transcendentals=0),
    )(at, *[pltpu.with_memory_space_constraint(piece, pltpu.HBM) for piece in own + recv], row_means)


def on_device(patterns, components):
    row = lax.axis_index("brow")
    col = lax.axis_index("bcol")
    k, y, xh = row % 2, (row // 2) % 4, row // 8
    z, xl = col % 4, col // 4
    first = k == 0
    same = jnp.where(first, y, z)
    cross = jnp.where(first, z, y)
    at = jnp.stack([(same + d) % 4 for d in STEPS] + [(cross + d) % 4 for d in STEPS]).astype(jnp.int32)
    sends = pick(at, patterns)
    got = [sends[0]]
    got += [permute(sends[n], spread_same(STEPS[n])) for n in range(1, 4)]
    got += [permute(sends[4 + n], spread_cross(STEPS[n])) for n in range(4)]
    own_half = jnp.where(first, xh, xl)
    at = jnp.stack(
        [own_half, jnp.where(first, own_half, 1 - own_half), jnp.where(first, 1 - own_half, own_half), 1 - own_half]
    ).astype(jnp.int32)
    sends = group(at, got)
    shape = (2, 4, LOCAL, PANEL)
    swap = lambda x, y, z, k: (x, y, z, 1 - k)
    high = lax.reduce_precision(components, 8, 7)
    comps = jnp.concatenate([high, components - high], axis=1).astype(BF16)
    group_own = sends[0]
    near = [permute(sends[1], across(1)), permute(sends[3], across(3))]
    ring_own = [permute(group_own, around(d)) for d in STEPS[1:]]
    late, ring_own = lax.optimization_barrier((sends[2], ring_own))
    far = permute(late, across(2))
    own = [jnp.stack([group_own] + ring_own).reshape((1, 4) + shape)]
    recv = [permute(own[0], swap)]
    recv, far = lax.optimization_barrier((recv, far))
    at = jnp.stack([k] * 5).astype(jnp.int32)
    group_near = jnp.stack(near)
    ring_near = [group_near] + [permute(group_near, around(d)) for d in STEPS[1:]]
    own_near = [r.reshape((2, 1) + shape) for r in ring_near]
    state = early(at, own, recv, SHAPE_OWN, comps)
    far, ring_near[1:], state = lax.optimization_barrier((far, ring_near[1:], state))
    recv_near = [permute(r, swap) for r in own_near]
    ring_far = [far] + [permute(far, around(d)) for d in STEPS[1:]]
    own_far = [r.reshape((1, 1) + shape) for r in ring_far]
    state = early(at, own_near, recv_near, SHAPE_NEAR, comps, state)
    recv_far = [permute(r, swap) for r in own_far]
    parts, row_means = early(at, own_far, recv_far, SHAPE_FAR, comps, state, True)
    own = own + own_near + own_far
    recv = recv + recv_near + recv_far
    parts = lax.all_to_all(parts, "bcol", 0, 0, tiled=True)
    covariance = gram(at, own, recv, row_means)
    projected = jnp.sum(parts, axis=0).T
    means_part = lax.dynamic_slice_in_dim(row_means[0], col * 128, 128, 0)
    return covariance, projected, means_part


def solution(mesh):
    return jax.shard_map(
        on_device,
        mesh=mesh,
        in_specs=(P(("brow", "bcol"), None), P("bcol", None)),
        out_specs=(P("brow", "bcol"), P(("brow", "bcol"), None), P(("brow", "bcol"))),
        check_vma=False,
    )
```

time: 154 us -> 128 us (0.83)
  waiting for transfers between devices: 61.6 us -> 41.3 us
  other arithmetic: 7.9 us -> 2.59 us
    ppermute x30 -> x28, waiting for transfers between devices: 61.6 us -> 41.3 us  [permute(): return lax.ppermute(value, AXES, pairs)]
    another operation x4, other arithmetic: 6.21 us -> 1.82 us  [the longest x1 1.3 us: on_device(): own = [jnp.stack([group_own] + ring_own).reshape((1, 4) + shape)]]
    all_to_all x0 -> x1, starting transfers between devices: none -> 3.64 us  [on_device(): parts = lax.all_to_all(parts, 'bcol', 0, 0, tiled=True)]
    ppermute x30 -> x28, starting transfers between devices: 40.2 us -> 37.5 us  [permute(): return lax.ppermute(value, AXES, pairs)]
    pallas_call x2 -> x4, Pallas kernels: 33.7 us -> 34.4 us  [the longest x3 18.8 us: early(): pl.pallas_call(functools.partial(early_kernel, shapes, not before, last),...]
  transfers between devices with their start and end apart: 30 -> 29, of which waited for: 11 -> 8; matrix products, arithmetic and copies ran while one was open for 6% -> 2% of each run, Pallas kernels for 11% -> 23%
where the time goes in v2:
time: 128 us
  waiting for transfers between devices  41.3 us (32%)
  starting transfers between devices  41.1 us (32%)
  Pallas kernels  39.2 us (31%)
  other arithmetic  2.59 us (2%)
  local copies, waits for them, and re-layouts  2.55 us (2%)
    ppermute x28, waiting for transfers between devices, permute(): return lax.ppermute(value, AXES, pairs)  41.3 us
    ppermute x28, starting transfers between devices, permute(): return lax.ppermute(value, AXES, pairs)  37.5 us
    pallas_call x3, Pallas kernels, early(): pl.pallas_call(functools.partial(early_kernel, shapes, not before, last),...  18.8 us
    pallas_call x1, Pallas kernels, gram(): pl.pallas_call(gram_kernel, out_shape=jax.ShapeDtypeStruct((HALF, PANEL),...  15.7 us
    all_to_all x1, starting transfers between devices, on_device(): parts = lax.all_to_all(parts, 'bcol', 0, 0, tiled=True)  3.64 us
    pallas_call x1, Pallas kernels, group(): pl.pallas_call(group_kernel, out_shape=[whole] * 4, in_specs=[pl.BlockSpe...  2.73 us
  transfers between devices with their start and end apart: 29, of which 8 were waited for; matrix products, arithmetic and copies ran while one was open for 2% of the time, Pallas kernels for 23%

profile of v2, /device:TPU:1, one launch (start us, length us, event | category | flops | bytes accessed | tf_op | source)
XLA Modules:
  0.0 128.0 jit_solution(4928195023665266501)
XLA Ops:
  1.4 2.1 %shard_map.49 = (bf16[2,16,2048]{2,1,0:T(8,128)(2,1)}, bf16[2,16,2048]{2,1,0:T(8,128)(2,1)}, bf16[2,16,2048]{2,1,0:T(8,128)(2,1)}, bf16[2,16,2048]{2,1,0:T(8,128...) custom-call(s32[8]{0:T(128)} %stack.94.at, ...), custom_call_target="tpu_custom_call" | custom-call | tf_op jit(solution)/shard_map/pallas_call | solution.py:63
  3.5 2.5 %collective-permute-start = (bf16[2,16,2048]{2,1,0:T(8,128)(2,1)}, bf16[2,16,2048]{2,1,0:T(8,128)(2,1)S(1)}, u32[]{:S(2)}, u32[]{:S(2)}) collective-permute-start(bf16[2,16,2048]{2,1,0:T(8,128)(2,1)} %get-tuple-element.37), channel_id=1, source_target_pairs={{0,16},{8,9},{1,17},{9,10},{2,18},{10,11},{3,19},{11,8},{16,32},{2... | collective-permute-start | bytes 393224 | tf_op jit(solution)/shard_map/ppermute | solution.py:35
  5.9 2.1 %collective-permute-start.1 = (bf16[2,16,2048]{2,1,0:T(8,128)(2,1)}, bf16[2,16,2048]{2,1,0:T(8,128)(2,1)S(1)}, u32[]{:S(2)}, u32[]{:S(2)}) collective-permute-start(bf16[2,16,2048]{2,1,0:T(8,128)(2,1)} %get-tuple-element.38), channel_id=1, source_target_pairs={{0,48},{8,11},{1,49},{9,8},{2,50},{10,9},{3,51},{11,10},{16,0},{24... | collective-permute-start | bytes 393224 | tf_op jit(solution)/shard_map/ppermute | solution.py:35
  8.1 1.3 collective-permute-start.2
  11.0 2.1 %collective-permute-start.5 = (bf16[2,16,2048]{2,1,0:T(8,128)(2,1)}, bf16[2,16,2048]{2,1,0:T(8,128)(2,1)S(1)}, u32[]{:S(2)}, u32[]{:S(2)}) collective-permute-start(bf16[2,16,2048]{2,1,0:T(8,128)(2,1)} %get-tuple-element.42), channel_id=1, source_target_pairs={{0,11},{8,48},{1,8},{9,49},{2,9},{10,50},{3,10},{11,51},{16,27},{2... | collective-permute-start | bytes 393224 | tf_op jit(solution)/shard_map/ppermute | solution.py:35
  13.1 3.0 %collective-permute-start.6 = (bf16[2,16,2048]{2,1,0:T(8,128)(2,1)}, bf16[2,16,2048]{2,1,0:T(8,128)(2,1)S(1)}, u32[]{:S(2)}, u32[]{:S(2)}) collective-permute-start(bf16[2,16,2048]{2,1,0:T(8,128)(2,1)} %get-tuple-element.43), channel_id=1, source_target_pairs={{0,10},{8,32},{1,11},{9,33},{2,8},{10,34},{3,9},{11,35},{16,26},{2... | collective-permute-start | bytes 393224 | tf_op jit(solution)/shard_map/ppermute | solution.py:35
  16.7 3.3 %collective-permute-done.6.refs_7_ = bf16[2,16,2048]{2,1,0:T(8,128)(2,1)S(1)} collective-permute-done((bf16[2,16,2048]{2,1,0:T(8,128)(2,1)}, bf16[2,16,2048]{2,1,0:T(8,128)(2,1)S(1)}, u32[]{:S(2)}, u32[]{:S(2)}) %collective-permute-start.6) | collective-permute-done | bytes 131104 | tf_op jit(solution)/shard_map/ppermute | solution.py:35
  20.6 2.7 %shard_map.50 = (bf16[8,16,2048]{2,1,0:T(8,128)(2,1)}, bf16[8,16,2048]{2,1,0:T(8,128)(2,1)}, bf16[8,16,2048]{2,1,0:T(8,128)(2,1)}, bf16[8,16,2048]{2,1,0:T(8,128)(2,1)}) custom-call(s32[4]{0:T(128)} %pad_add_fusion.at, bf16[2,16,2048]{2,1,0:T(8,128)(2,1)} %get-tuple-element.36.refs_0_, bf16[2,16,2048]{2,1,0:T(8,128)(2,1)} %copy-done.19, ...), custom_call_target="tpu_custom_call" | custom-call | tf_op jit(solution)/shard_map/pallas_call | solution.py:82
  24.3 1.5 %collective-permute-start.8 = (bf16[8,16,2048]{2,1,0:T(8,128)(2,1)}, bf16[8,16,2048]{2,1,0:T(8,128)(2,1)S(1)}, u32[]{:S(2)}, u32[]{:S(2)}) collective-permute-start(bf16[8,16,2048]{2,1,0:T(8,128)(2,1)} %get-tuple-element.44), channel_id=1, source_target_pairs={{0,3},{8,56},{1,0},{9,57},{2,1},{10,58},{3,2},{11,59},{16,19},{24,... | collective-permute-start | bytes 1572872 | tf_op jit(solution)/shard_map/ppermute | solution.py:35
  27.1 1.8 %collective-permute-start.11 = (bf16[8,16,2048]{2,1,0:T(8,128)(2,1)}, bf16[8,16,2048]{2,1,0:T(8,128)(2,1)S(1)}, u32[]{:S(2)}, u32[]{:S(2)}) collective-permute-start(bf16[8,16,2048]{2,1,0:T(8,128)(2,1)} %get-tuple-element.50), channel_id=1, source_target_pairs={{0,68},{8,76},{1,69},{9,77},{2,70},{10,78},{3,71},{11,79},{16,84},... | collective-permute-start | bytes 1572872 | tf_op jit(solution)/shard_map/ppermute | solution.py:35
  28.9 4.6 %collective-permute-done.9 = bf16[8,16,2048]{2,1,0:T(8,128)(2,1)S(1)} collective-permute-done((bf16[8,16,2048]{2,1,0:T(8,128)(2,1)}, bf16[8,16,2048]{2,1,0:T(8,128)(2,1)S(1)}, u32[]{:S(2)}, u32[]{:S(2)}) %collective-permute-start.9) | collective-permute-done | bytes 524320 | tf_op jit(solution)/shard_map/ppermute | solution.py:35
  33.4 3.9 %collective-permute-done.8 = bf16[8,16,2048]{2,1,0:T(8,128)(2,1)S(1)} collective-permute-done((bf16[8,16,2048]{2,1,0:T(8,128)(2,1)}, bf16[8,16,2048]{2,1,0:T(8,128)(2,1)S(1)}, u32[]{:S(2)}, u32[]{:S(2)}) %collective-permute-start.8) | collective-permute-done | bytes 524320 | tf_op jit(solution)/shard_map/ppermute | solution.py:35
  37.3 1.7 %collective-permute-done.7 = bf16[8,16,2048]{2,1,0:T(8,128)(2,1)S(1)} collective-permute-done((bf16[8,16,2048]{2,1,0:T(8,128)(2,1)}, bf16[8,16,2048]{2,1,0:T(8,128)(2,1)S(1)}, u32[]{:S(2)}, u32[]{:S(2)}) %collective-permute-start.7) | collective-permute-done | bytes 524320 | tf_op jit(solution)/shard_map/ppermute | solution.py:35
  39.0 1.3 %pad_maximum_fusion.refs_0_ = bf16[1,4,2,4,16,2048]{5,4,3,2,1,0:T(8,128)(2,1)S(1)} fusion(bf16[1,1,2,4,16,2048]{5,4,3,2,1,0:T(8,128)(2,1)S(1)} %bitcast.57, bf16[1,1,2,4,16,2048]{5,4,3,2,1,0:T(8,128)(2,1)S(1)} %bitcast.58, bf16[1,1,2,4,16,2048]{5,4,3,2,1,0:T(8,128)(2,1)S(1)} %bitcast.59, bf16[1,1,2,4,16,2048]{5,4,3,2,1,0:T(8,128)(2,1)} %bitcast.56), kind=kLoop, calls=%fused_computation.3 | loop fusion | flops 3145728 | bytes 4194304 | tf_op jit(solution)/shard_map/stack | solution.py:313
  40.3 1.7 %collective-permute-start.15 = (bf16[1,4,2,4,16,2048]{5,4,3,2,1,0:T(8,128)(2,1)S(1)}, bf16[1,4,2,4,16,2048]{5,4,3,2,1,0:T(8,128)(2,1)S(1)}, u32[]{:S(2)}, u32[]{:S(2)}) collective-permute-start(bf16[1,4,2,4,16,2048]{5,4,3,2,1,0:T(8,128)(2,1)S(1)} %pad_maximum_fusion.refs_0_), channel_id=1, source_target_pairs={{0,8},{8,0},{1,9},{9,1},{2,10},{10,2},{3,11},{11,3},{16,24},{24,16... | collective-permute-start | bytes 6291464 | tf_op jit(solution)/shard_map/ppermute | solution.py:35
  42.2 1.6 %collective-permute-start.14 = (bf16[2,8,16,2048]{3,2,1,0:T(8,128)(2,1)S(1)}, bf16[2,8,16,2048]{3,2,1,0:T(8,128)(2,1)S(1)}, u32[]{:S(2)}, u32[]{:S(2)}) collective-permute-start(bf16[2,8,16,2048]{3,2,1,0:T(8,128)(2,1)S(1)} %pad_maximum_fusion.3), channel_id=1, source_target_pairs={{0,2},{8,40},{1,3},{9,41},{2,0},{10,42},{3,1},{11,43},{16,18},{24,... | collective-permute-start | bytes 3145736 | tf_op jit(solution)/shard_map/ppermute | solution.py:35
  43.8 1.4 %collective-permute-start.13 = (bf16[2,8,16,2048]{3,2,1,0:T(8,128)(2,1)S(1)}, bf16[2,8,16,2048]{3,2,1,0:T(8,128)(2,1)S(1)}, u32[]{:S(2)}, u32[]{:S(2)}) collective-permute-start(bf16[2,8,16,2048]{3,2,1,0:T(8,128)(2,1)S(1)} %pad_maximum_fusion.3), channel_id=1, source_target_pairs={{0,3},{8,56},{1,0},{9,57},{2,1},{10,58},{3,2},{11,59},{16,19},{24,... | collective-permute-start | bytes 3145736 | tf_op jit(solution)/shard_map/ppermute | solution.py:35
  45.2 2.7 %collective-permute-start.16 = (bf16[8,16,2048]{2,1,0:T(8,128)(2,1)S(1)}, bf16[8,16,2048]{2,1,0:T(8,128)(2,1)S(1)}, u32[]{:S(2)}, u32[]{:S(2)}) collective-permute-start(bf16[8,16,2048]{2,1,0:T(8,128)(2,1)S(1)} %copy-done.26), channel_id=1, source_target_pairs={{0,64},{8,72},{1,65},{9,73},{2,66},{10,74},{3,67},{11,75},{16,80},... | collective-permute-start | bytes 1572872 | tf_op jit(solution)/shard_map/ppermute | solution.py:35
  48.1 10.6 %collective-permute-done.16 = bf16[8,16,2048]{2,1,0:T(8,128)(2,1)S(1)} collective-permute-done((bf16[8,16,2048]{2,1,0:T(8,128)(2,1)S(1)}, bf16[8,16,2048]{2,1,0:T(8,128)(2,1)S(1)}, u32[]{:S(2)}, u32[]{:S(2)}) %collective-permute-start.16) | collective-permute-done | bytes 524320 | tf_op jit(solution)/shard_map/ppermute | solution.py:35
  58.7 2.3 %collective-permute-start.20 = (bf16[2,1,2,4,16,2048]{5,4,3,2,1,0:T(8,128)(2,1)S(1)}, bf16[2,1,2,4,16,2048]{5,4,3,2,1,0:T(8,128)(2,1)S(1)}, u32[]{:S(2)}, u32[]{:S(2)}) collective-permute-start(bf16[2,1,2,4,16,2048]{5,4,3,2,1,0:T(8,128)(2,1)S(1)} %pad_maximum_fusion.2.refs_0_.refs_1_), channel_id=1, source_target_pairs={{0,8},{8,0},{1,9},{9,1},{2,10},{10,2},{3,11},{11,3},{16,24},{24,16... | collective-permute-start | bytes 3145736 | tf_op jit(solution)/shard_map/ppermute | solution.py:35
  61.1 7.7 %collective-permute-done.13 = bf16[2,8,16,2048]{3,2,1,0:T(8,128)(2,1)S(1)} collective-permute-done((bf16[2,8,16,2048]{3,2,1,0:T(8,128)(2,1)S(1)}, bf16[2,8,16,2048]{3,2,1,0:T(8,128)(2,1)S(1)}, u32[]{:S(2)}, u32[]{:S(2)}) %collective-permute-start.13) | collective-permute-done | bytes 1048608 | tf_op jit(solution)/shard_map/ppermute | solution.py:35
  68.9 1.8 %collective-permute-start.22 = (bf16[2,1,2,4,16,2048]{5,4,3,2,1,0:T(8,128)(2,1)S(1)}, bf16[2,1,2,4,16,2048]{5,4,3,2,1,0:T(8,128)(2,1)S(1)}, u32[]{:S(2)}, u32[]{:S(2)}) collective-permute-start(bf16[2,1,2,4,16,2048]{5,4,3,2,1,0:T(8,128)(2,1)S(1)} %bitcast.33), channel_id=1, source_target_pairs={{0,8},{8,0},{1,9},{9,1},{2,10},{10,2},{3,11},{11,3},{16,24},{24,16... | collective-permute-start | bytes 3145736 | tf_op jit(solution)/shard_map/ppermute | solution.py:35
  71.3 4.4 %shard_map.51 = (f32[256,1024]{1,0:T(8,128)S(1)}, f32[1,1024]{1,0:T(1,128)S(1)}, f32[1,256]{1,0:T(1,128)S(1)}, f32[1,256]{1,0:T(1,128)S(1)}) custom-call(s32[5]{0:T(128)S(1)} %stack.80.at, bf16[1,4,2,4,16,2048]{5,4,3,2,1,0:T(8,128)(2,1)S(1)} %pad_maximum_fusion.refs_0_, bf16[1,4,2,4,16,2048]{5,4,3,2,1,0:T(8,128)(2,1)S(1)} %collective-permute-done.15.refs_1_.refs_9_, ...), custom_call_target="tpu_custom_call" | custom-call | flops 2147483648 | bytes 4194304 | tf_op jit(solution)/shard_map/pallas_call | solution.py:210
  75.7 2.2 %collective-permute-start.19 = (bf16[8,16,2048]{2,1,0:T(8,128)(2,1)S(1)}, bf16[8,16,2048]{2,1,0:T(8,128)(2,1)S(1)}, u32[]{:S(2)}, u32[]{:S(2)}) collective-permute-start(bf16[8,16,2048]{2,1,0:T(8,128)(2,1)S(1)} %collective-permute-done.16), channel_id=1, source_target_pairs={{0,2},{8,40},{1,3},{9,41},{2,0},{10,42},{3,1},{11,43},{16,18},{24,... | collective-permute-start | bytes 1572872 | tf_op jit(solution)/shard_map/ppermute | solution.py:35
  79.4 1.3 collective-permute-start.24
  80.7 5.0 %collective-permute-done.19 = bf16[8,16,2048]{2,1,0:T(8,128)(2,1)S(1)} collective-permute-done((bf16[8,16,2048]{2,1,0:T(8,128)(2,1)S(1)}, bf16[8,16,2048]{2,1,0:T(8,128)(2,1)S(1)}, u32[]{:S(2)}, u32[]{:S(2)}) %collective-permute-start.19) | collective-permute-done | bytes 524320 | tf_op jit(solution)/shard_map/ppermute | solution.py:35
  85.7 1.4 %collective-permute-start.27 = (bf16[1,1,2,4,16,2048]{5,4,3,2,1,0:T(8,128)(2,1)S(1)}, bf16[1,1,2,4,16,2048]{5,4,3,2,1,0:T(8,128)(2,1)S(1)}, u32[]{:S(2)}, u32[]{:S(2)}) collective-permute-start(bf16[1,1,2,4,16,2048]{5,4,3,2,1,0:T(8,128)(2,1)S(1)} %bitcast.42), channel_id=1, source_target_pairs={{0,8},{8,0},{1,9},{9,1},{2,10},{10,2},{3,11},{11,3},{16,24},{24,16... | collective-permute-start | bytes 1572872 | tf_op jit(solution)/shard_map/ppermute | solution.py:35
  87.1 4.5 %collective-permute-done.18 = bf16[8,16,2048]{2,1,0:T(8,128)(2,1)S(1)} collective-permute-done((bf16[8,16,2048]{2,1,0:T(8,128)(2,1)S(1)}, bf16[8,16,2048]{2,1,0:T(8,128)(2,1)S(1)}, u32[]{:S(2)}, u32[]{:S(2)}) %collective-permute-start.18) | collective-permute-done | bytes 524320 | tf_op jit(solution)/shard_map/ppermute | solution.py:35
  92.8 8.8 %shard_map.52 = (f32[256,1024]{1,0:T(8,128)S(1)}, f32[1,1024]{1,0:T(1,128)S(1)}, f32[1,256]{1,0:T(1,128)S(1)}, f32[1,256]{1,0:T(1,128)S(1)}) custom-call(s32[5]{0:T(128)S(1)} %stack.80.at, bf16[2,1,2,4,16,2048]{5,4,3,2,1,0:T(8,128)(2,1)S(1)} %pad_maximum_fusion.2.refs_0_.refs_1_, bf16[2,1,2,4,16,2048]{5,4,3,2,1,0:T(8,128)(2,1)S(1)} %bitcast.37, ...), custom_call_target="tpu_custom_call" | custom-call | flops 4294967296 | bytes 8388608 | tf_op jit(solution)/shard_map/pallas_call | solution.py:210
  101.8 5.6 %shard_map.53 = (f32[8,256,128]{2,1,0:T(8,128)}, f32[1,1024]{1,0:T(1,128)S(1)}) custom-call(s32[5]{0:T(128)S(1)} %stack.80.at, bf16[1,1,2,4,16,2048]{5,4,3,2,1,0:T(8,128)(2,1)S(1)} %bitcast.40, bf16[1,1,2,4,16,2048]{5,4,3,2,1,0:T(8,128)(2,1)S(1)} %bitcast.49, bf16[1,1,2,4,16,2048]{5,4,3,2,1,0:T(8,128)(2,1)S(1)} %bitcast.46, ...), custom_call_target="tpu_custom_call" | custom-call | flops 2147483648 | bytes 4194304 | tf_op jit(solution)/shard_map/pallas_call | solution.py:210
  107.4 3.6 %all-to-all-start = ((f32[8,256,128]{2,1,0:T(8,128)}), f32[8,256,128]{2,1,0:T(8,128)S(1)}, u32[]{:S(2)}, u32[]{:S(2)}) async-start(f32[8,256,128]{2,1,0:T(8,128)} %get-tuple-element.68), calls=%async_computation | async-start | bytes 2097152 | tf_op jit(solution)/shard_map/all_to_all | solution.py:330
  111.5 15.7 %shard_map.54 = f32[1024,2048]{1,0:T(8,128)} custom-call(s32[5]{0:T(128)S(1)} %stack.80.at, bf16[1,4,2,4,16,2048]{5,4,3,2,1,0:T(8,128)(2,1)} %copy-done, bf16[2,1,2,4,16,2048]{5,4,3,2,1,0:T(8,128)(2,1)} %copy-done.1, bf16[2,1,2,4,16,2048]{5,4,3,2,1,0:T(8,128)(2,1)} %bitcast.38, bf16[2,1,2,4,16,2048]{5,4,3,2,1,0:T(8,128)(2,1)} %bitcast.35, ...), custom_call_target="tpu_custom_call" | custom-call | flops 8589934592 | bytes 20971520 | tf_op jit(solution)/shard_map/pallas_call | solution.py:268
  (97 shorter events, 10.7 us)
Async XLA Ops:
  3.5 7.6 %collective-permute-start = (bf16[2,16,2048]{2,1,0:T(8,128)(2,1)}, bf16[2,16,2048]{2,1,0:T(8,128)(2,1)S(1)}, u32[]{:S(2)}, u32[]{:S(2)}) collective-permute-start(bf16[2,16,2048]{2,1,0:T(8,128)(2,1)} %get-tuple-element.37), channel_id=1, source_target_pairs={{0,16},{8,9},{1,17},{9,10},{2,18},{10,11},{3,19},{11,8},{16,32},{2... | collective-permute-start | bytes 393224 | tf_op jit(solution)/shard_map/ppermute | solution.py:35
  5.9 7.2 %collective-permute-start.1 = (bf16[2,16,2048]{2,1,0:T(8,128)(2,1)}, bf16[2,16,2048]{2,1,0:T(8,128)(2,1)S(1)}, u32[]{:S(2)}, u32[]{:S(2)}) collective-permute-start(bf16[2,16,2048]{2,1,0:T(8,128)(2,1)} %get-tuple-element.38), channel_id=1, source_target_pairs={{0,48},{8,11},{1,49},{9,8},{2,50},{10,9},{3,51},{11,10},{16,0},{24... | collective-permute-start | bytes 393224 | tf_op jit(solution)/shard_map/ppermute | solution.py:35
  8.1 8.6 %collective-permute-start.2 = (bf16[2,16,2048]{2,1,0:T(8,128)(2,1)}, bf16[2,16,2048]{2,1,0:T(8,128)(2,1)S(1)}, u32[]{:S(2)}, u32[]{:S(2)}) collective-permute-start(bf16[2,16,2048]{2,1,0:T(8,128)(2,1)} %get-tuple-element.39), channel_id=1, source_target_pairs={{0,32},{8,10},{1,33},{9,11},{2,34},{10,8},{3,35},{11,9},{16,48},{2... | collective-permute-start | bytes 393224 | tf_op jit(solution)/shard_map/ppermute | solution.py:35
  9.4 7.3 %collective-permute-start.3 = (bf16[2,16,2048]{2,1,0:T(8,128)(2,1)}, bf16[2,16,2048]{2,1,0:T(8,128)(2,1)S(1)}, u32[]{:S(2)}, u32[]{:S(2)}) collective-permute-start(bf16[2,16,2048]{2,1,0:T(8,128)(2,1)} %get-tuple-element.40), channel_id=1, source_target_pairs={{0,8},{8,0},{1,9},{9,1},{2,10},{10,2},{3,11},{11,3},{16,24},{24,16... | collective-permute-start | bytes 393224 | tf_op jit(solution)/shard_map/ppermute | solution.py:35
  10.2 6.5 %collective-permute-start.4 = (bf16[2,16,2048]{2,1,0:T(8,128)(2,1)}, bf16[2,16,2048]{2,1,0:T(8,128)(2,1)S(1)}, u32[]{:S(2)}, u32[]{:S(2)}) collective-permute-start(bf16[2,16,2048]{2,1,0:T(8,128)(2,1)} %get-tuple-element.41), channel_id=1, source_target_pairs={{0,9},{8,16},{1,10},{9,17},{2,11},{10,18},{3,8},{11,19},{16,25},{2... | collective-permute-start | bytes 393224 | tf_op jit(solution)/shard_map/ppermute | solution.py:35
  11.0 5.6 %collective-permute-start.5 = (bf16[2,16,2048]{2,1,0:T(8,128)(2,1)}, bf16[2,16,2048]{2,1,0:T(8,128)(2,1)S(1)}, u32[]{:S(2)}, u32[]{:S(2)}) collective-permute-start(bf16[2,16,2048]{2,1,0:T(8,128)(2,1)} %get-tuple-element.42), channel_id=1, source_target_pairs={{0,11},{8,48},{1,8},{9,49},{2,9},{10,50},{3,10},{11,51},{16,27},{2... | collective-permute-start | bytes 393224 | tf_op jit(solution)/shard_map/ppermute | solution.py:35
  13.1 6.8 %collective-permute-start.6 = (bf16[2,16,2048]{2,1,0:T(8,128)(2,1)}, bf16[2,16,2048]{2,1,0:T(8,128)(2,1)S(1)}, u32[]{:S(2)}, u32[]{:S(2)}) collective-permute-start(bf16[2,16,2048]{2,1,0:T(8,128)(2,1)} %get-tuple-element.43), channel_id=1, source_target_pairs={{0,10},{8,32},{1,11},{9,33},{2,8},{10,34},{3,9},{11,35},{16,26},{2... | collective-permute-start | bytes 393224 | tf_op jit(solution)/shard_map/ppermute | solution.py:35
  23.3 10.1 %collective-permute-start.9 = (bf16[8,16,2048]{2,1,0:T(8,128)(2,1)}, bf16[8,16,2048]{2,1,0:T(8,128)(2,1)S(1)}, u32[]{:S(2)}, u32[]{:S(2)}) collective-permute-start(bf16[8,16,2048]{2,1,0:T(8,128)(2,1)} %get-tuple-element.44), channel_id=1, source_target_pairs={{0,2},{8,40},{1,3},{9,41},{2,0},{10,42},{3,1},{11,43},{16,18},{24,... | collective-permute-start | bytes 1572872 | tf_op jit(solution)/shard_map/ppermute | solution.py:35
  24.3 13.0 %collective-permute-start.8 = (bf16[8,16,2048]{2,1,0:T(8,128)(2,1)}, bf16[8,16,2048]{2,1,0:T(8,128)(2,1)S(1)}, u32[]{:S(2)}, u32[]{:S(2)}) collective-permute-start(bf16[8,16,2048]{2,1,0:T(8,128)(2,1)} %get-tuple-element.44), channel_id=1, source_target_pairs={{0,3},{8,56},{1,0},{9,57},{2,1},{10,58},{3,2},{11,59},{16,19},{24,... | collective-permute-start | bytes 1572872 | tf_op jit(solution)/shard_map/ppermute | solution.py:35
  25.8 13.2 %collective-permute-start.7 = (bf16[8,16,2048]{2,1,0:T(8,128)(2,1)}, bf16[8,16,2048]{2,1,0:T(8,128)(2,1)S(1)}, u32[]{:S(2)}, u32[]{:S(2)}) collective-permute-start(bf16[8,16,2048]{2,1,0:T(8,128)(2,1)} %get-tuple-element.44), channel_id=1, source_target_pairs={{0,1},{8,24},{1,2},{9,25},{2,3},{10,26},{3,0},{11,27},{16,17},{24,... | collective-permute-start | bytes 1572872 | tf_op jit(solution)/shard_map/ppermute | solution.py:35
  25.8 16.2 %collective-permute-start.10 = (bf16[8,16,2048]{2,1,0:T(8,128)(2,1)}, bf16[8,16,2048]{2,1,0:T(8,128)(2,1)S(1)}, u32[]{:S(2)}, u32[]{:S(2)}) collective-permute-start(bf16[8,16,2048]{2,1,0:T(8,128)(2,1)} %get-tuple-element.49), channel_id=1, source_target_pairs={{0,4},{8,12},{1,5},{9,13},{2,6},{10,14},{3,7},{11,15},{16,20},{24,... | collective-permute-start | bytes 1572872 | tf_op jit(solution)/shard_map/ppermute | solution.py:35
  27.1 15.0 %collective-permute-start.11 = (bf16[8,16,2048]{2,1,0:T(8,128)(2,1)}, bf16[8,16,2048]{2,1,0:T(8,128)(2,1)S(1)}, u32[]{:S(2)}, u32[]{:S(2)}) collective-permute-start(bf16[8,16,2048]{2,1,0:T(8,128)(2,1)} %get-tuple-element.50), channel_id=1, source_target_pairs={{0,68},{8,76},{1,69},{9,77},{2,70},{10,78},{3,71},{11,79},{16,84},... | collective-permute-start | bytes 1572872 | tf_op jit(solution)/shard_map/ppermute | solution.py:35
  40.3 31.0 %collective-permute-start.15 = (bf16[1,4,2,4,16,2048]{5,4,3,2,1,0:T(8,128)(2,1)S(1)}, bf16[1,4,2,4,16,2048]{5,4,3,2,1,0:T(8,128)(2,1)S(1)}, u32[]{:S(2)}, u32[]{:S(2)}) collective-permute-start(bf16[1,4,2,4,16,2048]{5,4,3,2,1,0:T(8,128)(2,1)S(1)} %pad_maximum_fusion.refs_0_), channel_id=1, source_target_pairs={{0,8},{8,0},{1,9},{9,1},{2,10},{10,2},{3,11},{11,3},{16,24},{24,16... | collective-permute-start | bytes 6291464 | tf_op jit(solution)/shard_map/ppermute | solution.py:35
  42.2 18.9 %collective-permute-start.14 = (bf16[2,8,16,2048]{3,2,1,0:T(8,128)(2,1)S(1)}, bf16[2,8,16,2048]{3,2,1,0:T(8,128)(2,1)S(1)}, u32[]{:S(2)}, u32[]{:S(2)}) collective-permute-start(bf16[2,8,16,2048]{3,2,1,0:T(8,128)(2,1)S(1)} %pad_maximum_fusion.3), channel_id=1, source_target_pairs={{0,2},{8,40},{1,3},{9,41},{2,0},{10,42},{3,1},{11,43},{16,18},{24,... | collective-permute-start | bytes 3145736 | tf_op jit(solution)/shard_map/ppermute | solution.py:35
  43.8 25.1 %collective-permute-start.13 = (bf16[2,8,16,2048]{3,2,1,0:T(8,128)(2,1)S(1)}, bf16[2,8,16,2048]{3,2,1,0:T(8,128)(2,1)S(1)}, u32[]{:S(2)}, u32[]{:S(2)}) collective-permute-start(bf16[2,8,16,2048]{3,2,1,0:T(8,128)(2,1)S(1)} %pad_maximum_fusion.3), channel_id=1, source_target_pairs={{0,3},{8,56},{1,0},{9,57},{2,1},{10,58},{3,2},{11,59},{16,19},{24,... | collective-permute-start | bytes 3145736 | tf_op jit(solution)/shard_map/ppermute | solution.py:35
  45.2 13.5 %collective-permute-start.16 = (bf16[8,16,2048]{2,1,0:T(8,128)(2,1)S(1)}, bf16[8,16,2048]{2,1,0:T(8,128)(2,1)S(1)}, u32[]{:S(2)}, u32[]{:S(2)}) collective-permute-start(bf16[8,16,2048]{2,1,0:T(8,128)(2,1)S(1)} %copy-done.26), channel_id=1, source_target_pairs={{0,64},{8,72},{1,65},{9,73},{2,66},{10,74},{3,67},{11,75},{16,80},... | collective-permute-start | bytes 1572872 | tf_op jit(solution)/shard_map/ppermute | solution.py:35
  47.9 23.1 %collective-permute-start.12 = (bf16[2,8,16,2048]{3,2,1,0:T(8,128)(2,1)S(1)}, bf16[2,8,16,2048]{3,2,1,0:T(8,128)(2,1)S(1)}, u32[]{:S(2)}, u32[]{:S(2)}) collective-permute-start(bf16[2,8,16,2048]{3,2,1,0:T(8,128)(2,1)S(1)} %pad_maximum_fusion.3), channel_id=1, source_target_pairs={{0,1},{8,24},{1,2},{9,25},{2,3},{10,26},{3,0},{11,27},{16,17},{24,... | collective-permute-start | bytes 3145736 | tf_op jit(solution)/shard_map/ppermute | solution.py:35
  48.1 44.6 %copy-start.1 = (bf16[2,1,2,4,16,2048]{5,4,3,2,1,0:T(8,128)(2,1)}, bf16[2,1,2,4,16,2048]{5,4,3,2,1,0:T(8,128)(2,1)S(1)}, u32[]{:S(2)}) copy-start(bf16[2,1,2,4,16,2048]{5,4,3,2,1,0:T(8,128)(2,1)S(1)} %pad_maximum_fusion.2.refs_0_.refs_1_) | copy-start | bytes 3145732
  58.7 43.0 %copy-start.10 = (bf16[8,16,2048]{2,1,0:T(8,128)(2,1)}, bf16[8,16,2048]{2,1,0:T(8,128)(2,1)S(1)}, u32[]{:S(2)}) copy-start(bf16[8,16,2048]{2,1,0:T(8,128)(2,1)S(1)} %collective-permute-done.16) | copy-start | bytes 1572868
  58.7 19.2 %collective-permute-start.20 = (bf16[2,1,2,4,16,2048]{5,4,3,2,1,0:T(8,128)(2,1)S(1)}, bf16[2,1,2,4,16,2048]{5,4,3,2,1,0:T(8,128)(2,1)S(1)}, u32[]{:S(2)}, u32[]{:S(2)}) collective-permute-start(bf16[2,1,2,4,16,2048]{5,4,3,2,1,0:T(8,128)(2,1)S(1)} %pad_maximum_fusion.2.refs_0_.refs_1_), channel_id=1, source_target_pairs={{0,8},{8,0},{1,9},{9,1},{2,10},{10,2},{3,11},{11,3},{16,24},{24,16... | collective-permute-start | bytes 3145736 | tf_op jit(solution)/shard_map/ppermute | solution.py:35
  61.0 31.7 %copy-start.3 = (bf16[2,8,16,2048]{3,2,1,0:T(8,128)(2,1)}, bf16[2,8,16,2048]{3,2,1,0:T(8,128)(2,1)S(1)}, u32[]{:S(2)}) copy-start(bf16[2,8,16,2048]{3,2,1,0:T(8,128)(2,1)S(1)} %collective-permute-done.14) | copy-start | bytes 3145732
  61.0 18.1 %collective-permute-start.23 = (bf16[2,1,2,4,16,2048]{5,4,3,2,1,0:T(8,128)(2,1)S(1)}, bf16[2,1,2,4,16,2048]{5,4,3,2,1,0:T(8,128)(2,1)S(1)}, u32[]{:S(2)}, u32[]{:S(2)}) collective-permute-start(bf16[2,1,2,4,16,2048]{5,4,3,2,1,0:T(8,128)(2,1)S(1)} %bitcast.30), channel_id=1, source_target_pairs={{0,8},{8,0},{1,9},{9,1},{2,10},{10,2},{3,11},{11,3},{16,24},{24,16... | collective-permute-start | bytes 3145736 | tf_op jit(solution)/shard_map/ppermute | solution.py:35
  68.9 10.5 %collective-permute-start.22 = (bf16[2,1,2,4,16,2048]{5,4,3,2,1,0:T(8,128)(2,1)S(1)}, bf16[2,1,2,4,16,2048]{5,4,3,2,1,0:T(8,128)(2,1)S(1)}, u32[]{:S(2)}, u32[]{:S(2)}) collective-permute-start(bf16[2,1,2,4,16,2048]{5,4,3,2,1,0:T(8,128)(2,1)S(1)} %bitcast.33), channel_id=1, source_target_pairs={{0,8},{8,0},{1,9},{9,1},{2,10},{10,2},{3,11},{11,3},{16,24},{24,16... | collective-permute-start | bytes 3145736 | tf_op jit(solution)/shard_map/ppermute | solution.py:35
  71.0 21.7 %collective-permute-start.21 = (bf16[2,1,2,4,16,2048]{5,4,3,2,1,0:T(8,128)(2,1)S(1)}, bf16[2,1,2,4,16,2048]{5,4,3,2,1,0:T(8,128)(2,1)S(1)}, u32[]{:S(2)}, u32[]{:S(2)}) collective-permute-start(bf16[2,1,2,4,16,2048]{5,4,3,2,1,0:T(8,128)(2,1)S(1)} %bitcast.36), channel_id=1, source_target_pairs={{0,8},{8,0},{1,9},{9,1},{2,10},{10,2},{3,11},{11,3},{16,24},{24,16... | collective-permute-start | bytes 3145736 | tf_op jit(solution)/shard_map/ppermute | solution.py:35
  75.7 10.0 %collective-permute-start.19 = (bf16[8,16,2048]{2,1,0:T(8,128)(2,1)S(1)}, bf16[8,16,2048]{2,1,0:T(8,128)(2,1)S(1)}, u32[]{:S(2)}, u32[]{:S(2)}) collective-permute-start(bf16[8,16,2048]{2,1,0:T(8,128)(2,1)S(1)} %collective-permute-done.16), channel_id=1, source_target_pairs={{0,2},{8,40},{1,3},{9,41},{2,0},{10,42},{3,1},{11,43},{16,18},{24,... | collective-permute-start | bytes 1572872 | tf_op jit(solution)/shard_map/ppermute | solution.py:35
  77.9 13.7 %collective-permute-start.18 = (bf16[8,16,2048]{2,1,0:T(8,128)(2,1)S(1)}, bf16[8,16,2048]{2,1,0:T(8,128)(2,1)S(1)}, u32[]{:S(2)}, u32[]{:S(2)}) collective-permute-start(bf16[8,16,2048]{2,1,0:T(8,128)(2,1)S(1)} %collective-permute-done.16), channel_id=1, source_target_pairs={{0,3},{8,56},{1,0},{9,57},{2,1},{10,58},{3,2},{11,59},{16,19},{24,... | collective-permute-start | bytes 1572872 | tf_op jit(solution)/shard_map/ppermute | solution.py:35
  79.1 13.5 %collective-permute-start.17 = (bf16[8,16,2048]{2,1,0:T(8,128)(2,1)S(1)}, bf16[8,16,2048]{2,1,0:T(8,128)(2,1)S(1)}, u32[]{:S(2)}, u32[]{:S(2)}) collective-permute-start(bf16[8,16,2048]{2,1,0:T(8,128)(2,1)S(1)} %collective-permute-done.16), channel_id=1, source_target_pairs={{0,1},{8,24},{1,2},{9,25},{2,3},{10,26},{3,0},{11,27},{16,17},{24,... | collective-permute-start | bytes 1572872 | tf_op jit(solution)/shard_map/ppermute | solution.py:35
  79.4 22.2 %collective-permute-start.24 = (bf16[1,1,2,4,16,2048]{5,4,3,2,1,0:T(8,128)(2,1)S(1)}, bf16[1,1,2,4,16,2048]{5,4,3,2,1,0:T(8,128)(2,1)S(1)}, u32[]{:S(2)}, u32[]{:S(2)}) collective-permute-start(bf16[1,1,2,4,16,2048]{5,4,3,2,1,0:T(8,128)(2,1)S(1)} %bitcast.39), channel_id=1, source_target_pairs={{0,8},{8,0},{1,9},{9,1},{2,10},{10,2},{3,11},{11,3},{16,24},{24,16... | collective-permute-start | bytes 1572872 | tf_op jit(solution)/shard_map/ppermute | solution.py:35
  85.7 16.0 %collective-permute-start.27 = (bf16[1,1,2,4,16,2048]{5,4,3,2,1,0:T(8,128)(2,1)S(1)}, bf16[1,1,2,4,16,2048]{5,4,3,2,1,0:T(8,128)(2,1)S(1)}, u32[]{:S(2)}, u32[]{:S(2)}) collective-permute-start(bf16[1,1,2,4,16,2048]{5,4,3,2,1,0:T(8,128)(2,1)S(1)} %bitcast.42), channel_id=1, source_target_pairs={{0,8},{8,0},{1,9},{9,1},{2,10},{10,2},{3,11},{11,3},{16,24},{24,16... | collective-permute-start | bytes 1572872 | tf_op jit(solution)/shard_map/ppermute | solution.py:35
  91.6 10.1 %collective-permute-start.26 = (bf16[1,1,2,4,16,2048]{5,4,3,2,1,0:T(8,128)(2,1)S(1)}, bf16[1,1,2,4,16,2048]{5,4,3,2,1,0:T(8,128)(2,1)S(1)}, u32[]{:S(2)}, u32[]{:S(2)}) collective-permute-start(bf16[1,1,2,4,16,2048]{5,4,3,2,1,0:T(8,128)(2,1)S(1)} %bitcast.45), channel_id=1, source_target_pairs={{0,8},{8,0},{1,9},{9,1},{2,10},{10,2},{3,11},{11,3},{16,24},{24,16... | collective-permute-start | bytes 1572872 | tf_op jit(solution)/shard_map/ppermute | solution.py:35
  92.6 9.1 %collective-permute-start.25 = (bf16[1,1,2,4,16,2048]{5,4,3,2,1,0:T(8,128)(2,1)S(1)}, bf16[1,1,2,4,16,2048]{5,4,3,2,1,0:T(8,128)(2,1)S(1)}, u32[]{:S(2)}, u32[]{:S(2)}) collective-permute-start(bf16[1,1,2,4,16,2048]{5,4,3,2,1,0:T(8,128)(2,1)S(1)} %bitcast.48), channel_id=1, source_target_pairs={{0,8},{8,0},{1,9},{9,1},{2,10},{10,2},{3,11},{11,3},{16,24},{24,16... | collective-permute-start | bytes 1572872 | tf_op jit(solution)/shard_map/ppermute | solution.py:35
  107.4 19.8 %all-to-all-start = ((f32[8,256,128]{2,1,0:T(8,128)}), f32[8,256,128]{2,1,0:T(8,128)S(1)}, u32[]{:S(2)}, u32[]{:S(2)}) async-start(f32[8,256,128]{2,1,0:T(8,128)} %get-tuple-element.68), calls=%async_computation | async-start | bytes 2097152 | tf_op jit(solution)/shard_map/all_to_all | solution.py:330
  (24 other events, 279.4 us)

commit v3 on v2

v3 whole, which is shorter than its diff:
```python
import functools

import jax
import jax.numpy as jnp
from jax import lax
from jax.experimental import pallas as pl
from jax.experimental.pallas import tpu as pltpu
from jax.sharding import PartitionSpec as P

F32 = jnp.float32
BF16 = jnp.bfloat16
AXES = ("brow", "bcol")
SCANS = 2048
PIXELS = 16384
COMPS = 256
LOCAL = 16
PANEL = 2048
HALF = 1024
STEPS = (0, 1, -1, 2)
ANY = pl.BlockSpec(memory_space=pl.ANY)
IN_VMEM = pl.BlockSpec(memory_space=pltpu.VMEM)
IN_SMEM = pl.BlockSpec(memory_space=pltpu.SMEM)
MIDDLE = pltpu.CompilerParams(vmem_limit_bytes=24 << 20)
SMALL = pltpu.CompilerParams(vmem_limit_bytes=8 << 20)


def flat(x, y, z, k):
    return (((x // 2) * 4 + y) * 2 + k) * 8 + (x % 2) * 4 + z


def permute(value, move):
    pairs = []
    for x in range(4):
        for y in range(4):
            for z in range(4):
                for k in range(2):
                    x2, y2, z2, k2 = move(x, y, z, k)
                    pairs.append((flat(x, y, z, k), flat(x2, y2 % 4, z2 % 4, k2)))
    return lax.ppermute(value, AXES, pairs)


def spread(d):
    return lambda x, y, z, k: (x, y + d, z, k) if k == 0 else (x, y, z + d, k)


def across(m):
    return lambda x, y, z, k: (x ^ m, y, z, k)


def around(d):
    return lambda x, y, z, k: (x, y, z + d, k) if k == 0 else (x, y + d, z, k)


def swap(x, y, z, k):
    return x, y, z, 1 - k


def pick_kernel(at, mine, other, *pieces):
    for n, piece in enumerate(pieces):
        for half in range(2):
            span = pl.ds(pl.multiple_of((half * 4 + at[n]) * PANEL, PANEL), PANEL)
            piece[half, 0] = mine[:, span]
            piece[half, 1] = other[:, span]


def pick(at, mine, other):
    return pl.pallas_call(
        pick_kernel,
        out_shape=[jax.ShapeDtypeStruct((2, 2, LOCAL, PANEL), BF16)] * 4,
        in_specs=[IN_SMEM] + [IN_VMEM] * 2,
        out_specs=[IN_VMEM] * 4,
        compiler_params=SMALL,
    )(at, mine, other)


def group_kernel(at, *refs):
    pieces, groups = refs[:4], refs[4:]
    for n, group in enumerate(groups):
        for i, piece in enumerate(pieces):
            for source in range(2):
                group[source, i] = piece[at[n], source]


def group(at, pieces):
    return pl.pallas_call(
        group_kernel,
        out_shape=[jax.ShapeDtypeStruct((2, 4, LOCAL, PANEL), BF16)] * 4,
        in_specs=[IN_SMEM] + [IN_VMEM] * 4,
        out_specs=[IN_VMEM] * 4,
        compiler_params=SMALL,
    )(at, *pieces)


OWN = tuple((0, step) for step in range(4))
SOON = ((1, 0), (2, 0), (1, 1), (2, 1), (1, 2), (2, 2), (3, 0))
LATE = ((1, 3), (3, 1), (2, 3), (3, 2), (3, 3))
ORDER = (OWN, SOON, LATE)
LEFT = (((0,), (0,)), ((), ()))


def fetch(core, own, recv, rows, cols, sems):
    def start(row_from, col_from, offset):
        for row, col, labels in zip(row_from, col_from, ORDER):
            for i, (m, step) in enumerate(labels):
                pltpu.make_async_copy(col.at[i], cols.at[m, step], sems.at[m]).start()
                for s in range(2):
                    pltpu.make_async_copy(
                        row.at[i, s, :, :, pl.ds(offset, HALF)], rows.at[m, :, 1 - s, step], sems.at[m]
                    ).start()

    @pl.when(core == 0)
    def _():
        start(own, recv, 0)

    @pl.when(core == 1)
    def _():
        start(recv, own, HALF)


def fetched(own, rows, cols, sems, which):
    for array, labels in zip(own, ORDER):
        for i, (m, step) in enumerate(labels):
            if m == which:
                pltpu.make_async_copy(array.at[i], cols.at[m, step], sems.at[m]).wait()
                for s in range(2):
                    pltpu.make_async_copy(
                        array.at[i, s, :, :, pl.ds(0, HALF)], rows.at[m, :, 1 - s, step], sems.at[m]
                    ).wait()


ROWS = pltpu.VMEM((4, 4, 2, 4, LOCAL, HALF), BF16)
COLS = pltpu.VMEM((4, 4, 2, 4, LOCAL, PANEL), BF16)


def ones_beside(block):
    return jnp.concatenate([block, jnp.ones((block.shape[0], 128), BF16)], axis=1)


def score_of(block, comps):
    score = jnp.dot(block, comps, preferred_element_type=F32)
    return score[:, :COMPS] + score[:, COMPS:]


def select(core, own, recv, use):
    @pl.when(core == 0)
    def _():
        use(own, recv, 0)

    @pl.when(core == 1)
    def _():
        use(recv, own, HALF)


def left_of(centred):
    high = centred.astype(BF16)
    low = (centred - high.astype(F32)).astype(BF16)
    return ones_beside(jnp.concatenate([high, low], axis=1))


def product_of(left, panel):
    product = lax.dot_general(left, panel, LEFT, preferred_element_type=F32)
    return product[:COMPS] + product[COMPS : 2 * COMPS], product[2 * COMPS : 2 * COMPS + 1]


def own_kernel(at, own, recv, comps, total, row_sum, score_sum, origin, rows, cols):
    def use(row_from, col_from, offset):
        for i in range(4):
            cols[i] = col_from[i]
            for s in range(2):
                rows[:, 1 - s, i] = row_from[i, s, :, :, offset : offset + HALF]

    select(at[0], own, recv, use)
    score = score_of(cols[...].reshape(512, PANEL), comps[...])
    score_sum[...] = jnp.sum(score, axis=0, keepdims=True)
    origin[...] = score_sum[...] * (1.0 / 512)
    total[...], row_sum[...] = product_of(left_of(score - origin[...]), rows[...].reshape(512, HALF))


def own_part(at, own, recv, comps):
    return pl.pallas_call(
        own_kernel,
        out_shape=[
            jax.ShapeDtypeStruct((COMPS, HALF), F32),
            jax.ShapeDtypeStruct((1, HALF), F32),
            jax.ShapeDtypeStruct((1, COMPS), F32),
            jax.ShapeDtypeStruct((1, COMPS), F32),
        ],
        in_specs=[IN_SMEM] + [IN_VMEM] * 3,
        out_specs=[IN_VMEM] * 4,
        scratch_shapes=[
            pltpu.VMEM((4, 2, 4, LOCAL, HALF), BF16),
            pltpu.VMEM((4, 2, 4, LOCAL, PANEL), BF16),
        ],
        compiler_params=MIDDLE,
        cost_estimate=pl.CostEstimate(flops=2 << 30, bytes_accessed=1 << 20, transcendentals=0),
    )(at, own, recv, comps)


def soon_kernel(at, own, recv, comps, scores, cols):
    def use(row_from, col_from, offset):
        for i in range(len(SOON)):
            cols[i] = col_from[i]

    select(at[0], own, recv, use)
    scores[...] = score_of(cols[...].reshape(len(SOON) * 128, PANEL), comps[...])


def soon_part(at, own, recv, comps):
    return pl.pallas_call(
        soon_kernel,
        out_shape=jax.ShapeDtypeStruct((len(SOON) * 128, COMPS), F32),
        in_specs=[IN_SMEM] + [IN_VMEM] * 3,
        out_specs=IN_VMEM,
        scratch_shapes=[pltpu.VMEM((len(SOON), 2, 4, LOCAL, PANEL), BF16)],
        compiler_params=MIDDLE,
        cost_estimate=pl.CostEstimate(flops=2 << 30, bytes_accessed=1 << 20, transcendentals=0),
    )(at, own, recv, comps)


def last_kernel(at, *refs):
    own_soon, recv_soon, own_late, recv_late, comps, soon, total_in, rs_in, ss_in, origin_in = refs[:10]
    parts, means, rows, cols, left = refs[10:]

    def use(row_from, col_from, offset):
        for array, labels in zip(row_from, (SOON, LATE)):
            for i, (m, step) in enumerate(labels):
                for s in range(2):
                    rows[m - 1, :, 1 - s, step] = array[i, s, :, :, offset : offset + HALF]
        for i in range(len(LATE)):
            cols[i] = col_from[1][i]

    select(at[0], (own_soon, own_late), (recv_soon, recv_late), use)
    late = score_of(cols[...].reshape(len(LATE) * 128, PANEL), comps[...])
    score_sum = ss_in[...] + jnp.sum(late, axis=0, keepdims=True) + jnp.sum(soon[...], axis=0, keepdims=True)
    origin = origin_in[...]
    for block, labels in ((soon[...], SOON), (late, LATE)):
        block = left_of(block - origin)
        for i, (m, step) in enumerate(labels):
            left[pl.ds(((m - 1) * 4 + step) * 128, 128), :] = block[i * 128 : (i + 1) * 128]
    total, row_sum = product_of(left[...], rows[...].reshape(1536, HALF))
    row_sum = row_sum + rs_in[...]
    shift = score_sum * (1.0 / SCANS) - origin
    shift = jnp.transpose(jnp.broadcast_to(shift, (128, COMPS)))[:, :1]
    total = (total + total_in[...] - shift * row_sum) * (1.0 / (SCANS - 1))
    for c in range(8):
        parts[c] = total[:, c * 128 : (c + 1) * 128]
    means[...] = row_sum * (1.0 / SCANS)


def last_part(at, pieces, comps, soon, state):
    return pl.pallas_call(
        last_kernel,
        out_shape=[jax.ShapeDtypeStruct((8, COMPS, 128), F32), jax.ShapeDtypeStruct((1, HALF), F32)],
        in_specs=[IN_SMEM] + [IN_VMEM] * 10,
        out_specs=[IN_VMEM] * 2,
        scratch_shapes=[
            pltpu.VMEM((3, 4, 2, 4, LOCAL, HALF), BF16),
            pltpu.VMEM((len(LATE), 2, 4, LOCAL, PANEL), BF16),
            pltpu.VMEM((1536, 2 * COMPS + 128), BF16),
        ],
        compiler_params=MIDDLE,
        cost_estimate=pl.CostEstimate(flops=4 << 30, bytes_accessed=4 << 20, transcendentals=0),
    )(at, *pieces, comps, soon, *state)


def gram_kernel(at, *refs):
    own, recv, row_means, out = refs[:3], refs[3:6], refs[6], refs[7]
    rows, cols, stage, col_sums, sems, out_sems = refs[8:]
    fetch(at[0], own, recv, rows, cols, sems)
    copies = []
    for i in range(4):
        slot = i % 2
        if i >= 2:
            copies[i - 2].wait()
        span_i = slice(i * 256, (i + 1) * 256)
        row_mean = jnp.transpose(jnp.broadcast_to(row_means[:, span_i], (128, 256)))[:, :1]
        if i == 0:
            for m in range(4):
                fetched(own, rows, cols, sems, m)
                left = ones_beside(rows[m, :, :, :, :, span_i].reshape(512, 256))
                for j in range(8):
                    span = slice(j * 256, (j + 1) * 256)
                    right = cols[m, :, :, :, :, span].reshape(512, 256)
                    both = lax.dot_general(left, right, LEFT, preferred_element_type=F32)
                    tile, col_sum = both[:256], both[256:257]
                    if m > 0:
                        tile += stage[slot, :, span]
                        col_sum += col_sums[:, span]
                    if m == 3:
                        tile = (tile - row_mean * col_sum) * (1.0 / (SCANS - 1))
                    stage[slot, :, span] = tile
                    col_sums[:, span] = col_sum
        else:
            left = rows[:, :, :, :, :, span_i].reshape(SCANS, 256)
            for j in range(8):
                span = slice(j * 256, (j + 1) * 256)
                right = cols[:, :, :, :, :, span].reshape(SCANS, 256)
                tile = lax.dot_general(left, right, LEFT, preferred_element_type=F32)
                stage[slot, :, span] = (tile - row_mean * col_sums[:, span]) * (1.0 / (SCANS - 1))
        copy = pltpu.make_async_copy(stage.at[slot], out.at[pl.ds(i * 256, 256), :], out_sems.at[slot])
        copy.start()
        copies.append(copy)
    for copy in copies[2:]:
        copy.wait()


def gram(at, own, recv, row_means):
    return pl.pallas_call(
        gram_kernel,
        out_shape=jax.ShapeDtypeStruct((HALF, PANEL), F32),
        in_specs=[IN_SMEM] + [ANY] * 6 + [IN_VMEM],
        out_specs=ANY,
        scratch_shapes=[
            ROWS,
            COLS,
            pltpu.VMEM((2, 256, PANEL), F32),
            pltpu.VMEM((1, PANEL), F32),
            pltpu.SemaphoreType.DMA((4,)),
            pltpu.SemaphoreType.DMA((2,)),
        ],
        compiler_params=pltpu.CompilerParams(vmem_limit_bytes=30 << 20),
        cost_estimate=pl.CostEstimate(flops=8 << 30, bytes_accessed=20 << 20, transcendentals=0),
    )(at, *[pltpu.with_memory_space_constraint(piece, pltpu.HBM) for piece in own + recv], row_means)


def on_device(patterns, components):
    row = lax.axis_index("brow")
    col = lax.axis_index("bcol")
    k, y, xh = row % 2, (row // 2) % 4, row // 8
    z, xl = col % 4, col // 4
    first = k == 0
    same = jnp.where(first, y, z)
    at = jnp.stack([(same + d) % 4 for d in STEPS]).astype(jnp.int32)
    sends = pick(at, patterns, permute(patterns, swap))
    got = [sends[0]] + [permute(sends[n], spread(STEPS[n])) for n in range(1, 4)]
    own_half = jnp.where(first, xh, xl)
    at = jnp.stack(
        [own_half, jnp.where(first, own_half, 1 - own_half), jnp.where(first, 1 - own_half, own_half), 1 - own_half]
    ).astype(jnp.int32)
    group_own, to_1, to_2, to_3 = group(at, got)
    high = lax.reduce_precision(components, 8, 7)
    comps = jnp.concatenate([high, components - high], axis=1).astype(BF16)
    near = [permute(to_1, across(1)), permute(to_3, across(3))]
    ring_own = [permute(group_own, around(d)) for d in STEPS[1:]]
    near, to_2, comps = lax.optimization_barrier((near, to_2, comps))
    ring_own, near[0] = lax.optimization_barrier((ring_own, near[0]))
    far = permute(to_2, across(2))
    at = jnp.reshape(k, (1,)).astype(jnp.int32)
    own = jnp.stack([group_own] + ring_own)
    recv = permute(own, swap)
    group_near = jnp.stack(near)
    ring_near = [permute(group_near, around(d)) for d in STEPS[1:3]]
    state = own_part(at, own, recv, comps)
    far, ring_near, state = lax.optimization_barrier((far, ring_near, state))
    late = [permute(jnp.stack([ring_near[n][n], far]), around(STEPS[n + 1])) for n in range(2)]
    late.append(permute(far[None], around(STEPS[3])))
    own_soon = jnp.concatenate([group_near] + ring_near + [far[None]])
    recv_soon = permute(own_soon, swap)
    soon = soon_part(at, own_soon, recv_soon, comps)
    late, soon = lax.optimization_barrier((late, soon))
    own_late = jnp.concatenate(late)
    recv_late = permute(own_late, swap)
    parts, row_means = last_part(at, (own_soon, recv_soon, own_late, recv_late), comps, soon, state)
    own = [own, own_soon, own_late]
    recv = [recv, recv_soon, recv_late]
    parts = lax.all_to_all(parts, "bcol", 0, 0, tiled=True)
    covariance = gram(at, own, recv, row_means)
    projected = jnp.sum(parts, axis=0).T
    means_part = lax.dynamic_slice_in_dim(row_means[0], col * 128, 128, 0)
    return covariance, projected, means_part


def solution(mesh):
    return jax.shard_map(
        on_device,
        mesh=mesh,
        in_specs=(P(("brow", "bcol"), None), P("bcol", None)),
        out_specs=(P("brow", "bcol"), P(("brow", "bcol"), None), P(("brow", "bcol"))),
        check_vma=False,
    )
```

time: 128 us -> 114 us (0.89)
  starting transfers between devices: 41.1 us -> 29.5 us
  Pallas kernels: 39.2 us -> 29.6 us
  waiting for transfers between devices: 41.3 us -> 48.4 us
    ppermute x28 -> x18, starting transfers between devices: 37.5 us -> 25.9 us  [permute(): return lax.ppermute(value, AXES, pairs)]
    pallas_call x5, Pallas kernels: 23.6 us -> 14.2 us  [the longest x1 6.98 us: last_part(): pl.pallas_call(last_kernel, out_shape=[jax.ShapeDtypeStruct((8, COMPS, 12...]
    ppermute x28 -> x18, waiting for transfers between devices: 41.3 us -> 48.4 us  [permute(): return lax.ppermute(value, AXES, pairs)]
  transfers between devices with their start and end apart: 29 -> 19, of which waited for: 8 -> 13; matrix products, arithmetic and copies ran while one was open for 2% -> 3% of each run, Pallas kernels for 23% -> 19%
where the time goes in v3:
time: 114 us
  waiting for transfers between devices  48.4 us (42%)
  Pallas kernels  29.6 us (26%)
  starting transfers between devices  29.5 us (26%)
  local copies, waits for them, and re-layouts  2.99 us (3%)
  other arithmetic  2.8 us (2%)
    ppermute x18, waiting for transfers between devices, permute(): return lax.ppermute(value, AXES, pairs)  48.4 us
    ppermute x18, starting transfers between devices, permute(): return lax.ppermute(value, AXES, pairs)  25.9 us
    pallas_call x1, Pallas kernels, gram(): pl.pallas_call(gram_kernel, out_shape=jax.ShapeDtypeStruct((HALF, PANEL),...  15.3 us
    pallas_call x1, Pallas kernels, last_part(): pl.pallas_call(last_kernel, out_shape=[jax.ShapeDtypeStruct((8, COMPS, 12...  6.98 us
    pallas_call x1, Pallas kernels, own_part(): pl.pallas_call(own_kernel, out_shape=[jax.ShapeDtypeStruct((COMPS, HALF),...  3.67 us
    all_to_all x1, starting transfers between devices, on_device(): parts = lax.all_to_all(parts, 'bcol', 0, 0, tiled=True)  3.56 us
    unnamed x21, local copies, waits for them, and re-layouts  2.31 us
    pallas_call x1, Pallas kernels, soon_part(): pl.pallas_call(soon_kernel, out_shape=jax.ShapeDtypeStruct((len(SOON) * 1...  2.3 us
  transfers between devices with their start and end apart: 19, of which 13 were waited for; matrix products, arithmetic and copies ran while one was open for 3% of the time, Pallas kernels for 19%

profile of v3, /device:TPU:1, one launch (start us, length us, event | category | flops | bytes accessed | tf_op | source)
XLA Modules:
  0.0 114.1 jit_solution(15965656111662118949)
XLA Ops:
  0.6 1.5 %collective-permute-start = (bf16[16,16384]{1,0:T(8,128)(2,1)}, bf16[16,16384]{1,0:T(8,128)(2,1)S(1)}, u32[]{:S(2)}, u32[]{:S(2)}) collective-permute-start(bf16[16,16384]{1,0:T(8,128)(2,1)} %mine.1), channel_id=1, source_target_pairs={{0,8},{8,0},{1,9},{9,1},{2,10},{10,2},{3,11},{11,3},{16,24},{24,16... | collective-permute-start | bytes 1572872 | tf_op jit(solution)/shard_map/ppermute | solution.py:39
  2.2 1.7 %collective-permute-done.other = bf16[16,16384]{1,0:T(8,128)(2,1)S(1)} collective-permute-done((bf16[16,16384]{1,0:T(8,128)(2,1)}, bf16[16,16384]{1,0:T(8,128)(2,1)S(1)}, u32[]{:S(2)}, u32[]{:S(2)}) %collective-permute-start) | collective-permute-done | bytes 524320 | tf_op jit(solution)/shard_map/ppermute | solution.py:39
  3.9 1.0 copy-done.5
  5.5 1.8 %collective-permute-start.1 = (bf16[2,2,16,2048]{3,2,1,0:T(8,128)(2,1)S(1)}, bf16[2,2,16,2048]{3,2,1,0:T(8,128)(2,1)S(1)}, u32[]{:S(2)}, u32[]{:S(2)}) collective-permute-start(bf16[2,2,16,2048]{3,2,1,0:T(8,128)(2,1)S(1)} %get-tuple-element.37), channel_id=1, source_target_pairs={{0,16},{8,9},{1,17},{9,10},{2,18},{10,11},{3,19},{11,8},{16,32},{2... | collective-permute-start | bytes 786440 | tf_op jit(solution)/shard_map/ppermute | solution.py:39
  7.3 2.2 %collective-permute-start.2 = (bf16[2,2,16,2048]{3,2,1,0:T(8,128)(2,1)S(1)}, bf16[2,2,16,2048]{3,2,1,0:T(8,128)(2,1)S(1)}, u32[]{:S(2)}, u32[]{:S(2)}) collective-permute-start(bf16[2,2,16,2048]{3,2,1,0:T(8,128)(2,1)S(1)} %get-tuple-element.38), channel_id=1, source_target_pairs={{0,48},{8,11},{1,49},{9,8},{2,50},{10,9},{3,51},{11,10},{16,0},{24... | collective-permute-start | bytes 786440 | tf_op jit(solution)/shard_map/ppermute | solution.py:39
  9.5 1.2 %collective-permute-start.3 = (bf16[2,2,16,2048]{3,2,1,0:T(8,128)(2,1)S(1)}, bf16[2,2,16,2048]{3,2,1,0:T(8,128)(2,1)S(1)}, u32[]{:S(2)}, u32[]{:S(2)}) collective-permute-start(bf16[2,2,16,2048]{3,2,1,0:T(8,128)(2,1)S(1)} %get-tuple-element.39), channel_id=1, source_target_pairs={{0,32},{8,10},{1,33},{9,11},{2,34},{10,8},{3,35},{11,9},{16,48},{2... | collective-permute-start | bytes 786440 | tf_op jit(solution)/shard_map/ppermute | solution.py:39
  10.8 2.4 %collective-permute-done.1.refs_1_ = bf16[2,2,16,2048]{3,2,1,0:T(8,128)(2,1)S(1)} collective-permute-done((bf16[2,2,16,2048]{3,2,1,0:T(8,128)(2,1)S(1)}, bf16[2,2,16,2048]{3,2,1,0:T(8,128)(2,1)S(1)}, u32[]{:S(2)}, u32[]{:S(2)}) %collective-permute-start.1) | collective-permute-done | bytes 262176 | tf_op jit(solution)/shard_map/ppermute | solution.py:39
  13.2 2.4 %collective-permute-done.2.refs_2_ = bf16[2,2,16,2048]{3,2,1,0:T(8,128)(2,1)S(1)} collective-permute-done((bf16[2,2,16,2048]{3,2,1,0:T(8,128)(2,1)S(1)}, bf16[2,2,16,2048]{3,2,1,0:T(8,128)(2,1)S(1)}, u32[]{:S(2)}, u32[]{:S(2)}) %collective-permute-start.2) | collective-permute-done | bytes 262176 | tf_op jit(solution)/shard_map/ppermute | solution.py:39
  15.7 1.6 %collective-permute-done.3.refs_3_ = bf16[2,2,16,2048]{3,2,1,0:T(8,128)(2,1)S(1)} collective-permute-done((bf16[2,2,16,2048]{3,2,1,0:T(8,128)(2,1)S(1)}, bf16[2,2,16,2048]{3,2,1,0:T(8,128)(2,1)S(1)}, u32[]{:S(2)}, u32[]{:S(2)}) %collective-permute-start.3) | collective-permute-done | bytes 262176 | tf_op jit(solution)/shard_map/ppermute | solution.py:39
  18.0 2.9 %collective-permute-start.6 = (bf16[2,4,16,2048]{3,2,1,0:T(8,128)(2,1)S(1)}, bf16[2,4,16,2048]{3,2,1,0:T(8,128)(2,1)S(1)}, u32[]{:S(2)}, u32[]{:S(2)}) collective-permute-start(bf16[2,4,16,2048]{3,2,1,0:T(8,128)(2,1)S(1)} %get-tuple-element.40), channel_id=1, source_target_pairs={{0,2},{8,40},{1,3},{9,41},{2,0},{10,42},{3,1},{11,43},{16,18},{24,... | collective-permute-start | bytes 1572872 | tf_op jit(solution)/shard_map/ppermute | solution.py:39
  22.3 1.2 %collective-permute-start.7 = (bf16[2,4,16,2048]{3,2,1,0:T(8,128)(2,1)S(1)}, bf16[2,4,16,2048]{3,2,1,0:T(8,128)(2,1)S(1)}, u32[]{:S(2)}, u32[]{:S(2)}) collective-permute-start(bf16[2,4,16,2048]{3,2,1,0:T(8,128)(2,1)S(1)} %get-tuple-element.41), channel_id=1, source_target_pairs={{0,4},{8,12},{1,5},{9,13},{2,6},{10,14},{3,7},{11,15},{16,20},{24,... | collective-permute-start | bytes 1572872 | tf_op jit(solution)/shard_map/ppermute | solution.py:39
  23.6 1.8 %collective-permute-start.8 = (bf16[2,4,16,2048]{3,2,1,0:T(8,128)(2,1)S(1)}, bf16[2,4,16,2048]{3,2,1,0:T(8,128)(2,1)S(1)}, u32[]{:S(2)}, u32[]{:S(2)}) collective-permute-start(bf16[2,4,16,2048]{3,2,1,0:T(8,128)(2,1)S(1)} %get-tuple-element.42), channel_id=1, source_target_pairs={{0,68},{8,76},{1,69},{9,77},{2,70},{10,78},{3,71},{11,79},{16,84},... | collective-permute-start | bytes 1572872 | tf_op jit(solution)/shard_map/ppermute | solution.py:39
  25.4 1.9 %reduce-precision_convert_fusion = (bf16[2048,256]{1,0:T(8,128)(2,1)S(1)}, bf16[2048,256]{1,0:T(8,128)(2,1)S(1)}) fusion(f32[2048,256]{1,0:T(8,128)} %param.3), kind=kLoop, calls=%fused_computation.1 | loop fusion | flops 2097152 | bytes 4194304 | tf_op jit(solution)/shard_map/convert
  27.5 6.3 %collective-permute-done.7 = bf16[2,4,16,2048]{3,2,1,0:T(8,128)(2,1)S(1)} collective-permute-done((bf16[2,4,16,2048]{3,2,1,0:T(8,128)(2,1)S(1)}, bf16[2,4,16,2048]{3,2,1,0:T(8,128)(2,1)S(1)}, u32[]{:S(2)}, u32[]{:S(2)}) %collective-permute-start.7) | collective-permute-done | bytes 524320 | tf_op jit(solution)/shard_map/ppermute | solution.py:39
  33.7 2.1 %collective-permute-done.8 = bf16[2,4,16,2048]{3,2,1,0:T(8,128)(2,1)S(1)} collective-permute-done((bf16[2,4,16,2048]{3,2,1,0:T(8,128)(2,1)S(1)}, bf16[2,4,16,2048]{3,2,1,0:T(8,128)(2,1)S(1)}, u32[]{:S(2)}, u32[]{:S(2)}) %collective-permute-start.8) | collective-permute-done | bytes 524320 | tf_op jit(solution)/shard_map/ppermute | solution.py:39
  36.2 3.3 %collective-permute-start.12 = (bf16[4,2,4,16,2048]{4,3,2,1,0:T(8,128)(2,1)S(1)}, bf16[4,2,4,16,2048]{4,3,2,1,0:T(8,128)(2,1)S(1)}, u32[]{:S(2)}, u32[]{:S(2)}) collective-permute-start(bf16[4,2,4,16,2048]{4,3,2,1,0:T(8,128)(2,1)S(1)} %pad_maximum_fusion.1.own.refs_0_), channel_id=1, source_target_pairs={{0,8},{8,0},{1,9},{9,1},{2,10},{10,2},{3,11},{11,3},{16,24},{24,16... | collective-permute-start | bytes 6291464 | tf_op jit(solution)/shard_map/ppermute | solution.py:39
  39.6 2.1 %collective-permute-start.11 = (bf16[2,2,4,16,2048]{4,3,2,1,0:T(8,128)(2,1)S(1)}, bf16[2,2,4,16,2048]{4,3,2,1,0:T(8,128)(2,1)S(1)}, u32[]{:S(2)}, u32[]{:S(2)}) collective-permute-start(bf16[2,2,4,16,2048]{4,3,2,1,0:T(8,128)(2,1)S(1)} %pad_maximum_fusion.4), channel_id=1, source_target_pairs={{0,3},{8,56},{1,0},{9,57},{2,1},{10,58},{3,2},{11,59},{16,19},{24,... | collective-permute-start | bytes 3145736 | tf_op jit(solution)/shard_map/ppermute | solution.py:39
  41.6 1.2 %collective-permute-start.9 = (bf16[2,4,16,2048]{3,2,1,0:T(8,128)(2,1)S(1)}, bf16[2,4,16,2048]{3,2,1,0:T(8,128)(2,1)S(1)}, u32[]{:S(2)}, u32[]{:S(2)}) collective-permute-start(bf16[2,4,16,2048]{3,2,1,0:T(8,128)(2,1)S(1)} %get-tuple-element.50), channel_id=1, source_target_pairs={{0,64},{8,72},{1,65},{9,73},{2,66},{10,74},{3,67},{11,75},{16,80},... | collective-permute-start | bytes 1572872 | tf_op jit(solution)/shard_map/ppermute | solution.py:39
  43.3 3.7 %shard_map.51 = (f32[256,1024]{1,0:T(8,128)S(1)}, f32[1,1024]{1,0:T(1,128)S(1)}, f32[1,256]{1,0:T(1,128)S(1)}, f32[1,256]{1,0:T(1,128)S(1)}) custom-call(s32[1]{0:T(128)} %bitcast.at, bf16[4,2,4,16,2048]{4,3,2,1,0:T(8,128)(2,1)S(1)} %pad_maximum_fusion.1.own.refs_0_, bf16[4,2,4,16,2048]{4,3,2,1,0:T(8,128)(2,1)S(1)} %collective-permute-done.12.recv.refs_3_, ...), custom_call_target="tpu_custom_call" | custom-call | flops 2147483648 | bytes 1048576 | tf_op jit(solution)/shard_map/pallas_call | solution.py:180
  47.0 9.7 %collective-permute-done.9 = bf16[2,4,16,2048]{3,2,1,0:T(8,128)(2,1)S(1)} collective-permute-done((bf16[2,4,16,2048]{3,2,1,0:T(8,128)(2,1)S(1)}, bf16[2,4,16,2048]{3,2,1,0:T(8,128)(2,1)S(1)}, u32[]{:S(2)}, u32[]{:S(2)}) %collective-permute-start.9) | collective-permute-done | bytes 524320 | tf_op jit(solution)/shard_map/ppermute | solution.py:39
  57.1 1.0 collective-permute-start.16
  58.3 2.2 %collective-permute-start.14 = (bf16[2,2,4,16,2048]{4,3,2,1,0:T(8,128)(2,1)S(1)}, bf16[2,2,4,16,2048]{4,3,2,1,0:T(8,128)(2,1)S(1)}, u32[]{:S(2)}, u32[]{:S(2)}) collective-permute-start(bf16[2,2,4,16,2048]{4,3,2,1,0:T(8,128)(2,1)S(1)} %get-tuple-element.74), channel_id=1, source_target_pairs={{0,3},{8,56},{1,0},{9,57},{2,1},{10,58},{3,2},{11,59},{16,19},{24,... | collective-permute-start | bytes 3145736 | tf_op jit(solution)/shard_map/ppermute | solution.py:39
  60.5 1.3 %collective-permute-start.15 = (bf16[1,2,4,16,2048]{4,3,2,1,0:T(8,128)(2,1)S(1)}, bf16[1,2,4,16,2048]{4,3,2,1,0:T(8,128)(2,1)S(1)}, u32[]{:S(2)}, u32[]{:S(2)}) collective-permute-start(bf16[1,2,4,16,2048]{4,3,2,1,0:T(8,128)(2,1)S(1)} %bitcast.24), channel_id=1, source_target_pairs={{0,2},{8,40},{1,3},{9,41},{2,0},{10,42},{3,1},{11,43},{16,18},{24,... | collective-permute-start | bytes 1572872 | tf_op jit(solution)/shard_map/ppermute | solution.py:39
  61.8 2.3 %collective-permute-done.16.recv.refs_1_.refs_4_ = bf16[7,2,4,16,2048]{4,3,2,1,0:T(8,128)(2,1)S(1)} collective-permute-done((bf16[7,2,4,16,2048]{4,3,2,1,0:T(8,128)(2,1)S(1)}, bf16[7,2,4,16,2048]{4,3,2,1,0:T(8,128)(2,1)S(1)}, u32[]{:S(2)}, u32[]{:S(2)}) %collective-permute-start.16) | collective-permute-done | bytes 3670048 | tf_op jit(solution)/shard_map/ppermute | solution.py:39
  64.1 2.3 %shard_map.52.refs_5_ = f32[896,256]{1,0:T(8,128)S(1)} custom-call(s32[1]{0:T(128)} %bitcast.at, bf16[7,2,4,16,2048]{4,3,2,1,0:T(8,128)(2,1)S(1)} %constant_dynamic-update-slice_fusion.own.refs_0_.refs_1_, bf16[7,2,4,16,2048]{4,3,2,1,0:T(8,128)(2,1)S(1)} %collective-permute-done.16.recv.refs_1_.refs_4_, bf16[2048,512]{1,0:T(8,128)(2,1)S(1)} %pad_maximum_fusion.comps.refs_4_), custom_call_target="tpu_custom_call" | custom-call | flops 2147483648 | bytes 1048576 | tf_op jit(solution)/shard_map/pallas_call | solution.py:209
  66.4 13.4 %collective-permute-done.15 = bf16[1,2,4,16,2048]{4,3,2,1,0:T(8,128)(2,1)S(1)} collective-permute-done((bf16[1,2,4,16,2048]{4,3,2,1,0:T(8,128)(2,1)S(1)}, bf16[1,2,4,16,2048]{4,3,2,1,0:T(8,128)(2,1)S(1)}, u32[]{:S(2)}, u32[]{:S(2)}) %collective-permute-start.15) | collective-permute-done | bytes 524320 | tf_op jit(solution)/shard_map/ppermute | solution.py:39
  79.8 1.5 %collective-permute-done.13 = bf16[2,2,4,16,2048]{4,3,2,1,0:T(8,128)(2,1)S(1)} collective-permute-done((bf16[2,2,4,16,2048]{4,3,2,1,0:T(8,128)(2,1)S(1)}, bf16[2,2,4,16,2048]{4,3,2,1,0:T(8,128)(2,1)S(1)}, u32[]{:S(2)}, u32[]{:S(2)}) %collective-permute-start.13) | collective-permute-done | bytes 1048608 | tf_op jit(solution)/shard_map/ppermute | solution.py:39
  81.6 0.8 collective-permute-start.17
  82.4 4.5 %collective-permute-done.17.refs_3_.refs_5_ = bf16[5,2,4,16,2048]{4,3,2,1,0:T(8,128)(2,1)S(1)} collective-permute-done((bf16[5,2,4,16,2048]{4,3,2,1,0:T(8,128)(2,1)S(1)}, bf16[5,2,4,16,2048]{4,3,2,1,0:T(8,128)(2,1)S(1)}, u32[]{:S(2)}, u32[]{:S(2)}) %collective-permute-start.17) | collective-permute-done | bytes 2621472 | tf_op jit(solution)/shard_map/ppermute | solution.py:39
  86.9 7.0 %shard_map.53 = (f32[8,256,128]{2,1,0:T(8,128)}, f32[1,1024]{1,0:T(1,128)S(1)}) custom-call(s32[1]{0:T(128)} %bitcast.at, bf16[7,2,4,16,2048]{4,3,2,1,0:T(8,128)(2,1)S(1)} %constant_dynamic-update-slice_fusion.own.refs_0_.refs_1_, bf16[7,2,4,16,2048]{4,3,2,1,0:T(8,128)(2,1)S(1)} %collective-permute-done.16.recv.refs_1_.refs_4_, ...), custom_call_target="tpu_custom_call" | custom-call | flops 4294967296 | bytes 4194304 | tf_op jit(solution)/shard_map/pallas_call | solution.py:251
  93.9 3.6 %all-to-all-start = ((f32[8,256,128]{2,1,0:T(8,128)}), f32[8,256,128]{2,1,0:T(8,128)S(1)}, u32[]{:S(2)}, u32[]{:S(2)}) async-start(f32[8,256,128]{2,1,0:T(8,128)} %get-tuple-element.68), calls=%async_computation | async-start | bytes 2097152 | tf_op jit(solution)/shard_map/all_to_all | solution.py:366
  98.0 15.3 %shard_map.54 = f32[1024,2048]{1,0:T(8,128)} custom-call(s32[1]{0:T(128)} %bitcast.at, bf16[4,2,4,16,2048]{4,3,2,1,0:T(8,128)(2,1)} %copy-done.4, bf16[7,2,4,16,2048]{4,3,2,1,0:T(8,128)(2,1)} %copy-done, bf16[5,2,4,16,2048]{4,3,2,1,0:T(8,128)(2,1)} %copy-done.2, bf16[4,2,4,16,2048]{4,3,2,1,0:T(8,128)(2,1)} %copy-done.6, ...), custom_call_target="tpu_custom_call" | custom-call | flops 8589934592 | bytes 20971520 | tf_op jit(solution)/shard_map/pallas_call | solution.py:308
  (46 shorter events, 6.1 us)
Async XLA Ops:
  0.6 3.2 %collective-permute-start = (bf16[16,16384]{1,0:T(8,128)(2,1)}, bf16[16,16384]{1,0:T(8,128)(2,1)S(1)}, u32[]{:S(2)}, u32[]{:S(2)}) collective-permute-start(bf16[16,16384]{1,0:T(8,128)(2,1)} %mine.1), channel_id=1, source_target_pairs={{0,8},{8,0},{1,9},{9,1},{2,10},{10,2},{3,11},{11,3},{16,24},{24,16... | collective-permute-start | bytes 1572872 | tf_op jit(solution)/shard_map/ppermute | solution.py:39
  3.9 1.0 copy-start.5
  5.5 7.7 %collective-permute-start.1 = (bf16[2,2,16,2048]{3,2,1,0:T(8,128)(2,1)S(1)}, bf16[2,2,16,2048]{3,2,1,0:T(8,128)(2,1)S(1)}, u32[]{:S(2)}, u32[]{:S(2)}) collective-permute-start(bf16[2,2,16,2048]{3,2,1,0:T(8,128)(2,1)S(1)} %get-tuple-element.37), channel_id=1, source_target_pairs={{0,16},{8,9},{1,17},{9,10},{2,18},{10,11},{3,19},{11,8},{16,32},{2... | collective-permute-start | bytes 786440 | tf_op jit(solution)/shard_map/ppermute | solution.py:39
  7.3 8.3 %collective-permute-start.2 = (bf16[2,2,16,2048]{3,2,1,0:T(8,128)(2,1)S(1)}, bf16[2,2,16,2048]{3,2,1,0:T(8,128)(2,1)S(1)}, u32[]{:S(2)}, u32[]{:S(2)}) collective-permute-start(bf16[2,2,16,2048]{3,2,1,0:T(8,128)(2,1)S(1)} %get-tuple-element.38), channel_id=1, source_target_pairs={{0,48},{8,11},{1,49},{9,8},{2,50},{10,9},{3,51},{11,10},{16,0},{24... | collective-permute-start | bytes 786440 | tf_op jit(solution)/shard_map/ppermute | solution.py:39
  9.5 7.8 %collective-permute-start.3 = (bf16[2,2,16,2048]{3,2,1,0:T(8,128)(2,1)S(1)}, bf16[2,2,16,2048]{3,2,1,0:T(8,128)(2,1)S(1)}, u32[]{:S(2)}, u32[]{:S(2)}) collective-permute-start(bf16[2,2,16,2048]{3,2,1,0:T(8,128)(2,1)S(1)} %get-tuple-element.39), channel_id=1, source_target_pairs={{0,32},{8,10},{1,33},{9,11},{2,34},{10,8},{3,35},{11,9},{16,48},{2... | collective-permute-start | bytes 786440 | tf_op jit(solution)/shard_map/ppermute | solution.py:39
  18.0 17.9 %collective-permute-start.6 = (bf16[2,4,16,2048]{3,2,1,0:T(8,128)(2,1)S(1)}, bf16[2,4,16,2048]{3,2,1,0:T(8,128)(2,1)S(1)}, u32[]{:S(2)}, u32[]{:S(2)}) collective-permute-start(bf16[2,4,16,2048]{3,2,1,0:T(8,128)(2,1)S(1)} %get-tuple-element.40), channel_id=1, source_target_pairs={{0,2},{8,40},{1,3},{9,41},{2,0},{10,42},{3,1},{11,43},{16,18},{24,... | collective-permute-start | bytes 1572872 | tf_op jit(solution)/shard_map/ppermute | solution.py:39
  20.9 15.0 %collective-permute-start.5 = (bf16[2,4,16,2048]{3,2,1,0:T(8,128)(2,1)S(1)}, bf16[2,4,16,2048]{3,2,1,0:T(8,128)(2,1)S(1)}, u32[]{:S(2)}, u32[]{:S(2)}) collective-permute-start(bf16[2,4,16,2048]{3,2,1,0:T(8,128)(2,1)S(1)} %get-tuple-element.40), channel_id=1, source_target_pairs={{0,3},{8,56},{1,0},{9,57},{2,1},{10,58},{3,2},{11,59},{16,19},{24,... | collective-permute-start | bytes 1572872 | tf_op jit(solution)/shard_map/ppermute | solution.py:39
  21.7 14.2 %collective-permute-start.4 = (bf16[2,4,16,2048]{3,2,1,0:T(8,128)(2,1)S(1)}, bf16[2,4,16,2048]{3,2,1,0:T(8,128)(2,1)S(1)}, u32[]{:S(2)}, u32[]{:S(2)}) collective-permute-start(bf16[2,4,16,2048]{3,2,1,0:T(8,128)(2,1)S(1)} %get-tuple-element.40), channel_id=1, source_target_pairs={{0,1},{8,24},{1,2},{9,25},{2,3},{10,26},{3,0},{11,27},{16,17},{24,... | collective-permute-start | bytes 1572872 | tf_op jit(solution)/shard_map/ppermute | solution.py:39
  22.3 11.4 %collective-permute-start.7 = (bf16[2,4,16,2048]{3,2,1,0:T(8,128)(2,1)S(1)}, bf16[2,4,16,2048]{3,2,1,0:T(8,128)(2,1)S(1)}, u32[]{:S(2)}, u32[]{:S(2)}) collective-permute-start(bf16[2,4,16,2048]{3,2,1,0:T(8,128)(2,1)S(1)} %get-tuple-element.41), channel_id=1, source_target_pairs={{0,4},{8,12},{1,5},{9,13},{2,6},{10,14},{3,7},{11,15},{16,20},{24,... | collective-permute-start | bytes 1572872 | tf_op jit(solution)/shard_map/ppermute | solution.py:39
  23.6 12.3 %collective-permute-start.8 = (bf16[2,4,16,2048]{3,2,1,0:T(8,128)(2,1)S(1)}, bf16[2,4,16,2048]{3,2,1,0:T(8,128)(2,1)S(1)}, u32[]{:S(2)}, u32[]{:S(2)}) collective-permute-start(bf16[2,4,16,2048]{3,2,1,0:T(8,128)(2,1)S(1)} %get-tuple-element.42), channel_id=1, source_target_pairs={{0,68},{8,76},{1,69},{9,77},{2,70},{10,78},{3,71},{11,79},{16,84},... | collective-permute-start | bytes 1572872 | tf_op jit(solution)/shard_map/ppermute | solution.py:39
  36.2 10.8 %copy-start.4 = (bf16[4,2,4,16,2048]{4,3,2,1,0:T(8,128)(2,1)}, bf16[4,2,4,16,2048]{4,3,2,1,0:T(8,128)(2,1)S(1)}, u32[]{:S(2)}) copy-start(bf16[4,2,4,16,2048]{4,3,2,1,0:T(8,128)(2,1)S(1)} %pad_maximum_fusion.1.own.refs_0_) | copy-start | bytes 6291460
  36.2 7.1 %collective-permute-start.12 = (bf16[4,2,4,16,2048]{4,3,2,1,0:T(8,128)(2,1)S(1)}, bf16[4,2,4,16,2048]{4,3,2,1,0:T(8,128)(2,1)S(1)}, u32[]{:S(2)}, u32[]{:S(2)}) collective-permute-start(bf16[4,2,4,16,2048]{4,3,2,1,0:T(8,128)(2,1)S(1)} %pad_maximum_fusion.1.own.refs_0_), channel_id=1, source_target_pairs={{0,8},{8,0},{1,9},{9,1},{2,10},{10,2},{3,11},{11,3},{16,24},{24,16... | collective-permute-start | bytes 6291464 | tf_op jit(solution)/shard_map/ppermute | solution.py:39
  39.6 17.1 %collective-permute-start.11 = (bf16[2,2,4,16,2048]{4,3,2,1,0:T(8,128)(2,1)S(1)}, bf16[2,2,4,16,2048]{4,3,2,1,0:T(8,128)(2,1)S(1)}, u32[]{:S(2)}, u32[]{:S(2)}) collective-permute-start(bf16[2,2,4,16,2048]{4,3,2,1,0:T(8,128)(2,1)S(1)} %pad_maximum_fusion.4), channel_id=1, source_target_pairs={{0,3},{8,56},{1,0},{9,57},{2,1},{10,58},{3,2},{11,59},{16,19},{24,... | collective-permute-start | bytes 3145736 | tf_op jit(solution)/shard_map/ppermute | solution.py:39
  41.6 15.2 %collective-permute-start.10 = (bf16[2,2,4,16,2048]{4,3,2,1,0:T(8,128)(2,1)S(1)}, bf16[2,2,4,16,2048]{4,3,2,1,0:T(8,128)(2,1)S(1)}, u32[]{:S(2)}, u32[]{:S(2)}) collective-permute-start(bf16[2,2,4,16,2048]{4,3,2,1,0:T(8,128)(2,1)S(1)} %pad_maximum_fusion.4), channel_id=1, source_target_pairs={{0,1},{8,24},{1,2},{9,25},{2,3},{10,26},{3,0},{11,27},{16,17},{24,... | collective-permute-start | bytes 3145736 | tf_op jit(solution)/shard_map/ppermute | solution.py:39
  41.6 15.0 %collective-permute-start.9 = (bf16[2,4,16,2048]{3,2,1,0:T(8,128)(2,1)S(1)}, bf16[2,4,16,2048]{3,2,1,0:T(8,128)(2,1)S(1)}, u32[]{:S(2)}, u32[]{:S(2)}) collective-permute-start(bf16[2,4,16,2048]{3,2,1,0:T(8,128)(2,1)S(1)} %get-tuple-element.50), channel_id=1, source_target_pairs={{0,64},{8,72},{1,65},{9,73},{2,66},{10,74},{3,67},{11,75},{16,80},... | collective-permute-start | bytes 1572872 | tf_op jit(solution)/shard_map/ppermute | solution.py:39
  43.3 3.7 %copy-start.6 = (bf16[4,2,4,16,2048]{4,3,2,1,0:T(8,128)(2,1)}, bf16[4,2,4,16,2048]{4,3,2,1,0:T(8,128)(2,1)S(1)}, u32[]{:S(2)}) copy-start(bf16[4,2,4,16,2048]{4,3,2,1,0:T(8,128)(2,1)S(1)} %collective-permute-done.12.recv.refs_3_) | copy-start | bytes 6291460
  57.1 29.8 %copy-start = (bf16[7,2,4,16,2048]{4,3,2,1,0:T(8,128)(2,1)}, bf16[7,2,4,16,2048]{4,3,2,1,0:T(8,128)(2,1)S(1)}, u32[]{:S(2)}) copy-start(bf16[7,2,4,16,2048]{4,3,2,1,0:T(8,128)(2,1)S(1)} %constant_dynamic-update-slice_fusion.own.refs_0_.refs_1_) | copy-start | bytes 11010052
  57.1 7.0 %collective-permute-start.16 = (bf16[7,2,4,16,2048]{4,3,2,1,0:T(8,128)(2,1)S(1)}, bf16[7,2,4,16,2048]{4,3,2,1,0:T(8,128)(2,1)S(1)}, u32[]{:S(2)}, u32[]{:S(2)}) collective-permute-start(bf16[7,2,4,16,2048]{4,3,2,1,0:T(8,128)(2,1)S(1)} %constant_dynamic-update-slice_fusion.own.refs_0_.refs_1_), channel_id=1, source_target_pairs={{0,8},{8,0},{1,9},{9,1},{2,10},{10,2},{3,11},{11,3},{16,24},{24,16... | collective-permute-start | bytes 11010056 | tf_op jit(solution)/shard_map/ppermute | solution.py:39
  58.3 21.5 %collective-permute-start.14 = (bf16[2,2,4,16,2048]{4,3,2,1,0:T(8,128)(2,1)S(1)}, bf16[2,2,4,16,2048]{4,3,2,1,0:T(8,128)(2,1)S(1)}, u32[]{:S(2)}, u32[]{:S(2)}) collective-permute-start(bf16[2,2,4,16,2048]{4,3,2,1,0:T(8,128)(2,1)S(1)} %get-tuple-element.74), channel_id=1, source_target_pairs={{0,3},{8,56},{1,0},{9,57},{2,1},{10,58},{3,2},{11,59},{16,19},{24,... | collective-permute-start | bytes 3145736 | tf_op jit(solution)/shard_map/ppermute | solution.py:39
  60.5 20.8 %collective-permute-start.13 = (bf16[2,2,4,16,2048]{4,3,2,1,0:T(8,128)(2,1)S(1)}, bf16[2,2,4,16,2048]{4,3,2,1,0:T(8,128)(2,1)S(1)}, u32[]{:S(2)}, u32[]{:S(2)}) collective-permute-start(bf16[2,2,4,16,2048]{4,3,2,1,0:T(8,128)(2,1)S(1)} %get-tuple-element.75), channel_id=1, source_target_pairs={{0,1},{8,24},{1,2},{9,25},{2,3},{10,26},{3,0},{11,27},{16,17},{24,... | collective-permute-start | bytes 3145736 | tf_op jit(solution)/shard_map/ppermute | solution.py:39
  60.5 19.3 %collective-permute-start.15 = (bf16[1,2,4,16,2048]{4,3,2,1,0:T(8,128)(2,1)S(1)}, bf16[1,2,4,16,2048]{4,3,2,1,0:T(8,128)(2,1)S(1)}, u32[]{:S(2)}, u32[]{:S(2)}) collective-permute-start(bf16[1,2,4,16,2048]{4,3,2,1,0:T(8,128)(2,1)S(1)} %bitcast.24), channel_id=1, source_target_pairs={{0,2},{8,40},{1,3},{9,41},{2,0},{10,42},{3,1},{11,43},{16,18},{24,... | collective-permute-start | bytes 1572872 | tf_op jit(solution)/shard_map/ppermute | solution.py:39
  64.1 22.8 %copy-start.1 = (bf16[7,2,4,16,2048]{4,3,2,1,0:T(8,128)(2,1)}, bf16[7,2,4,16,2048]{4,3,2,1,0:T(8,128)(2,1)S(1)}, u32[]{:S(2)}) copy-start(bf16[7,2,4,16,2048]{4,3,2,1,0:T(8,128)(2,1)S(1)} %collective-permute-done.16.recv.refs_1_.refs_4_) | copy-start | bytes 11010052
  81.6 12.3 %copy-start.2 = (bf16[5,2,4,16,2048]{4,3,2,1,0:T(8,128)(2,1)}, bf16[5,2,4,16,2048]{4,3,2,1,0:T(8,128)(2,1)S(1)}, u32[]{:S(2)}) copy-start(bf16[5,2,4,16,2048]{4,3,2,1,0:T(8,128)(2,1)S(1)} %constant_dynamic-update-slice_fusion.5.refs_2_) | copy-start | bytes 7864324
  81.6 5.3 %collective-permute-start.17 = (bf16[5,2,4,16,2048]{4,3,2,1,0:T(8,128)(2,1)S(1)}, bf16[5,2,4,16,2048]{4,3,2,1,0:T(8,128)(2,1)S(1)}, u32[]{:S(2)}, u32[]{:S(2)}) collective-permute-start(bf16[5,2,4,16,2048]{4,3,2,1,0:T(8,128)(2,1)S(1)} %constant_dynamic-update-slice_fusion.5.refs_2_), channel_id=1, source_target_pairs={{0,8},{8,0},{1,9},{9,1},{2,10},{10,2},{3,11},{11,3},{16,24},{24,16... | collective-permute-start | bytes 7864328 | tf_op jit(solution)/shard_map/ppermute | solution.py:39
  86.9 7.0 %copy-start.3 = (bf16[5,2,4,16,2048]{4,3,2,1,0:T(8,128)(2,1)}, bf16[5,2,4,16,2048]{4,3,2,1,0:T(8,128)(2,1)S(1)}, u32[]{:S(2)}) copy-start(bf16[5,2,4,16,2048]{4,3,2,1,0:T(8,128)(2,1)S(1)} %collective-permute-done.17.refs_3_.refs_5_) | copy-start | bytes 7864324
  93.9 19.4 %all-to-all-start = ((f32[8,256,128]{2,1,0:T(8,128)}), f32[8,256,128]{2,1,0:T(8,128)S(1)}, u32[]{:S(2)}, u32[]{:S(2)}) async-start(f32[8,256,128]{2,1,0:T(8,128)} %get-tuple-element.68), calls=%async_computation | async-start | bytes 2097152 | tf_op jit(solution)/shard_map/all_to_all | solution.py:366

commit v4 on v3

--- a/solution.py
+++ b/solution.py
@@ -55,20 +55,29 @@
     return x, y, z, 1 - k
 
 
-def pick_kernel(at, mine, other, *pieces):
+def pick_kernel(at, mine, other, *refs):
+    pieces, sems = refs[:4], refs[4]
+    copies = []
     for n, piece in enumerate(pieces):
         for half in range(2):
             span = pl.ds(pl.multiple_of((half * 4 + at[n]) * PANEL, PANEL), PANEL)
-            piece[half, 0] = mine[:, span]
+            copies.append(pltpu.make_async_copy(mine.at[:, span], piece.at[half, 0], sems.at[2 * n + half]))
+            copies[-1].start()
+    for n, piece in enumerate(pieces):
+        for half in range(2):
+            span = pl.ds(pl.multiple_of((half * 4 + at[n]) * PANEL, PANEL), PANEL)
             piece[half, 1] = other[:, span]
+    for copy in copies:
+        copy.wait()
 
 
 def pick(at, mine, other):
     return pl.pallas_call(
         pick_kernel,
         out_shape=[jax.ShapeDtypeStruct((2, 2, LOCAL, PANEL), BF16)] * 4,
-        in_specs=[IN_SMEM] + [IN_VMEM] * 2,
+        in_specs=[IN_SMEM, ANY, IN_VMEM],
         out_specs=[IN_VMEM] * 4,
+        scratch_shapes=[pltpu.SemaphoreType.DMA((8,))],
         compiler_params=SMALL,
     )(at, mine, other)
 
@@ -91,10 +100,31 @@
     )(at, *pieces)
 
 
-OWN = tuple((0, step) for step in range(4))
-SOON = ((1, 0), (2, 0), (1, 1), (2, 1), (1, 2), (2, 2), (3, 0))
-LATE = ((1, 3), (3, 1), (2, 3), (3, 2), (3, 3))
-ORDER = (OWN, SOON, LATE)
+def pack_kernel(plan, *refs):
+    sources, packed = refs[: -len(plan)], refs[-len(plan) :]
+    for out, parts in zip(packed, plan):
+        at = 0
+        for n, first, last in parts:
+            out[at : at + last - first] = sources[n][first:last]
+            at += last - first
+
+
+def pack(plan, *sources):
+    sizes = [sum(last - first for _, first, last in parts) for parts in plan]
+    return pl.pallas_call(
+        functools.partial(pack_kernel, plan),
+        out_shape=[jax.ShapeDtypeStruct((size, 4, LOCAL, PANEL), BF16) for size in sizes],
+        in_specs=[IN_VMEM] * len(sources),
+        out_specs=[IN_VMEM] * len(sizes),
+        compiler_params=SMALL,
+    )(*sources)
+
+
+EARLY = [(0, 0), (0, 1), (0, 2), (1, 0), (2, 0)]
+SOON = [(0, 3), (1, 1), (2, 1), (1, 2), (2, 2), (3, 0)]
+LATE = [(1, 3), (3, 1), (2, 3), (3, 2), (3, 3)]
+ORDER = (EARLY, SOON, LATE)
+WIDTH = 128
 LEFT = (((0,), (0,)), ((), ()))
 
 
@@ -136,9 +166,20 @@
     return jnp.concatenate([block, jnp.ones((block.shape[0], 128), BF16)], axis=1)
 
 
-def score_of(block, comps):
+def score_of(comps, block):
     score = jnp.dot(block, comps, preferred_element_type=F32)
-    return score[:, :COMPS] + score[:, COMPS:]
+    return (score[:, :COMPS] + score[:, COMPS:]).T
+
+
+def left_of(centred):
+    high = centred.astype(BF16)
+    low = (centred - high.astype(F32)).astype(BF16)
+    return jnp.concatenate([high, low, jnp.ones((16, centred.shape[1]), BF16)], axis=0)
+
+
+def product_of(left, panel):
+    product = jnp.dot(left, panel, preferred_element_type=F32)
+    return product[:COMPS] + product[COMPS : 2 * COMPS], product[2 * COMPS : 2 * COMPS + 1]
 
 
 def select(core, own, recv, use):
@@ -151,116 +192,139 @@
         use(recv, own, HALF)
 
 
-def left_of(centred):
-    high = centred.astype(BF16)
-    low = (centred - high.astype(F32)).astype(BF16)
-    return ones_beside(jnp.concatenate([high, low], axis=1))
-
-
-def product_of(left, panel):
-    product = lax.dot_general(left, panel, LEFT, preferred_element_type=F32)
-    return product[:COMPS] + product[COMPS : 2 * COMPS], product[2 * COMPS : 2 * COMPS + 1]
-
-
-def own_kernel(at, own, recv, comps, total, row_sum, score_sum, origin, rows, cols):
+def early_kernel(at, own, recv, components, scores, origin, comps, cols):
+    comps[:, :COMPS] = components[...].astype(BF16)
+    comps[:, COMPS:] = (components[...] - comps[:, :COMPS].astype(F32)).astype(BF16)
+
     def use(row_from, col_from, offset):
-        for i in range(4):
-            cols[i] = col_from[i]
+        cols[...] = col_from[...]
+
+    select(at[0], own, recv, use)
+    score = score_of(comps[...], cols[...].reshape(len(EARLY) * WIDTH, PANEL))
+    scores[...] = score
+    mean = jnp.sum(score, axis=1, keepdims=True) * (1.0 / score.shape[1])
+    origin[...] = jnp.broadcast_to(mean, (COMPS, 128))
+
+
+def early_part(at, own, recv, comps):
+    return pl.pallas_call(
+        early_kernel,
+        out_shape=[
+            jax.ShapeDtypeStruct((COMPS, len(EARLY) * WIDTH), F32),
+            jax.ShapeDtypeStruct((COMPS, 128), F32),
+            jax.ShapeDtypeStruct((PANEL, 2 * COMPS), BF16),
+        ],
+        in_specs=[IN_SMEM] + [IN_VMEM] * 3,
+        out_specs=[IN_VMEM] * 3,
+        scratch_shapes=[pltpu.VMEM((len(EARLY), 2, 4, LOCAL, PANEL), BF16)],
+        compiler_params=MIDDLE,
+        cost_estimate=pl.CostEstimate(flops=1 << 30, bytes_accessed=1 << 20, transcendentals=0),
+    )(at, own, recv, comps)
+
+
+def fill_rows(rows, groups, pieces, offset):
+    for n, m in enumerate(groups):
+        for step in range(4):
+            array, i = pieces(m, step)
             for s in range(2):
-                rows[:, 1 - s, i] = row_from[i, s, :, :, offset : offset + HALF]
+                rows[n, :, 1 - s, step] = array[i, s, :, :, offset : offset + HALF]
+
+
+def find(arrays, m, step):
+    for array, labels in zip(arrays, ORDER):
+        if (m, step) in labels:
+            return array, labels.index((m, step))
+
+
+def soon_kernel(at, *refs):
+    own, recv, comps, early, origin, scores, total, row_sum, rows, cols = refs[:2], refs[2:4], *refs[4:]
+
+    def use(row_from, col_from, offset):
+        cols[...] = col_from[1][...]
+        fill_rows(rows, (0,), lambda m, step: find(row_from, m, step), offset)
 
     select(at[0], own, recv, use)
-    score = score_of(cols[...].reshape(512, PANEL), comps[...])
-    score_sum[...] = jnp.sum(score, axis=0, keepdims=True)
-    origin[...] = score_sum[...] * (1.0 / 512)
-    total[...], row_sum[...] = product_of(left_of(score - origin[...]), rows[...].reshape(512, HALF))
-
-
-def own_part(at, own, recv, comps):
-    return pl.pallas_call(
-        own_kernel,
+    score = score_of(comps[...], cols[...].reshape(len(SOON) * WIDTH, PANEL))
+    scores[...] = score
+    first = jnp.concatenate([early[:, : 3 * WIDTH], score[:, :WIDTH]], axis=1)
+    total[...], row_sum[...] = product_of(left_of(first - origin[:, :1]), rows[...].reshape(4 * WIDTH, HALF))
+
+
+def soon_part(at, own, recv, comps, early):
+    return pl.pallas_call(
+        soon_kernel,
         out_shape=[
+            jax.ShapeDtypeStruct((COMPS, len(SOON) * WIDTH), F32),
             jax.ShapeDtypeStruct((COMPS, HALF), F32),
             jax.ShapeDtypeStruct((1, HALF), F32),
-            jax.ShapeDtypeStruct((1, COMPS), F32),
-            jax.ShapeDtypeStruct((1, COMPS), F32),
         ],
-        in_specs=[IN_SMEM] + [IN_VMEM] * 3,
-        out_specs=[IN_VMEM] * 4,
+        in_specs=[IN_SMEM] + [IN_VMEM] * 7,
+        out_specs=[IN_VMEM] * 3,
         scratch_shapes=[
-            pltpu.VMEM((4, 2, 4, LOCAL, HALF), BF16),
-            pltpu.VMEM((4, 2, 4, LOCAL, PANEL), BF16),
+            pltpu.VMEM((1, 4, 2, 4, LOCAL, HALF), BF16),
+            pltpu.VMEM((len(SOON), 2, 4, LOCAL, PANEL), BF16),
         ],
         compiler_params=MIDDLE,
         cost_estimate=pl.CostEstimate(flops=2 << 30, bytes_accessed=1 << 20, transcendentals=0),
-    )(at, own, recv, comps)
-
-
-def soon_kernel(at, own, recv, comps, scores, cols):
+    )(at, *own, *recv, comps, *early)
+
+
+def late_kernel(own, comps, scores):
+    scores[...] = score_of(comps[...], own[...].reshape(len(LATE) * WIDTH, PANEL))
+
+
+def late_part(own, comps):
+    return pl.pallas_call(
+        late_kernel,
+        out_shape=jax.ShapeDtypeStruct((COMPS, len(LATE) * WIDTH), F32),
+        in_specs=[IN_VMEM] * 2,
+        out_specs=IN_VMEM,
+        compiler_params=SMALL,
+        cost_estimate=pl.CostEstimate(flops=1 << 30, bytes_accessed=1 << 20, transcendentals=0),
+    )(own, comps)
+
+
+def last_kernel(at, *refs):
+    own, recv, early, origin, soon, total_in, rs_in, late_own, late_recv = refs[:3], refs[3:6], *refs[6:13]
+    parts, means, rows, left = refs[13:]
+
+    def put(block, labels):
+        for i, (m, step) in enumerate(labels):
+            if m > 0:
+                at_scan = ((m - 1) * 4 + step) * WIDTH
+                left[:, at_scan : at_scan + WIDTH] = left_of(block[:, i * WIDTH : (i + 1) * WIDTH] - origin[:, :1])
+
     def use(row_from, col_from, offset):
-        for i in range(len(SOON)):
-            cols[i] = col_from[i]
+        fill_rows(rows, (1, 2, 3), lambda m, step: find(row_from, m, step), offset)
+        put(late_recv if offset == 0 else late_own, LATE)
 
     select(at[0], own, recv, use)
-    scores[...] = score_of(cols[...].reshape(len(SOON) * 128, PANEL), comps[...])
-
-
-def soon_part(at, own, recv, comps):
-    return pl.pallas_call(
-        soon_kernel,
-        out_shape=jax.ShapeDtypeStruct((len(SOON) * 128, COMPS), F32),
-        in_specs=[IN_SMEM] + [IN_VMEM] * 3,
-        out_specs=IN_VMEM,
-        scratch_shapes=[pltpu.VMEM((len(SOON), 2, 4, LOCAL, PANEL), BF16)],
-        compiler_params=MIDDLE,
-        cost_estimate=pl.CostEstimate(flops=2 << 30, bytes_accessed=1 << 20, transcendentals=0),
-    )(at, own, recv, comps)
-
-
-def last_kernel(at, *refs):
-    own_soon, recv_soon, own_late, recv_late, comps, soon, total_in, rs_in, ss_in, origin_in = refs[:10]
-    parts, means, rows, cols, left = refs[10:]
-
-    def use(row_from, col_from, offset):
-        for array, labels in zip(row_from, (SOON, LATE)):
-            for i, (m, step) in enumerate(labels):
-                for s in range(2):
-                    rows[m - 1, :, 1 - s, step] = array[i, s, :, :, offset : offset + HALF]
-        for i in range(len(LATE)):
-            cols[i] = col_from[1][i]
-
-    select(at[0], (own_soon, own_late), (recv_soon, recv_late), use)
-    late = score_of(cols[...].reshape(len(LATE) * 128, PANEL), comps[...])
-    score_sum = ss_in[...] + jnp.sum(late, axis=0, keepdims=True) + jnp.sum(soon[...], axis=0, keepdims=True)
-    origin = origin_in[...]
-    for block, labels in ((soon[...], SOON), (late, LATE)):
-        block = left_of(block - origin)
-        for i, (m, step) in enumerate(labels):
-            left[pl.ds(((m - 1) * 4 + step) * 128, 128), :] = block[i * 128 : (i + 1) * 128]
-    total, row_sum = product_of(left[...], rows[...].reshape(1536, HALF))
+    put(early, EARLY)
+    put(soon, SOON)
+    late = jnp.where(at[0] == 0, late_recv[...], late_own[...])
+    score_sum = sum(jnp.sum(block, axis=1, keepdims=True) for block in (early[...], soon[...], late))
+    total, row_sum = product_of(left[...], rows[...].reshape(12 * WIDTH, HALF))
     row_sum = row_sum + rs_in[...]
-    shift = score_sum * (1.0 / SCANS) - origin
-    shift = jnp.transpose(jnp.broadcast_to(shift, (128, COMPS)))[:, :1]
+    shift = score_sum * (1.0 / SCANS) - origin[:, :1]
     total = (total + total_in[...] - shift * row_sum) * (1.0 / (SCANS - 1))
     for c in range(8):
         parts[c] = total[:, c * 128 : (c + 1) * 128]
     means[...] = row_sum * (1.0 / SCANS)
 
 
-def last_part(at, pieces, comps, soon, state):
+def last_part(at, own, recv, state):
     return pl.pallas_call(
         last_kernel,
         out_shape=[jax.ShapeDtypeStruct((8, COMPS, 128), F32), jax.ShapeDtypeStruct((1, HALF), F32)],
-        in_specs=[IN_SMEM] + [IN_VMEM] * 10,
+        in_specs=[IN_SMEM] + [IN_VMEM] * 13,
         out_specs=[IN_VMEM] * 2,
         scratch_shapes=[
             pltpu.VMEM((3, 4, 2, 4, LOCAL, HALF), BF16),
-            pltpu.VMEM((len(LATE), 2, 4, LOCAL, PANEL), BF16),
-            pltpu.VMEM((1536, 2 * COMPS + 128), BF16),
+            pltpu.VMEM((2 * COMPS + 16, 12 * WIDTH), BF16),
         ],
         compiler_params=MIDDLE,
         cost_estimate=pl.CostEstimate(flops=4 << 30, bytes_accessed=4 << 20, transcendentals=0),
-    )(at, *pieces, comps, soon, *state)
+    )(at, *own, *recv, *state)
 
 
 def gram_kernel(at, *refs):
@@ -338,31 +402,33 @@
         [own_half, jnp.where(first, own_half, 1 - own_half), jnp.where(first, 1 - own_half, own_half), 1 - own_half]
     ).astype(jnp.int32)
     group_own, to_1, to_2, to_3 = group(at, got)
-    high = lax.reduce_precision(components, 8, 7)
-    comps = jnp.concatenate([high, components - high], axis=1).astype(BF16)
+    at = jnp.reshape(k, (1,)).astype(jnp.int32)
     near = [permute(to_1, across(1)), permute(to_3, across(3))]
-    ring_own = [permute(group_own, around(d)) for d in STEPS[1:]]
-    near, to_2, comps = lax.optimization_barrier((near, to_2, comps))
-    ring_own, near[0] = lax.optimization_barrier((ring_own, near[0]))
+    ring_own = [permute(group_own, around(d)) for d in STEPS[1:3]]
+    near, ring_own, to_2 = lax.optimization_barrier((near, ring_own, to_2))
     far = permute(to_2, across(2))
-    at = jnp.reshape(k, (1,)).astype(jnp.int32)
-    own = jnp.stack([group_own] + ring_own)
-    recv = permute(own, swap)
-    group_near = jnp.stack(near)
-    ring_near = [permute(group_near, around(d)) for d in STEPS[1:3]]
-    state = own_part(at, own, recv, comps)
-    far, ring_near, state = lax.optimization_barrier((far, ring_near, state))
-    late = [permute(jnp.stack([ring_near[n][n], far]), around(STEPS[n + 1])) for n in range(2)]
-    late.append(permute(far[None], around(STEPS[3])))
-    own_soon = jnp.concatenate([group_near] + ring_near + [far[None]])
+    ring = pack((((0, 0, 2), (1, 0, 2), (2, 0, 1)), ((0, 0, 2), (1, 0, 2), (3, 1, 2))), *near, *ring_own)
+    ring = [permute(ring[n], around(STEPS[n + 1])) for n in range(2)]
+    (own_early,) = pack((tuple((n, 0, 2) for n in range(5)),), group_own, *ring_own, *near)
+    own_early = own_early.reshape((5, 2, 4, LOCAL, PANEL))
+    recv_early = permute(own_early, swap)
+    *early, comps = early_part(at, own_early, recv_early, components)
+    far, ring, early = lax.optimization_barrier((far, ring, early))
+    late = pack((((0, 0, 2), (2, 0, 2)), ((1, 2, 4), (2, 0, 2))), *ring, far)
+    late = [permute(late[n], around(STEPS[n + 1])) for n in range(2)]
+    late.append(permute(far, around(STEPS[3])))
+    (own_soon,) = pack((((0, 4, 5), (1, 4, 5), (0, 0, 4), (1, 0, 4), (2, 0, 2)),), *ring, far)
+    own_soon = own_soon.reshape((6, 2, 4, LOCAL, PANEL))
     recv_soon = permute(own_soon, swap)
-    soon = soon_part(at, own_soon, recv_soon, comps)
+    soon = soon_part(at, (own_early, own_soon), (recv_early, recv_soon), comps, early)
     late, soon = lax.optimization_barrier((late, soon))
-    own_late = jnp.concatenate(late)
+    (own_late,) = pack((((0, 0, 4), (1, 0, 4), (2, 0, 2)),), *late)
+    own_late = own_late.reshape((5, 2, 4, LOCAL, PANEL))
     recv_late = permute(own_late, swap)
-    parts, row_means = last_part(at, (own_soon, recv_soon, own_late, recv_late), comps, soon, state)
-    own = [own, own_soon, own_late]
-    recv = [recv, recv_soon, recv_late]
+    own = [own_early, own_soon, own_late]
+    recv = [recv_early, recv_soon, recv_late]
+    scores = late_part(own_late, comps)
+    parts, row_means = last_part(at, own, recv, (*early, *soon, scores, permute(scores, swap)))
     parts = lax.all_to_all(parts, "bcol", 0, 0, tiled=True)
     covariance = gram(at, own, recv, row_means)
     projected = jnp.sum(parts, axis=0).T

time: 114 us -> 110 us (0.965)
  other arithmetic: 2.8 us -> 0.21 us
    pallas_call x1, Pallas kernels: 6.98 us -> 3.56 us  [last_part(): pl.pallas_call(last_kernel, out_shape=[jax.ShapeDtypeStruct((8, COMPS, 12...]
    another operation x4 -> x0, other arithmetic: 2.43 us -> none
    pallas_call x2 -> x8, Pallas kernels: 5.97 us -> 8.32 us  [the longest x1 3.57 us: soon_part(): pl.pallas_call(soon_kernel, out_shape=[jax.ShapeDtypeStruct((COMPS, len(S...]
    unnamed x21 -> x17, local copies, waits for them, and re-layouts: 2.31 us -> 1.83 us
  transfers between devices with their start and end apart: 19 -> 19, of which waited for: 13 -> 12; matrix products, arithmetic and copies ran while one was open for 3% -> 1% of each run, Pallas kernels for 19% -> 21%
where the time goes in v4:
time: 110 us
  waiting for transfers between devices  48.5 us (44%)
  starting transfers between devices  28.9 us (26%)
  Pallas kernels  28.9 us (26%)
  local copies, waits for them, and re-layouts  2.34 us (2%)
    ppermute x18, waiting for transfers between devices, permute(): return lax.ppermute(value, AXES, pairs)  48.5 us
    ppermute x18, starting transfers between devices, permute(): return lax.ppermute(value, AXES, pairs)  25.3 us
    pallas_call x1, Pallas kernels, gram(): pl.pallas_call(gram_kernel, out_shape=jax.ShapeDtypeStruct((HALF, PANEL),...  15.3 us
    pallas_call x1, Pallas kernels, soon_part(): pl.pallas_call(soon_kernel, out_shape=[jax.ShapeDtypeStruct((COMPS, len(S...  3.57 us
    pallas_call x1, Pallas kernels, last_part(): pl.pallas_call(last_kernel, out_shape=[jax.ShapeDtypeStruct((8, COMPS, 12...  3.56 us
    all_to_all x1, starting transfers between devices, on_device(): parts = lax.all_to_all(parts, 'bcol', 0, 0, tiled=True)  3.56 us
    pallas_call x1, Pallas kernels, early_part(): pl.pallas_call(early_kernel, out_shape=[jax.ShapeDtypeStruct((COMPS, len(...  2.31 us
  transfers between devices with their start and end apart: 19, of which 12 were waited for; matrix products, arithmetic and copies ran while one was open for 1% of the time, Pallas kernels for 21%

profile of v4, /device:TPU:1, one launch (start us, length us, event | category | flops | bytes accessed | tf_op | source)
XLA Modules:
  0.0 109.7 jit_solution(4360037103386440050)
XLA Ops:
  0.6 1.5 %collective-permute-start = (bf16[16,16384]{1,0:T(8,128)(2,1)}, bf16[16,16384]{1,0:T(8,128)(2,1)S(1)}, u32[]{:S(2)}, u32[]{:S(2)}) collective-permute-start(bf16[16,16384]{1,0:T(8,128)(2,1)} %mine.1), channel_id=1, source_target_pairs={{0,8},{8,0},{1,9},{9,1},{2,10},{10,2},{3,11},{11,3},{16,24},{24,16... | collective-permute-start | bytes 1572872 | tf_op jit(solution)/shard_map/ppermute | solution.py:39
  2.2 1.7 %collective-permute-done.other = bf16[16,16384]{1,0:T(8,128)(2,1)S(1)} collective-permute-done((bf16[16,16384]{1,0:T(8,128)(2,1)}, bf16[16,16384]{1,0:T(8,128)(2,1)S(1)}, u32[]{:S(2)}, u32[]{:S(2)}) %collective-permute-start) | collective-permute-done | bytes 524320 | tf_op jit(solution)/shard_map/ppermute | solution.py:39
  3.9 1.0 copy-done.7
  4.9 1.0 shard_map.49
  6.0 1.8 %collective-permute-start.1 = (bf16[2,2,16,2048]{3,2,1,0:T(8,128)(2,1)S(1)}, bf16[2,2,16,2048]{3,2,1,0:T(8,128)(2,1)S(1)}, u32[]{:S(2)}, u32[]{:S(2)}) collective-permute-start(bf16[2,2,16,2048]{3,2,1,0:T(8,128)(2,1)S(1)} %get-tuple-element.40), channel_id=1, source_target_pairs={{0,16},{8,9},{1,17},{9,10},{2,18},{10,11},{3,19},{11,8},{16,32},{2... | collective-permute-start | bytes 786440 | tf_op jit(solution)/shard_map/ppermute | solution.py:39
  7.8 2.2 %collective-permute-start.2 = (bf16[2,2,16,2048]{3,2,1,0:T(8,128)(2,1)S(1)}, bf16[2,2,16,2048]{3,2,1,0:T(8,128)(2,1)S(1)}, u32[]{:S(2)}, u32[]{:S(2)}) collective-permute-start(bf16[2,2,16,2048]{3,2,1,0:T(8,128)(2,1)S(1)} %get-tuple-element.41), channel_id=1, source_target_pairs={{0,48},{8,11},{1,49},{9,8},{2,50},{10,9},{3,51},{11,10},{16,0},{24... | collective-permute-start | bytes 786440 | tf_op jit(solution)/shard_map/ppermute | solution.py:39
  10.0 1.2 %collective-permute-start.3 = (bf16[2,2,16,2048]{3,2,1,0:T(8,128)(2,1)S(1)}, bf16[2,2,16,2048]{3,2,1,0:T(8,128)(2,1)S(1)}, u32[]{:S(2)}, u32[]{:S(2)}) collective-permute-start(bf16[2,2,16,2048]{3,2,1,0:T(8,128)(2,1)S(1)} %get-tuple-element.42), channel_id=1, source_target_pairs={{0,32},{8,10},{1,33},{9,11},{2,34},{10,8},{3,35},{11,9},{16,48},{2... | collective-permute-start | bytes 786440 | tf_op jit(solution)/shard_map/ppermute | solution.py:39
  11.3 2.4 %collective-permute-done.1.refs_1_ = bf16[2,2,16,2048]{3,2,1,0:T(8,128)(2,1)S(1)} collective-permute-done((bf16[2,2,16,2048]{3,2,1,0:T(8,128)(2,1)S(1)}, bf16[2,2,16,2048]{3,2,1,0:T(8,128)(2,1)S(1)}, u32[]{:S(2)}, u32[]{:S(2)}) %collective-permute-start.1) | collective-permute-done | bytes 262176 | tf_op jit(solution)/shard_map/ppermute | solution.py:39
  13.6 2.4 %collective-permute-done.2.refs_2_ = bf16[2,2,16,2048]{3,2,1,0:T(8,128)(2,1)S(1)} collective-permute-done((bf16[2,2,16,2048]{3,2,1,0:T(8,128)(2,1)S(1)}, bf16[2,2,16,2048]{3,2,1,0:T(8,128)(2,1)S(1)}, u32[]{:S(2)}, u32[]{:S(2)}) %collective-permute-start.2) | collective-permute-done | bytes 262176 | tf_op jit(solution)/shard_map/ppermute | solution.py:39
  16.1 1.6 %collective-permute-done.3.refs_3_ = bf16[2,2,16,2048]{3,2,1,0:T(8,128)(2,1)S(1)} collective-permute-done((bf16[2,2,16,2048]{3,2,1,0:T(8,128)(2,1)S(1)}, bf16[2,2,16,2048]{3,2,1,0:T(8,128)(2,1)S(1)}, u32[]{:S(2)}, u32[]{:S(2)}) %collective-permute-start.3) | collective-permute-done | bytes 262176 | tf_op jit(solution)/shard_map/ppermute | solution.py:39
  18.4 1.3 %collective-permute-start.4 = (bf16[2,4,16,2048]{3,2,1,0:T(8,128)(2,1)S(1)}, bf16[2,4,16,2048]{3,2,1,0:T(8,128)(2,1)S(1)}, u32[]{:S(2)}, u32[]{:S(2)}) collective-permute-start(bf16[2,4,16,2048]{3,2,1,0:T(8,128)(2,1)S(1)} %get-tuple-element.44), channel_id=1, source_target_pairs={{0,4},{8,12},{1,5},{9,13},{2,6},{10,14},{3,7},{11,15},{16,20},{24,... | collective-permute-start | bytes 1572872 | tf_op jit(solution)/shard_map/ppermute | solution.py:39
  19.7 1.8 %collective-permute-start.5 = (bf16[2,4,16,2048]{3,2,1,0:T(8,128)(2,1)S(1)}, bf16[2,4,16,2048]{3,2,1,0:T(8,128)(2,1)S(1)}, u32[]{:S(2)}, u32[]{:S(2)}) collective-permute-start(bf16[2,4,16,2048]{3,2,1,0:T(8,128)(2,1)S(1)} %get-tuple-element.45), channel_id=1, source_target_pairs={{0,68},{8,76},{1,69},{9,77},{2,70},{10,78},{3,71},{11,79},{16,84},... | collective-permute-start | bytes 1572872 | tf_op jit(solution)/shard_map/ppermute | solution.py:39
  21.5 2.6 %collective-permute-start.7 = (bf16[2,4,16,2048]{3,2,1,0:T(8,128)(2,1)S(1)}, bf16[2,4,16,2048]{3,2,1,0:T(8,128)(2,1)S(1)}, u32[]{:S(2)}, u32[]{:S(2)}) collective-permute-start(bf16[2,4,16,2048]{3,2,1,0:T(8,128)(2,1)S(1)} %get-tuple-element.43.refs_0_), channel_id=1, source_target_pairs={{0,3},{8,56},{1,0},{9,57},{2,1},{10,58},{3,2},{11,59},{16,19},{24,... | collective-permute-start | bytes 1572872 | tf_op jit(solution)/shard_map/ppermute | solution.py:39
  24.2 7.5 %collective-permute-done.4.refs_3_.refs_0_ = bf16[2,4,16,2048]{3,2,1,0:T(8,128)(2,1)S(1)} collective-permute-done((bf16[2,4,16,2048]{3,2,1,0:T(8,128)(2,1)S(1)}, bf16[2,4,16,2048]{3,2,1,0:T(8,128)(2,1)S(1)}, u32[]{:S(2)}, u32[]{:S(2)}) %collective-permute-start.4) | collective-permute-done | bytes 524320 | tf_op jit(solution)/shard_map/ppermute | solution.py:39
  31.6 2.1 %collective-permute-done.5.refs_4_.refs_1_ = bf16[2,4,16,2048]{3,2,1,0:T(8,128)(2,1)S(1)} collective-permute-done((bf16[2,4,16,2048]{3,2,1,0:T(8,128)(2,1)S(1)}, bf16[2,4,16,2048]{3,2,1,0:T(8,128)(2,1)S(1)}, u32[]{:S(2)}, u32[]{:S(2)}) %collective-permute-start.5) | collective-permute-done | bytes 524320 | tf_op jit(solution)/shard_map/ppermute | solution.py:39
  33.9 3.3 %collective-permute-start.11 = (bf16[5,2,4,16,2048]{4,3,2,1,0:T(8,128)(2,1)S(1)}, bf16[5,2,4,16,2048]{4,3,2,1,0:T(8,128)(2,1)S(1)}, u32[]{:S(2)}, u32[]{:S(2)}) collective-permute-start(bf16[5,2,4,16,2048]{4,3,2,1,0:T(8,128)(2,1)S(1)} %bitcast.15), channel_id=1, source_target_pairs={{0,8},{8,0},{1,9},{9,1},{2,10},{10,2},{3,11},{11,3},{16,24},{24,16... | collective-permute-start | bytes 7864328 | tf_op jit(solution)/shard_map/ppermute | solution.py:39
  37.3 1.2 %collective-permute-start.9 = (bf16[5,4,16,2048]{3,2,1,0:T(8,128)(2,1)S(1)}, bf16[5,4,16,2048]{3,2,1,0:T(8,128)(2,1)S(1)}, u32[]{:S(2)}, u32[]{:S(2)}) collective-permute-start(bf16[5,4,16,2048]{3,2,1,0:T(8,128)(2,1)S(1)} %get-tuple-element.52), channel_id=1, source_target_pairs={{0,1},{8,24},{1,2},{9,25},{2,3},{10,26},{3,0},{11,27},{16,17},{24,... | collective-permute-start | bytes 3932168 | tf_op jit(solution)/shard_map/ppermute | solution.py:39
  38.6 1.5 %collective-permute-start.10 = (bf16[5,4,16,2048]{3,2,1,0:T(8,128)(2,1)S(1)}, bf16[5,4,16,2048]{3,2,1,0:T(8,128)(2,1)S(1)}, u32[]{:S(2)}, u32[]{:S(2)}) collective-permute-start(bf16[5,4,16,2048]{3,2,1,0:T(8,128)(2,1)S(1)} %get-tuple-element.53), channel_id=1, source_target_pairs={{0,3},{8,56},{1,0},{9,57},{2,1},{10,58},{3,2},{11,59},{16,19},{24,... | collective-permute-start | bytes 3932168 | tf_op jit(solution)/shard_map/ppermute | solution.py:39
  40.5 1.3 %collective-permute-done.11.recv.refs_2_.refs_3_ = bf16[5,2,4,16,2048]{4,3,2,1,0:T(8,128)(2,1)S(1)} collective-permute-done((bf16[5,2,4,16,2048]{4,3,2,1,0:T(8,128)(2,1)S(1)}, bf16[5,2,4,16,2048]{4,3,2,1,0:T(8,128)(2,1)S(1)}, u32[]{:S(2)}, u32[]{:S(2)}) %collective-permute-start.11) | collective-permute-done | bytes 2621472 | tf_op jit(solution)/shard_map/ppermute | solution.py:39
  41.7 2.3 %shard_map.53 = (f32[256,640]{1,0:T(8,128)S(1)}, f32[256,128]{1,0:T(8,128)S(1)}, bf16[2048,512]{1,0:T(8,128)(2,1)S(1)}) custom-call(s32[1]{0:T(128)} %bitcast.at, bf16[5,2,4,16,2048]{4,3,2,1,0:T(8,128)(2,1)S(1)} %bitcast.16, bf16[5,2,4,16,2048]{4,3,2,1,0:T(8,128)(2,1)S(1)} %collective-permute-done.11.recv.refs_2_.refs_3_, f32[2048,256]{1,0:T(8,128)S(1)} %copy-done.6), custom_call_target="tpu_custom_call" | custom-call | flops 1073741824 | bytes 1048576 | tf_op jit(solution)/shard_map/pallas_call | solution.py:210
  44.0 10.5 %collective-permute-done.8.refs_2_ = bf16[2,4,16,2048]{3,2,1,0:T(8,128)(2,1)S(1)} collective-permute-done((bf16[2,4,16,2048]{3,2,1,0:T(8,128)(2,1)S(1)}, bf16[2,4,16,2048]{3,2,1,0:T(8,128)(2,1)S(1)}, u32[]{:S(2)}, u32[]{:S(2)}) %collective-permute-start.8) | collective-permute-done | bytes 524320 | tf_op jit(solution)/shard_map/ppermute | solution.py:39
  56.7 1.2 %collective-permute-start.12 = (bf16[4,4,16,2048]{3,2,1,0:T(8,128)(2,1)S(1)}, bf16[4,4,16,2048]{3,2,1,0:T(8,128)(2,1)S(1)}, u32[]{:S(2)}, u32[]{:S(2)}) collective-permute-start(bf16[4,4,16,2048]{3,2,1,0:T(8,128)(2,1)S(1)} %get-tuple-element.59), channel_id=1, source_target_pairs={{0,1},{8,24},{1,2},{9,25},{2,3},{10,26},{3,0},{11,27},{16,17},{24,... | collective-permute-start | bytes 3145736 | tf_op jit(solution)/shard_map/ppermute | solution.py:39
  57.9 1.5 %collective-permute-start.13 = (bf16[4,4,16,2048]{3,2,1,0:T(8,128)(2,1)S(1)}, bf16[4,4,16,2048]{3,2,1,0:T(8,128)(2,1)S(1)}, u32[]{:S(2)}, u32[]{:S(2)}) collective-permute-start(bf16[4,4,16,2048]{3,2,1,0:T(8,128)(2,1)S(1)} %get-tuple-element.60), channel_id=1, source_target_pairs={{0,3},{8,56},{1,0},{9,57},{2,1},{10,58},{3,2},{11,59},{16,19},{24,... | collective-permute-start | bytes 3145736 | tf_op jit(solution)/shard_map/ppermute | solution.py:39
  59.8 2.1 %collective-permute-done.15.refs_3_.refs_4_ = bf16[6,2,4,16,2048]{4,3,2,1,0:T(8,128)(2,1)S(1)} collective-permute-done((bf16[6,2,4,16,2048]{4,3,2,1,0:T(8,128)(2,1)S(1)}, bf16[6,2,4,16,2048]{4,3,2,1,0:T(8,128)(2,1)S(1)}, u32[]{:S(2)}, u32[]{:S(2)}) %collective-permute-start.15) | collective-permute-done | bytes 3145760 | tf_op jit(solution)/shard_map/ppermute | solution.py:39
  61.8 3.6 %shard_map.56 = (f32[256,768]{1,0:T(8,128)S(1)}, f32[256,1024]{1,0:T(8,128)S(1)}, f32[1,1024]{1,0:T(1,128)S(1)}) custom-call(s32[1]{0:T(128)} %bitcast.at, bf16[5,2,4,16,2048]{4,3,2,1,0:T(8,128)(2,1)S(1)} %bitcast.17, bf16[6,2,4,16,2048]{4,3,2,1,0:T(8,128)(2,1)S(1)} %bitcast.21, ...), custom_call_target="tpu_custom_call" | custom-call | flops 2147483648 | bytes 1048576 | tf_op jit(solution)/shard_map/pallas_call | solution.py:254
  65.4 12.3 %collective-permute-done.14.refs_2_ = bf16[2,4,16,2048]{3,2,1,0:T(8,128)(2,1)S(1)} collective-permute-done((bf16[2,4,16,2048]{3,2,1,0:T(8,128)(2,1)S(1)}, bf16[2,4,16,2048]{3,2,1,0:T(8,128)(2,1)S(1)}, u32[]{:S(2)}, u32[]{:S(2)}) %collective-permute-start.14) | collective-permute-done | bytes 524320 | tf_op jit(solution)/shard_map/ppermute | solution.py:39
  78.0 2.4 %collective-permute-start.16 = (bf16[5,2,4,16,2048]{4,3,2,1,0:T(8,128)(2,1)S(1)}, bf16[5,2,4,16,2048]{4,3,2,1,0:T(8,128)(2,1)S(1)}, u32[]{:S(2)}, u32[]{:S(2)}) collective-permute-start(bf16[5,2,4,16,2048]{4,3,2,1,0:T(8,128)(2,1)S(1)} %bitcast.24), channel_id=1, source_target_pairs={{0,8},{8,0},{1,9},{9,1},{2,10},{10,2},{3,11},{11,3},{16,24},{24,16... | collective-permute-start | bytes 7864328 | tf_op jit(solution)/shard_map/ppermute | solution.py:39
  80.3 1.6 %shard_map.58.refs_11_ = f32[256,640]{1,0:T(8,128)S(1)} custom-call(bf16[5,2,4,16,2048]{4,3,2,1,0:T(8,128)(2,1)S(1)} %bitcast.25, bf16[2048,512]{1,0:T(8,128)(2,1)S(1)} %get-tuple-element.61.refs_4_.comps), custom_call_target="tpu_custom_call" | custom-call | flops 1073741824 | bytes 1048576 | tf_op jit(solution)/shard_map/pallas_call | solution.py:277
  82.0 3.8 %collective-permute-done.17.refs_12_ = f32[256,640]{1,0:T(8,128)S(1)} collective-permute-done((f32[256,640]{1,0:T(8,128)S(1)}, f32[256,640]{1,0:T(8,128)S(1)}, u32[]{:S(2)}, u32[]{:S(2)}) %collective-permute-start.17) | collective-permute-done | bytes 655392 | tf_op jit(solution)/shard_map/ppermute | solution.py:39
  85.8 3.6 %shard_map.59 = (f32[8,256,128]{2,1,0:T(8,128)}, f32[1,1024]{1,0:T(1,128)S(1)}) custom-call(s32[1]{0:T(128)} %bitcast.at, bf16[5,2,4,16,2048]{4,3,2,1,0:T(8,128)(2,1)S(1)} %bitcast.18, bf16[6,2,4,16,2048]{4,3,2,1,0:T(8,128)(2,1)S(1)} %bitcast.22, bf16[5,2,4,16,2048]{4,3,2,1,0:T(8,128)(2,1)S(1)} %bitcast.26, ...), custom_call_target="tpu_custom_call" | custom-call | flops 4294967296 | bytes 4194304 | tf_op jit(solution)/shard_map/pallas_call | solution.py:316
  89.4 3.6 %all-to-all-start = ((f32[8,256,128]{2,1,0:T(8,128)}), f32[8,256,128]{2,1,0:T(8,128)S(1)}, u32[]{:S(2)}, u32[]{:S(2)}) async-start(f32[8,256,128]{2,1,0:T(8,128)} %get-tuple-element.74), calls=%async_computation | async-start | bytes 2097152 | tf_op jit(solution)/shard_map/all_to_all | solution.py:432
  93.5 15.3 %shard_map.60 = f32[1024,2048]{1,0:T(8,128)} custom-call(s32[1]{0:T(128)} %bitcast.at, bf16[5,2,4,16,2048]{4,3,2,1,0:T(8,128)(2,1)} %bitcast.19, bf16[6,2,4,16,2048]{4,3,2,1,0:T(8,128)(2,1)} %bitcast.23, bf16[5,2,4,16,2048]{4,3,2,1,0:T(8,128)(2,1)} %bitcast.27, bf16[5,2,4,16,2048]{4,3,2,1,0:T(8,128)(2,1)} %copy-done.3, ...), custom_call_target="tpu_custom_call" | custom-call | flops 8589934592 | bytes 20971520 | tf_op jit(solution)/shard_map/pallas_call | solution.py:372
  (39 shorter events, 5.7 us)
Async XLA Ops:
  0.6 3.2 %collective-permute-start = (bf16[16,16384]{1,0:T(8,128)(2,1)}, bf16[16,16384]{1,0:T(8,128)(2,1)S(1)}, u32[]{:S(2)}, u32[]{:S(2)}) collective-permute-start(bf16[16,16384]{1,0:T(8,128)(2,1)} %mine.1), channel_id=1, source_target_pairs={{0,8},{8,0},{1,9},{9,1},{2,10},{10,2},{3,11},{11,3},{16,24},{24,16... | collective-permute-start | bytes 1572872 | tf_op jit(solution)/shard_map/ppermute | solution.py:39
  3.9 1.0 copy-start.7
  6.0 7.7 %collective-permute-start.1 = (bf16[2,2,16,2048]{3,2,1,0:T(8,128)(2,1)S(1)}, bf16[2,2,16,2048]{3,2,1,0:T(8,128)(2,1)S(1)}, u32[]{:S(2)}, u32[]{:S(2)}) collective-permute-start(bf16[2,2,16,2048]{3,2,1,0:T(8,128)(2,1)S(1)} %get-tuple-element.40), channel_id=1, source_target_pairs={{0,16},{8,9},{1,17},{9,10},{2,18},{10,11},{3,19},{11,8},{16,32},{2... | collective-permute-start | bytes 786440 | tf_op jit(solution)/shard_map/ppermute | solution.py:39
  7.8 8.3 %collective-permute-start.2 = (bf16[2,2,16,2048]{3,2,1,0:T(8,128)(2,1)S(1)}, bf16[2,2,16,2048]{3,2,1,0:T(8,128)(2,1)S(1)}, u32[]{:S(2)}, u32[]{:S(2)}) collective-permute-start(bf16[2,2,16,2048]{3,2,1,0:T(8,128)(2,1)S(1)} %get-tuple-element.41), channel_id=1, source_target_pairs={{0,48},{8,11},{1,49},{9,8},{2,50},{10,9},{3,51},{11,10},{16,0},{24... | collective-permute-start | bytes 786440 | tf_op jit(solution)/shard_map/ppermute | solution.py:39
  10.0 7.8 %collective-permute-start.3 = (bf16[2,2,16,2048]{3,2,1,0:T(8,128)(2,1)S(1)}, bf16[2,2,16,2048]{3,2,1,0:T(8,128)(2,1)S(1)}, u32[]{:S(2)}, u32[]{:S(2)}) collective-permute-start(bf16[2,2,16,2048]{3,2,1,0:T(8,128)(2,1)S(1)} %get-tuple-element.42), channel_id=1, source_target_pairs={{0,32},{8,10},{1,33},{9,11},{2,34},{10,8},{3,35},{11,9},{16,48},{2... | collective-permute-start | bytes 786440 | tf_op jit(solution)/shard_map/ppermute | solution.py:39
  18.4 13.2 %collective-permute-start.4 = (bf16[2,4,16,2048]{3,2,1,0:T(8,128)(2,1)S(1)}, bf16[2,4,16,2048]{3,2,1,0:T(8,128)(2,1)S(1)}, u32[]{:S(2)}, u32[]{:S(2)}) collective-permute-start(bf16[2,4,16,2048]{3,2,1,0:T(8,128)(2,1)S(1)} %get-tuple-element.44), channel_id=1, source_target_pairs={{0,4},{8,12},{1,5},{9,13},{2,6},{10,14},{3,7},{11,15},{16,20},{24,... | collective-permute-start | bytes 1572872 | tf_op jit(solution)/shard_map/ppermute | solution.py:39
  19.7 14.0 %collective-permute-start.5 = (bf16[2,4,16,2048]{3,2,1,0:T(8,128)(2,1)S(1)}, bf16[2,4,16,2048]{3,2,1,0:T(8,128)(2,1)S(1)}, u32[]{:S(2)}, u32[]{:S(2)}) collective-permute-start(bf16[2,4,16,2048]{3,2,1,0:T(8,128)(2,1)S(1)} %get-tuple-element.45), channel_id=1, source_target_pairs={{0,68},{8,76},{1,69},{9,77},{2,70},{10,78},{3,71},{11,79},{16,84},... | collective-permute-start | bytes 1572872 | tf_op jit(solution)/shard_map/ppermute | solution.py:39
  21.5 12.2 %collective-permute-start.7 = (bf16[2,4,16,2048]{3,2,1,0:T(8,128)(2,1)S(1)}, bf16[2,4,16,2048]{3,2,1,0:T(8,128)(2,1)S(1)}, u32[]{:S(2)}, u32[]{:S(2)}) collective-permute-start(bf16[2,4,16,2048]{3,2,1,0:T(8,128)(2,1)S(1)} %get-tuple-element.43.refs_0_), channel_id=1, source_target_pairs={{0,3},{8,56},{1,0},{9,57},{2,1},{10,58},{3,2},{11,59},{16,19},{24,... | collective-permute-start | bytes 1572872 | tf_op jit(solution)/shard_map/ppermute | solution.py:39
  24.2 9.6 %collective-permute-start.6 = (bf16[2,4,16,2048]{3,2,1,0:T(8,128)(2,1)S(1)}, bf16[2,4,16,2048]{3,2,1,0:T(8,128)(2,1)S(1)}, u32[]{:S(2)}, u32[]{:S(2)}) collective-permute-start(bf16[2,4,16,2048]{3,2,1,0:T(8,128)(2,1)S(1)} %get-tuple-element.43.refs_0_), channel_id=1, source_target_pairs={{0,1},{8,24},{1,2},{9,25},{2,3},{10,26},{3,0},{11,27},{16,17},{24,... | collective-permute-start | bytes 1572872 | tf_op jit(solution)/shard_map/ppermute | solution.py:39
  33.7 8.0 %copy-start.6 = (f32[2048,256]{1,0:T(8,128)S(1)}, f32[2048,256]{1,0:T(8,128)}, u32[]{:S(2)}) copy-start(f32[2048,256]{1,0:T(8,128)} %components.1) | copy-start | bytes 6291460
  33.9 51.9 %copy-start = (bf16[10,4,16,2048]{3,2,1,0:T(8,128)(2,1)}, bf16[10,4,16,2048]{3,2,1,0:T(8,128)(2,1)S(1)}, u32[]{:S(2)}) copy-start(bf16[10,4,16,2048]{3,2,1,0:T(8,128)(2,1)S(1)} %shard_map.51) | copy-start | bytes 7864324
  33.9 7.8 %collective-permute-start.11 = (bf16[5,2,4,16,2048]{4,3,2,1,0:T(8,128)(2,1)S(1)}, bf16[5,2,4,16,2048]{4,3,2,1,0:T(8,128)(2,1)S(1)}, u32[]{:S(2)}, u32[]{:S(2)}) collective-permute-start(bf16[5,2,4,16,2048]{4,3,2,1,0:T(8,128)(2,1)S(1)} %bitcast.15), channel_id=1, source_target_pairs={{0,8},{8,0},{1,9},{9,1},{2,10},{10,2},{3,11},{11,3},{16,24},{24,16... | collective-permute-start | bytes 7864328 | tf_op jit(solution)/shard_map/ppermute | solution.py:39
  37.3 18.0 %collective-permute-start.9 = (bf16[5,4,16,2048]{3,2,1,0:T(8,128)(2,1)S(1)}, bf16[5,4,16,2048]{3,2,1,0:T(8,128)(2,1)S(1)}, u32[]{:S(2)}, u32[]{:S(2)}) collective-permute-start(bf16[5,4,16,2048]{3,2,1,0:T(8,128)(2,1)S(1)} %get-tuple-element.52), channel_id=1, source_target_pairs={{0,1},{8,24},{1,2},{9,25},{2,3},{10,26},{3,0},{11,27},{16,17},{24,... | collective-permute-start | bytes 3932168 | tf_op jit(solution)/shard_map/ppermute | solution.py:39
  38.6 16.8 %collective-permute-start.10 = (bf16[5,4,16,2048]{3,2,1,0:T(8,128)(2,1)S(1)}, bf16[5,4,16,2048]{3,2,1,0:T(8,128)(2,1)S(1)}, u32[]{:S(2)}, u32[]{:S(2)}) collective-permute-start(bf16[5,4,16,2048]{3,2,1,0:T(8,128)(2,1)S(1)} %get-tuple-element.53), channel_id=1, source_target_pairs={{0,3},{8,56},{1,0},{9,57},{2,1},{10,58},{3,2},{11,59},{16,19},{24,... | collective-permute-start | bytes 3932168 | tf_op jit(solution)/shard_map/ppermute | solution.py:39
  40.1 14.4 %collective-permute-start.8 = (bf16[2,4,16,2048]{3,2,1,0:T(8,128)(2,1)S(1)}, bf16[2,4,16,2048]{3,2,1,0:T(8,128)(2,1)S(1)}, u32[]{:S(2)}, u32[]{:S(2)}) collective-permute-start(bf16[2,4,16,2048]{3,2,1,0:T(8,128)(2,1)S(1)} %get-tuple-element.51), channel_id=1, source_target_pairs={{0,64},{8,72},{1,65},{9,73},{2,66},{10,74},{3,67},{11,75},{16,80},... | collective-permute-start | bytes 1572872 | tf_op jit(solution)/shard_map/ppermute | solution.py:39
  41.7 44.1 %copy-start.3 = (bf16[5,2,4,16,2048]{4,3,2,1,0:T(8,128)(2,1)}, bf16[5,2,4,16,2048]{4,3,2,1,0:T(8,128)(2,1)S(1)}, u32[]{:S(2)}) copy-start(bf16[5,2,4,16,2048]{4,3,2,1,0:T(8,128)(2,1)S(1)} %collective-permute-done.11.recv.refs_2_.refs_3_) | copy-start | bytes 7864324
  55.6 30.2 %copy-start.1 = (bf16[12,4,16,2048]{3,2,1,0:T(8,128)(2,1)}, bf16[12,4,16,2048]{3,2,1,0:T(8,128)(2,1)S(1)}, u32[]{:S(2)}) copy-start(bf16[12,4,16,2048]{3,2,1,0:T(8,128)(2,1)S(1)} %shard_map.54) | copy-start | bytes 9437188
  55.6 6.2 %collective-permute-start.15 = (bf16[6,2,4,16,2048]{4,3,2,1,0:T(8,128)(2,1)S(1)}, bf16[6,2,4,16,2048]{4,3,2,1,0:T(8,128)(2,1)S(1)}, u32[]{:S(2)}, u32[]{:S(2)}) collective-permute-start(bf16[6,2,4,16,2048]{4,3,2,1,0:T(8,128)(2,1)S(1)} %bitcast.20), channel_id=1, source_target_pairs={{0,8},{8,0},{1,9},{9,1},{2,10},{10,2},{3,11},{11,3},{16,24},{24,16... | collective-permute-start | bytes 9437192 | tf_op jit(solution)/shard_map/ppermute | solution.py:39
  56.7 21.1 %collective-permute-start.12 = (bf16[4,4,16,2048]{3,2,1,0:T(8,128)(2,1)S(1)}, bf16[4,4,16,2048]{3,2,1,0:T(8,128)(2,1)S(1)}, u32[]{:S(2)}, u32[]{:S(2)}) collective-permute-start(bf16[4,4,16,2048]{3,2,1,0:T(8,128)(2,1)S(1)} %get-tuple-element.59), channel_id=1, source_target_pairs={{0,1},{8,24},{1,2},{9,25},{2,3},{10,26},{3,0},{11,27},{16,17},{24,... | collective-permute-start | bytes 3145736 | tf_op jit(solution)/shard_map/ppermute | solution.py:39
  57.9 19.9 %collective-permute-start.13 = (bf16[4,4,16,2048]{3,2,1,0:T(8,128)(2,1)S(1)}, bf16[4,4,16,2048]{3,2,1,0:T(8,128)(2,1)S(1)}, u32[]{:S(2)}, u32[]{:S(2)}) collective-permute-start(bf16[4,4,16,2048]{3,2,1,0:T(8,128)(2,1)S(1)} %get-tuple-element.60), channel_id=1, source_target_pairs={{0,3},{8,56},{1,0},{9,57},{2,1},{10,58},{3,2},{11,59},{16,19},{24,... | collective-permute-start | bytes 3145736 | tf_op jit(solution)/shard_map/ppermute | solution.py:39
  59.4 18.3 %collective-permute-start.14 = (bf16[2,4,16,2048]{3,2,1,0:T(8,128)(2,1)S(1)}, bf16[2,4,16,2048]{3,2,1,0:T(8,128)(2,1)S(1)}, u32[]{:S(2)}, u32[]{:S(2)}) collective-permute-start(bf16[2,4,16,2048]{3,2,1,0:T(8,128)(2,1)S(1)} %collective-permute-done.8.refs_2_), channel_id=1, source_target_pairs={{0,2},{8,40},{1,3},{9,41},{2,0},{10,42},{3,1},{11,43},{16,18},{24,... | collective-permute-start | bytes 1572872 | tf_op jit(solution)/shard_map/ppermute | solution.py:39
  61.8 24.0 %copy-start.4 = (bf16[6,2,4,16,2048]{4,3,2,1,0:T(8,128)(2,1)}, bf16[6,2,4,16,2048]{4,3,2,1,0:T(8,128)(2,1)S(1)}, u32[]{:S(2)}) copy-start(bf16[6,2,4,16,2048]{4,3,2,1,0:T(8,128)(2,1)S(1)} %collective-permute-done.15.refs_3_.refs_4_) | copy-start | bytes 9437188
  77.9 7.9 %copy-start.2 = (bf16[10,4,16,2048]{3,2,1,0:T(8,128)(2,1)}, bf16[10,4,16,2048]{3,2,1,0:T(8,128)(2,1)S(1)}, u32[]{:S(2)}) copy-start(bf16[10,4,16,2048]{3,2,1,0:T(8,128)(2,1)S(1)} %shard_map.57) | copy-start | bytes 7864324
  78.0 7.8 %collective-permute-start.16 = (bf16[5,2,4,16,2048]{4,3,2,1,0:T(8,128)(2,1)S(1)}, bf16[5,2,4,16,2048]{4,3,2,1,0:T(8,128)(2,1)S(1)}, u32[]{:S(2)}, u32[]{:S(2)}) collective-permute-start(bf16[5,2,4,16,2048]{4,3,2,1,0:T(8,128)(2,1)S(1)} %bitcast.24), channel_id=1, source_target_pairs={{0,8},{8,0},{1,9},{9,1},{2,10},{10,2},{3,11},{11,3},{16,24},{24,16... | collective-permute-start | bytes 7864328 | tf_op jit(solution)/shard_map/ppermute | solution.py:39
  81.9 3.9 %collective-permute-start.17 = (f32[256,640]{1,0:T(8,128)S(1)}, f32[256,640]{1,0:T(8,128)S(1)}, u32[]{:S(2)}, u32[]{:S(2)}) collective-permute-start(f32[256,640]{1,0:T(8,128)S(1)} %shard_map.58.refs_11_), channel_id=1, source_target_pairs={{0,8},{8,0},{1,9},{9,1},{2,10},{10,2},{3,11},{11,3},{16,24},{24,16... | collective-permute-start | bytes 1966088 | tf_op jit(solution)/shard_map/ppermute | solution.py:39
  85.8 3.6 %copy-start.5 = (bf16[5,2,4,16,2048]{4,3,2,1,0:T(8,128)(2,1)}, bf16[5,2,4,16,2048]{4,3,2,1,0:T(8,128)(2,1)S(1)}, u32[]{:S(2)}) copy-start(bf16[5,2,4,16,2048]{4,3,2,1,0:T(8,128)(2,1)S(1)} %collective-permute-done.16.refs_5_) | copy-start | bytes 7864324
  89.4 19.4 %all-to-all-start = ((f32[8,256,128]{2,1,0:T(8,128)}), f32[8,256,128]{2,1,0:T(8,128)S(1)}, u32[]{:S(2)}, u32[]{:S(2)}) async-start(f32[8,256,128]{2,1,0:T(8,128)} %get-tuple-element.74), calls=%async_computation | async-start | bytes 2097152 | tf_op jit(solution)/shard_map/all_to_all | solution.py:432

commit v5 on v4

--- a/solution.py
+++ b/solution.py
@@ -55,49 +55,70 @@
     return x, y, z, 1 - k
 
 
-def pick_kernel(at, mine, other, *refs):
+def span_of(place, n, half):
+    start = (half * 4 + lax.rem(place[0] + STEPS[n] + 4, 4)) * PANEL
+    return pl.ds(pl.multiple_of(start, PANEL), PANEL)
+
+
+def pick_kernel(place, mine, *refs):
     pieces, sems = refs[:4], refs[4]
     copies = []
     for n, piece in enumerate(pieces):
         for half in range(2):
-            span = pl.ds(pl.multiple_of((half * 4 + at[n]) * PANEL, PANEL), PANEL)
-            copies.append(pltpu.make_async_copy(mine.at[:, span], piece.at[half, 0], sems.at[2 * n + half]))
+            span = span_of(place, n, half)
+            copies.append(pltpu.make_async_copy(mine.at[:, span], piece.at[half], sems.at[2 * n + half]))
             copies[-1].start()
-    for n, piece in enumerate(pieces):
-        for half in range(2):
-            span = pl.ds(pl.multiple_of((half * 4 + at[n]) * PANEL, PANEL), PANEL)
-            piece[half, 1] = other[:, span]
     for copy in copies:
         copy.wait()
 
 
-def pick(at, mine, other):
+def pick(at, mine):
     return pl.pallas_call(
         pick_kernel,
-        out_shape=[jax.ShapeDtypeStruct((2, 2, LOCAL, PANEL), BF16)] * 4,
-        in_specs=[IN_SMEM, ANY, IN_VMEM],
+        out_shape=[jax.ShapeDtypeStruct((2, LOCAL, PANEL), BF16)] * 4,
+        in_specs=[IN_SMEM, ANY],
         out_specs=[IN_VMEM] * 4,
         scratch_shapes=[pltpu.SemaphoreType.DMA((8,))],
         compiler_params=SMALL,
-    )(at, mine, other)
-
-
-def group_kernel(at, *refs):
+    )(at, mine)
+
+
+def join_kernel(place, other, *refs):
+    for n, (mine, piece) in enumerate(zip(refs[:4], refs[4:])):
+        for half in range(2):
+            span = span_of(place, n, half)
+            piece[half, 0] = mine[half]
+            piece[half, 1] = other[:, span]
+
+
+def join(at, other, mine):
+    return pl.pallas_call(
+        join_kernel,
+        out_shape=[jax.ShapeDtypeStruct((2, 2, LOCAL, PANEL), BF16)] * 4,
+        in_specs=[IN_SMEM] + [IN_VMEM] * 5,
+        out_specs=[IN_VMEM] * 4,
+        compiler_params=SMALL,
+    )(at, other, *mine)
+
+
+def group_kernel(core, own_half, *refs):
     pieces, groups = refs[:4], refs[4:]
-    for n, group in enumerate(groups):
+    half = own_half[0]
+    crossed = half + core[0] - 2 * half * core[0]
+    for group, choice in zip(groups, (half, crossed, 1 - crossed, 1 - half)):
         for i, piece in enumerate(pieces):
             for source in range(2):
-                group[source, i] = piece[at[n], source]
-
-
-def group(at, pieces):
+                group[source, i] = piece[choice, source]
+
+
+def group(core, own_half, pieces):
     return pl.pallas_call(
         group_kernel,
         out_shape=[jax.ShapeDtypeStruct((2, 4, LOCAL, PANEL), BF16)] * 4,
-        in_specs=[IN_SMEM] + [IN_VMEM] * 4,
+        in_specs=[IN_SMEM] * 2 + [IN_VMEM] * 4,
         out_specs=[IN_VMEM] * 4,
         compiler_params=SMALL,
-    )(at, *pieces)
+    )(core, own_half, *pieces)
 
 
 def pack_kernel(plan, *refs):
@@ -284,9 +305,9 @@
     )(own, comps)
 
 
-def last_kernel(at, *refs):
+def last_kernel(at, column, *refs):
     own, recv, early, origin, soon, total_in, rs_in, late_own, late_recv = refs[:3], refs[3:6], *refs[6:13]
-    parts, means, rows, left = refs[13:]
+    parts, means, means_part, rows, left = refs[13:]
 
     def put(block, labels):
         for i, (m, step) in enumerate(labels):
@@ -310,21 +331,26 @@
     for c in range(8):
         parts[c] = total[:, c * 128 : (c + 1) * 128]
     means[...] = row_sum * (1.0 / SCANS)
-
-
-def last_part(at, own, recv, state):
+    means_part[...] = means[:, pl.ds(pl.multiple_of(column[0] * 128, 128), 128)]
+
+
+def last_part(at, column, own, recv, state):
     return pl.pallas_call(
         last_kernel,
-        out_shape=[jax.ShapeDtypeStruct((8, COMPS, 128), F32), jax.ShapeDtypeStruct((1, HALF), F32)],
-        in_specs=[IN_SMEM] + [IN_VMEM] * 13,
-        out_specs=[IN_VMEM] * 2,
+        out_shape=[
+            jax.ShapeDtypeStruct((8, COMPS, 128), F32),
+            jax.ShapeDtypeStruct((1, HALF), F32),
+            jax.ShapeDtypeStruct((1, 128), F32),
+        ],
+        in_specs=[IN_SMEM] * 2 + [IN_VMEM] * 13,
+        out_specs=[IN_VMEM] * 3,
         scratch_shapes=[
             pltpu.VMEM((3, 4, 2, 4, LOCAL, HALF), BF16),
             pltpu.VMEM((2 * COMPS + 16, 12 * WIDTH), BF16),
         ],
         compiler_params=MIDDLE,
         cost_estimate=pl.CostEstimate(flops=4 << 30, bytes_accessed=4 << 20, transcendentals=0),
-    )(at, *own, *recv, *state)
+    )(at, column, *own, *recv, *state)
 
 
 def gram_kernel(at, *refs):
@@ -387,6 +413,10 @@
     )(at, *[pltpu.with_memory_space_constraint(piece, pltpu.HBM) for piece in own + recv], row_means)
 
 
+def scalar(value):
+    return jnp.reshape(value, (1,)).astype(jnp.int32)
+
+
 def on_device(patterns, components):
     row = lax.axis_index("brow")
     col = lax.axis_index("bcol")
@@ -394,15 +424,14 @@
     z, xl = col % 4, col // 4
     first = k == 0
     same = jnp.where(first, y, z)
-    at = jnp.stack([(same + d) % 4 for d in STEPS]).astype(jnp.int32)
-    sends = pick(at, patterns, permute(patterns, swap))
-    got = [sends[0]] + [permute(sends[n], spread(STEPS[n])) for n in range(1, 4)]
+    at = scalar(same)
+    mine = pick(at, pltpu.with_memory_space_constraint(patterns, pltpu.HBM))
+    sends = join(at, permute(patterns, swap), mine)
+    got = {n: permute(sends[n], spread(STEPS[n])) for n in (3, 1, 2)}
+    got = [sends[0]] + [got[n] for n in range(1, 4)]
     own_half = jnp.where(first, xh, xl)
-    at = jnp.stack(
-        [own_half, jnp.where(first, own_half, 1 - own_half), jnp.where(first, 1 - own_half, own_half), 1 - own_half]
-    ).astype(jnp.int32)
-    group_own, to_1, to_2, to_3 = group(at, got)
-    at = jnp.reshape(k, (1,)).astype(jnp.int32)
+    group_own, to_1, to_2, to_3 = group(scalar(k), scalar(own_half), got)
+    at = scalar(k)
     near = [permute(to_1, across(1)), permute(to_3, across(3))]
     ring_own = [permute(group_own, around(d)) for d in STEPS[1:3]]
     near, ring_own, to_2 = lax.optimization_barrier((near, ring_own, to_2))
@@ -415,8 +444,8 @@
     *early, comps = early_part(at, own_early, recv_early, components)
     far, ring, early = lax.optimization_barrier((far, ring, early))
     late = pack((((0, 0, 2), (2, 0, 2)), ((1, 2, 4), (2, 0, 2))), *ring, far)
-    late = [permute(late[n], around(STEPS[n + 1])) for n in range(2)]
-    late.append(permute(far, around(STEPS[3])))
+    opposite = permute(far, around(STEPS[3]))
+    late = [permute(late[n], around(STEPS[n + 1])) for n in range(2)] + [opposite]
     (own_soon,) = pack((((0, 4, 5), (1, 4, 5), (0, 0, 4), (1, 0, 4), (2, 0, 2)),), *ring, far)
     own_soon = own_soon.reshape((6, 2, 4, LOCAL, PANEL))
     recv_soon = permute(own_soon, swap)
@@ -428,12 +457,11 @@
     own = [own_early, own_soon, own_late]
     recv = [recv_early, recv_soon, recv_late]
     scores = late_part(own_late, comps)
-    parts, row_means = last_part(at, own, recv, (*early, *soon, scores, permute(scores, swap)))
+    parts, row_means, means_part = last_part(at, scalar(col), own, recv, (*early, *soon, scores, permute(scores, swap)))
     parts = lax.all_to_all(parts, "bcol", 0, 0, tiled=True)
     covariance = gram(at, own, recv, row_means)
     projected = jnp.sum(parts, axis=0).T
-    means_part = lax.dynamic_slice_in_dim(row_means[0], col * 128, 128, 0)
-    return covariance, projected, means_part
+    return covariance, projected, means_part[0]
 
 
 def solution(mesh):

time: 110 us -> 107 us (0.973)
  local copies, waits for them, and re-layouts: 2.34 us -> 0.78 us
  transfers between devices with their start and end apart: 19 -> 19, of which waited for: 12 -> 12; matrix products, arithmetic and copies ran while one was open for 1% -> 0% of each run, Pallas kernels for 21% -> 23%
where the time goes in v5:
time: 107 us
  waiting for transfers between devices  47.5 us (44%)
  starting transfers between devices  28.9 us (27%)
  Pallas kernels  28.6 us (27%)
    ppermute x18, waiting for transfers between devices, permute(): return lax.ppermute(value, AXES, pairs)  47.5 us
    ppermute x18, starting transfers between devices, permute(): return lax.ppermute(value, AXES, pairs)  25.3 us
    pallas_call x1, Pallas kernels, gram(): pl.pallas_call(gram_kernel, out_shape=jax.ShapeDtypeStruct((HALF, PANEL),...  15.3 us
    pallas_call x1, Pallas kernels, soon_part(): pl.pallas_call(soon_kernel, out_shape=[jax.ShapeDtypeStruct((COMPS, len(S...  3.58 us
    pallas_call x1, Pallas kernels, last_part(): pl.pallas_call(last_kernel, out_shape=[jax.ShapeDtypeStruct((8, COMPS, 12...  3.57 us
    all_to_all x1, starting transfers between devices, on_device(): parts = lax.all_to_all(parts, 'bcol', 0, 0, tiled=True)  3.56 us
    pallas_call x1, Pallas kernels, early_part(): pl.pallas_call(early_kernel, out_shape=[jax.ShapeDtypeStruct((COMPS, len(...  2.31 us
  transfers between devices with their start and end apart: 19, of which 12 were waited for; matrix products, arithmetic and copies ran while one was open for 0% of the time, Pallas kernels for 23%

profile of v5, /device:TPU:1, one launch (start us, length us, event | category | flops | bytes accessed | tf_op | source)
XLA Modules:
  0.0 106.6 jit_solution(2864566497208150438)
XLA Ops:
  0.6 1.5 %collective-permute-start = (bf16[16,16384]{1,0:T(8,128)(2,1)}, bf16[16,16384]{1,0:T(8,128)(2,1)S(1)}, u32[]{:S(2)}, u32[]{:S(2)}) collective-permute-start(bf16[16,16384]{1,0:T(8,128)(2,1)} %mine.1), channel_id=1, source_target_pairs={{0,8},{8,0},{1,9},{9,1},{2,10},{10,2},{3,11},{11,3},{16,24},{24,16... | collective-permute-start | bytes 1572872 | tf_op jit(solution)/shard_map/ppermute | solution.py:39
  2.1 1.1 %shard_map.49 = (bf16[2,16,2048]{2,1,0:T(8,128)(2,1)S(1)}, bf16[2,16,2048]{2,1,0:T(8,128)(2,1)S(1)}, bf16[2,16,2048]{2,1,0:T(8,128)(2,1)S(1)}, bf16[2,16,2048]{2,1,0:T(8,128)(2,1)S(1)}) custom-call(s32[1]{0:T(128)} %bitcast.2.place, bf16[16,16384]{1,0:T(8,128)(2,1)} %mine.1), custom_call_target="tpu_custom_call" | custom-call | tf_op jit(solution)/shard_map/pallas_call | solution.py:76
  4.0 1.8 %collective-permute-start.1 = (bf16[2,2,16,2048]{3,2,1,0:T(8,128)(2,1)S(1)}, bf16[2,2,16,2048]{3,2,1,0:T(8,128)(2,1)S(1)}, u32[]{:S(2)}, u32[]{:S(2)}) collective-permute-start(bf16[2,2,16,2048]{3,2,1,0:T(8,128)(2,1)S(1)} %get-tuple-element.49), channel_id=1, source_target_pairs={{0,16},{8,9},{1,17},{9,10},{2,18},{10,11},{3,19},{11,8},{16,32},{2... | collective-permute-start | bytes 786440 | tf_op jit(solution)/shard_map/ppermute | solution.py:39
  5.7 2.2 %collective-permute-start.2 = (bf16[2,2,16,2048]{3,2,1,0:T(8,128)(2,1)S(1)}, bf16[2,2,16,2048]{3,2,1,0:T(8,128)(2,1)S(1)}, u32[]{:S(2)}, u32[]{:S(2)}) collective-permute-start(bf16[2,2,16,2048]{3,2,1,0:T(8,128)(2,1)S(1)} %get-tuple-element.50), channel_id=1, source_target_pairs={{0,48},{8,11},{1,49},{9,8},{2,50},{10,9},{3,51},{11,10},{16,0},{24... | collective-permute-start | bytes 786440 | tf_op jit(solution)/shard_map/ppermute | solution.py:39
  7.9 1.2 %collective-permute-start.3 = (bf16[2,2,16,2048]{3,2,1,0:T(8,128)(2,1)S(1)}, bf16[2,2,16,2048]{3,2,1,0:T(8,128)(2,1)S(1)}, u32[]{:S(2)}, u32[]{:S(2)}) collective-permute-start(bf16[2,2,16,2048]{3,2,1,0:T(8,128)(2,1)S(1)} %get-tuple-element.51), channel_id=1, source_target_pairs={{0,32},{8,10},{1,33},{9,11},{2,34},{10,8},{3,35},{11,9},{16,48},{2... | collective-permute-start | bytes 786440 | tf_op jit(solution)/shard_map/ppermute | solution.py:39
  9.2 2.5 %collective-permute-done.1.refs_1_ = bf16[2,2,16,2048]{3,2,1,0:T(8,128)(2,1)S(1)} collective-permute-done((bf16[2,2,16,2048]{3,2,1,0:T(8,128)(2,1)S(1)}, bf16[2,2,16,2048]{3,2,1,0:T(8,128)(2,1)S(1)}, u32[]{:S(2)}, u32[]{:S(2)}) %collective-permute-start.1) | collective-permute-done | bytes 262176 | tf_op jit(solution)/shard_map/ppermute | solution.py:39
  11.6 2.4 %collective-permute-done.2.refs_2_ = bf16[2,2,16,2048]{3,2,1,0:T(8,128)(2,1)S(1)} collective-permute-done((bf16[2,2,16,2048]{3,2,1,0:T(8,128)(2,1)S(1)}, bf16[2,2,16,2048]{3,2,1,0:T(8,128)(2,1)S(1)}, u32[]{:S(2)}, u32[]{:S(2)}) %collective-permute-start.2) | collective-permute-done | bytes 262176 | tf_op jit(solution)/shard_map/ppermute | solution.py:39
  14.1 1.6 %collective-permute-done.3.refs_3_ = bf16[2,2,16,2048]{3,2,1,0:T(8,128)(2,1)S(1)} collective-permute-done((bf16[2,2,16,2048]{3,2,1,0:T(8,128)(2,1)S(1)}, bf16[2,2,16,2048]{3,2,1,0:T(8,128)(2,1)S(1)}, u32[]{:S(2)}, u32[]{:S(2)}) %collective-permute-start.3) | collective-permute-done | bytes 262176 | tf_op jit(solution)/shard_map/ppermute | solution.py:39
  15.9 1.3 %collective-permute-start.4 = (bf16[2,4,16,2048]{3,2,1,0:T(8,128)(2,1)S(1)}, bf16[2,4,16,2048]{3,2,1,0:T(8,128)(2,1)S(1)}, u32[]{:S(2)}, u32[]{:S(2)}) collective-permute-start(bf16[2,4,16,2048]{3,2,1,0:T(8,128)(2,1)S(1)} %get-tuple-element.53), channel_id=1, source_target_pairs={{0,4},{8,12},{1,5},{9,13},{2,6},{10,14},{3,7},{11,15},{16,20},{24,... | collective-permute-start | bytes 1572872 | tf_op jit(solution)/shard_map/ppermute | solution.py:39
  17.1 1.8 %collective-permute-start.5 = (bf16[2,4,16,2048]{3,2,1,0:T(8,128)(2,1)S(1)}, bf16[2,4,16,2048]{3,2,1,0:T(8,128)(2,1)S(1)}, u32[]{:S(2)}, u32[]{:S(2)}) collective-permute-start(bf16[2,4,16,2048]{3,2,1,0:T(8,128)(2,1)S(1)} %get-tuple-element.54), channel_id=1, source_target_pairs={{0,68},{8,76},{1,69},{9,77},{2,70},{10,78},{3,71},{11,79},{16,84},... | collective-permute-start | bytes 1572872 | tf_op jit(solution)/shard_map/ppermute | solution.py:39
  19.0 2.6 %collective-permute-start.7 = (bf16[2,4,16,2048]{3,2,1,0:T(8,128)(2,1)S(1)}, bf16[2,4,16,2048]{3,2,1,0:T(8,128)(2,1)S(1)}, u32[]{:S(2)}, u32[]{:S(2)}) collective-permute-start(bf16[2,4,16,2048]{3,2,1,0:T(8,128)(2,1)S(1)} %get-tuple-element.52.refs_0_), channel_id=1, source_target_pairs={{0,3},{8,56},{1,0},{9,57},{2,1},{10,58},{3,2},{11,59},{16,19},{24,... | collective-permute-start | bytes 1572872 | tf_op jit(solution)/shard_map/ppermute | solution.py:39
  21.6 7.5 %collective-permute-done.4.refs_3_.refs_0_ = bf16[2,4,16,2048]{3,2,1,0:T(8,128)(2,1)S(1)} collective-permute-done((bf16[2,4,16,2048]{3,2,1,0:T(8,128)(2,1)S(1)}, bf16[2,4,16,2048]{3,2,1,0:T(8,128)(2,1)S(1)}, u32[]{:S(2)}, u32[]{:S(2)}) %collective-permute-start.4) | collective-permute-done | bytes 524320 | tf_op jit(solution)/shard_map/ppermute | solution.py:39
  29.0 2.1 %collective-permute-done.5.refs_4_.refs_1_ = bf16[2,4,16,2048]{3,2,1,0:T(8,128)(2,1)S(1)} collective-permute-done((bf16[2,4,16,2048]{3,2,1,0:T(8,128)(2,1)S(1)}, bf16[2,4,16,2048]{3,2,1,0:T(8,128)(2,1)S(1)}, u32[]{:S(2)}, u32[]{:S(2)}) %collective-permute-start.5) | collective-permute-done | bytes 524320 | tf_op jit(solution)/shard_map/ppermute | solution.py:39
  31.3 3.3 %collective-permute-start.11 = (bf16[5,2,4,16,2048]{4,3,2,1,0:T(8,128)(2,1)S(1)}, bf16[5,2,4,16,2048]{4,3,2,1,0:T(8,128)(2,1)S(1)}, u32[]{:S(2)}, u32[]{:S(2)}) collective-permute-start(bf16[5,2,4,16,2048]{4,3,2,1,0:T(8,128)(2,1)S(1)} %bitcast.9), channel_id=1, source_target_pairs={{0,8},{8,0},{1,9},{9,1},{2,10},{10,2},{3,11},{11,3},{16,24},{24,16... | collective-permute-start | bytes 7864328 | tf_op jit(solution)/shard_map/ppermute | solution.py:39
  34.8 1.2 %collective-permute-start.9 = (bf16[5,4,16,2048]{3,2,1,0:T(8,128)(2,1)S(1)}, bf16[5,4,16,2048]{3,2,1,0:T(8,128)(2,1)S(1)}, u32[]{:S(2)}, u32[]{:S(2)}) collective-permute-start(bf16[5,4,16,2048]{3,2,1,0:T(8,128)(2,1)S(1)} %get-tuple-element.61), channel_id=1, source_target_pairs={{0,1},{8,24},{1,2},{9,25},{2,3},{10,26},{3,0},{11,27},{16,17},{24,... | collective-permute-start | bytes 3932168 | tf_op jit(solution)/shard_map/ppermute | solution.py:39
  36.0 1.5 %collective-permute-start.10 = (bf16[5,4,16,2048]{3,2,1,0:T(8,128)(2,1)S(1)}, bf16[5,4,16,2048]{3,2,1,0:T(8,128)(2,1)S(1)}, u32[]{:S(2)}, u32[]{:S(2)}) collective-permute-start(bf16[5,4,16,2048]{3,2,1,0:T(8,128)(2,1)S(1)} %get-tuple-element.62), channel_id=1, source_target_pairs={{0,3},{8,56},{1,0},{9,57},{2,1},{10,58},{3,2},{11,59},{16,19},{24,... | collective-permute-start | bytes 3932168 | tf_op jit(solution)/shard_map/ppermute | solution.py:39
  37.9 1.3 %collective-permute-done.11.recv.refs_2_.refs_3_ = bf16[5,2,4,16,2048]{4,3,2,1,0:T(8,128)(2,1)S(1)} collective-permute-done((bf16[5,2,4,16,2048]{4,3,2,1,0:T(8,128)(2,1)S(1)}, bf16[5,2,4,16,2048]{4,3,2,1,0:T(8,128)(2,1)S(1)}, u32[]{:S(2)}, u32[]{:S(2)}) %collective-permute-start.11) | collective-permute-done | bytes 2621472 | tf_op jit(solution)/shard_map/ppermute | solution.py:39
  39.2 2.3 %shard_map.54 = (f32[256,640]{1,0:T(8,128)S(1)}, f32[256,128]{1,0:T(8,128)S(1)}, bf16[2048,512]{1,0:T(8,128)(2,1)S(1)}) custom-call(s32[1]{0:T(128)} %bitcast.core.at, bf16[5,2,4,16,2048]{4,3,2,1,0:T(8,128)(2,1)S(1)} %bitcast.10, bf16[5,2,4,16,2048]{4,3,2,1,0:T(8,128)(2,1)S(1)} %collective-permute-done.11.recv.refs_2_.refs_3_, f32[2048,256]{1,0:T(8,128)S(1)} %copy-done.6), custom_call_target="tpu_custom_call" | custom-call | flops 1073741824 | bytes 1048576 | tf_op jit(solution)/shard_map/pallas_call | solution.py:231
  41.5 10.5 %collective-permute-done.8.refs_2_ = bf16[2,4,16,2048]{3,2,1,0:T(8,128)(2,1)S(1)} collective-permute-done((bf16[2,4,16,2048]{3,2,1,0:T(8,128)(2,1)S(1)}, bf16[2,4,16,2048]{3,2,1,0:T(8,128)(2,1)S(1)}, u32[]{:S(2)}, u32[]{:S(2)}) %collective-permute-start.8) | collective-permute-done | bytes 524320 | tf_op jit(solution)/shard_map/ppermute | solution.py:39
  51.9 0.9 collective-permute-done.9.refs_0_
  53.0 1.0 collective-permute-start.15
  54.1 1.2 %collective-permute-start.12 = (bf16[4,4,16,2048]{3,2,1,0:T(8,128)(2,1)S(1)}, bf16[4,4,16,2048]{3,2,1,0:T(8,128)(2,1)S(1)}, u32[]{:S(2)}, u32[]{:S(2)}) collective-permute-start(bf16[4,4,16,2048]{3,2,1,0:T(8,128)(2,1)S(1)} %get-tuple-element.68), channel_id=1, source_target_pairs={{0,1},{8,24},{1,2},{9,25},{2,3},{10,26},{3,0},{11,27},{16,17},{24,... | collective-permute-start | bytes 3145736 | tf_op jit(solution)/shard_map/ppermute | solution.py:39
  55.3 1.5 %collective-permute-start.13 = (bf16[4,4,16,2048]{3,2,1,0:T(8,128)(2,1)S(1)}, bf16[4,4,16,2048]{3,2,1,0:T(8,128)(2,1)S(1)}, u32[]{:S(2)}, u32[]{:S(2)}) collective-permute-start(bf16[4,4,16,2048]{3,2,1,0:T(8,128)(2,1)S(1)} %get-tuple-element.69), channel_id=1, source_target_pairs={{0,3},{8,56},{1,0},{9,57},{2,1},{10,58},{3,2},{11,59},{16,19},{24,... | collective-permute-start | bytes 3145736 | tf_op jit(solution)/shard_map/ppermute | solution.py:39
  57.2 2.1 %collective-permute-done.15.refs_3_.refs_4_ = bf16[6,2,4,16,2048]{4,3,2,1,0:T(8,128)(2,1)S(1)} collective-permute-done((bf16[6,2,4,16,2048]{4,3,2,1,0:T(8,128)(2,1)S(1)}, bf16[6,2,4,16,2048]{4,3,2,1,0:T(8,128)(2,1)S(1)}, u32[]{:S(2)}, u32[]{:S(2)}) %collective-permute-start.15) | collective-permute-done | bytes 3145760 | tf_op jit(solution)/shard_map/ppermute | solution.py:39
  59.3 3.6 %shard_map.57 = (f32[256,768]{1,0:T(8,128)S(1)}, f32[256,1024]{1,0:T(8,128)S(1)}, f32[1,1024]{1,0:T(1,128)S(1)}) custom-call(s32[1]{0:T(128)} %bitcast.core.at, bf16[5,2,4,16,2048]{4,3,2,1,0:T(8,128)(2,1)S(1)} %bitcast.11, bf16[6,2,4,16,2048]{4,3,2,1,0:T(8,128)(2,1)S(1)} %bitcast.15, ...), custom_call_target="tpu_custom_call" | custom-call | flops 2147483648 | bytes 1048576 | tf_op jit(solution)/shard_map/pallas_call | solution.py:275
  62.9 12.3 %collective-permute-done.14.refs_2_ = bf16[2,4,16,2048]{3,2,1,0:T(8,128)(2,1)S(1)} collective-permute-done((bf16[2,4,16,2048]{3,2,1,0:T(8,128)(2,1)S(1)}, bf16[2,4,16,2048]{3,2,1,0:T(8,128)(2,1)S(1)}, u32[]{:S(2)}, u32[]{:S(2)}) %collective-permute-start.14) | collective-permute-done | bytes 524320 | tf_op jit(solution)/shard_map/ppermute | solution.py:39
  75.4 2.4 %collective-permute-start.16 = (bf16[5,2,4,16,2048]{4,3,2,1,0:T(8,128)(2,1)S(1)}, bf16[5,2,4,16,2048]{4,3,2,1,0:T(8,128)(2,1)S(1)}, u32[]{:S(2)}, u32[]{:S(2)}) collective-permute-start(bf16[5,2,4,16,2048]{4,3,2,1,0:T(8,128)(2,1)S(1)} %bitcast.18), channel_id=1, source_target_pairs={{0,8},{8,0},{1,9},{9,1},{2,10},{10,2},{3,11},{11,3},{16,24},{24,16... | collective-permute-start | bytes 7864328 | tf_op jit(solution)/shard_map/ppermute | solution.py:39
  77.8 1.6 %shard_map.59.refs_11_ = f32[256,640]{1,0:T(8,128)S(1)} custom-call(bf16[5,2,4,16,2048]{4,3,2,1,0:T(8,128)(2,1)S(1)} %bitcast.19, bf16[2048,512]{1,0:T(8,128)(2,1)S(1)} %get-tuple-element.70.refs_4_.comps), custom_call_target="tpu_custom_call" | custom-call | flops 1073741824 | bytes 1048576 | tf_op jit(solution)/shard_map/pallas_call | solution.py:298
  79.4 3.8 %collective-permute-done.17.refs_12_ = f32[256,640]{1,0:T(8,128)S(1)} collective-permute-done((f32[256,640]{1,0:T(8,128)S(1)}, f32[256,640]{1,0:T(8,128)S(1)}, u32[]{:S(2)}, u32[]{:S(2)}) %collective-permute-start.17) | collective-permute-done | bytes 655392 | tf_op jit(solution)/shard_map/ppermute | solution.py:39
  83.3 3.6 %shard_map.60 = (f32[8,256,128]{2,1,0:T(8,128)}, f32[1,1024]{1,0:T(1,128)S(1)}, f32[1,128]{1,0:T(1,128)}) custom-call(s32[1]{0:T(128)} %bitcast.core.at, s32[1]{0:T(128)} %bitcast.6.column, bf16[5,2,4,16,2048]{4,3,2,1,0:T(8,128)(2,1)S(1)} %bitcast.12, bf16[6,2,4,16,2048]{4,3,2,1,0:T(8,128)(2,1)S(1)} %bitcast.16, bf16[5,2,4,16,2048]{4,3,2,1,0:T(8,128)(2,1)S(1)} %bitcast.20, ...), custom_call_target="tpu_custom_call" | custom-call | flops 4294967296 | bytes 4194304 | tf_op jit(solution)/shard_map/pallas_call | solution.py:338
  86.8 3.6 %all-to-all-start = ((f32[8,256,128]{2,1,0:T(8,128)}), f32[8,256,128]{2,1,0:T(8,128)S(1)}, u32[]{:S(2)}, u32[]{:S(2)}) async-start(f32[8,256,128]{2,1,0:T(8,128)} %get-tuple-element.83), calls=%async_computation | async-start | bytes 2097152 | tf_op jit(solution)/shard_map/all_to_all | solution.py:461
  90.4 15.3 %shard_map.61 = f32[1024,2048]{1,0:T(8,128)} custom-call(s32[1]{0:T(128)} %bitcast.core.at, bf16[5,2,4,16,2048]{4,3,2,1,0:T(8,128)(2,1)} %bitcast.13, bf16[6,2,4,16,2048]{4,3,2,1,0:T(8,128)(2,1)} %bitcast.17, bf16[5,2,4,16,2048]{4,3,2,1,0:T(8,128)(2,1)} %bitcast.21, bf16[5,2,4,16,2048]{4,3,2,1,0:T(8,128)(2,1)} %copy-done.3, ...), custom_call_target="tpu_custom_call" | custom-call | flops 8589934592 | bytes 20971520 | tf_op jit(solution)/shard_map/pallas_call | solution.py:398
  (35 shorter events, 3.3 us)
Async XLA Ops:
  0.6 3.2 %collective-permute-start = (bf16[16,16384]{1,0:T(8,128)(2,1)}, bf16[16,16384]{1,0:T(8,128)(2,1)S(1)}, u32[]{:S(2)}, u32[]{:S(2)}) collective-permute-start(bf16[16,16384]{1,0:T(8,128)(2,1)} %mine.1), channel_id=1, source_target_pairs={{0,8},{8,0},{1,9},{9,1},{2,10},{10,2},{3,11},{11,3},{16,24},{24,16... | collective-permute-start | bytes 1572872 | tf_op jit(solution)/shard_map/ppermute | solution.py:39
  4.0 7.7 %collective-permute-start.1 = (bf16[2,2,16,2048]{3,2,1,0:T(8,128)(2,1)S(1)}, bf16[2,2,16,2048]{3,2,1,0:T(8,128)(2,1)S(1)}, u32[]{:S(2)}, u32[]{:S(2)}) collective-permute-start(bf16[2,2,16,2048]{3,2,1,0:T(8,128)(2,1)S(1)} %get-tuple-element.49), channel_id=1, source_target_pairs={{0,16},{8,9},{1,17},{9,10},{2,18},{10,11},{3,19},{11,8},{16,32},{2... | collective-permute-start | bytes 786440 | tf_op jit(solution)/shard_map/ppermute | solution.py:39
  5.7 8.3 %collective-permute-start.2 = (bf16[2,2,16,2048]{3,2,1,0:T(8,128)(2,1)S(1)}, bf16[2,2,16,2048]{3,2,1,0:T(8,128)(2,1)S(1)}, u32[]{:S(2)}, u32[]{:S(2)}) collective-permute-start(bf16[2,2,16,2048]{3,2,1,0:T(8,128)(2,1)S(1)} %get-tuple-element.50), channel_id=1, source_target_pairs={{0,48},{8,11},{1,49},{9,8},{2,50},{10,9},{3,51},{11,10},{16,0},{24... | collective-permute-start | bytes 786440 | tf_op jit(solution)/shard_map/ppermute | solution.py:39
  7.9 7.8 %collective-permute-start.3 = (bf16[2,2,16,2048]{3,2,1,0:T(8,128)(2,1)S(1)}, bf16[2,2,16,2048]{3,2,1,0:T(8,128)(2,1)S(1)}, u32[]{:S(2)}, u32[]{:S(2)}) collective-permute-start(bf16[2,2,16,2048]{3,2,1,0:T(8,128)(2,1)S(1)} %get-tuple-element.51), channel_id=1, source_target_pairs={{0,32},{8,10},{1,33},{9,11},{2,34},{10,8},{3,35},{11,9},{16,48},{2... | collective-permute-start | bytes 786440 | tf_op jit(solution)/shard_map/ppermute | solution.py:39
  15.9 13.2 %collective-permute-start.4 = (bf16[2,4,16,2048]{3,2,1,0:T(8,128)(2,1)S(1)}, bf16[2,4,16,2048]{3,2,1,0:T(8,128)(2,1)S(1)}, u32[]{:S(2)}, u32[]{:S(2)}) collective-permute-start(bf16[2,4,16,2048]{3,2,1,0:T(8,128)(2,1)S(1)} %get-tuple-element.53), channel_id=1, source_target_pairs={{0,4},{8,12},{1,5},{9,13},{2,6},{10,14},{3,7},{11,15},{16,20},{24,... | collective-permute-start | bytes 1572872 | tf_op jit(solution)/shard_map/ppermute | solution.py:39
  17.1 14.0 %collective-permute-start.5 = (bf16[2,4,16,2048]{3,2,1,0:T(8,128)(2,1)S(1)}, bf16[2,4,16,2048]{3,2,1,0:T(8,128)(2,1)S(1)}, u32[]{:S(2)}, u32[]{:S(2)}) collective-permute-start(bf16[2,4,16,2048]{3,2,1,0:T(8,128)(2,1)S(1)} %get-tuple-element.54), channel_id=1, source_target_pairs={{0,68},{8,76},{1,69},{9,77},{2,70},{10,78},{3,71},{11,79},{16,84},... | collective-permute-start | bytes 1572872 | tf_op jit(solution)/shard_map/ppermute | solution.py:39
  19.0 12.2 %collective-permute-start.7 = (bf16[2,4,16,2048]{3,2,1,0:T(8,128)(2,1)S(1)}, bf16[2,4,16,2048]{3,2,1,0:T(8,128)(2,1)S(1)}, u32[]{:S(2)}, u32[]{:S(2)}) collective-permute-start(bf16[2,4,16,2048]{3,2,1,0:T(8,128)(2,1)S(1)} %get-tuple-element.52.refs_0_), channel_id=1, source_target_pairs={{0,3},{8,56},{1,0},{9,57},{2,1},{10,58},{3,2},{11,59},{16,19},{24,... | collective-permute-start | bytes 1572872 | tf_op jit(solution)/shard_map/ppermute | solution.py:39
  21.6 9.6 %collective-permute-start.6 = (bf16[2,4,16,2048]{3,2,1,0:T(8,128)(2,1)S(1)}, bf16[2,4,16,2048]{3,2,1,0:T(8,128)(2,1)S(1)}, u32[]{:S(2)}, u32[]{:S(2)}) collective-permute-start(bf16[2,4,16,2048]{3,2,1,0:T(8,128)(2,1)S(1)} %get-tuple-element.52.refs_0_), channel_id=1, source_target_pairs={{0,1},{8,24},{1,2},{9,25},{2,3},{10,26},{3,0},{11,27},{16,17},{24,... | collective-permute-start | bytes 1572872 | tf_op jit(solution)/shard_map/ppermute | solution.py:39
  31.2 8.0 %copy-start.6 = (f32[2048,256]{1,0:T(8,128)S(1)}, f32[2048,256]{1,0:T(8,128)}, u32[]{:S(2)}) copy-start(f32[2048,256]{1,0:T(8,128)} %components.1) | copy-start | bytes 6291460
  31.3 51.9 %copy-start = (bf16[10,4,16,2048]{3,2,1,0:T(8,128)(2,1)}, bf16[10,4,16,2048]{3,2,1,0:T(8,128)(2,1)S(1)}, u32[]{:S(2)}) copy-start(bf16[10,4,16,2048]{3,2,1,0:T(8,128)(2,1)S(1)} %shard_map.52) | copy-start | bytes 7864324
  31.3 7.8 %collective-permute-start.11 = (bf16[5,2,4,16,2048]{4,3,2,1,0:T(8,128)(2,1)S(1)}, bf16[5,2,4,16,2048]{4,3,2,1,0:T(8,128)(2,1)S(1)}, u32[]{:S(2)}, u32[]{:S(2)}) collective-permute-start(bf16[5,2,4,16,2048]{4,3,2,1,0:T(8,128)(2,1)S(1)} %bitcast.9), channel_id=1, source_target_pairs={{0,8},{8,0},{1,9},{9,1},{2,10},{10,2},{3,11},{11,3},{16,24},{24,16... | collective-permute-start | bytes 7864328 | tf_op jit(solution)/shard_map/ppermute | solution.py:39
  34.8 18.0 %collective-permute-start.9 = (bf16[5,4,16,2048]{3,2,1,0:T(8,128)(2,1)S(1)}, bf16[5,4,16,2048]{3,2,1,0:T(8,128)(2,1)S(1)}, u32[]{:S(2)}, u32[]{:S(2)}) collective-permute-start(bf16[5,4,16,2048]{3,2,1,0:T(8,128)(2,1)S(1)} %get-tuple-element.61), channel_id=1, source_target_pairs={{0,1},{8,24},{1,2},{9,25},{2,3},{10,26},{3,0},{11,27},{16,17},{24,... | collective-permute-start | bytes 3932168 | tf_op jit(solution)/shard_map/ppermute | solution.py:39
  36.0 16.8 %collective-permute-start.10 = (bf16[5,4,16,2048]{3,2,1,0:T(8,128)(2,1)S(1)}, bf16[5,4,16,2048]{3,2,1,0:T(8,128)(2,1)S(1)}, u32[]{:S(2)}, u32[]{:S(2)}) collective-permute-start(bf16[5,4,16,2048]{3,2,1,0:T(8,128)(2,1)S(1)} %get-tuple-element.62), channel_id=1, source_target_pairs={{0,3},{8,56},{1,0},{9,57},{2,1},{10,58},{3,2},{11,59},{16,19},{24,... | collective-permute-start | bytes 3932168 | tf_op jit(solution)/shard_map/ppermute | solution.py:39
  37.5 14.4 %collective-permute-start.8 = (bf16[2,4,16,2048]{3,2,1,0:T(8,128)(2,1)S(1)}, bf16[2,4,16,2048]{3,2,1,0:T(8,128)(2,1)S(1)}, u32[]{:S(2)}, u32[]{:S(2)}) collective-permute-start(bf16[2,4,16,2048]{3,2,1,0:T(8,128)(2,1)S(1)} %get-tuple-element.60), channel_id=1, source_target_pairs={{0,64},{8,72},{1,65},{9,73},{2,66},{10,74},{3,67},{11,75},{16,80},... | collective-permute-start | bytes 1572872 | tf_op jit(solution)/shard_map/ppermute | solution.py:39
  39.2 44.1 %copy-start.3 = (bf16[5,2,4,16,2048]{4,3,2,1,0:T(8,128)(2,1)}, bf16[5,2,4,16,2048]{4,3,2,1,0:T(8,128)(2,1)S(1)}, u32[]{:S(2)}) copy-start(bf16[5,2,4,16,2048]{4,3,2,1,0:T(8,128)(2,1)S(1)} %collective-permute-done.11.recv.refs_2_.refs_3_) | copy-start | bytes 7864324
  53.0 30.2 %copy-start.1 = (bf16[12,4,16,2048]{3,2,1,0:T(8,128)(2,1)}, bf16[12,4,16,2048]{3,2,1,0:T(8,128)(2,1)S(1)}, u32[]{:S(2)}) copy-start(bf16[12,4,16,2048]{3,2,1,0:T(8,128)(2,1)S(1)} %shard_map.55) | copy-start | bytes 9437188
  53.0 6.2 %collective-permute-start.15 = (bf16[6,2,4,16,2048]{4,3,2,1,0:T(8,128)(2,1)S(1)}, bf16[6,2,4,16,2048]{4,3,2,1,0:T(8,128)(2,1)S(1)}, u32[]{:S(2)}, u32[]{:S(2)}) collective-permute-start(bf16[6,2,4,16,2048]{4,3,2,1,0:T(8,128)(2,1)S(1)} %bitcast.14), channel_id=1, source_target_pairs={{0,8},{8,0},{1,9},{9,1},{2,10},{10,2},{3,11},{11,3},{16,24},{24,16... | collective-permute-start | bytes 9437192 | tf_op jit(solution)/shard_map/ppermute | solution.py:39
  54.1 21.1 %collective-permute-start.12 = (bf16[4,4,16,2048]{3,2,1,0:T(8,128)(2,1)S(1)}, bf16[4,4,16,2048]{3,2,1,0:T(8,128)(2,1)S(1)}, u32[]{:S(2)}, u32[]{:S(2)}) collective-permute-start(bf16[4,4,16,2048]{3,2,1,0:T(8,128)(2,1)S(1)} %get-tuple-element.68), channel_id=1, source_target_pairs={{0,1},{8,24},{1,2},{9,25},{2,3},{10,26},{3,0},{11,27},{16,17},{24,... | collective-permute-start | bytes 3145736 | tf_op jit(solution)/shard_map/ppermute | solution.py:39
  55.3 19.9 %collective-permute-start.13 = (bf16[4,4,16,2048]{3,2,1,0:T(8,128)(2,1)S(1)}, bf16[4,4,16,2048]{3,2,1,0:T(8,128)(2,1)S(1)}, u32[]{:S(2)}, u32[]{:S(2)}) collective-permute-start(bf16[4,4,16,2048]{3,2,1,0:T(8,128)(2,1)S(1)} %get-tuple-element.69), channel_id=1, source_target_pairs={{0,3},{8,56},{1,0},{9,57},{2,1},{10,58},{3,2},{11,59},{16,19},{24,... | collective-permute-start | bytes 3145736 | tf_op jit(solution)/shard_map/ppermute | solution.py:39
  56.9 18.3 %collective-permute-start.14 = (bf16[2,4,16,2048]{3,2,1,0:T(8,128)(2,1)S(1)}, bf16[2,4,16,2048]{3,2,1,0:T(8,128)(2,1)S(1)}, u32[]{:S(2)}, u32[]{:S(2)}) collective-permute-start(bf16[2,4,16,2048]{3,2,1,0:T(8,128)(2,1)S(1)} %collective-permute-done.8.refs_2_), channel_id=1, source_target_pairs={{0,2},{8,40},{1,3},{9,41},{2,0},{10,42},{3,1},{11,43},{16,18},{24,... | collective-permute-start | bytes 1572872 | tf_op jit(solution)/shard_map/ppermute | solution.py:39
  59.3 24.0 %copy-start.4 = (bf16[6,2,4,16,2048]{4,3,2,1,0:T(8,128)(2,1)}, bf16[6,2,4,16,2048]{4,3,2,1,0:T(8,128)(2,1)S(1)}, u32[]{:S(2)}) copy-start(bf16[6,2,4,16,2048]{4,3,2,1,0:T(8,128)(2,1)S(1)} %collective-permute-done.15.refs_3_.refs_4_) | copy-start | bytes 9437188
  75.4 7.9 %copy-start.2 = (bf16[10,4,16,2048]{3,2,1,0:T(8,128)(2,1)}, bf16[10,4,16,2048]{3,2,1,0:T(8,128)(2,1)S(1)}, u32[]{:S(2)}) copy-start(bf16[10,4,16,2048]{3,2,1,0:T(8,128)(2,1)S(1)} %shard_map.58) | copy-start | bytes 7864324
  75.4 7.8 %collective-permute-start.16 = (bf16[5,2,4,16,2048]{4,3,2,1,0:T(8,128)(2,1)S(1)}, bf16[5,2,4,16,2048]{4,3,2,1,0:T(8,128)(2,1)S(1)}, u32[]{:S(2)}, u32[]{:S(2)}) collective-permute-start(bf16[5,2,4,16,2048]{4,3,2,1,0:T(8,128)(2,1)S(1)} %bitcast.18), channel_id=1, source_target_pairs={{0,8},{8,0},{1,9},{9,1},{2,10},{10,2},{3,11},{11,3},{16,24},{24,16... | collective-permute-start | bytes 7864328 | tf_op jit(solution)/shard_map/ppermute | solution.py:39
  79.3 3.9 %collective-permute-start.17 = (f32[256,640]{1,0:T(8,128)S(1)}, f32[256,640]{1,0:T(8,128)S(1)}, u32[]{:S(2)}, u32[]{:S(2)}) collective-permute-start(f32[256,640]{1,0:T(8,128)S(1)} %shard_map.59.refs_11_), channel_id=1, source_target_pairs={{0,8},{8,0},{1,9},{9,1},{2,10},{10,2},{3,11},{11,3},{16,24},{24,16... | collective-permute-start | bytes 1966088 | tf_op jit(solution)/shard_map/ppermute | solution.py:39
  83.2 3.6 %copy-start.5 = (bf16[5,2,4,16,2048]{4,3,2,1,0:T(8,128)(2,1)}, bf16[5,2,4,16,2048]{4,3,2,1,0:T(8,128)(2,1)S(1)}, u32[]{:S(2)}) copy-start(bf16[5,2,4,16,2048]{4,3,2,1,0:T(8,128)(2,1)S(1)} %collective-permute-done.16.refs_5_) | copy-start | bytes 7864324
  86.8 18.9 %all-to-all-start = ((f32[8,256,128]{2,1,0:T(8,128)}), f32[8,256,128]{2,1,0:T(8,128)S(1)}, u32[]{:S(2)}, u32[]{:S(2)}) async-start(f32[8,256,128]{2,1,0:T(8,128)} %get-tuple-element.83), calls=%async_computation | async-start | bytes 2097152 | tf_op jit(solution)/shard_map/all_to_all | solution.py:461

commit v6 on v5

--- a/solution.py
+++ b/solution.py
@@ -20,7 +20,7 @@
 ANY = pl.BlockSpec(memory_space=pl.ANY)
 IN_VMEM = pl.BlockSpec(memory_space=pltpu.VMEM)
 IN_SMEM = pl.BlockSpec(memory_space=pltpu.SMEM)
-MIDDLE = pltpu.CompilerParams(vmem_limit_bytes=24 << 20)
+MIDDLE = pltpu.CompilerParams(vmem_limit_bytes=20 << 20)
 SMALL = pltpu.CompilerParams(vmem_limit_bytes=8 << 20)
 
 
@@ -243,14 +243,6 @@
     )(at, own, recv, comps)
 
 
-def fill_rows(rows, groups, pieces, offset):
-    for n, m in enumerate(groups):
-        for step in range(4):
-            array, i = pieces(m, step)
-            for s in range(2):
-                rows[n, :, 1 - s, step] = array[i, s, :, :, offset : offset + HALF]
-
-
 def find(arrays, m, step):
     for array, labels in zip(arrays, ORDER):
         if (m, step) in labels:
@@ -258,17 +250,44 @@
 
 
 def soon_kernel(at, *refs):
-    own, recv, comps, early, origin, scores, total, row_sum, rows, cols = refs[:2], refs[2:4], *refs[4:]
+    own, recv, comps, early, origin = refs[:2], refs[2:4], *refs[4:7]
+    scores, total, row_sum, left_last, rows, cols = refs[7:]
 
     def use(row_from, col_from, offset):
         cols[...] = col_from[1][...]
-        fill_rows(rows, (0,), lambda m, step: find(row_from, m, step), offset)
+        for m in range(3):
+            for step in range(4 if m == 0 else 3):
+                array, i = find(row_from, m, step)
+                for s in range(2):
+                    rows[m, :, 1 - s, step] = array[i, s, :, :, offset : offset + HALF]
 
     select(at[0], own, recv, use)
+    rows[1:, :, :, 3] = jnp.zeros((2, 4, 2, LOCAL, HALF), BF16)
     score = score_of(comps[...], cols[...].reshape(len(SOON) * WIDTH, PANEL))
     scores[...] = score
-    first = jnp.concatenate([early[:, : 3 * WIDTH], score[:, :WIDTH]], axis=1)
-    total[...], row_sum[...] = product_of(left_of(first - origin[:, :1]), rows[...].reshape(4 * WIDTH, HALF))
+    known = (early[...], score)
+
+    def piece(m, step):
+        block, i = find(known, m, step)
+        return block[:, i * WIDTH : (i + 1) * WIDTH] - origin[:, :1]
+
+    sums = []
+    for m in range(3):
+        steps = range(4 if m == 0 else 3)
+        left = left_of(jnp.concatenate([piece(m, step) for step in steps], axis=1))
+        sums.append(product_of(left, rows[m, : len(steps)].reshape(len(steps) * WIDTH, HALF)))
+    total[...] = sums[0][0] + sums[1][0] + sums[2][0]
+    row_sum[...] = sums[0][1] + sums[1][1] + sums[2][1]
+    turned = (early[...].T, score.T)
+    blocks = []
+    for m in (1, 2):
+        for step in range(3):
+            block, i = find(turned, m, step)
+            for s in range(2):
+                start = i * WIDTH + (s * 4 + 3) * LOCAL
+                blocks.append(block[start : start + LOCAL])
+    blocks.append(jnp.zeros((4 * LOCAL, COMPS), F32))
+    left_last[...] = left_of(jnp.concatenate(blocks, axis=0).T - origin[:, :1])
 
 
 def soon_part(at, own, recv, comps, early):
@@ -278,11 +297,12 @@
             jax.ShapeDtypeStruct((COMPS, len(SOON) * WIDTH), F32),
             jax.ShapeDtypeStruct((COMPS, HALF), F32),
             jax.ShapeDtypeStruct((1, HALF), F32),
+            jax.ShapeDtypeStruct((2 * COMPS + 16, 2 * WIDTH), BF16),
         ],
         in_specs=[IN_SMEM] + [IN_VMEM] * 7,
-        out_specs=[IN_VMEM] * 3,
+        out_specs=[IN_VMEM] * 4,
         scratch_shapes=[
-            pltpu.VMEM((1, 4, 2, 4, LOCAL, HALF), BF16),
+            pltpu.VMEM((3, 4, 2, 4, LOCAL, HALF), BF16),
             pltpu.VMEM((len(SOON), 2, 4, LOCAL, PANEL), BF16),
         ],
         compiler_params=MIDDLE,
@@ -306,25 +326,39 @@
 
 
 def last_kernel(at, column, *refs):
-    own, recv, early, origin, soon, total_in, rs_in, late_own, late_recv = refs[:3], refs[3:6], *refs[6:13]
-    parts, means, means_part, rows, left = refs[13:]
-
-    def put(block, labels):
-        for i, (m, step) in enumerate(labels):
-            if m > 0:
-                at_scan = ((m - 1) * 4 + step) * WIDTH
-                left[:, at_scan : at_scan + WIDTH] = left_of(block[:, i * WIDTH : (i + 1) * WIDTH] - origin[:, :1])
+    own, recv, early, origin, soon, total_in, rs_in, left_in = refs[:3], refs[3:6], *refs[6:12]
+    late_own, late_recv, parts, means, means_part, rows, left = refs[12:]
+
+    def put(place, scores, m, step):
+        block, i = find(scores, m, step)
+        left[:, place : place + WIDTH] = left_of(block[:, i * WIDTH : (i + 1) * WIDTH] - origin[:, :1])
 
     def use(row_from, col_from, offset):
-        fill_rows(rows, (1, 2, 3), lambda m, step: find(row_from, m, step), offset)
-        put(late_recv if offset == 0 else late_own, LATE)
+        def row(m, step, s, spread):
+            array, i = find(row_from, m, step)
+            return array[i, 1 - s, spread, :, offset : offset + HALF]
+
+        for s in range(2):
+            for m in (1, 2):
+                for c in range(3):
+                    rows[((m - 1) * 3 + c) * 2 + s] = row(m, 3, s, c)
+                for step in range(4):
+                    rows[8 + m * 8 + s * 4 + step] = row(m, step, s, 3)
+            for c in range(4):
+                for step in range(4):
+                    rows[32 + c * 8 + s * 4 + step] = row(3, step, s, c)
+        scores = (early, soon, late_recv if offset == 0 else late_own)
+        for m in (1, 2):
+            put((m + 1) * WIDTH, scores, m, 3)
+        for c in range(4):
+            put((4 + c) * WIDTH, scores, 3, c)
 
     select(at[0], own, recv, use)
-    put(early, EARLY)
-    put(soon, SOON)
+    rows[12:16] = jnp.zeros((4, LOCAL, HALF), BF16)
+    left[:, : 2 * WIDTH] = left_in[...]
     late = jnp.where(at[0] == 0, late_recv[...], late_own[...])
     score_sum = sum(jnp.sum(block, axis=1, keepdims=True) for block in (early[...], soon[...], late))
-    total, row_sum = product_of(left[...], rows[...].reshape(12 * WIDTH, HALF))
+    total, row_sum = product_of(left[...], rows[...].reshape(8 * WIDTH, HALF))
     row_sum = row_sum + rs_in[...]
     shift = score_sum * (1.0 / SCANS) - origin[:, :1]
     total = (total + total_in[...] - shift * row_sum) * (1.0 / (SCANS - 1))
@@ -342,11 +376,11 @@
             jax.ShapeDtypeStruct((1, HALF), F32),
             jax.ShapeDtypeStruct((1, 128), F32),
         ],
-        in_specs=[IN_SMEM] * 2 + [IN_VMEM] * 13,
+        in_specs=[IN_SMEM] * 2 + [IN_VMEM] * 14,
         out_specs=[IN_VMEM] * 3,
         scratch_shapes=[
-            pltpu.VMEM((3, 4, 2, 4, LOCAL, HALF), BF16),
-            pltpu.VMEM((2 * COMPS + 16, 12 * WIDTH), BF16),
+            pltpu.VMEM((64, LOCAL, HALF), BF16),
+            pltpu.VMEM((2 * COMPS + 16, 8 * WIDTH), BF16),
         ],
         compiler_params=MIDDLE,
         cost_estimate=pl.CostEstimate(flops=4 << 30, bytes_accessed=4 << 20, transcendentals=0),
@@ -408,7 +442,7 @@
             pltpu.SemaphoreType.DMA((4,)),
             pltpu.SemaphoreType.DMA((2,)),
         ],
-        compiler_params=pltpu.CompilerParams(vmem_limit_bytes=30 << 20),
+        compiler_params=pltpu.CompilerParams(vmem_limit_bytes=22 << 20),
         cost_estimate=pl.CostEstimate(flops=8 << 30, bytes_accessed=20 << 20, transcendentals=0),
     )(at, *[pltpu.with_memory_space_constraint(piece, pltpu.HBM) for piece in own + recv], row_means)
 

time: 107 us -> 106 us (level)
  waiting for transfers between devices: 47.5 us -> 44 us
  Pallas kernels: 28.6 us -> 31.4 us
    pallas_call x1, Pallas kernels: 3.58 us -> 7.11 us  [soon_part(): pl.pallas_call(soon_kernel, out_shape=[jax.ShapeDtypeStruct((COMPS, len(S...]
    ppermute x18, waiting for transfers between devices: 47.5 us -> 44 us  [permute(): return lax.ppermute(value, AXES, pairs)]
  transfers between devices with their start and end apart: 19 -> 19, of which waited for: 12 -> 12; matrix products, arithmetic and copies ran while one was open for 0% -> 0% of each run, Pallas kernels for 23% -> 26%
where the time goes in v6:
time: 106 us
  waiting for transfers between devices  44 us (42%)
  Pallas kernels  31.4 us (30%)
  starting transfers between devices  28.7 us (27%)
    ppermute x18, waiting for transfers between devices, permute(): return lax.ppermute(value, AXES, pairs)  44 us
    ppermute x18, starting transfers between devices, permute(): return lax.ppermute(value, AXES, pairs)  25.1 us
    pallas_call x1, Pallas kernels, gram(): pl.pallas_call(gram_kernel, out_shape=jax.ShapeDtypeStruct((HALF, PANEL),...  15.3 us
    pallas_call x1, Pallas kernels, soon_part(): pl.pallas_call(soon_kernel, out_shape=[jax.ShapeDtypeStruct((COMPS, len(S...  7.11 us
    all_to_all x1, starting transfers between devices, on_device(): parts = lax.all_to_all(parts, 'bcol', 0, 0, tiled=True)  3.56 us
    pallas_call x1, Pallas kernels, last_part(): pl.pallas_call(last_kernel, out_shape=[jax.ShapeDtypeStruct((8, COMPS, 12...  2.91 us
    pallas_call x1, Pallas kernels, early_part(): pl.pallas_call(early_kernel, out_shape=[jax.ShapeDtypeStruct((COMPS, len(...  2.31 us
  transfers between devices with their start and end apart: 19, of which 12 were waited for; matrix products, arithmetic and copies ran while one was open for 0% of the time, Pallas kernels for 26%

profile of v6, /device:TPU:1, one launch (start us, length us, event | category | flops | bytes accessed | tf_op | source)
XLA Modules:
  0.0 105.8 jit_solution(17851242805266112563)
XLA Ops:
  0.6 1.5 %collective-permute-start = (bf16[16,16384]{1,0:T(8,128)(2,1)}, bf16[16,16384]{1,0:T(8,128)(2,1)S(1)}, u32[]{:S(2)}, u32[]{:S(2)}) collective-permute-start(bf16[16,16384]{1,0:T(8,128)(2,1)} %mine.1), channel_id=1, source_target_pairs={{0,8},{8,0},{1,9},{9,1},{2,10},{10,2},{3,11},{11,3},{16,24},{24,16... | collective-permute-start | bytes 1572872 | tf_op jit(solution)/shard_map/ppermute | solution.py:39
  2.1 1.1 %shard_map.49 = (bf16[2,16,2048]{2,1,0:T(8,128)(2,1)S(1)}, bf16[2,16,2048]{2,1,0:T(8,128)(2,1)S(1)}, bf16[2,16,2048]{2,1,0:T(8,128)(2,1)S(1)}, bf16[2,16,2048]{2,1,0:T(8,128)(2,1)S(1)}) custom-call(s32[1]{0:T(128)} %bitcast.2.place, bf16[16,16384]{1,0:T(8,128)(2,1)} %mine.1), custom_call_target="tpu_custom_call" | custom-call | tf_op jit(solution)/shard_map/pallas_call | solution.py:76
  4.0 1.8 %collective-permute-start.1 = (bf16[2,2,16,2048]{3,2,1,0:T(8,128)(2,1)S(1)}, bf16[2,2,16,2048]{3,2,1,0:T(8,128)(2,1)S(1)}, u32[]{:S(2)}, u32[]{:S(2)}) collective-permute-start(bf16[2,2,16,2048]{3,2,1,0:T(8,128)(2,1)S(1)} %get-tuple-element.51), channel_id=1, source_target_pairs={{0,16},{8,9},{1,17},{9,10},{2,18},{10,11},{3,19},{11,8},{16,32},{2... | collective-permute-start | bytes 786440 | tf_op jit(solution)/shard_map/ppermute | solution.py:39
  5.7 2.2 %collective-permute-start.2 = (bf16[2,2,16,2048]{3,2,1,0:T(8,128)(2,1)S(1)}, bf16[2,2,16,2048]{3,2,1,0:T(8,128)(2,1)S(1)}, u32[]{:S(2)}, u32[]{:S(2)}) collective-permute-start(bf16[2,2,16,2048]{3,2,1,0:T(8,128)(2,1)S(1)} %get-tuple-element.52), channel_id=1, source_target_pairs={{0,48},{8,11},{1,49},{9,8},{2,50},{10,9},{3,51},{11,10},{16,0},{24... | collective-permute-start | bytes 786440 | tf_op jit(solution)/shard_map/ppermute | solution.py:39
  7.9 1.2 %collective-permute-start.3 = (bf16[2,2,16,2048]{3,2,1,0:T(8,128)(2,1)S(1)}, bf16[2,2,16,2048]{3,2,1,0:T(8,128)(2,1)S(1)}, u32[]{:S(2)}, u32[]{:S(2)}) collective-permute-start(bf16[2,2,16,2048]{3,2,1,0:T(8,128)(2,1)S(1)} %get-tuple-element.53), channel_id=1, source_target_pairs={{0,32},{8,10},{1,33},{9,11},{2,34},{10,8},{3,35},{11,9},{16,48},{2... | collective-permute-start | bytes 786440 | tf_op jit(solution)/shard_map/ppermute | solution.py:39
  9.2 2.5 %collective-permute-done.1.refs_1_ = bf16[2,2,16,2048]{3,2,1,0:T(8,128)(2,1)S(1)} collective-permute-done((bf16[2,2,16,2048]{3,2,1,0:T(8,128)(2,1)S(1)}, bf16[2,2,16,2048]{3,2,1,0:T(8,128)(2,1)S(1)}, u32[]{:S(2)}, u32[]{:S(2)}) %collective-permute-start.1) | collective-permute-done | bytes 262176 | tf_op jit(solution)/shard_map/ppermute | solution.py:39
  11.6 2.4 %collective-permute-done.2.refs_2_ = bf16[2,2,16,2048]{3,2,1,0:T(8,128)(2,1)S(1)} collective-permute-done((bf16[2,2,16,2048]{3,2,1,0:T(8,128)(2,1)S(1)}, bf16[2,2,16,2048]{3,2,1,0:T(8,128)(2,1)S(1)}, u32[]{:S(2)}, u32[]{:S(2)}) %collective-permute-start.2) | collective-permute-done | bytes 262176 | tf_op jit(solution)/shard_map/ppermute | solution.py:39
  14.1 1.6 %collective-permute-done.3.refs_3_ = bf16[2,2,16,2048]{3,2,1,0:T(8,128)(2,1)S(1)} collective-permute-done((bf16[2,2,16,2048]{3,2,1,0:T(8,128)(2,1)S(1)}, bf16[2,2,16,2048]{3,2,1,0:T(8,128)(2,1)S(1)}, u32[]{:S(2)}, u32[]{:S(2)}) %collective-permute-start.3) | collective-permute-done | bytes 262176 | tf_op jit(solution)/shard_map/ppermute | solution.py:39
  15.9 1.3 %collective-permute-start.4 = (bf16[2,4,16,2048]{3,2,1,0:T(8,128)(2,1)S(1)}, bf16[2,4,16,2048]{3,2,1,0:T(8,128)(2,1)S(1)}, u32[]{:S(2)}, u32[]{:S(2)}) collective-permute-start(bf16[2,4,16,2048]{3,2,1,0:T(8,128)(2,1)S(1)} %get-tuple-element.55), channel_id=1, source_target_pairs={{0,4},{8,12},{1,5},{9,13},{2,6},{10,14},{3,7},{11,15},{16,20},{24,... | collective-permute-start | bytes 1572872 | tf_op jit(solution)/shard_map/ppermute | solution.py:39
  17.1 1.8 %collective-permute-start.5 = (bf16[2,4,16,2048]{3,2,1,0:T(8,128)(2,1)S(1)}, bf16[2,4,16,2048]{3,2,1,0:T(8,128)(2,1)S(1)}, u32[]{:S(2)}, u32[]{:S(2)}) collective-permute-start(bf16[2,4,16,2048]{3,2,1,0:T(8,128)(2,1)S(1)} %get-tuple-element.56), channel_id=1, source_target_pairs={{0,68},{8,76},{1,69},{9,77},{2,70},{10,78},{3,71},{11,79},{16,84},... | collective-permute-start | bytes 1572872 | tf_op jit(solution)/shard_map/ppermute | solution.py:39
  19.0 2.6 %collective-permute-start.7 = (bf16[2,4,16,2048]{3,2,1,0:T(8,128)(2,1)S(1)}, bf16[2,4,16,2048]{3,2,1,0:T(8,128)(2,1)S(1)}, u32[]{:S(2)}, u32[]{:S(2)}) collective-permute-start(bf16[2,4,16,2048]{3,2,1,0:T(8,128)(2,1)S(1)} %get-tuple-element.54.refs_0_), channel_id=1, source_target_pairs={{0,3},{8,56},{1,0},{9,57},{2,1},{10,58},{3,2},{11,59},{16,19},{24,... | collective-permute-start | bytes 1572872 | tf_op jit(solution)/shard_map/ppermute | solution.py:39
  21.6 7.5 %collective-permute-done.4.refs_3_.refs_0_ = bf16[2,4,16,2048]{3,2,1,0:T(8,128)(2,1)S(1)} collective-permute-done((bf16[2,4,16,2048]{3,2,1,0:T(8,128)(2,1)S(1)}, bf16[2,4,16,2048]{3,2,1,0:T(8,128)(2,1)S(1)}, u32[]{:S(2)}, u32[]{:S(2)}) %collective-permute-start.4) | collective-permute-done | bytes 524320 | tf_op jit(solution)/shard_map/ppermute | solution.py:39
  29.0 2.1 %collective-permute-done.5.refs_4_.refs_1_ = bf16[2,4,16,2048]{3,2,1,0:T(8,128)(2,1)S(1)} collective-permute-done((bf16[2,4,16,2048]{3,2,1,0:T(8,128)(2,1)S(1)}, bf16[2,4,16,2048]{3,2,1,0:T(8,128)(2,1)S(1)}, u32[]{:S(2)}, u32[]{:S(2)}) %collective-permute-start.5) | collective-permute-done | bytes 524320 | tf_op jit(solution)/shard_map/ppermute | solution.py:39
  31.3 3.3 %collective-permute-start.11 = (bf16[5,2,4,16,2048]{4,3,2,1,0:T(8,128)(2,1)S(1)}, bf16[5,2,4,16,2048]{4,3,2,1,0:T(8,128)(2,1)S(1)}, u32[]{:S(2)}, u32[]{:S(2)}) collective-permute-start(bf16[5,2,4,16,2048]{4,3,2,1,0:T(8,128)(2,1)S(1)} %bitcast.9), channel_id=1, source_target_pairs={{0,8},{8,0},{1,9},{9,1},{2,10},{10,2},{3,11},{11,3},{16,24},{24,16... | collective-permute-start | bytes 7864328 | tf_op jit(solution)/shard_map/ppermute | solution.py:39
  34.8 1.2 %collective-permute-start.9 = (bf16[5,4,16,2048]{3,2,1,0:T(8,128)(2,1)S(1)}, bf16[5,4,16,2048]{3,2,1,0:T(8,128)(2,1)S(1)}, u32[]{:S(2)}, u32[]{:S(2)}) collective-permute-start(bf16[5,4,16,2048]{3,2,1,0:T(8,128)(2,1)S(1)} %get-tuple-element.63), channel_id=1, source_target_pairs={{0,1},{8,24},{1,2},{9,25},{2,3},{10,26},{3,0},{11,27},{16,17},{24,... | collective-permute-start | bytes 3932168 | tf_op jit(solution)/shard_map/ppermute | solution.py:39
  36.0 1.5 %collective-permute-start.10 = (bf16[5,4,16,2048]{3,2,1,0:T(8,128)(2,1)S(1)}, bf16[5,4,16,2048]{3,2,1,0:T(8,128)(2,1)S(1)}, u32[]{:S(2)}, u32[]{:S(2)}) collective-permute-start(bf16[5,4,16,2048]{3,2,1,0:T(8,128)(2,1)S(1)} %get-tuple-element.64), channel_id=1, source_target_pairs={{0,3},{8,56},{1,0},{9,57},{2,1},{10,58},{3,2},{11,59},{16,19},{24,... | collective-permute-start | bytes 3932168 | tf_op jit(solution)/shard_map/ppermute | solution.py:39
  37.9 1.3 %collective-permute-done.11.recv.refs_2_.refs_3_ = bf16[5,2,4,16,2048]{4,3,2,1,0:T(8,128)(2,1)S(1)} collective-permute-done((bf16[5,2,4,16,2048]{4,3,2,1,0:T(8,128)(2,1)S(1)}, bf16[5,2,4,16,2048]{4,3,2,1,0:T(8,128)(2,1)S(1)}, u32[]{:S(2)}, u32[]{:S(2)}) %collective-permute-start.11) | collective-permute-done | bytes 2621472 | tf_op jit(solution)/shard_map/ppermute | solution.py:39
  39.2 2.3 %shard_map.54 = (f32[256,640]{1,0:T(8,128)S(1)}, f32[256,128]{1,0:T(8,128)S(1)}, bf16[2048,512]{1,0:T(8,128)(2,1)S(1)}) custom-call(s32[1]{0:T(128)} %bitcast.core.at, bf16[5,2,4,16,2048]{4,3,2,1,0:T(8,128)(2,1)S(1)} %bitcast.10, bf16[5,2,4,16,2048]{4,3,2,1,0:T(8,128)(2,1)S(1)} %collective-permute-done.11.recv.refs_2_.refs_3_, f32[2048,256]{1,0:T(8,128)S(1)} %copy-done.6), custom_call_target="tpu_custom_call" | custom-call | flops 1073741824 | bytes 1048576 | tf_op jit(solution)/shard_map/pallas_call | solution.py:231
  41.5 10.5 %collective-permute-done.8.refs_2_ = bf16[2,4,16,2048]{3,2,1,0:T(8,128)(2,1)S(1)} collective-permute-done((bf16[2,4,16,2048]{3,2,1,0:T(8,128)(2,1)S(1)}, bf16[2,4,16,2048]{3,2,1,0:T(8,128)(2,1)S(1)}, u32[]{:S(2)}, u32[]{:S(2)}) %collective-permute-start.8) | collective-permute-done | bytes 524320 | tf_op jit(solution)/shard_map/ppermute | solution.py:39
  51.9 0.9 collective-permute-done.9.refs_0_
  53.0 1.0 collective-permute-start.15
  54.1 1.2 %collective-permute-start.12 = (bf16[4,4,16,2048]{3,2,1,0:T(8,128)(2,1)S(1)}, bf16[4,4,16,2048]{3,2,1,0:T(8,128)(2,1)S(1)}, u32[]{:S(2)}, u32[]{:S(2)}) collective-permute-start(bf16[4,4,16,2048]{3,2,1,0:T(8,128)(2,1)S(1)} %get-tuple-element.70), channel_id=1, source_target_pairs={{0,1},{8,24},{1,2},{9,25},{2,3},{10,26},{3,0},{11,27},{16,17},{24,... | collective-permute-start | bytes 3145736 | tf_op jit(solution)/shard_map/ppermute | solution.py:39
  55.3 1.5 %collective-permute-start.13 = (bf16[4,4,16,2048]{3,2,1,0:T(8,128)(2,1)S(1)}, bf16[4,4,16,2048]{3,2,1,0:T(8,128)(2,1)S(1)}, u32[]{:S(2)}, u32[]{:S(2)}) collective-permute-start(bf16[4,4,16,2048]{3,2,1,0:T(8,128)(2,1)S(1)} %get-tuple-element.71), channel_id=1, source_target_pairs={{0,3},{8,56},{1,0},{9,57},{2,1},{10,58},{3,2},{11,59},{16,19},{24,... | collective-permute-start | bytes 3145736 | tf_op jit(solution)/shard_map/ppermute | solution.py:39
  57.2 2.1 %collective-permute-done.15.refs_3_.refs_4_ = bf16[6,2,4,16,2048]{4,3,2,1,0:T(8,128)(2,1)S(1)} collective-permute-done((bf16[6,2,4,16,2048]{4,3,2,1,0:T(8,128)(2,1)S(1)}, bf16[6,2,4,16,2048]{4,3,2,1,0:T(8,128)(2,1)S(1)}, u32[]{:S(2)}, u32[]{:S(2)}) %collective-permute-start.15) | collective-permute-done | bytes 3145760 | tf_op jit(solution)/shard_map/ppermute | solution.py:39
  59.3 7.1 %shard_map.57 = (f32[256,768]{1,0:T(8,128)S(1)}, f32[256,1024]{1,0:T(8,128)S(1)}, f32[1,1024]{1,0:T(1,128)S(1)}, bf16[528,256]{1,0:T(8,128)(2,1)S(1)}) custom-call(s32[1]{0:T(128)} %bitcast.core.at, bf16[5,2,4,16,2048]{4,3,2,1,0:T(8,128)(2,1)S(1)} %bitcast.11, bf16[6,2,4,16,2048]{4,3,2,1,0:T(8,128)(2,1)S(1)} %bitcast.15, ...), custom_call_target="tpu_custom_call" | custom-call | flops 2147483648 | bytes 1048576 | tf_op jit(solution)/shard_map/pallas_call | solution.py:294
  66.4 8.8 %collective-permute-done.14.refs_2_ = bf16[2,4,16,2048]{3,2,1,0:T(8,128)(2,1)S(1)} collective-permute-done((bf16[2,4,16,2048]{3,2,1,0:T(8,128)(2,1)S(1)}, bf16[2,4,16,2048]{3,2,1,0:T(8,128)(2,1)S(1)}, u32[]{:S(2)}, u32[]{:S(2)}) %collective-permute-start.14) | collective-permute-done | bytes 524320 | tf_op jit(solution)/shard_map/ppermute | solution.py:39
  75.4 2.2 %collective-permute-start.16 = (bf16[5,2,4,16,2048]{4,3,2,1,0:T(8,128)(2,1)S(1)}, bf16[5,2,4,16,2048]{4,3,2,1,0:T(8,128)(2,1)S(1)}, u32[]{:S(2)}, u32[]{:S(2)}) collective-permute-start(bf16[5,2,4,16,2048]{4,3,2,1,0:T(8,128)(2,1)S(1)} %bitcast.18), channel_id=1, source_target_pairs={{0,8},{8,0},{1,9},{9,1},{2,10},{10,2},{3,11},{11,3},{16,24},{24,16... | collective-permute-start | bytes 7864328 | tf_op jit(solution)/shard_map/ppermute | solution.py:39
  77.6 1.6 %shard_map.59.refs_12_ = f32[256,640]{1,0:T(8,128)S(1)} custom-call(bf16[5,2,4,16,2048]{4,3,2,1,0:T(8,128)(2,1)S(1)} %bitcast.19, bf16[2048,512]{1,0:T(8,128)(2,1)S(1)} %get-tuple-element.72.refs_4_.comps), custom_call_target="tpu_custom_call" | custom-call | flops 1073741824 | bytes 1048576 | tf_op jit(solution)/shard_map/pallas_call | solution.py:318
  79.3 3.8 %collective-permute-done.17.refs_13_ = f32[256,640]{1,0:T(8,128)S(1)} collective-permute-done((f32[256,640]{1,0:T(8,128)S(1)}, f32[256,640]{1,0:T(8,128)S(1)}, u32[]{:S(2)}, u32[]{:S(2)}) %collective-permute-start.17) | collective-permute-done | bytes 655392 | tf_op jit(solution)/shard_map/ppermute | solution.py:39
  83.1 2.9 %shard_map.60 = (f32[8,256,128]{2,1,0:T(8,128)}, f32[1,1024]{1,0:T(1,128)S(1)}, f32[1,128]{1,0:T(1,128)}) custom-call(s32[1]{0:T(128)} %bitcast.core.at, s32[1]{0:T(128)} %bitcast.6.column, bf16[5,2,4,16,2048]{4,3,2,1,0:T(8,128)(2,1)S(1)} %bitcast.12, bf16[6,2,4,16,2048]{4,3,2,1,0:T(8,128)(2,1)S(1)} %bitcast.16, bf16[5,2,4,16,2048]{4,3,2,1,0:T(8,128)(2,1)S(1)} %bitcast.20, ...), custom_call_target="tpu_custom_call" | custom-call | flops 4294967296 | bytes 4194304 | tf_op jit(solution)/shard_map/pallas_call | solution.py:372
  86.0 3.6 %all-to-all-start = ((f32[8,256,128]{2,1,0:T(8,128)}), f32[8,256,128]{2,1,0:T(8,128)S(1)}, u32[]{:S(2)}, u32[]{:S(2)}) async-start(f32[8,256,128]{2,1,0:T(8,128)} %get-tuple-element.87), calls=%async_computation | async-start | bytes 2097152 | tf_op jit(solution)/shard_map/all_to_all | solution.py:495
  89.6 15.3 %shard_map.61 = f32[1024,2048]{1,0:T(8,128)} custom-call(s32[1]{0:T(128)} %bitcast.core.at, bf16[5,2,4,16,2048]{4,3,2,1,0:T(8,128)(2,1)} %bitcast.13, bf16[6,2,4,16,2048]{4,3,2,1,0:T(8,128)(2,1)} %bitcast.17, bf16[5,2,4,16,2048]{4,3,2,1,0:T(8,128)(2,1)} %bitcast.21, bf16[5,2,4,16,2048]{4,3,2,1,0:T(8,128)(2,1)} %copy-done.3, ...), custom_call_target="tpu_custom_call" | custom-call | flops 8589934592 | bytes 20971520 | tf_op jit(solution)/shard_map/pallas_call | solution.py:432
  (35 shorter events, 3.3 us)
Async XLA Ops:
  0.6 3.2 %collective-permute-start = (bf16[16,16384]{1,0:T(8,128)(2,1)}, bf16[16,16384]{1,0:T(8,128)(2,1)S(1)}, u32[]{:S(2)}, u32[]{:S(2)}) collective-permute-start(bf16[16,16384]{1,0:T(8,128)(2,1)} %mine.1), channel_id=1, source_target_pairs={{0,8},{8,0},{1,9},{9,1},{2,10},{10,2},{3,11},{11,3},{16,24},{24,16... | collective-permute-start | bytes 1572872 | tf_op jit(solution)/shard_map/ppermute | solution.py:39
  4.0 7.7 %collective-permute-start.1 = (bf16[2,2,16,2048]{3,2,1,0:T(8,128)(2,1)S(1)}, bf16[2,2,16,2048]{3,2,1,0:T(8,128)(2,1)S(1)}, u32[]{:S(2)}, u32[]{:S(2)}) collective-permute-start(bf16[2,2,16,2048]{3,2,1,0:T(8,128)(2,1)S(1)} %get-tuple-element.51), channel_id=1, source_target_pairs={{0,16},{8,9},{1,17},{9,10},{2,18},{10,11},{3,19},{11,8},{16,32},{2... | collective-permute-start | bytes 786440 | tf_op jit(solution)/shard_map/ppermute | solution.py:39
  5.7 8.3 %collective-permute-start.2 = (bf16[2,2,16,2048]{3,2,1,0:T(8,128)(2,1)S(1)}, bf16[2,2,16,2048]{3,2,1,0:T(8,128)(2,1)S(1)}, u32[]{:S(2)}, u32[]{:S(2)}) collective-permute-start(bf16[2,2,16,2048]{3,2,1,0:T(8,128)(2,1)S(1)} %get-tuple-element.52), channel_id=1, source_target_pairs={{0,48},{8,11},{1,49},{9,8},{2,50},{10,9},{3,51},{11,10},{16,0},{24... | collective-permute-start | bytes 786440 | tf_op jit(solution)/shard_map/ppermute | solution.py:39
  7.9 7.8 %collective-permute-start.3 = (bf16[2,2,16,2048]{3,2,1,0:T(8,128)(2,1)S(1)}, bf16[2,2,16,2048]{3,2,1,0:T(8,128)(2,1)S(1)}, u32[]{:S(2)}, u32[]{:S(2)}) collective-permute-start(bf16[2,2,16,2048]{3,2,1,0:T(8,128)(2,1)S(1)} %get-tuple-element.53), channel_id=1, source_target_pairs={{0,32},{8,10},{1,33},{9,11},{2,34},{10,8},{3,35},{11,9},{16,48},{2... | collective-permute-start | bytes 786440 | tf_op jit(solution)/shard_map/ppermute | solution.py:39
  15.9 13.2 %collective-permute-start.4 = (bf16[2,4,16,2048]{3,2,1,0:T(8,128)(2,1)S(1)}, bf16[2,4,16,2048]{3,2,1,0:T(8,128)(2,1)S(1)}, u32[]{:S(2)}, u32[]{:S(2)}) collective-permute-start(bf16[2,4,16,2048]{3,2,1,0:T(8,128)(2,1)S(1)} %get-tuple-element.55), channel_id=1, source_target_pairs={{0,4},{8,12},{1,5},{9,13},{2,6},{10,14},{3,7},{11,15},{16,20},{24,... | collective-permute-start | bytes 1572872 | tf_op jit(solution)/shard_map/ppermute | solution.py:39
  17.1 14.0 %collective-permute-start.5 = (bf16[2,4,16,2048]{3,2,1,0:T(8,128)(2,1)S(1)}, bf16[2,4,16,2048]{3,2,1,0:T(8,128)(2,1)S(1)}, u32[]{:S(2)}, u32[]{:S(2)}) collective-permute-start(bf16[2,4,16,2048]{3,2,1,0:T(8,128)(2,1)S(1)} %get-tuple-element.56), channel_id=1, source_target_pairs={{0,68},{8,76},{1,69},{9,77},{2,70},{10,78},{3,71},{11,79},{16,84},... | collective-permute-start | bytes 1572872 | tf_op jit(solution)/shard_map/ppermute | solution.py:39
  19.0 12.2 %collective-permute-start.7 = (bf16[2,4,16,2048]{3,2,1,0:T(8,128)(2,1)S(1)}, bf16[2,4,16,2048]{3,2,1,0:T(8,128)(2,1)S(1)}, u32[]{:S(2)}, u32[]{:S(2)}) collective-permute-start(bf16[2,4,16,2048]{3,2,1,0:T(8,128)(2,1)S(1)} %get-tuple-element.54.refs_0_), channel_id=1, source_target_pairs={{0,3},{8,56},{1,0},{9,57},{2,1},{10,58},{3,2},{11,59},{16,19},{24,... | collective-permute-start | bytes 1572872 | tf_op jit(solution)/shard_map/ppermute | solution.py:39
  21.6 9.6 %collective-permute-start.6 = (bf16[2,4,16,2048]{3,2,1,0:T(8,128)(2,1)S(1)}, bf16[2,4,16,2048]{3,2,1,0:T(8,128)(2,1)S(1)}, u32[]{:S(2)}, u32[]{:S(2)}) collective-permute-start(bf16[2,4,16,2048]{3,2,1,0:T(8,128)(2,1)S(1)} %get-tuple-element.54.refs_0_), channel_id=1, source_target_pairs={{0,1},{8,24},{1,2},{9,25},{2,3},{10,26},{3,0},{11,27},{16,17},{24,... | collective-permute-start | bytes 1572872 | tf_op jit(solution)/shard_map/ppermute | solution.py:39
  31.2 8.0 %copy-start.6 = (f32[2048,256]{1,0:T(8,128)S(1)}, f32[2048,256]{1,0:T(8,128)}, u32[]{:S(2)}) copy-start(f32[2048,256]{1,0:T(8,128)} %components.1) | copy-start | bytes 6291460
  31.3 51.7 %copy-start = (bf16[10,4,16,2048]{3,2,1,0:T(8,128)(2,1)}, bf16[10,4,16,2048]{3,2,1,0:T(8,128)(2,1)S(1)}, u32[]{:S(2)}) copy-start(bf16[10,4,16,2048]{3,2,1,0:T(8,128)(2,1)S(1)} %shard_map.52) | copy-start | bytes 7864324
  31.3 7.8 %collective-permute-start.11 = (bf16[5,2,4,16,2048]{4,3,2,1,0:T(8,128)(2,1)S(1)}, bf16[5,2,4,16,2048]{4,3,2,1,0:T(8,128)(2,1)S(1)}, u32[]{:S(2)}, u32[]{:S(2)}) collective-permute-start(bf16[5,2,4,16,2048]{4,3,2,1,0:T(8,128)(2,1)S(1)} %bitcast.9), channel_id=1, source_target_pairs={{0,8},{8,0},{1,9},{9,1},{2,10},{10,2},{3,11},{11,3},{16,24},{24,16... | collective-permute-start | bytes 7864328 | tf_op jit(solution)/shard_map/ppermute | solution.py:39
  34.8 18.0 %collective-permute-start.9 = (bf16[5,4,16,2048]{3,2,1,0:T(8,128)(2,1)S(1)}, bf16[5,4,16,2048]{3,2,1,0:T(8,128)(2,1)S(1)}, u32[]{:S(2)}, u32[]{:S(2)}) collective-permute-start(bf16[5,4,16,2048]{3,2,1,0:T(8,128)(2,1)S(1)} %get-tuple-element.63), channel_id=1, source_target_pairs={{0,1},{8,24},{1,2},{9,25},{2,3},{10,26},{3,0},{11,27},{16,17},{24,... | collective-permute-start | bytes 3932168 | tf_op jit(solution)/shard_map/ppermute | solution.py:39
  36.0 16.8 %collective-permute-start.10 = (bf16[5,4,16,2048]{3,2,1,0:T(8,128)(2,1)S(1)}, bf16[5,4,16,2048]{3,2,1,0:T(8,128)(2,1)S(1)}, u32[]{:S(2)}, u32[]{:S(2)}) collective-permute-start(bf16[5,4,16,2048]{3,2,1,0:T(8,128)(2,1)S(1)} %get-tuple-element.64), channel_id=1, source_target_pairs={{0,3},{8,56},{1,0},{9,57},{2,1},{10,58},{3,2},{11,59},{16,19},{24,... | collective-permute-start | bytes 3932168 | tf_op jit(solution)/shard_map/ppermute | solution.py:39
  37.5 14.4 %collective-permute-start.8 = (bf16[2,4,16,2048]{3,2,1,0:T(8,128)(2,1)S(1)}, bf16[2,4,16,2048]{3,2,1,0:T(8,128)(2,1)S(1)}, u32[]{:S(2)}, u32[]{:S(2)}) collective-permute-start(bf16[2,4,16,2048]{3,2,1,0:T(8,128)(2,1)S(1)} %get-tuple-element.62), channel_id=1, source_target_pairs={{0,64},{8,72},{1,65},{9,73},{2,66},{10,74},{3,67},{11,75},{16,80},... | collective-permute-start | bytes 1572872 | tf_op jit(solution)/shard_map/ppermute | solution.py:39
  39.2 43.9 %copy-start.3 = (bf16[5,2,4,16,2048]{4,3,2,1,0:T(8,128)(2,1)}, bf16[5,2,4,16,2048]{4,3,2,1,0:T(8,128)(2,1)S(1)}, u32[]{:S(2)}) copy-start(bf16[5,2,4,16,2048]{4,3,2,1,0:T(8,128)(2,1)S(1)} %collective-permute-done.11.recv.refs_2_.refs_3_) | copy-start | bytes 7864324
  53.0 30.0 %copy-start.1 = (bf16[12,4,16,2048]{3,2,1,0:T(8,128)(2,1)}, bf16[12,4,16,2048]{3,2,1,0:T(8,128)(2,1)S(1)}, u32[]{:S(2)}) copy-start(bf16[12,4,16,2048]{3,2,1,0:T(8,128)(2,1)S(1)} %shard_map.55) | copy-start | bytes 9437188
  53.0 6.2 %collective-permute-start.15 = (bf16[6,2,4,16,2048]{4,3,2,1,0:T(8,128)(2,1)S(1)}, bf16[6,2,4,16,2048]{4,3,2,1,0:T(8,128)(2,1)S(1)}, u32[]{:S(2)}, u32[]{:S(2)}) collective-permute-start(bf16[6,2,4,16,2048]{4,3,2,1,0:T(8,128)(2,1)S(1)} %bitcast.14), channel_id=1, source_target_pairs={{0,8},{8,0},{1,9},{9,1},{2,10},{10,2},{3,11},{11,3},{16,24},{24,16... | collective-permute-start | bytes 9437192 | tf_op jit(solution)/shard_map/ppermute | solution.py:39
  54.1 21.1 %collective-permute-start.12 = (bf16[4,4,16,2048]{3,2,1,0:T(8,128)(2,1)S(1)}, bf16[4,4,16,2048]{3,2,1,0:T(8,128)(2,1)S(1)}, u32[]{:S(2)}, u32[]{:S(2)}) collective-permute-start(bf16[4,4,16,2048]{3,2,1,0:T(8,128)(2,1)S(1)} %get-tuple-element.70), channel_id=1, source_target_pairs={{0,1},{8,24},{1,2},{9,25},{2,3},{10,26},{3,0},{11,27},{16,17},{24,... | collective-permute-start | bytes 3145736 | tf_op jit(solution)/shard_map/ppermute | solution.py:39
  55.3 19.9 %collective-permute-start.13 = (bf16[4,4,16,2048]{3,2,1,0:T(8,128)(2,1)S(1)}, bf16[4,4,16,2048]{3,2,1,0:T(8,128)(2,1)S(1)}, u32[]{:S(2)}, u32[]{:S(2)}) collective-permute-start(bf16[4,4,16,2048]{3,2,1,0:T(8,128)(2,1)S(1)} %get-tuple-element.71), channel_id=1, source_target_pairs={{0,3},{8,56},{1,0},{9,57},{2,1},{10,58},{3,2},{11,59},{16,19},{24,... | collective-permute-start | bytes 3145736 | tf_op jit(solution)/shard_map/ppermute | solution.py:39
  56.9 18.3 %collective-permute-start.14 = (bf16[2,4,16,2048]{3,2,1,0:T(8,128)(2,1)S(1)}, bf16[2,4,16,2048]{3,2,1,0:T(8,128)(2,1)S(1)}, u32[]{:S(2)}, u32[]{:S(2)}) collective-permute-start(bf16[2,4,16,2048]{3,2,1,0:T(8,128)(2,1)S(1)} %collective-permute-done.8.refs_2_), channel_id=1, source_target_pairs={{0,2},{8,40},{1,3},{9,41},{2,0},{10,42},{3,1},{11,43},{16,18},{24,... | collective-permute-start | bytes 1572872 | tf_op jit(solution)/shard_map/ppermute | solution.py:39
  59.3 23.8 %copy-start.4 = (bf16[6,2,4,16,2048]{4,3,2,1,0:T(8,128)(2,1)}, bf16[6,2,4,16,2048]{4,3,2,1,0:T(8,128)(2,1)S(1)}, u32[]{:S(2)}) copy-start(bf16[6,2,4,16,2048]{4,3,2,1,0:T(8,128)(2,1)S(1)} %collective-permute-done.15.refs_3_.refs_4_) | copy-start | bytes 9437188
  75.4 7.7 %copy-start.2 = (bf16[10,4,16,2048]{3,2,1,0:T(8,128)(2,1)}, bf16[10,4,16,2048]{3,2,1,0:T(8,128)(2,1)S(1)}, u32[]{:S(2)}) copy-start(bf16[10,4,16,2048]{3,2,1,0:T(8,128)(2,1)S(1)} %shard_map.58) | copy-start | bytes 7864324
  75.4 7.7 %collective-permute-start.16 = (bf16[5,2,4,16,2048]{4,3,2,1,0:T(8,128)(2,1)S(1)}, bf16[5,2,4,16,2048]{4,3,2,1,0:T(8,128)(2,1)S(1)}, u32[]{:S(2)}, u32[]{:S(2)}) collective-permute-start(bf16[5,2,4,16,2048]{4,3,2,1,0:T(8,128)(2,1)S(1)} %bitcast.18), channel_id=1, source_target_pairs={{0,8},{8,0},{1,9},{9,1},{2,10},{10,2},{3,11},{11,3},{16,24},{24,16... | collective-permute-start | bytes 7864328 | tf_op jit(solution)/shard_map/ppermute | solution.py:39
  79.2 3.9 %collective-permute-start.17 = (f32[256,640]{1,0:T(8,128)S(1)}, f32[256,640]{1,0:T(8,128)S(1)}, u32[]{:S(2)}, u32[]{:S(2)}) collective-permute-start(f32[256,640]{1,0:T(8,128)S(1)} %shard_map.59.refs_12_), channel_id=1, source_target_pairs={{0,8},{8,0},{1,9},{9,1},{2,10},{10,2},{3,11},{11,3},{16,24},{24,16... | collective-permute-start | bytes 1966088 | tf_op jit(solution)/shard_map/ppermute | solution.py:39
  83.1 3.0 %copy-start.5 = (bf16[5,2,4,16,2048]{4,3,2,1,0:T(8,128)(2,1)}, bf16[5,2,4,16,2048]{4,3,2,1,0:T(8,128)(2,1)S(1)}, u32[]{:S(2)}) copy-start(bf16[5,2,4,16,2048]{4,3,2,1,0:T(8,128)(2,1)S(1)} %collective-permute-done.16.refs_5_) | copy-start | bytes 7864324
  86.0 18.9 %all-to-all-start = ((f32[8,256,128]{2,1,0:T(8,128)}), f32[8,256,128]{2,1,0:T(8,128)S(1)}, u32[]{:S(2)}, u32[]{:S(2)}) async-start(f32[8,256,128]{2,1,0:T(8,128)} %get-tuple-element.87), calls=%async_computation | async-start | bytes 2097152 | tf_op jit(solution)/shard_map/all_to_all | solution.py:495

commit v7 on v6

--- a/solution.py
+++ b/solution.py
@@ -184,7 +184,7 @@
 
 
 def ones_beside(block):
-    return jnp.concatenate([block, jnp.ones((block.shape[0], 128), BF16)], axis=1)
+    return jnp.concatenate([block, jnp.ones((block.shape[0], 16), BF16)], axis=1)
 
 
 def score_of(comps, block):

time: 106 us -> 106 us (level)
  transfers between devices with their start and end apart: 19 -> 19, of which waited for: 12 -> 13; matrix products, arithmetic and copies ran while one was open for 0% -> 0% of each run, Pallas kernels for 26% -> 26%
where the time goes in v7:
time: 106 us; the launch traced here: 105 us
  waiting for transfers between devices  44.3 us (42%)
  Pallas kernels  30.7 us (29%)
  starting transfers between devices  28.7 us (27%)
    ppermute x18, waiting for transfers between devices, permute(): return lax.ppermute(value, AXES, pairs)  44 us
    ppermute x18, starting transfers between devices, permute(): return lax.ppermute(value, AXES, pairs)  25.1 us
    pallas_call x1, Pallas kernels, gram(): pl.pallas_call(gram_kernel, out_shape=jax.ShapeDtypeStruct((HALF, PANEL),...  14.6 us
    pallas_call x1, Pallas kernels, soon_part(): pl.pallas_call(soon_kernel, out_shape=[jax.ShapeDtypeStruct((COMPS, len(S...  7.11 us
    all_to_all x1, starting transfers between devices, on_device(): parts = lax.all_to_all(parts, 'bcol', 0, 0, tiled=True)  3.56 us
    pallas_call x1, Pallas kernels, last_part(): pl.pallas_call(last_kernel, out_shape=[jax.ShapeDtypeStruct((8, COMPS, 12...  2.91 us
    pallas_call x1, Pallas kernels, early_part(): pl.pallas_call(early_kernel, out_shape=[jax.ShapeDtypeStruct((COMPS, len(...  2.31 us
  transfers between devices with their start and end apart: 19, of which 13 were waited for; matrix products, arithmetic and copies ran while one was open for 0% of the time, Pallas kernels for 26%

profile of v7, /device:TPU:1, one launch (start us, length us, event | category | flops | bytes accessed | tf_op | source)
XLA Modules:
  0.0 105.3 jit_solution(5269721386109077289)
XLA Ops:
  0.6 1.5 %collective-permute-start = (bf16[16,16384]{1,0:T(8,128)(2,1)}, bf16[16,16384]{1,0:T(8,128)(2,1)S(1)}, u32[]{:S(2)}, u32[]{:S(2)}) collective-permute-start(bf16[16,16384]{1,0:T(8,128)(2,1)} %mine.1), channel_id=1, source_target_pairs={{0,8},{8,0},{1,9},{9,1},{2,10},{10,2},{3,11},{11,3},{16,24},{24,16... | collective-permute-start | bytes 1572872 | tf_op jit(solution)/shard_map/ppermute | solution.py:39
  2.1 1.1 %shard_map.49 = (bf16[2,16,2048]{2,1,0:T(8,128)(2,1)S(1)}, bf16[2,16,2048]{2,1,0:T(8,128)(2,1)S(1)}, bf16[2,16,2048]{2,1,0:T(8,128)(2,1)S(1)}, bf16[2,16,2048]{2,1,0:T(8,128)(2,1)S(1)}) custom-call(s32[1]{0:T(128)} %bitcast.2.place, bf16[16,16384]{1,0:T(8,128)(2,1)} %mine.1), custom_call_target="tpu_custom_call" | custom-call | tf_op jit(solution)/shard_map/pallas_call | solution.py:76
  4.0 1.8 %collective-permute-start.1 = (bf16[2,2,16,2048]{3,2,1,0:T(8,128)(2,1)S(1)}, bf16[2,2,16,2048]{3,2,1,0:T(8,128)(2,1)S(1)}, u32[]{:S(2)}, u32[]{:S(2)}) collective-permute-start(bf16[2,2,16,2048]{3,2,1,0:T(8,128)(2,1)S(1)} %get-tuple-element.51), channel_id=1, source_target_pairs={{0,16},{8,9},{1,17},{9,10},{2,18},{10,11},{3,19},{11,8},{16,32},{2... | collective-permute-start | bytes 786440 | tf_op jit(solution)/shard_map/ppermute | solution.py:39
  5.7 2.2 %collective-permute-start.2 = (bf16[2,2,16,2048]{3,2,1,0:T(8,128)(2,1)S(1)}, bf16[2,2,16,2048]{3,2,1,0:T(8,128)(2,1)S(1)}, u32[]{:S(2)}, u32[]{:S(2)}) collective-permute-start(bf16[2,2,16,2048]{3,2,1,0:T(8,128)(2,1)S(1)} %get-tuple-element.52), channel_id=1, source_target_pairs={{0,48},{8,11},{1,49},{9,8},{2,50},{10,9},{3,51},{11,10},{16,0},{24... | collective-permute-start | bytes 786440 | tf_op jit(solution)/shard_map/ppermute | solution.py:39
  7.9 1.2 %collective-permute-start.3 = (bf16[2,2,16,2048]{3,2,1,0:T(8,128)(2,1)S(1)}, bf16[2,2,16,2048]{3,2,1,0:T(8,128)(2,1)S(1)}, u32[]{:S(2)}, u32[]{:S(2)}) collective-permute-start(bf16[2,2,16,2048]{3,2,1,0:T(8,128)(2,1)S(1)} %get-tuple-element.53), channel_id=1, source_target_pairs={{0,32},{8,10},{1,33},{9,11},{2,34},{10,8},{3,35},{11,9},{16,48},{2... | collective-permute-start | bytes 786440 | tf_op jit(solution)/shard_map/ppermute | solution.py:39
  9.2 2.5 %collective-permute-done.1.refs_1_ = bf16[2,2,16,2048]{3,2,1,0:T(8,128)(2,1)S(1)} collective-permute-done((bf16[2,2,16,2048]{3,2,1,0:T(8,128)(2,1)S(1)}, bf16[2,2,16,2048]{3,2,1,0:T(8,128)(2,1)S(1)}, u32[]{:S(2)}, u32[]{:S(2)}) %collective-permute-start.1) | collective-permute-done | bytes 262176 | tf_op jit(solution)/shard_map/ppermute | solution.py:39
  11.6 2.4 %collective-permute-done.2.refs_2_ = bf16[2,2,16,2048]{3,2,1,0:T(8,128)(2,1)S(1)} collective-permute-done((bf16[2,2,16,2048]{3,2,1,0:T(8,128)(2,1)S(1)}, bf16[2,2,16,2048]{3,2,1,0:T(8,128)(2,1)S(1)}, u32[]{:S(2)}, u32[]{:S(2)}) %collective-permute-start.2) | collective-permute-done | bytes 262176 | tf_op jit(solution)/shard_map/ppermute | solution.py:39
  14.1 1.6 %collective-permute-done.3.refs_3_ = bf16[2,2,16,2048]{3,2,1,0:T(8,128)(2,1)S(1)} collective-permute-done((bf16[2,2,16,2048]{3,2,1,0:T(8,128)(2,1)S(1)}, bf16[2,2,16,2048]{3,2,1,0:T(8,128)(2,1)S(1)}, u32[]{:S(2)}, u32[]{:S(2)}) %collective-permute-start.3) | collective-permute-done | bytes 262176 | tf_op jit(solution)/shard_map/ppermute | solution.py:39
  15.9 1.3 %collective-permute-start.4 = (bf16[2,4,16,2048]{3,2,1,0:T(8,128)(2,1)S(1)}, bf16[2,4,16,2048]{3,2,1,0:T(8,128)(2,1)S(1)}, u32[]{:S(2)}, u32[]{:S(2)}) collective-permute-start(bf16[2,4,16,2048]{3,2,1,0:T(8,128)(2,1)S(1)} %get-tuple-element.55), channel_id=1, source_target_pairs={{0,4},{8,12},{1,5},{9,13},{2,6},{10,14},{3,7},{11,15},{16,20},{24,... | collective-permute-start | bytes 1572872 | tf_op jit(solution)/shard_map/ppermute | solution.py:39
  17.1 1.8 %collective-permute-start.5 = (bf16[2,4,16,2048]{3,2,1,0:T(8,128)(2,1)S(1)}, bf16[2,4,16,2048]{3,2,1,0:T(8,128)(2,1)S(1)}, u32[]{:S(2)}, u32[]{:S(2)}) collective-permute-start(bf16[2,4,16,2048]{3,2,1,0:T(8,128)(2,1)S(1)} %get-tuple-element.56), channel_id=1, source_target_pairs={{0,68},{8,76},{1,69},{9,77},{2,70},{10,78},{3,71},{11,79},{16,84},... | collective-permute-start | bytes 1572872 | tf_op jit(solution)/shard_map/ppermute | solution.py:39
  19.0 2.6 %collective-permute-start.7 = (bf16[2,4,16,2048]{3,2,1,0:T(8,128)(2,1)S(1)}, bf16[2,4,16,2048]{3,2,1,0:T(8,128)(2,1)S(1)}, u32[]{:S(2)}, u32[]{:S(2)}) collective-permute-start(bf16[2,4,16,2048]{3,2,1,0:T(8,128)(2,1)S(1)} %get-tuple-element.54.refs_0_), channel_id=1, source_target_pairs={{0,3},{8,56},{1,0},{9,57},{2,1},{10,58},{3,2},{11,59},{16,19},{24,... | collective-permute-start | bytes 1572872 | tf_op jit(solution)/shard_map/ppermute | solution.py:39
  21.6 7.5 %collective-permute-done.4.refs_3_.refs_0_ = bf16[2,4,16,2048]{3,2,1,0:T(8,128)(2,1)S(1)} collective-permute-done((bf16[2,4,16,2048]{3,2,1,0:T(8,128)(2,1)S(1)}, bf16[2,4,16,2048]{3,2,1,0:T(8,128)(2,1)S(1)}, u32[]{:S(2)}, u32[]{:S(2)}) %collective-permute-start.4) | collective-permute-done | bytes 524320 | tf_op jit(solution)/shard_map/ppermute | solution.py:39
  29.0 2.1 %collective-permute-done.5.refs_4_.refs_1_ = bf16[2,4,16,2048]{3,2,1,0:T(8,128)(2,1)S(1)} collective-permute-done((bf16[2,4,16,2048]{3,2,1,0:T(8,128)(2,1)S(1)}, bf16[2,4,16,2048]{3,2,1,0:T(8,128)(2,1)S(1)}, u32[]{:S(2)}, u32[]{:S(2)}) %collective-permute-start.5) | collective-permute-done | bytes 524320 | tf_op jit(solution)/shard_map/ppermute | solution.py:39
  31.3 3.3 %collective-permute-start.11 = (bf16[5,2,4,16,2048]{4,3,2,1,0:T(8,128)(2,1)S(1)}, bf16[5,2,4,16,2048]{4,3,2,1,0:T(8,128)(2,1)S(1)}, u32[]{:S(2)}, u32[]{:S(2)}) collective-permute-start(bf16[5,2,4,16,2048]{4,3,2,1,0:T(8,128)(2,1)S(1)} %bitcast.9), channel_id=1, source_target_pairs={{0,8},{8,0},{1,9},{9,1},{2,10},{10,2},{3,11},{11,3},{16,24},{24,16... | collective-permute-start | bytes 7864328 | tf_op jit(solution)/shard_map/ppermute | solution.py:39
  34.8 1.2 %collective-permute-start.9 = (bf16[5,4,16,2048]{3,2,1,0:T(8,128)(2,1)S(1)}, bf16[5,4,16,2048]{3,2,1,0:T(8,128)(2,1)S(1)}, u32[]{:S(2)}, u32[]{:S(2)}) collective-permute-start(bf16[5,4,16,2048]{3,2,1,0:T(8,128)(2,1)S(1)} %get-tuple-element.63), channel_id=1, source_target_pairs={{0,1},{8,24},{1,2},{9,25},{2,3},{10,26},{3,0},{11,27},{16,17},{24,... | collective-permute-start | bytes 3932168 | tf_op jit(solution)/shard_map/ppermute | solution.py:39
  36.0 1.5 %collective-permute-start.10 = (bf16[5,4,16,2048]{3,2,1,0:T(8,128)(2,1)S(1)}, bf16[5,4,16,2048]{3,2,1,0:T(8,128)(2,1)S(1)}, u32[]{:S(2)}, u32[]{:S(2)}) collective-permute-start(bf16[5,4,16,2048]{3,2,1,0:T(8,128)(2,1)S(1)} %get-tuple-element.64), channel_id=1, source_target_pairs={{0,3},{8,56},{1,0},{9,57},{2,1},{10,58},{3,2},{11,59},{16,19},{24,... | collective-permute-start | bytes 3932168 | tf_op jit(solution)/shard_map/ppermute | solution.py:39
  37.9 1.3 %collective-permute-done.11.recv.refs_2_.refs_3_ = bf16[5,2,4,16,2048]{4,3,2,1,0:T(8,128)(2,1)S(1)} collective-permute-done((bf16[5,2,4,16,2048]{4,3,2,1,0:T(8,128)(2,1)S(1)}, bf16[5,2,4,16,2048]{4,3,2,1,0:T(8,128)(2,1)S(1)}, u32[]{:S(2)}, u32[]{:S(2)}) %collective-permute-start.11) | collective-permute-done | bytes 2621472 | tf_op jit(solution)/shard_map/ppermute | solution.py:39
  39.2 2.3 %shard_map.54 = (f32[256,640]{1,0:T(8,128)S(1)}, f32[256,128]{1,0:T(8,128)S(1)}, bf16[2048,512]{1,0:T(8,128)(2,1)S(1)}) custom-call(s32[1]{0:T(128)} %bitcast.core.at, bf16[5,2,4,16,2048]{4,3,2,1,0:T(8,128)(2,1)S(1)} %bitcast.10, bf16[5,2,4,16,2048]{4,3,2,1,0:T(8,128)(2,1)S(1)} %collective-permute-done.11.recv.refs_2_.refs_3_, f32[2048,256]{1,0:T(8,128)S(1)} %copy-done.6), custom_call_target="tpu_custom_call" | custom-call | flops 1073741824 | bytes 1048576 | tf_op jit(solution)/shard_map/pallas_call | solution.py:231
  41.5 10.5 %collective-permute-done.8.refs_2_ = bf16[2,4,16,2048]{3,2,1,0:T(8,128)(2,1)S(1)} collective-permute-done((bf16[2,4,16,2048]{3,2,1,0:T(8,128)(2,1)S(1)}, bf16[2,4,16,2048]{3,2,1,0:T(8,128)(2,1)S(1)}, u32[]{:S(2)}, u32[]{:S(2)}) %collective-permute-start.8) | collective-permute-done | bytes 524320 | tf_op jit(solution)/shard_map/ppermute | solution.py:39
  51.9 0.9 collective-permute-done.9.refs_0_
  53.0 1.0 collective-permute-start.15
  54.1 1.2 %collective-permute-start.12 = (bf16[4,4,16,2048]{3,2,1,0:T(8,128)(2,1)S(1)}, bf16[4,4,16,2048]{3,2,1,0:T(8,128)(2,1)S(1)}, u32[]{:S(2)}, u32[]{:S(2)}) collective-permute-start(bf16[4,4,16,2048]{3,2,1,0:T(8,128)(2,1)S(1)} %get-tuple-element.70), channel_id=1, source_target_pairs={{0,1},{8,24},{1,2},{9,25},{2,3},{10,26},{3,0},{11,27},{16,17},{24,... | collective-permute-start | bytes 3145736 | tf_op jit(solution)/shard_map/ppermute | solution.py:39
  55.3 1.5 %collective-permute-start.13 = (bf16[4,4,16,2048]{3,2,1,0:T(8,128)(2,1)S(1)}, bf16[4,4,16,2048]{3,2,1,0:T(8,128)(2,1)S(1)}, u32[]{:S(2)}, u32[]{:S(2)}) collective-permute-start(bf16[4,4,16,2048]{3,2,1,0:T(8,128)(2,1)S(1)} %get-tuple-element.71), channel_id=1, source_target_pairs={{0,3},{8,56},{1,0},{9,57},{2,1},{10,58},{3,2},{11,59},{16,19},{24,... | collective-permute-start | bytes 3145736 | tf_op jit(solution)/shard_map/ppermute | solution.py:39
  57.2 2.1 %collective-permute-done.15.refs_3_.refs_4_ = bf16[6,2,4,16,2048]{4,3,2,1,0:T(8,128)(2,1)S(1)} collective-permute-done((bf16[6,2,4,16,2048]{4,3,2,1,0:T(8,128)(2,1)S(1)}, bf16[6,2,4,16,2048]{4,3,2,1,0:T(8,128)(2,1)S(1)}, u32[]{:S(2)}, u32[]{:S(2)}) %collective-permute-start.15) | collective-permute-done | bytes 3145760 | tf_op jit(solution)/shard_map/ppermute | solution.py:39
  59.3 7.1 %shard_map.57 = (f32[256,768]{1,0:T(8,128)S(1)}, f32[256,1024]{1,0:T(8,128)S(1)}, f32[1,1024]{1,0:T(1,128)S(1)}, bf16[528,256]{1,0:T(8,128)(2,1)S(1)}) custom-call(s32[1]{0:T(128)} %bitcast.core.at, bf16[5,2,4,16,2048]{4,3,2,1,0:T(8,128)(2,1)S(1)} %bitcast.11, bf16[6,2,4,16,2048]{4,3,2,1,0:T(8,128)(2,1)S(1)} %bitcast.15, ...), custom_call_target="tpu_custom_call" | custom-call | flops 2147483648 | bytes 1048576 | tf_op jit(solution)/shard_map/pallas_call | solution.py:294
  66.4 8.8 %collective-permute-done.14.refs_2_ = bf16[2,4,16,2048]{3,2,1,0:T(8,128)(2,1)S(1)} collective-permute-done((bf16[2,4,16,2048]{3,2,1,0:T(8,128)(2,1)S(1)}, bf16[2,4,16,2048]{3,2,1,0:T(8,128)(2,1)S(1)}, u32[]{:S(2)}, u32[]{:S(2)}) %collective-permute-start.14) | collective-permute-done | bytes 524320 | tf_op jit(solution)/shard_map/ppermute | solution.py:39
  75.4 2.2 %collective-permute-start.16 = (bf16[5,2,4,16,2048]{4,3,2,1,0:T(8,128)(2,1)S(1)}, bf16[5,2,4,16,2048]{4,3,2,1,0:T(8,128)(2,1)S(1)}, u32[]{:S(2)}, u32[]{:S(2)}) collective-permute-start(bf16[5,2,4,16,2048]{4,3,2,1,0:T(8,128)(2,1)S(1)} %bitcast.18), channel_id=1, source_target_pairs={{0,8},{8,0},{1,9},{9,1},{2,10},{10,2},{3,11},{11,3},{16,24},{24,16... | collective-permute-start | bytes 7864328 | tf_op jit(solution)/shard_map/ppermute | solution.py:39
  77.6 1.6 %shard_map.59.refs_12_ = f32[256,640]{1,0:T(8,128)S(1)} custom-call(bf16[5,2,4,16,2048]{4,3,2,1,0:T(8,128)(2,1)S(1)} %bitcast.19, bf16[2048,512]{1,0:T(8,128)(2,1)S(1)} %get-tuple-element.72.refs_4_.comps), custom_call_target="tpu_custom_call" | custom-call | flops 1073741824 | bytes 1048576 | tf_op jit(solution)/shard_map/pallas_call | solution.py:318
  79.3 3.8 %collective-permute-done.17.refs_13_ = f32[256,640]{1,0:T(8,128)S(1)} collective-permute-done((f32[256,640]{1,0:T(8,128)S(1)}, f32[256,640]{1,0:T(8,128)S(1)}, u32[]{:S(2)}, u32[]{:S(2)}) %collective-permute-start.17) | collective-permute-done | bytes 655392 | tf_op jit(solution)/shard_map/ppermute | solution.py:39
  83.1 2.9 %shard_map.60 = (f32[8,256,128]{2,1,0:T(8,128)}, f32[1,1024]{1,0:T(1,128)S(1)}, f32[1,128]{1,0:T(1,128)}) custom-call(s32[1]{0:T(128)} %bitcast.core.at, s32[1]{0:T(128)} %bitcast.6.column, bf16[5,2,4,16,2048]{4,3,2,1,0:T(8,128)(2,1)S(1)} %bitcast.12, bf16[6,2,4,16,2048]{4,3,2,1,0:T(8,128)(2,1)S(1)} %bitcast.16, bf16[5,2,4,16,2048]{4,3,2,1,0:T(8,128)(2,1)S(1)} %bitcast.20, ...), custom_call_target="tpu_custom_call" | custom-call | flops 4294967296 | bytes 4194304 | tf_op jit(solution)/shard_map/pallas_call | solution.py:372
  86.0 3.6 %all-to-all-start = ((f32[8,256,128]{2,1,0:T(8,128)}), f32[8,256,128]{2,1,0:T(8,128)S(1)}, u32[]{:S(2)}, u32[]{:S(2)}) async-start(f32[8,256,128]{2,1,0:T(8,128)} %get-tuple-element.87), calls=%async_computation | async-start | bytes 2097152 | tf_op jit(solution)/shard_map/all_to_all | solution.py:495
  89.6 14.6 %shard_map.61 = f32[1024,2048]{1,0:T(8,128)} custom-call(s32[1]{0:T(128)} %bitcast.core.at, bf16[5,2,4,16,2048]{4,3,2,1,0:T(8,128)(2,1)} %bitcast.13, bf16[6,2,4,16,2048]{4,3,2,1,0:T(8,128)(2,1)} %bitcast.17, bf16[5,2,4,16,2048]{4,3,2,1,0:T(8,128)(2,1)} %bitcast.21, bf16[5,2,4,16,2048]{4,3,2,1,0:T(8,128)(2,1)} %copy-done.3, ...), custom_call_target="tpu_custom_call" | custom-call | flops 8589934592 | bytes 20971520 | tf_op jit(solution)/shard_map/pallas_call | solution.py:432
  (35 shorter events, 3.6 us)
Async XLA Ops:
  0.6 3.2 %collective-permute-start = (bf16[16,16384]{1,0:T(8,128)(2,1)}, bf16[16,16384]{1,0:T(8,128)(2,1)S(1)}, u32[]{:S(2)}, u32[]{:S(2)}) collective-permute-start(bf16[16,16384]{1,0:T(8,128)(2,1)} %mine.1), channel_id=1, source_target_pairs={{0,8},{8,0},{1,9},{9,1},{2,10},{10,2},{3,11},{11,3},{16,24},{24,16... | collective-permute-start | bytes 1572872 | tf_op jit(solution)/shard_map/ppermute | solution.py:39
  4.0 7.7 %collective-permute-start.1 = (bf16[2,2,16,2048]{3,2,1,0:T(8,128)(2,1)S(1)}, bf16[2,2,16,2048]{3,2,1,0:T(8,128)(2,1)S(1)}, u32[]{:S(2)}, u32[]{:S(2)}) collective-permute-start(bf16[2,2,16,2048]{3,2,1,0:T(8,128)(2,1)S(1)} %get-tuple-element.51), channel_id=1, source_target_pairs={{0,16},{8,9},{1,17},{9,10},{2,18},{10,11},{3,19},{11,8},{16,32},{2... | collective-permute-start | bytes 786440 | tf_op jit(solution)/shard_map/ppermute | solution.py:39
  5.7 8.3 %collective-permute-start.2 = (bf16[2,2,16,2048]{3,2,1,0:T(8,128)(2,1)S(1)}, bf16[2,2,16,2048]{3,2,1,0:T(8,128)(2,1)S(1)}, u32[]{:S(2)}, u32[]{:S(2)}) collective-permute-start(bf16[2,2,16,2048]{3,2,1,0:T(8,128)(2,1)S(1)} %get-tuple-element.52), channel_id=1, source_target_pairs={{0,48},{8,11},{1,49},{9,8},{2,50},{10,9},{3,51},{11,10},{16,0},{24... | collective-permute-start | bytes 786440 | tf_op jit(solution)/shard_map/ppermute | solution.py:39
  7.9 7.8 %collective-permute-start.3 = (bf16[2,2,16,2048]{3,2,1,0:T(8,128)(2,1)S(1)}, bf16[2,2,16,2048]{3,2,1,0:T(8,128)(2,1)S(1)}, u32[]{:S(2)}, u32[]{:S(2)}) collective-permute-start(bf16[2,2,16,2048]{3,2,1,0:T(8,128)(2,1)S(1)} %get-tuple-element.53), channel_id=1, source_target_pairs={{0,32},{8,10},{1,33},{9,11},{2,34},{10,8},{3,35},{11,9},{16,48},{2... | collective-permute-start | bytes 786440 | tf_op jit(solution)/shard_map/ppermute | solution.py:39
  15.9 13.2 %collective-permute-start.4 = (bf16[2,4,16,2048]{3,2,1,0:T(8,128)(2,1)S(1)}, bf16[2,4,16,2048]{3,2,1,0:T(8,128)(2,1)S(1)}, u32[]{:S(2)}, u32[]{:S(2)}) collective-permute-start(bf16[2,4,16,2048]{3,2,1,0:T(8,128)(2,1)S(1)} %get-tuple-element.55), channel_id=1, source_target_pairs={{0,4},{8,12},{1,5},{9,13},{2,6},{10,14},{3,7},{11,15},{16,20},{24,... | collective-permute-start | bytes 1572872 | tf_op jit(solution)/shard_map/ppermute | solution.py:39
  17.1 14.0 %collective-permute-start.5 = (bf16[2,4,16,2048]{3,2,1,0:T(8,128)(2,1)S(1)}, bf16[2,4,16,2048]{3,2,1,0:T(8,128)(2,1)S(1)}, u32[]{:S(2)}, u32[]{:S(2)}) collective-permute-start(bf16[2,4,16,2048]{3,2,1,0:T(8,128)(2,1)S(1)} %get-tuple-element.56), channel_id=1, source_target_pairs={{0,68},{8,76},{1,69},{9,77},{2,70},{10,78},{3,71},{11,79},{16,84},... | collective-permute-start | bytes 1572872 | tf_op jit(solution)/shard_map/ppermute | solution.py:39
  19.0 12.2 %collective-permute-start.7 = (bf16[2,4,16,2048]{3,2,1,0:T(8,128)(2,1)S(1)}, bf16[2,4,16,2048]{3,2,1,0:T(8,128)(2,1)S(1)}, u32[]{:S(2)}, u32[]{:S(2)}) collective-permute-start(bf16[2,4,16,2048]{3,2,1,0:T(8,128)(2,1)S(1)} %get-tuple-element.54.refs_0_), channel_id=1, source_target_pairs={{0,3},{8,56},{1,0},{9,57},{2,1},{10,58},{3,2},{11,59},{16,19},{24,... | collective-permute-start | bytes 1572872 | tf_op jit(solution)/shard_map/ppermute | solution.py:39
  21.6 9.6 %collective-permute-start.6 = (bf16[2,4,16,2048]{3,2,1,0:T(8,128)(2,1)S(1)}, bf16[2,4,16,2048]{3,2,1,0:T(8,128)(2,1)S(1)}, u32[]{:S(2)}, u32[]{:S(2)}) collective-permute-start(bf16[2,4,16,2048]{3,2,1,0:T(8,128)(2,1)S(1)} %get-tuple-element.54.refs_0_), channel_id=1, source_target_pairs={{0,1},{8,24},{1,2},{9,25},{2,3},{10,26},{3,0},{11,27},{16,17},{24,... | collective-permute-start | bytes 1572872 | tf_op jit(solution)/shard_map/ppermute | solution.py:39
  31.2 8.0 %copy-start.6 = (f32[2048,256]{1,0:T(8,128)S(1)}, f32[2048,256]{1,0:T(8,128)}, u32[]{:S(2)}) copy-start(f32[2048,256]{1,0:T(8,128)} %components.1) | copy-start | bytes 6291460
  31.3 51.7 %copy-start = (bf16[10,4,16,2048]{3,2,1,0:T(8,128)(2,1)}, bf16[10,4,16,2048]{3,2,1,0:T(8,128)(2,1)S(1)}, u32[]{:S(2)}) copy-start(bf16[10,4,16,2048]{3,2,1,0:T(8,128)(2,1)S(1)} %shard_map.52) | copy-start | bytes 7864324
  31.3 7.8 %collective-permute-start.11 = (bf16[5,2,4,16,2048]{4,3,2,1,0:T(8,128)(2,1)S(1)}, bf16[5,2,4,16,2048]{4,3,2,1,0:T(8,128)(2,1)S(1)}, u32[]{:S(2)}, u32[]{:S(2)}) collective-permute-start(bf16[5,2,4,16,2048]{4,3,2,1,0:T(8,128)(2,1)S(1)} %bitcast.9), channel_id=1, source_target_pairs={{0,8},{8,0},{1,9},{9,1},{2,10},{10,2},{3,11},{11,3},{16,24},{24,16... | collective-permute-start | bytes 7864328 | tf_op jit(solution)/shard_map/ppermute | solution.py:39
  34.8 18.0 %collective-permute-start.9 = (bf16[5,4,16,2048]{3,2,1,0:T(8,128)(2,1)S(1)}, bf16[5,4,16,2048]{3,2,1,0:T(8,128)(2,1)S(1)}, u32[]{:S(2)}, u32[]{:S(2)}) collective-permute-start(bf16[5,4,16,2048]{3,2,1,0:T(8,128)(2,1)S(1)} %get-tuple-element.63), channel_id=1, source_target_pairs={{0,1},{8,24},{1,2},{9,25},{2,3},{10,26},{3,0},{11,27},{16,17},{24,... | collective-permute-start | bytes 3932168 | tf_op jit(solution)/shard_map/ppermute | solution.py:39
  36.0 16.8 %collective-permute-start.10 = (bf16[5,4,16,2048]{3,2,1,0:T(8,128)(2,1)S(1)}, bf16[5,4,16,2048]{3,2,1,0:T(8,128)(2,1)S(1)}, u32[]{:S(2)}, u32[]{:S(2)}) collective-permute-start(bf16[5,4,16,2048]{3,2,1,0:T(8,128)(2,1)S(1)} %get-tuple-element.64), channel_id=1, source_target_pairs={{0,3},{8,56},{1,0},{9,57},{2,1},{10,58},{3,2},{11,59},{16,19},{24,... | collective-permute-start | bytes 3932168 | tf_op jit(solution)/shard_map/ppermute | solution.py:39
  37.5 14.4 %collective-permute-start.8 = (bf16[2,4,16,2048]{3,2,1,0:T(8,128)(2,1)S(1)}, bf16[2,4,16,2048]{3,2,1,0:T(8,128)(2,1)S(1)}, u32[]{:S(2)}, u32[]{:S(2)}) collective-permute-start(bf16[2,4,16,2048]{3,2,1,0:T(8,128)(2,1)S(1)} %get-tuple-element.62), channel_id=1, source_target_pairs={{0,64},{8,72},{1,65},{9,73},{2,66},{10,74},{3,67},{11,75},{16,80},... | collective-permute-start | bytes 1572872 | tf_op jit(solution)/shard_map/ppermute | solution.py:39
  39.2 43.9 %copy-start.3 = (bf16[5,2,4,16,2048]{4,3,2,1,0:T(8,128)(2,1)}, bf16[5,2,4,16,2048]{4,3,2,1,0:T(8,128)(2,1)S(1)}, u32[]{:S(2)}) copy-start(bf16[5,2,4,16,2048]{4,3,2,1,0:T(8,128)(2,1)S(1)} %collective-permute-done.11.recv.refs_2_.refs_3_) | copy-start | bytes 7864324
  53.0 30.0 %copy-start.1 = (bf16[12,4,16,2048]{3,2,1,0:T(8,128)(2,1)}, bf16[12,4,16,2048]{3,2,1,0:T(8,128)(2,1)S(1)}, u32[]{:S(2)}) copy-start(bf16[12,4,16,2048]{3,2,1,0:T(8,128)(2,1)S(1)} %shard_map.55) | copy-start | bytes 9437188
  53.0 6.2 %collective-permute-start.15 = (bf16[6,2,4,16,2048]{4,3,2,1,0:T(8,128)(2,1)S(1)}, bf16[6,2,4,16,2048]{4,3,2,1,0:T(8,128)(2,1)S(1)}, u32[]{:S(2)}, u32[]{:S(2)}) collective-permute-start(bf16[6,2,4,16,2048]{4,3,2,1,0:T(8,128)(2,1)S(1)} %bitcast.14), channel_id=1, source_target_pairs={{0,8},{8,0},{1,9},{9,1},{2,10},{10,2},{3,11},{11,3},{16,24},{24,16... | collective-permute-start | bytes 9437192 | tf_op jit(solution)/shard_map/ppermute | solution.py:39
  54.1 21.1 %collective-permute-start.12 = (bf16[4,4,16,2048]{3,2,1,0:T(8,128)(2,1)S(1)}, bf16[4,4,16,2048]{3,2,1,0:T(8,128)(2,1)S(1)}, u32[]{:S(2)}, u32[]{:S(2)}) collective-permute-start(bf16[4,4,16,2048]{3,2,1,0:T(8,128)(2,1)S(1)} %get-tuple-element.70), channel_id=1, source_target_pairs={{0,1},{8,24},{1,2},{9,25},{2,3},{10,26},{3,0},{11,27},{16,17},{24,... | collective-permute-start | bytes 3145736 | tf_op jit(solution)/shard_map/ppermute | solution.py:39
  55.3 19.9 %collective-permute-start.13 = (bf16[4,4,16,2048]{3,2,1,0:T(8,128)(2,1)S(1)}, bf16[4,4,16,2048]{3,2,1,0:T(8,128)(2,1)S(1)}, u32[]{:S(2)}, u32[]{:S(2)}) collective-permute-start(bf16[4,4,16,2048]{3,2,1,0:T(8,128)(2,1)S(1)} %get-tuple-element.71), channel_id=1, source_target_pairs={{0,3},{8,56},{1,0},{9,57},{2,1},{10,58},{3,2},{11,59},{16,19},{24,... | collective-permute-start | bytes 3145736 | tf_op jit(solution)/shard_map/ppermute | solution.py:39
  56.9 18.3 %collective-permute-start.14 = (bf16[2,4,16,2048]{3,2,1,0:T(8,128)(2,1)S(1)}, bf16[2,4,16,2048]{3,2,1,0:T(8,128)(2,1)S(1)}, u32[]{:S(2)}, u32[]{:S(2)}) collective-permute-start(bf16[2,4,16,2048]{3,2,1,0:T(8,128)(2,1)S(1)} %collective-permute-done.8.refs_2_), channel_id=1, source_target_pairs={{0,2},{8,40},{1,3},{9,41},{2,0},{10,42},{3,1},{11,43},{16,18},{24,... | collective-permute-start | bytes 1572872 | tf_op jit(solution)/shard_map/ppermute | solution.py:39
  59.3 23.8 %copy-start.4 = (bf16[6,2,4,16,2048]{4,3,2,1,0:T(8,128)(2,1)}, bf16[6,2,4,16,2048]{4,3,2,1,0:T(8,128)(2,1)S(1)}, u32[]{:S(2)}) copy-start(bf16[6,2,4,16,2048]{4,3,2,1,0:T(8,128)(2,1)S(1)} %collective-permute-done.15.refs_3_.refs_4_) | copy-start | bytes 9437188
  75.4 7.7 %copy-start.2 = (bf16[10,4,16,2048]{3,2,1,0:T(8,128)(2,1)}, bf16[10,4,16,2048]{3,2,1,0:T(8,128)(2,1)S(1)}, u32[]{:S(2)}) copy-start(bf16[10,4,16,2048]{3,2,1,0:T(8,128)(2,1)S(1)} %shard_map.58) | copy-start | bytes 7864324
  75.4 7.7 %collective-permute-start.16 = (bf16[5,2,4,16,2048]{4,3,2,1,0:T(8,128)(2,1)S(1)}, bf16[5,2,4,16,2048]{4,3,2,1,0:T(8,128)(2,1)S(1)}, u32[]{:S(2)}, u32[]{:S(2)}) collective-permute-start(bf16[5,2,4,16,2048]{4,3,2,1,0:T(8,128)(2,1)S(1)} %bitcast.18), channel_id=1, source_target_pairs={{0,8},{8,0},{1,9},{9,1},{2,10},{10,2},{3,11},{11,3},{16,24},{24,16... | collective-permute-start | bytes 7864328 | tf_op jit(solution)/shard_map/ppermute | solution.py:39
  79.2 3.9 %collective-permute-start.17 = (f32[256,640]{1,0:T(8,128)S(1)}, f32[256,640]{1,0:T(8,128)S(1)}, u32[]{:S(2)}, u32[]{:S(2)}) collective-permute-start(f32[256,640]{1,0:T(8,128)S(1)} %shard_map.59.refs_12_), channel_id=1, source_target_pairs={{0,8},{8,0},{1,9},{9,1},{2,10},{10,2},{3,11},{11,3},{16,24},{24,16... | collective-permute-start | bytes 1966088 | tf_op jit(solution)/shard_map/ppermute | solution.py:39
  83.1 3.0 %copy-start.5 = (bf16[5,2,4,16,2048]{4,3,2,1,0:T(8,128)(2,1)}, bf16[5,2,4,16,2048]{4,3,2,1,0:T(8,128)(2,1)S(1)}, u32[]{:S(2)}) copy-start(bf16[5,2,4,16,2048]{4,3,2,1,0:T(8,128)(2,1)S(1)} %collective-permute-done.16.refs_5_) | copy-start | bytes 7864324
  86.0 18.5 %all-to-all-start = ((f32[8,256,128]{2,1,0:T(8,128)}), f32[8,256,128]{2,1,0:T(8,128)S(1)}, u32[]{:S(2)}, u32[]{:S(2)}) async-start(f32[8,256,128]{2,1,0:T(8,128)} %get-tuple-element.87), calls=%async_computation | async-start | bytes 2097152 | tf_op jit(solution)/shard_map/all_to_all | solution.py:495

commit v8 on v7

--- a/solution.py
+++ b/solution.py
@@ -445,6 +445,23 @@
         compiler_params=pltpu.CompilerParams(vmem_limit_bytes=22 << 20),
         cost_estimate=pl.CostEstimate(flops=8 << 30, bytes_accessed=20 << 20, transcendentals=0),
     )(at, *[pltpu.with_memory_space_constraint(piece, pltpu.HBM) for piece in own + recv], row_means)
+
+
+def add_up_kernel(parts, out):
+    total = parts[0]
+    for n in range(1, parts.shape[0]):
+        total = total + parts[n]
+    out[...] = total.T
+
+
+def add_up(parts):
+    return pl.pallas_call(
+        add_up_kernel,
+        out_shape=jax.ShapeDtypeStruct(parts.shape[:0:-1], F32),
+        in_specs=[IN_VMEM],
+        out_specs=IN_VMEM,
+        compiler_params=SMALL,
+    )(parts)
 
 
 def scalar(value):
@@ -494,7 +511,7 @@
     parts, row_means, means_part = last_part(at, scalar(col), own, recv, (*early, *soon, scores, permute(scores, swap)))
     parts = lax.all_to_all(parts, "bcol", 0, 0, tiled=True)
     covariance = gram(at, own, recv, row_means)
-    projected = jnp.sum(parts, axis=0).T
+    projected = add_up(parts)
     return covariance, projected, means_part[0]
 
 

time: 106 us -> 105 us (level)
  no operation moved by 1% of the time
where the time goes in v8:
time: 105 us
  waiting for transfers between devices  44.3 us (42%)
  Pallas kernels  31.5 us (30%)
  starting transfers between devices  28.7 us (27%)
    ppermute x18, waiting for transfers between devices, permute(): return lax.ppermute(value, AXES, pairs)  44 us
    ppermute x18, starting transfers between devices, permute(): return lax.ppermute(value, AXES, pairs)  25.1 us
    pallas_call x1, Pallas kernels, gram(): pl.pallas_call(gram_kernel, out_shape=jax.ShapeDtypeStruct((HALF, PANEL),...  14.6 us
    pallas_call x1, Pallas kernels, soon_part(): pl.pallas_call(soon_kernel, out_shape=[jax.ShapeDtypeStruct((COMPS, len(S...  7.11 us
    all_to_all x1, starting transfers between devices, on_device(): parts = lax.all_to_all(parts, 'bcol', 0, 0, tiled=True)  3.56 us
    pallas_call x1, Pallas kernels, last_part(): pl.pallas_call(last_kernel, out_shape=[jax.ShapeDtypeStruct((8, COMPS, 12...  2.92 us
    pallas_call x1, Pallas kernels, early_part(): pl.pallas_call(early_kernel, out_shape=[jax.ShapeDtypeStruct((COMPS, len(...  2.31 us
  transfers between devices with their start and end apart: 19, of which 13 were waited for; matrix products, arithmetic and copies ran while one was open for 0% of the time, Pallas kernels for 26%

profile of v8, /device:TPU:1, one launch (start us, length us, event | category | flops | bytes accessed | tf_op | source)
XLA Modules:
  0.0 105.3 jit_solution(17220085357650832777)
XLA Ops:
  0.6 1.5 %collective-permute-start = (bf16[16,16384]{1,0:T(8,128)(2,1)}, bf16[16,16384]{1,0:T(8,128)(2,1)S(1)}, u32[]{:S(2)}, u32[]{:S(2)}) collective-permute-start(bf16[16,16384]{1,0:T(8,128)(2,1)} %mine.1), channel_id=1, source_target_pairs={{0,8},{8,0},{1,9},{9,1},{2,10},{10,2},{3,11},{11,3},{16,24},{24,16... | collective-permute-start | bytes 1572872 | tf_op jit(solution)/shard_map/ppermute | solution.py:39
  2.1 1.1 %shard_map.49 = (bf16[2,16,2048]{2,1,0:T(8,128)(2,1)S(1)}, bf16[2,16,2048]{2,1,0:T(8,128)(2,1)S(1)}, bf16[2,16,2048]{2,1,0:T(8,128)(2,1)S(1)}, bf16[2,16,2048]{2,1,0:T(8,128)(2,1)S(1)}) custom-call(s32[1]{0:T(128)} %bitcast.2.place, bf16[16,16384]{1,0:T(8,128)(2,1)} %mine.1), custom_call_target="tpu_custom_call" | custom-call | tf_op jit(solution)/shard_map/pallas_call | solution.py:76
  4.0 1.8 %collective-permute-start.1 = (bf16[2,2,16,2048]{3,2,1,0:T(8,128)(2,1)S(1)}, bf16[2,2,16,2048]{3,2,1,0:T(8,128)(2,1)S(1)}, u32[]{:S(2)}, u32[]{:S(2)}) collective-permute-start(bf16[2,2,16,2048]{3,2,1,0:T(8,128)(2,1)S(1)} %get-tuple-element.51), channel_id=1, source_target_pairs={{0,16},{8,9},{1,17},{9,10},{2,18},{10,11},{3,19},{11,8},{16,32},{2... | collective-permute-start | bytes 786440 | tf_op jit(solution)/shard_map/ppermute | solution.py:39
  5.7 2.2 %collective-permute-start.2 = (bf16[2,2,16,2048]{3,2,1,0:T(8,128)(2,1)S(1)}, bf16[2,2,16,2048]{3,2,1,0:T(8,128)(2,1)S(1)}, u32[]{:S(2)}, u32[]{:S(2)}) collective-permute-start(bf16[2,2,16,2048]{3,2,1,0:T(8,128)(2,1)S(1)} %get-tuple-element.52), channel_id=1, source_target_pairs={{0,48},{8,11},{1,49},{9,8},{2,50},{10,9},{3,51},{11,10},{16,0},{24... | collective-permute-start | bytes 786440 | tf_op jit(solution)/shard_map/ppermute | solution.py:39
  7.9 1.2 %collective-permute-start.3 = (bf16[2,2,16,2048]{3,2,1,0:T(8,128)(2,1)S(1)}, bf16[2,2,16,2048]{3,2,1,0:T(8,128)(2,1)S(1)}, u32[]{:S(2)}, u32[]{:S(2)}) collective-permute-start(bf16[2,2,16,2048]{3,2,1,0:T(8,128)(2,1)S(1)} %get-tuple-element.53), channel_id=1, source_target_pairs={{0,32},{8,10},{1,33},{9,11},{2,34},{10,8},{3,35},{11,9},{16,48},{2... | collective-permute-start | bytes 786440 | tf_op jit(solution)/shard_map/ppermute | solution.py:39
  9.2 2.5 %collective-permute-done.1.refs_1_ = bf16[2,2,16,2048]{3,2,1,0:T(8,128)(2,1)S(1)} collective-permute-done((bf16[2,2,16,2048]{3,2,1,0:T(8,128)(2,1)S(1)}, bf16[2,2,16,2048]{3,2,1,0:T(8,128)(2,1)S(1)}, u32[]{:S(2)}, u32[]{:S(2)}) %collective-permute-start.1) | collective-permute-done | bytes 262176 | tf_op jit(solution)/shard_map/ppermute | solution.py:39
  11.6 2.4 %collective-permute-done.2.refs_2_ = bf16[2,2,16,2048]{3,2,1,0:T(8,128)(2,1)S(1)} collective-permute-done((bf16[2,2,16,2048]{3,2,1,0:T(8,128)(2,1)S(1)}, bf16[2,2,16,2048]{3,2,1,0:T(8,128)(2,1)S(1)}, u32[]{:S(2)}, u32[]{:S(2)}) %collective-permute-start.2) | collective-permute-done | bytes 262176 | tf_op jit(solution)/shard_map/ppermute | solution.py:39
  14.1 1.6 %collective-permute-done.3.refs_3_ = bf16[2,2,16,2048]{3,2,1,0:T(8,128)(2,1)S(1)} collective-permute-done((bf16[2,2,16,2048]{3,2,1,0:T(8,128)(2,1)S(1)}, bf16[2,2,16,2048]{3,2,1,0:T(8,128)(2,1)S(1)}, u32[]{:S(2)}, u32[]{:S(2)}) %collective-permute-start.3) | collective-permute-done | bytes 262176 | tf_op jit(solution)/shard_map/ppermute | solution.py:39
  15.9 1.3 %collective-permute-start.4 = (bf16[2,4,16,2048]{3,2,1,0:T(8,128)(2,1)S(1)}, bf16[2,4,16,2048]{3,2,1,0:T(8,128)(2,1)S(1)}, u32[]{:S(2)}, u32[]{:S(2)}) collective-permute-start(bf16[2,4,16,2048]{3,2,1,0:T(8,128)(2,1)S(1)} %get-tuple-element.55), channel_id=1, source_target_pairs={{0,4},{8,12},{1,5},{9,13},{2,6},{10,14},{3,7},{11,15},{16,20},{24,... | collective-permute-start | bytes 1572872 | tf_op jit(solution)/shard_map/ppermute | solution.py:39
  17.1 1.8 %collective-permute-start.5 = (bf16[2,4,16,2048]{3,2,1,0:T(8,128)(2,1)S(1)}, bf16[2,4,16,2048]{3,2,1,0:T(8,128)(2,1)S(1)}, u32[]{:S(2)}, u32[]{:S(2)}) collective-permute-start(bf16[2,4,16,2048]{3,2,1,0:T(8,128)(2,1)S(1)} %get-tuple-element.56), channel_id=1, source_target_pairs={{0,68},{8,76},{1,69},{9,77},{2,70},{10,78},{3,71},{11,79},{16,84},... | collective-permute-start | bytes 1572872 | tf_op jit(solution)/shard_map/ppermute | solution.py:39
  19.0 2.6 %collective-permute-start.7 = (bf16[2,4,16,2048]{3,2,1,0:T(8,128)(2,1)S(1)}, bf16[2,4,16,2048]{3,2,1,0:T(8,128)(2,1)S(1)}, u32[]{:S(2)}, u32[]{:S(2)}) collective-permute-start(bf16[2,4,16,2048]{3,2,1,0:T(8,128)(2,1)S(1)} %get-tuple-element.54.refs_0_), channel_id=1, source_target_pairs={{0,3},{8,56},{1,0},{9,57},{2,1},{10,58},{3,2},{11,59},{16,19},{24,... | collective-permute-start | bytes 1572872 | tf_op jit(solution)/shard_map/ppermute | solution.py:39
  21.6 7.5 %collective-permute-done.4.refs_3_.refs_0_ = bf16[2,4,16,2048]{3,2,1,0:T(8,128)(2,1)S(1)} collective-permute-done((bf16[2,4,16,2048]{3,2,1,0:T(8,128)(2,1)S(1)}, bf16[2,4,16,2048]{3,2,1,0:T(8,128)(2,1)S(1)}, u32[]{:S(2)}, u32[]{:S(2)}) %collective-permute-start.4) | collective-permute-done | bytes 524320 | tf_op jit(solution)/shard_map/ppermute | solution.py:39
  29.0 2.1 %collective-permute-done.5.refs_4_.refs_1_ = bf16[2,4,16,2048]{3,2,1,0:T(8,128)(2,1)S(1)} collective-permute-done((bf16[2,4,16,2048]{3,2,1,0:T(8,128)(2,1)S(1)}, bf16[2,4,16,2048]{3,2,1,0:T(8,128)(2,1)S(1)}, u32[]{:S(2)}, u32[]{:S(2)}) %collective-permute-start.5) | collective-permute-done | bytes 524320 | tf_op jit(solution)/shard_map/ppermute | solution.py:39
  31.3 3.3 %collective-permute-start.11 = (bf16[5,2,4,16,2048]{4,3,2,1,0:T(8,128)(2,1)S(1)}, bf16[5,2,4,16,2048]{4,3,2,1,0:T(8,128)(2,1)S(1)}, u32[]{:S(2)}, u32[]{:S(2)}) collective-permute-start(bf16[5,2,4,16,2048]{4,3,2,1,0:T(8,128)(2,1)S(1)} %bitcast.8), channel_id=1, source_target_pairs={{0,8},{8,0},{1,9},{9,1},{2,10},{10,2},{3,11},{11,3},{16,24},{24,16... | collective-permute-start | bytes 7864328 | tf_op jit(solution)/shard_map/ppermute | solution.py:39
  34.8 1.2 %collective-permute-start.9 = (bf16[5,4,16,2048]{3,2,1,0:T(8,128)(2,1)S(1)}, bf16[5,4,16,2048]{3,2,1,0:T(8,128)(2,1)S(1)}, u32[]{:S(2)}, u32[]{:S(2)}) collective-permute-start(bf16[5,4,16,2048]{3,2,1,0:T(8,128)(2,1)S(1)} %get-tuple-element.63), channel_id=1, source_target_pairs={{0,1},{8,24},{1,2},{9,25},{2,3},{10,26},{3,0},{11,27},{16,17},{24,... | collective-permute-start | bytes 3932168 | tf_op jit(solution)/shard_map/ppermute | solution.py:39
  36.0 1.5 %collective-permute-start.10 = (bf16[5,4,16,2048]{3,2,1,0:T(8,128)(2,1)S(1)}, bf16[5,4,16,2048]{3,2,1,0:T(8,128)(2,1)S(1)}, u32[]{:S(2)}, u32[]{:S(2)}) collective-permute-start(bf16[5,4,16,2048]{3,2,1,0:T(8,128)(2,1)S(1)} %get-tuple-element.64), channel_id=1, source_target_pairs={{0,3},{8,56},{1,0},{9,57},{2,1},{10,58},{3,2},{11,59},{16,19},{24,... | collective-permute-start | bytes 3932168 | tf_op jit(solution)/shard_map/ppermute | solution.py:39
  37.9 1.3 %collective-permute-done.11.recv.refs_2_.refs_3_ = bf16[5,2,4,16,2048]{4,3,2,1,0:T(8,128)(2,1)S(1)} collective-permute-done((bf16[5,2,4,16,2048]{4,3,2,1,0:T(8,128)(2,1)S(1)}, bf16[5,2,4,16,2048]{4,3,2,1,0:T(8,128)(2,1)S(1)}, u32[]{:S(2)}, u32[]{:S(2)}) %collective-permute-start.11) | collective-permute-done | bytes 2621472 | tf_op jit(solution)/shard_map/ppermute | solution.py:39
  39.2 2.3 %shard_map.54 = (f32[256,640]{1,0:T(8,128)S(1)}, f32[256,128]{1,0:T(8,128)S(1)}, bf16[2048,512]{1,0:T(8,128)(2,1)S(1)}) custom-call(s32[1]{0:T(128)} %bitcast.core.at, bf16[5,2,4,16,2048]{4,3,2,1,0:T(8,128)(2,1)S(1)} %bitcast.9, bf16[5,2,4,16,2048]{4,3,2,1,0:T(8,128)(2,1)S(1)} %collective-permute-done.11.recv.refs_2_.refs_3_, f32[2048,256]{1,0:T(8,128)S(1)} %copy-done.6), custom_call_target="tpu_custom_call" | custom-call | flops 1073741824 | bytes 1048576 | tf_op jit(solution)/shard_map/pallas_call | solution.py:231
  41.5 10.5 %collective-permute-done.8.refs_2_ = bf16[2,4,16,2048]{3,2,1,0:T(8,128)(2,1)S(1)} collective-permute-done((bf16[2,4,16,2048]{3,2,1,0:T(8,128)(2,1)S(1)}, bf16[2,4,16,2048]{3,2,1,0:T(8,128)(2,1)S(1)}, u32[]{:S(2)}, u32[]{:S(2)}) %collective-permute-start.8) | collective-permute-done | bytes 524320 | tf_op jit(solution)/shard_map/ppermute | solution.py:39
  51.9 0.9 collective-permute-done.9.refs_0_
  53.0 1.0 collective-permute-start.15
  54.1 1.2 %collective-permute-start.12 = (bf16[4,4,16,2048]{3,2,1,0:T(8,128)(2,1)S(1)}, bf16[4,4,16,2048]{3,2,1,0:T(8,128)(2,1)S(1)}, u32[]{:S(2)}, u32[]{:S(2)}) collective-permute-start(bf16[4,4,16,2048]{3,2,1,0:T(8,128)(2,1)S(1)} %get-tuple-element.70), channel_id=1, source_target_pairs={{0,1},{8,24},{1,2},{9,25},{2,3},{10,26},{3,0},{11,27},{16,17},{24,... | collective-permute-start | bytes 3145736 | tf_op jit(solution)/shard_map/ppermute | solution.py:39
  55.3 1.5 %collective-permute-start.13 = (bf16[4,4,16,2048]{3,2,1,0:T(8,128)(2,1)S(1)}, bf16[4,4,16,2048]{3,2,1,0:T(8,128)(2,1)S(1)}, u32[]{:S(2)}, u32[]{:S(2)}) collective-permute-start(bf16[4,4,16,2048]{3,2,1,0:T(8,128)(2,1)S(1)} %get-tuple-element.71), channel_id=1, source_target_pairs={{0,3},{8,56},{1,0},{9,57},{2,1},{10,58},{3,2},{11,59},{16,19},{24,... | collective-permute-start | bytes 3145736 | tf_op jit(solution)/shard_map/ppermute | solution.py:39
  57.2 2.1 %collective-permute-done.15.refs_3_.refs_4_ = bf16[6,2,4,16,2048]{4,3,2,1,0:T(8,128)(2,1)S(1)} collective-permute-done((bf16[6,2,4,16,2048]{4,3,2,1,0:T(8,128)(2,1)S(1)}, bf16[6,2,4,16,2048]{4,3,2,1,0:T(8,128)(2,1)S(1)}, u32[]{:S(2)}, u32[]{:S(2)}) %collective-permute-start.15) | collective-permute-done | bytes 3145760 | tf_op jit(solution)/shard_map/ppermute | solution.py:39
  59.3 7.1 %shard_map.57 = (f32[256,768]{1,0:T(8,128)S(1)}, f32[256,1024]{1,0:T(8,128)S(1)}, f32[1,1024]{1,0:T(1,128)S(1)}, bf16[528,256]{1,0:T(8,128)(2,1)S(1)}) custom-call(s32[1]{0:T(128)} %bitcast.core.at, bf16[5,2,4,16,2048]{4,3,2,1,0:T(8,128)(2,1)S(1)} %bitcast.10, bf16[6,2,4,16,2048]{4,3,2,1,0:T(8,128)(2,1)S(1)} %bitcast.14, ...), custom_call_target="tpu_custom_call" | custom-call | flops 2147483648 | bytes 1048576 | tf_op jit(solution)/shard_map/pallas_call | solution.py:294
  66.4 8.8 %collective-permute-done.14.refs_2_ = bf16[2,4,16,2048]{3,2,1,0:T(8,128)(2,1)S(1)} collective-permute-done((bf16[2,4,16,2048]{3,2,1,0:T(8,128)(2,1)S(1)}, bf16[2,4,16,2048]{3,2,1,0:T(8,128)(2,1)S(1)}, u32[]{:S(2)}, u32[]{:S(2)}) %collective-permute-start.14) | collective-permute-done | bytes 524320 | tf_op jit(solution)/shard_map/ppermute | solution.py:39
  75.4 2.2 %collective-permute-start.16 = (bf16[5,2,4,16,2048]{4,3,2,1,0:T(8,128)(2,1)S(1)}, bf16[5,2,4,16,2048]{4,3,2,1,0:T(8,128)(2,1)S(1)}, u32[]{:S(2)}, u32[]{:S(2)}) collective-permute-start(bf16[5,2,4,16,2048]{4,3,2,1,0:T(8,128)(2,1)S(1)} %bitcast.17), channel_id=1, source_target_pairs={{0,8},{8,0},{1,9},{9,1},{2,10},{10,2},{3,11},{11,3},{16,24},{24,16... | collective-permute-start | bytes 7864328 | tf_op jit(solution)/shard_map/ppermute | solution.py:39
  77.6 1.6 %shard_map.59.refs_12_ = f32[256,640]{1,0:T(8,128)S(1)} custom-call(bf16[5,2,4,16,2048]{4,3,2,1,0:T(8,128)(2,1)S(1)} %bitcast.18, bf16[2048,512]{1,0:T(8,128)(2,1)S(1)} %get-tuple-element.72.refs_4_.comps), custom_call_target="tpu_custom_call" | custom-call | flops 1073741824 | bytes 1048576 | tf_op jit(solution)/shard_map/pallas_call | solution.py:318
  79.3 3.8 %collective-permute-done.17.refs_13_ = f32[256,640]{1,0:T(8,128)S(1)} collective-permute-done((f32[256,640]{1,0:T(8,128)S(1)}, f32[256,640]{1,0:T(8,128)S(1)}, u32[]{:S(2)}, u32[]{:S(2)}) %collective-permute-start.17) | collective-permute-done | bytes 655392 | tf_op jit(solution)/shard_map/ppermute | solution.py:39
  83.1 2.9 %shard_map.60 = (f32[8,256,128]{2,1,0:T(8,128)}, f32[1,1024]{1,0:T(1,128)S(1)}, f32[1,128]{1,0:T(1,128)}) custom-call(s32[1]{0:T(128)} %bitcast.core.at, s32[1]{0:T(128)} %bitcast.6.column, bf16[5,2,4,16,2048]{4,3,2,1,0:T(8,128)(2,1)S(1)} %bitcast.11, bf16[6,2,4,16,2048]{4,3,2,1,0:T(8,128)(2,1)S(1)} %bitcast.15, bf16[5,2,4,16,2048]{4,3,2,1,0:T(8,128)(2,1)S(1)} %bitcast.19, ...), custom_call_target="tpu_custom_call" | custom-call | flops 4294967296 | bytes 4194304 | tf_op jit(solution)/shard_map/pallas_call | solution.py:372
  86.0 3.6 %all-to-all-start = ((f32[8,256,128]{2,1,0:T(8,128)}), f32[8,256,128]{2,1,0:T(8,128)S(1)}, u32[]{:S(2)}, u32[]{:S(2)}) async-start(f32[8,256,128]{2,1,0:T(8,128)} %get-tuple-element.87), calls=%async_computation | async-start | bytes 2097152 | tf_op jit(solution)/shard_map/all_to_all | solution.py:512
  89.6 14.6 %shard_map.61 = f32[1024,2048]{1,0:T(8,128)} custom-call(s32[1]{0:T(128)} %bitcast.core.at, bf16[5,2,4,16,2048]{4,3,2,1,0:T(8,128)(2,1)} %bitcast.12, bf16[6,2,4,16,2048]{4,3,2,1,0:T(8,128)(2,1)} %bitcast.16, bf16[5,2,4,16,2048]{4,3,2,1,0:T(8,128)(2,1)} %bitcast.20, bf16[5,2,4,16,2048]{4,3,2,1,0:T(8,128)(2,1)} %copy-done.3, ...), custom_call_target="tpu_custom_call" | custom-call | flops 8589934592 | bytes 20971520 | tf_op jit(solution)/shard_map/pallas_call | solution.py:432
  (34 shorter events, 3.6 us)
Async XLA Ops:
  0.6 3.2 %collective-permute-start = (bf16[16,16384]{1,0:T(8,128)(2,1)}, bf16[16,16384]{1,0:T(8,128)(2,1)S(1)}, u32[]{:S(2)}, u32[]{:S(2)}) collective-permute-start(bf16[16,16384]{1,0:T(8,128)(2,1)} %mine.1), channel_id=1, source_target_pairs={{0,8},{8,0},{1,9},{9,1},{2,10},{10,2},{3,11},{11,3},{16,24},{24,16... | collective-permute-start | bytes 1572872 | tf_op jit(solution)/shard_map/ppermute | solution.py:39
  4.0 7.7 %collective-permute-start.1 = (bf16[2,2,16,2048]{3,2,1,0:T(8,128)(2,1)S(1)}, bf16[2,2,16,2048]{3,2,1,0:T(8,128)(2,1)S(1)}, u32[]{:S(2)}, u32[]{:S(2)}) collective-permute-start(bf16[2,2,16,2048]{3,2,1,0:T(8,128)(2,1)S(1)} %get-tuple-element.51), channel_id=1, source_target_pairs={{0,16},{8,9},{1,17},{9,10},{2,18},{10,11},{3,19},{11,8},{16,32},{2... | collective-permute-start | bytes 786440 | tf_op jit(solution)/shard_map/ppermute | solution.py:39
  5.7 8.3 %collective-permute-start.2 = (bf16[2,2,16,2048]{3,2,1,0:T(8,128)(2,1)S(1)}, bf16[2,2,16,2048]{3,2,1,0:T(8,128)(2,1)S(1)}, u32[]{:S(2)}, u32[]{:S(2)}) collective-permute-start(bf16[2,2,16,2048]{3,2,1,0:T(8,128)(2,1)S(1)} %get-tuple-element.52), channel_id=1, source_target_pairs={{0,48},{8,11},{1,49},{9,8},{2,50},{10,9},{3,51},{11,10},{16,0},{24... | collective-permute-start | bytes 786440 | tf_op jit(solution)/shard_map/ppermute | solution.py:39
  7.9 7.8 %collective-permute-start.3 = (bf16[2,2,16,2048]{3,2,1,0:T(8,128)(2,1)S(1)}, bf16[2,2,16,2048]{3,2,1,0:T(8,128)(2,1)S(1)}, u32[]{:S(2)}, u32[]{:S(2)}) collective-permute-start(bf16[2,2,16,2048]{3,2,1,0:T(8,128)(2,1)S(1)} %get-tuple-element.53), channel_id=1, source_target_pairs={{0,32},{8,10},{1,33},{9,11},{2,34},{10,8},{3,35},{11,9},{16,48},{2... | collective-permute-start | bytes 786440 | tf_op jit(solution)/shard_map/ppermute | solution.py:39
  15.9 13.2 %collective-permute-start.4 = (bf16[2,4,16,2048]{3,2,1,0:T(8,128)(2,1)S(1)}, bf16[2,4,16,2048]{3,2,1,0:T(8,128)(2,1)S(1)}, u32[]{:S(2)}, u32[]{:S(2)}) collective-permute-start(bf16[2,4,16,2048]{3,2,1,0:T(8,128)(2,1)S(1)} %get-tuple-element.55), channel_id=1, source_target_pairs={{0,4},{8,12},{1,5},{9,13},{2,6},{10,14},{3,7},{11,15},{16,20},{24,... | collective-permute-start | bytes 1572872 | tf_op jit(solution)/shard_map/ppermute | solution.py:39
  17.1 14.0 %collective-permute-start.5 = (bf16[2,4,16,2048]{3,2,1,0:T(8,128)(2,1)S(1)}, bf16[2,4,16,2048]{3,2,1,0:T(8,128)(2,1)S(1)}, u32[]{:S(2)}, u32[]{:S(2)}) collective-permute-start(bf16[2,4,16,2048]{3,2,1,0:T(8,128)(2,1)S(1)} %get-tuple-element.56), channel_id=1, source_target_pairs={{0,68},{8,76},{1,69},{9,77},{2,70},{10,78},{3,71},{11,79},{16,84},... | collective-permute-start | bytes 1572872 | tf_op jit(solution)/shard_map/ppermute | solution.py:39
  19.0 12.2 %collective-permute-start.7 = (bf16[2,4,16,2048]{3,2,1,0:T(8,128)(2,1)S(1)}, bf16[2,4,16,2048]{3,2,1,0:T(8,128)(2,1)S(1)}, u32[]{:S(2)}, u32[]{:S(2)}) collective-permute-start(bf16[2,4,16,2048]{3,2,1,0:T(8,128)(2,1)S(1)} %get-tuple-element.54.refs_0_), channel_id=1, source_target_pairs={{0,3},{8,56},{1,0},{9,57},{2,1},{10,58},{3,2},{11,59},{16,19},{24,... | collective-permute-start | bytes 1572872 | tf_op jit(solution)/shard_map/ppermute | solution.py:39
  21.6 9.6 %collective-permute-start.6 = (bf16[2,4,16,2048]{3,2,1,0:T(8,128)(2,1)S(1)}, bf16[2,4,16,2048]{3,2,1,0:T(8,128)(2,1)S(1)}, u32[]{:S(2)}, u32[]{:S(2)}) collective-permute-start(bf16[2,4,16,2048]{3,2,1,0:T(8,128)(2,1)S(1)} %get-tuple-element.54.refs_0_), channel_id=1, source_target_pairs={{0,1},{8,24},{1,2},{9,25},{2,3},{10,26},{3,0},{11,27},{16,17},{24,... | collective-permute-start | bytes 1572872 | tf_op jit(solution)/shard_map/ppermute | solution.py:39
  31.2 8.0 %copy-start.6 = (f32[2048,256]{1,0:T(8,128)S(1)}, f32[2048,256]{1,0:T(8,128)}, u32[]{:S(2)}) copy-start(f32[2048,256]{1,0:T(8,128)} %components.1) | copy-start | bytes 6291460
  31.3 51.7 %copy-start = (bf16[10,4,16,2048]{3,2,1,0:T(8,128)(2,1)}, bf16[10,4,16,2048]{3,2,1,0:T(8,128)(2,1)S(1)}, u32[]{:S(2)}) copy-start(bf16[10,4,16,2048]{3,2,1,0:T(8,128)(2,1)S(1)} %shard_map.52) | copy-start | bytes 7864324
  31.3 7.8 %collective-permute-start.11 = (bf16[5,2,4,16,2048]{4,3,2,1,0:T(8,128)(2,1)S(1)}, bf16[5,2,4,16,2048]{4,3,2,1,0:T(8,128)(2,1)S(1)}, u32[]{:S(2)}, u32[]{:S(2)}) collective-permute-start(bf16[5,2,4,16,2048]{4,3,2,1,0:T(8,128)(2,1)S(1)} %bitcast.8), channel_id=1, source_target_pairs={{0,8},{8,0},{1,9},{9,1},{2,10},{10,2},{3,11},{11,3},{16,24},{24,16... | collective-permute-start | bytes 7864328 | tf_op jit(solution)/shard_map/ppermute | solution.py:39
  34.8 18.0 %collective-permute-start.9 = (bf16[5,4,16,2048]{3,2,1,0:T(8,128)(2,1)S(1)}, bf16[5,4,16,2048]{3,2,1,0:T(8,128)(2,1)S(1)}, u32[]{:S(2)}, u32[]{:S(2)}) collective-permute-start(bf16[5,4,16,2048]{3,2,1,0:T(8,128)(2,1)S(1)} %get-tuple-element.63), channel_id=1, source_target_pairs={{0,1},{8,24},{1,2},{9,25},{2,3},{10,26},{3,0},{11,27},{16,17},{24,... | collective-permute-start | bytes 3932168 | tf_op jit(solution)/shard_map/ppermute | solution.py:39
  36.0 16.8 %collective-permute-start.10 = (bf16[5,4,16,2048]{3,2,1,0:T(8,128)(2,1)S(1)}, bf16[5,4,16,2048]{3,2,1,0:T(8,128)(2,1)S(1)}, u32[]{:S(2)}, u32[]{:S(2)}) collective-permute-start(bf16[5,4,16,2048]{3,2,1,0:T(8,128)(2,1)S(1)} %get-tuple-element.64), channel_id=1, source_target_pairs={{0,3},{8,56},{1,0},{9,57},{2,1},{10,58},{3,2},{11,59},{16,19},{24,... | collective-permute-start | bytes 3932168 | tf_op jit(solution)/shard_map/ppermute | solution.py:39
  37.5 14.4 %collective-permute-start.8 = (bf16[2,4,16,2048]{3,2,1,0:T(8,128)(2,1)S(1)}, bf16[2,4,16,2048]{3,2,1,0:T(8,128)(2,1)S(1)}, u32[]{:S(2)}, u32[]{:S(2)}) collective-permute-start(bf16[2,4,16,2048]{3,2,1,0:T(8,128)(2,1)S(1)} %get-tuple-element.62), channel_id=1, source_target_pairs={{0,64},{8,72},{1,65},{9,73},{2,66},{10,74},{3,67},{11,75},{16,80},... | collective-permute-start | bytes 1572872 | tf_op jit(solution)/shard_map/ppermute | solution.py:39
  39.2 43.9 %copy-start.3 = (bf16[5,2,4,16,2048]{4,3,2,1,0:T(8,128)(2,1)}, bf16[5,2,4,16,2048]{4,3,2,1,0:T(8,128)(2,1)S(1)}, u32[]{:S(2)}) copy-start(bf16[5,2,4,16,2048]{4,3,2,1,0:T(8,128)(2,1)S(1)} %collective-permute-done.11.recv.refs_2_.refs_3_) | copy-start | bytes 7864324
  53.0 30.0 %copy-start.1 = (bf16[12,4,16,2048]{3,2,1,0:T(8,128)(2,1)}, bf16[12,4,16,2048]{3,2,1,0:T(8,128)(2,1)S(1)}, u32[]{:S(2)}) copy-start(bf16[12,4,16,2048]{3,2,1,0:T(8,128)(2,1)S(1)} %shard_map.55) | copy-start | bytes 9437188
  53.0 6.2 %collective-permute-start.15 = (bf16[6,2,4,16,2048]{4,3,2,1,0:T(8,128)(2,1)S(1)}, bf16[6,2,4,16,2048]{4,3,2,1,0:T(8,128)(2,1)S(1)}, u32[]{:S(2)}, u32[]{:S(2)}) collective-permute-start(bf16[6,2,4,16,2048]{4,3,2,1,0:T(8,128)(2,1)S(1)} %bitcast.13), channel_id=1, source_target_pairs={{0,8},{8,0},{1,9},{9,1},{2,10},{10,2},{3,11},{11,3},{16,24},{24,16... | collective-permute-start | bytes 9437192 | tf_op jit(solution)/shard_map/ppermute | solution.py:39
  54.1 21.1 %collective-permute-start.12 = (bf16[4,4,16,2048]{3,2,1,0:T(8,128)(2,1)S(1)}, bf16[4,4,16,2048]{3,2,1,0:T(8,128)(2,1)S(1)}, u32[]{:S(2)}, u32[]{:S(2)}) collective-permute-start(bf16[4,4,16,2048]{3,2,1,0:T(8,128)(2,1)S(1)} %get-tuple-element.70), channel_id=1, source_target_pairs={{0,1},{8,24},{1,2},{9,25},{2,3},{10,26},{3,0},{11,27},{16,17},{24,... | collective-permute-start | bytes 3145736 | tf_op jit(solution)/shard_map/ppermute | solution.py:39
  55.3 19.9 %collective-permute-start.13 = (bf16[4,4,16,2048]{3,2,1,0:T(8,128)(2,1)S(1)}, bf16[4,4,16,2048]{3,2,1,0:T(8,128)(2,1)S(1)}, u32[]{:S(2)}, u32[]{:S(2)}) collective-permute-start(bf16[4,4,16,2048]{3,2,1,0:T(8,128)(2,1)S(1)} %get-tuple-element.71), channel_id=1, source_target_pairs={{0,3},{8,56},{1,0},{9,57},{2,1},{10,58},{3,2},{11,59},{16,19},{24,... | collective-permute-start | bytes 3145736 | tf_op jit(solution)/shard_map/ppermute | solution.py:39
  56.9 18.3 %collective-permute-start.14 = (bf16[2,4,16,2048]{3,2,1,0:T(8,128)(2,1)S(1)}, bf16[2,4,16,2048]{3,2,1,0:T(8,128)(2,1)S(1)}, u32[]{:S(2)}, u32[]{:S(2)}) collective-permute-start(bf16[2,4,16,2048]{3,2,1,0:T(8,128)(2,1)S(1)} %collective-permute-done.8.refs_2_), channel_id=1, source_target_pairs={{0,2},{8,40},{1,3},{9,41},{2,0},{10,42},{3,1},{11,43},{16,18},{24,... | collective-permute-start | bytes 1572872 | tf_op jit(solution)/shard_map/ppermute | solution.py:39
  59.3 23.8 %copy-start.4 = (bf16[6,2,4,16,2048]{4,3,2,1,0:T(8,128)(2,1)}, bf16[6,2,4,16,2048]{4,3,2,1,0:T(8,128)(2,1)S(1)}, u32[]{:S(2)}) copy-start(bf16[6,2,4,16,2048]{4,3,2,1,0:T(8,128)(2,1)S(1)} %collective-permute-done.15.refs_3_.refs_4_) | copy-start | bytes 9437188
  75.4 7.7 %copy-start.2 = (bf16[10,4,16,2048]{3,2,1,0:T(8,128)(2,1)}, bf16[10,4,16,2048]{3,2,1,0:T(8,128)(2,1)S(1)}, u32[]{:S(2)}) copy-start(bf16[10,4,16,2048]{3,2,1,0:T(8,128)(2,1)S(1)} %shard_map.58) | copy-start | bytes 7864324
  75.4 7.7 %collective-permute-start.16 = (bf16[5,2,4,16,2048]{4,3,2,1,0:T(8,128)(2,1)S(1)}, bf16[5,2,4,16,2048]{4,3,2,1,0:T(8,128)(2,1)S(1)}, u32[]{:S(2)}, u32[]{:S(2)}) collective-permute-start(bf16[5,2,4,16,2048]{4,3,2,1,0:T(8,128)(2,1)S(1)} %bitcast.17), channel_id=1, source_target_pairs={{0,8},{8,0},{1,9},{9,1},{2,10},{10,2},{3,11},{11,3},{16,24},{24,16... | collective-permute-start | bytes 7864328 | tf_op jit(solution)/shard_map/ppermute | solution.py:39
  79.2 3.9 %collective-permute-start.17 = (f32[256,640]{1,0:T(8,128)S(1)}, f32[256,640]{1,0:T(8,128)S(1)}, u32[]{:S(2)}, u32[]{:S(2)}) collective-permute-start(f32[256,640]{1,0:T(8,128)S(1)} %shard_map.59.refs_12_), channel_id=1, source_target_pairs={{0,8},{8,0},{1,9},{9,1},{2,10},{10,2},{3,11},{11,3},{16,24},{24,16... | collective-permute-start | bytes 1966088 | tf_op jit(solution)/shard_map/ppermute | solution.py:39
  83.1 3.0 %copy-start.5 = (bf16[5,2,4,16,2048]{4,3,2,1,0:T(8,128)(2,1)}, bf16[5,2,4,16,2048]{4,3,2,1,0:T(8,128)(2,1)S(1)}, u32[]{:S(2)}) copy-start(bf16[5,2,4,16,2048]{4,3,2,1,0:T(8,128)(2,1)S(1)} %collective-permute-done.16.refs_5_) | copy-start | bytes 7864324
  86.0 18.5 %all-to-all-start = ((f32[8,256,128]{2,1,0:T(8,128)}), f32[8,256,128]{2,1,0:T(8,128)S(1)}, u32[]{:S(2)}, u32[]{:S(2)}) async-start(f32[8,256,128]{2,1,0:T(8,128)} %get-tuple-element.87), calls=%async_computation | async-start | bytes 2097152 | tf_op jit(solution)/shard_map/all_to_all | solution.py:512
